TPU v7x, 128 devices: a whole 4x4x4 slice. The times are simulated.
128 devices in a mesh: gx: 8 (over x, y_lo), gy: 16 (over y_hi, z, core).
Axes of the slice: x: 4, y: 4 (y_hi: 2, y_lo: 2; y = y_hi * 2 + y_lo), z: 4, core: 2. Of those that a mesh axis runs over, the one named last changes fastest.
Arguments:
- right_side: float32 [70, 192, 2048], P(None, 'gx', 'gy'), may hold values from -6 to 6
- helm_coef: float32 [70, 192, 2048], P(None, 'gx', 'gy'), may hold values from 0.5 to 4
- vert_coef: float32 [71], replicated, may hold values from 1 to 10
- block_inverse: float32 [4, 5, 14, 14], replicated, may hold values from -0.1 to 0.45, as said below
- edge_flip: int32 [8, 16, 4], P('gx', 'gy'), may hold values 0 or 1
Outputs:
- correction: float32 [70, 192, 2048], P(None, 'gx', 'gy')
Inputs may be any that keep to these rules, and one draw needn't show every extreme that they name: `block_inverse`: each block's diagonal entries are positive and larger than the off-diagonal ones.
All inputs are finite; a program needn't handle non-finite values. No bound on the sum of `edge_flip` on one device may be relied on, other than what follows from the above.
Results may differ from a plain program's by a relative error of at most 0.0001.
Values sent between devices are 32-bit elements; how exact they have to be, the bound alone decides.
No kernel may reach another device: no remote copies, remote signals or barrier semaphores. Data moves between devices by JAX's collectives and lax.ppermute only.
A program may use at most 128 MiB of HBM per device.

v0:
```python
import jax
import jax.numpy as jnp
from jax import lax
from jax.experimental import pallas as pl
from jax.experimental.pallas import tpu as pltpu
from jax.sharding import PartitionSpec as P

BLK = 14
NBLK = 5
NZ = 70
Z = 72
LANES = 128
F32 = jnp.float32
BF16 = jnp.bfloat16

GEOM = ((24, 1, 128), (6, 2, 64), (6, 1, 32), (3, 1, 16))


def lane_ids(shape):
    return lax.broadcasted_iota(jnp.int32, shape, len(shape) - 1)


def zl():
    return lane_ids((Z, LANES))


def roll(x, shift):
    shift = shift % x.shape[-1]
    return x if shift == 0 else pltpu.roll(x, shift, axis=1)


def col(x, k):
    return jnp.broadcast_to(x[:, k : k + 1], (Z, LANES))


def iota2(n, m):
    return lax.broadcasted_iota(jnp.int32, (n, m), 0), lax.broadcasted_iota(jnp.int32, (n, m), 1)


def lane_dot(x, mat):
    hi = x.astype(BF16).astype(F32)
    both = jnp.concatenate([hi, x - hi], axis=1).astype(BF16)
    twice = jnp.concatenate([mat, mat], axis=0).astype(BF16)
    return jnp.dot(both, twice, preferred_element_type=F32)


def block_dot(winv, x):
    hi = x.astype(BF16).astype(F32)
    parts = jnp.concatenate([hi, hi, x - hi], axis=0).astype(BF16)
    return jnp.dot(winv, parts, preferred_element_type=F32)


def reverse_matrix(width, blocks=(0,)):
    a, b = iota2(LANES, LANES)
    out = jnp.zeros((LANES, LANES), F32)
    for base in blocks:
        inside = (b >= base) & (b < base + width)
        out = jnp.where(inside & (a == 2 * base + width - 1 - b), 1.0, out)
    return out


def flag_row(flags, k):
    return jnp.broadcast_to(flags[k : k + 1, :], (Z, LANES))


class Coef:
    def __init__(self, ref):
        self.mid = jnp.broadcast_to(ref[:, 0:1], (Z, LANES))
        self.up = jnp.broadcast_to(ref[:, 1:2], (Z, LANES))
        self.down = jnp.broadcast_to(ref[:, 2:3], (Z, LANES))


def residual(co, f, c, v, beside):
    above = pltpu.roll(v, Z - 1, axis=0)
    below = pltpu.roll(v, 1, axis=0)
    return f - (c * 0.0625 + co.mid) * v + beside * 0.0625 + co.up * above + co.down * below


def row_of(geom, v, row):
    m_rows, _, ty = geom
    q, m = divmod(row, m_rows)
    return roll(v[m], -q * ty)


def corners(geom, v):
    m_rows, groups, ty = geom
    lane = zl()
    last = v[m_rows - 1]
    base = (groups - 1) * ty
    out = jnp.where(lane == 0, col(v[0], 0), 0.0)
    out = jnp.where(lane == 1, col(v[0], ty - 1), out)
    out = jnp.where(lane == 2, col(last, base), out)
    return jnp.where(lane == 3, col(last, base + ty - 1), out)


def place_col(geom, v, y, offset, out):
    m_rows, groups, ty = geom
    lane = zl()
    for m in range(m_rows):
        row = v[m]
        for q in range(groups):
            out = jnp.where(lane == offset + q * m_rows + m, col(row, q * ty + y), out)
    return out


def pack(geom, parts):
    ty = geom[2]
    per = LANES // ty
    out = []
    for first in range(0, len(parts), per):
        lane = zl()
        acc = parts[first]
        for k, part in enumerate(parts[first + 1 : first + per], 1):
            acc = jnp.where(lane < k * ty, acc, roll(part, k * ty))
        out.append(acc)
    return out


def packed(geom, count):
    per = LANES // geom[2]
    return -(-count // per)


def part_of(geom, ref, k):
    ty = geom[2]
    per = LANES // ty
    return roll(ref[(k // per) * Z : (k // per + 1) * Z, :], -(k % per) * ty)


def put_x(geom, v, c, up, down, flags=None):
    m_rows, groups, _ = geom
    tx = m_rows * groups
    extra = corners(geom, v)
    for ref, edge, second in ((up, tx - 1, tx - 2), (down, 0, 1)):
        parts = [row_of(geom, v, edge), row_of(geom, v, second)]
        if c is not None:
            parts.append(row_of(geom, c, edge))
        parts.append(extra)
        whole = pack(geom, parts)
        for k, part in enumerate(whole):
            ref[k * Z : (k + 1) * Z, :] = part
        if flags is not None:
            ref[len(whole) * Z : len(whole) * Z + 8, :] = flags


def put_y(geom, v, c, up, down):
    ty = geom[2]
    for ref, edge, second in ((up, ty - 1, ty - 2), (down, 0, 1)):
        out = place_col(geom, v, edge, 0, jnp.zeros((Z, LANES), F32))
        out = place_col(geom, v, second, 32, out)
        if c is not None:
            out = place_col(geom, c, edge, 64, out)
        ref[0:Z, :] = out


def merge_y(lo_extra, hi_extra, flags, up, down):
    lane = zl()
    f0, f1 = flag_row(flags, 0) > 0.5, flag_row(flags, 1) > 0.5

    def fill(part, values):
        for k, value in enumerate(values):
            part = jnp.where(lane == 96 + k, value, part)
        return part

    lo = [col(lo_extra, k) for k in range(4)]
    hi = [col(hi_extra, k) for k in range(4)]
    up_new = fill(up, [lo[3], lo[1], hi[1], hi[3], jnp.where(f0, lo[2], lo[3]), jnp.where(f1, hi[0], hi[1])])
    down_new = fill(down, [lo[2], lo[0], hi[0], hi[2], jnp.where(f0, lo[3], lo[2]), jnp.where(f1, hi[1], hi[0])])
    return up_new, down_new


class Halo:
    def __init__(self, lo, lo2, hi, hi2, dn, un):
        self.lo, self.lo2, self.hi, self.hi2, self.dn, self.un = lo, lo2, hi, hi2, dn, un

    def sides(self):
        return jnp.where(zl() < 64, self.dn, roll(self.un, 64))

    def seconds(self):
        return jnp.where(zl() < 64, roll(self.dn, -32), roll(self.un, 32))


class Flags:
    def __init__(self, own, lo, hi, dn, un):
        self.own, self.lo, self.hi, self.dn, self.un = own, lo, hi, dn, un


def turn_row(geom, row, flag):
    return jnp.where(flag > 0.5, lane_dot(row, reverse_matrix(geom[2])), row)


def turn_sides(geom, sides, flag_dn, flag_un):
    tx = geom[0] * geom[1]
    flag = jnp.where(zl() < 64, flag_dn, flag_un)
    return jnp.where(flag > 0.5, lane_dot(sides, reverse_matrix(tx, (0, 64))), sides)


def frame(geom, fl, lo, hi, sides):
    return (
        turn_row(geom, lo, flag_row(fl.own, 0)),
        turn_row(geom, hi, flag_row(fl.own, 1)),
        turn_sides(geom, sides, flag_row(fl.own, 2), flag_row(fl.own, 3)),
    )


def relax_edges(geom, winv, co, v, halo, fl, f_lo, c_lo, f_hi, c_hi, f_sides, c_sides):
    m_rows, groups, ty = geom
    tx = m_rows * groups
    lane = zl()
    dn, un = halo.dn, halo.un

    def beside_row(edge, second, mine, low, high):
        left = jnp.where(lane == 0, low, roll(edge, 1))
        right = jnp.where(lane == ty - 1, high, roll(edge, -1))
        return second + mine + left + right

    def choose(flags, k, first, other):
        return jnp.where(flag_row(flags, k) > 0.5, other, first)

    b_lo = beside_row(
        halo.lo,
        halo.lo2,
        turn_row(geom, row_of(geom, v, 0), flag_row(fl.lo, 1)),
        choose(fl.lo, 2, col(dn, 96), col(dn, 97)),
        choose(fl.lo, 3, col(un, 96), col(un, 97)),
    )
    b_hi = beside_row(
        halo.hi,
        halo.hi2,
        turn_row(geom, row_of(geom, v, tx - 1), flag_row(fl.hi, 0)),
        choose(fl.hi, 2, col(dn, 98), col(dn, 99)),
        choose(fl.hi, 3, col(un, 98), col(un, 99)),
    )
    edge = halo.sides()
    mine = place_col(geom, v, 0, 0, jnp.zeros((Z, LANES), F32))
    mine = place_col(geom, v, ty - 1, 64, mine)
    mine = turn_sides(geom, mine, flag_row(fl.dn, 3), flag_row(fl.un, 2))
    below = jnp.where(lane == 0, col(dn, 100), roll(edge, 1))
    below = jnp.where(lane == 64, col(un, 100), below)
    above = jnp.where(lane == tx - 1, col(dn, 101), roll(edge, -1))
    above = jnp.where(lane == 64 + tx - 1, col(un, 101), above)
    b_sides = halo.seconds() + mine + below + above
    r_lo = residual(co, f_lo, c_lo, halo.lo, b_lo)
    r_hi = residual(co, f_hi, c_hi, halo.hi, b_hi)
    r_sides = residual(co, f_sides, c_sides, edge, b_sides)
    d = block_dot(winv, jnp.concatenate([r_lo, r_hi, r_sides], axis=1))
    return halo.lo + d[:, :LANES], halo.hi + d[:, LANES : 2 * LANES], edge + d[:, 2 * LANES :]


def tile_residual(geom, co, v, f, c, lo, hi, sides, m):
    m_rows, groups, ty = geom
    lane = zl()
    here = v[m]
    if m > 0:
        low_x = v[m - 1]
    else:
        low_x = lo if groups == 1 else jnp.where(lane < ty, lo, roll(v[m_rows - 1], ty))
    if m < m_rows - 1:
        high_x = v[m + 1]
    elif groups == 1:
        high_x = hi
    else:
        high_x = jnp.where(lane < (groups - 1) * ty, roll(v[0], -ty), roll(hi, (groups - 1) * ty))
    low_y, high_y = roll(here, 1), roll(here, -1)
    for q in range(groups):
        row = q * m_rows + m
        low_y = jnp.where(lane == q * ty, col(sides, row), low_y)
        high_y = jnp.where(lane == q * ty + ty - 1, col(sides, 64 + row), high_y)
    return residual(co, f[m], c[m], here, low_x + high_x + low_y + high_y)


def relax_tile(geom, winv, co, v, f, c, edges, store):
    lo, hi, sides = edges
    for m in range(0, geom[0], 2):
        rows = [k for k in (m, m + 1) if k < geom[0]]
        r = [tile_residual(geom, co, v, f, c, lo, hi, sides, k) for k in rows]
        d = block_dot(winv, r[0] if len(r) == 1 else jnp.concatenate(r, axis=1))
        for i, k in enumerate(rows):
            store(k, v[k] + d[:, i * LANES : (i + 1) * LANES])


def start_tile(geom, winv, f, store):
    for m in range(0, geom[0], 2):
        rows = [k for k in (m, m + 1) if k < geom[0]]
        parts = [f[k] for k in rows]
        d = block_dot(winv, parts[0] if len(parts) == 1 else jnp.concatenate(parts, axis=1))
        for i, k in enumerate(rows):
            store(k, d[:, i * LANES : (i + 1) * LANES])


def restrict(fine, coarse, v, out):
    m_rows, _, ty = fine
    cm, cq, cty = coarse
    a, b = iota2(LANES, LANES)
    for mc in range(cm):
        acc = None
        for qc in range(cq):
            q, m = divmod(2 * (qc * cm + mc), m_rows)
            inside = (b >= qc * cty) & (b < (qc + 1) * cty) & (a // 2 == b - qc * cty + q * (ty // 2))
            term = lane_dot(v[m] + v[m + 1], jnp.where(inside, 0.25, 0.0))
            acc = term if acc is None else acc + term
        out[mc] = acc


def prolong_add(fine, coarse, e, v, out):
    m_rows, groups, ty = fine
    cm, _, cty = coarse
    a, b = iota2(LANES, LANES)
    for m in range(0, m_rows, 2):
        acc = None
        for q in range(groups):
            qc, mc = divmod((q * m_rows + m) // 2, cm)
            inside = (b >= q * ty) & (b < (q + 1) * ty) & (a - qc * cty == (b - q * ty) // 2)
            term = lane_dot(e[mc], jnp.where(inside, 1.0, 0.0))
            acc = term if acc is None else acc + term
        out[m] = v[m] + acc
        out[m + 1] = v[m + 1] + acc


class Setter:
    def __init__(self, ref):
        self.ref = ref

    def __call__(self, m, value):
        self.ref[m] = value


def messages(geom, xlo, xhi, ydn, yun, winv):
    n = packed(geom, 4)
    raw = [part_of(geom, xlo, 0), part_of(geom, xlo, 1), part_of(geom, xhi, 0), part_of(geom, xhi, 1), ydn[0:Z, :], yun[0:Z, :]]
    d = block_dot(winv, jnp.concatenate(raw, axis=1))
    halo = Halo(*[d[:, k * LANES : (k + 1) * LANES] for k in range(6)])
    return halo, n


def own_data(geom, xlo, xhi, ydn, yun):
    lane = zl()
    dn, un = ydn[0:Z, :], yun[0:Z, :]
    f_sides = jnp.where(lane < 64, dn, roll(un, 64))
    c_sides = jnp.where(lane < 64, roll(dn, -64), un)
    return (
        part_of(geom, xlo, 0),
        part_of(geom, xlo, 2),
        part_of(geom, xhi, 0),
        part_of(geom, xhi, 2),
        f_sides,
        c_sides,
    )


def flags_of(geom, own, xlo, xhi, ydn, yun):
    n = packed(geom, 4)
    return Flags(own[...], xlo[n * Z : n * Z + 8, :], xhi[n * Z : n * Z + 8, :], ydn[Z : Z + 8, :], yun[Z : Z + 8, :])


def load_top(src, dst):
    for x in range(24):
        dst[x, 0:NZ, :] = src[pl.ds(x, NZ, stride=24), :]
        dst[x, NZ:Z, :] = jnp.zeros((Z - NZ, LANES), F32)


VMEM = pl.BlockSpec(memory_space=pltpu.VMEM)


def call(kernel, outs, args, scratch=(), name=None):
    return pl.pallas_call(
        kernel,
        out_shape=[jax.ShapeDtypeStruct(s, F32) for s in outs],
        in_specs=[VMEM] * len(args),
        out_specs=[VMEM] * len(outs),
        scratch_shapes=[pltpu.VMEM(s, F32) for s in scratch],
        compiler_params=pltpu.CompilerParams(vmem_limit_bytes=48 * 1024 * 1024),
        name=name,
    )(*args)


def tile_shape(level):
    return (GEOM[level][0], Z, LANES)


def x_shape(level, count, flags):
    return (packed(GEOM[level], count) * Z + (8 if flags else 0), LANES)


Y_FULL = (Z + 8, LANES)


def open_kernel(f_in, c_in, flags, f, c, up, down, yup, ydown):
    load_top(f_in, f)
    load_top(c_in, c)
    put_x(GEOM[0], f, c, up, down, flags[...])
    put_y(GEOM[0], f, c, yup, ydown)
    yup[Z : Z + 8, :] = flags[...]
    ydown[Z : Z + 8, :] = flags[...]


def merge_kernel(level, count):
    geom = GEOM[level]

    def kernel(xlo, xhi, flags, yup, ydown, up, down):
        lo, hi = part_of(geom, xlo, count - 1), part_of(geom, xhi, count - 1)
        up[...] = yup[...]
        down[...] = ydown[...]
        a, b = merge_y(lo, hi, flags, yup[0:Z, :], ydown[0:Z, :])
        up[0:Z, :] = a
        down[0:Z, :] = b

    return kernel


def pre_kernel(level):
    geom, coarse = GEOM[level], GEOM[level + 1]

    def kernel(f, c, w, vz, own, xlo, xhi, ydn, yun, v_out, f_next, c_next, up, down, yup, ydown, one, res):
        winv = w[...].astype(BF16)
        co = Coef(vz)
        fl = flags_of(geom, own, xlo, xhi, ydn, yun)
        start_tile(geom, winv, f, Setter(one))
        halo, _ = messages(geom, xlo, xhi, ydn, yun, winv)
        lo2, hi2, sides2 = relax_edges(geom, winv, co, one, halo, fl, *own_data(geom, xlo, xhi, ydn, yun))
        relax_tile(geom, winv, co, one, f, c, frame(geom, fl, halo.lo, halo.hi, halo.sides()), Setter(v_out))
        lo, hi, sides = frame(geom, fl, lo2, hi2, sides2)
        for m in range(geom[0]):
            res[m] = tile_residual(geom, co, v_out, f, c, lo, hi, sides, m)
        restrict(geom, coarse, res, f_next)
        restrict(geom, coarse, c, c_next)
        put_x(coarse, f_next, c_next, up, down, own[...])
        put_y(coarse, f_next, c_next, yup, ydown)
        yup[Z : Z + 8, :] = own[...]
        ydown[Z : Z + 8, :] = own[...]

    return kernel


def bottom_kernel(f, c, w, vz, own, xlo, xhi, ydn, yun, v_out, up, down, yup, ydown, one):
    geom = GEOM[3]
    winv = w[...].astype(BF16)
    co = Coef(vz)
    fl = flags_of(geom, own, xlo, xhi, ydn, yun)
    start_tile(geom, winv, f, Setter(v_out))
    halo, _ = messages(geom, xlo, xhi, ydn, yun, winv)
    lo2, hi2, sides2 = relax_edges(geom, winv, co, v_out, halo, fl, *own_data(geom, xlo, xhi, ydn, yun))
    relax_tile(geom, winv, co, v_out, f, c, frame(geom, fl, halo.lo, halo.hi, halo.sides()), Setter(one))
    relax_tile(geom, winv, co, one, f, c, frame(geom, fl, lo2, hi2, sides2), Setter(v_out))
    put_x(geom, v_out, None, up, down)
    put_y(geom, v_out, None, yup, ydown)


def last_kernel(f, c, w, vz, own, xlo, xhi, ydn, yun, v, fine_v, g, up, down, yup, ydown, e):
    geom, fine = GEOM[3], GEOM[2]
    winv = w[...].astype(BF16)
    co = Coef(vz)
    fl = Flags(own[...], None, None, None, None)
    sides = jnp.where(zl() < 64, ydn[...], roll(yun[...], 64))
    edges = frame(geom, fl, part_of(geom, xlo, 0), part_of(geom, xhi, 0), sides)
    relax_tile(geom, winv, co, v, f, c, edges, Setter(e))
    prolong_add(fine, geom, e, fine_v, g)
    put_x(fine, g, None, up, down)
    put_y(fine, g, None, yup, ydown)


def post_kernel(level):
    geom = GEOM[level]

    def sweeps(f, c, w, vz, own, xlo, xhi, ydn, yun, g, glo, ghi, gdn, gun, one, store):
        winv = w[...].astype(BF16)
        co = Coef(vz)
        fl = flags_of(geom, own, xlo, xhi, ydn, yun)
        halo = Halo(
            part_of(geom, glo, 0), part_of(geom, glo, 1), part_of(geom, ghi, 0), part_of(geom, ghi, 1), gdn[...], gun[...]
        )
        lo2, hi2, sides2 = relax_edges(geom, winv, co, g, halo, fl, *own_data(geom, xlo, xhi, ydn, yun))
        relax_tile(geom, winv, co, g, f, c, frame(geom, fl, halo.lo, halo.hi, halo.sides()), Setter(one))
        relax_tile(geom, winv, co, one, f, c, frame(geom, fl, lo2, hi2, sides2), store)

    if level == 0:

        def kernel(f, c, w, vz, own, xlo, xhi, ydn, yun, g, glo, ghi, gdn, gun, out, one):
            def store(x, value):
                out[pl.ds(x, NZ, stride=24), :] = value[0:NZ, :]

            sweeps(f, c, w, vz, own, xlo, xhi, ydn, yun, g, glo, ghi, gdn, gun, one, store)

        return kernel

    fine = GEOM[level - 1]

    def kernel(f, c, w, vz, own, xlo, xhi, ydn, yun, g, glo, ghi, gdn, gun, fine_v, g_out, up, down, yup, ydown, one, e):
        sweeps(f, c, w, vz, own, xlo, xhi, ydn, yun, g, glo, ghi, gdn, gun, one, Setter(e))
        prolong_add(fine, geom, e, fine_v, g_out)
        put_x(fine, g_out, None, up, down)
        put_y(fine, g_out, None, yup, ydown)

    return kernel


def both_ways(up, down, axis):
    n = lax.axis_size(axis)
    fwd = [(i, (i + 1) % n) for i in range(n)]
    back = [((i + 1) % n, i) for i in range(n)]
    return lax.ppermute(up, axis, fwd), lax.ppermute(down, axis, back)


def block_matrices(block_inverse):
    levels = block_inverse.shape[0]
    whole = jnp.zeros((levels, Z, Z), F32)
    for k in range(NBLK):
        lo, hi = k * BLK, Z - (k + 1) * BLK
        whole = whole + jnp.pad(block_inverse[:, k], ((0, 0), (lo, hi), (lo, hi)))
    high = lax.reduce_precision(whole, 8, 7)
    low = lax.reduce_precision(whole - high, 8, 7)
    return jnp.concatenate([high, low, high], axis=2)


def vertical_columns(vert_coef):
    zero = jnp.zeros((1,), F32)
    up = jnp.concatenate([vert_coef[1:], zero, zero])
    down = jnp.concatenate([vert_coef[:-1], zero, zero])
    cols = jnp.stack([4.0 + up + down, up, down], axis=1) * 0.0625
    return jnp.pad(cols, ((0, 0), (0, LANES - 3)))


def on_device(right_side, helm_coef, vert_coef, block_inverse, edge_flip):
    own = jnp.pad(jnp.broadcast_to(edge_flip.reshape(4, 1).astype(F32), (4, LANES)), ((0, 4), (0, 0)))
    vz = vertical_columns(vert_coef)
    w = block_matrices(block_inverse)
    f_in = right_side.reshape(NZ * 24, LANES)
    c_in = helm_coef.reshape(NZ * 24, LANES)

    def exchange(level, count, up, down, yup, ydown):
        xlo, xhi = both_ways(up, down, "gx")
        shape = yup.shape
        yup, ydown = call(merge_kernel(level, count), [shape, shape], [xlo, xhi, own, yup, ydown], name=f"merge{level}")
        ydn, yun = both_ways(yup, ydown, "gy")
        return xlo, xhi, ydn, yun

    xs = x_shape(0, 4, True)
    f, c, *msg = call(
        open_kernel, [tile_shape(0)] * 2 + [xs, xs, Y_FULL, Y_FULL], [f_in, c_in, own], name="open"
    )
    saved = []
    for level in range(3):
        got = exchange(level, 4, *msg)
        xs = x_shape(level + 1, 4, True)
        t = tile_shape(level)
        nxt = tile_shape(level + 1)
        v, f_next, c_next, *msg = call(
            pre_kernel(level),
            [t, nxt, nxt, xs, xs, Y_FULL, Y_FULL],
            [f, c, w[level], vz, own, *got],
            [t, t],
            name=f"pre{level}",
        )
        saved.append((f, c, got, v))
        f, c = f_next, c_next
    got = exchange(3, 4, *msg)
    t = tile_shape(3)
    xs, ys = x_shape(3, 3, False), (Z, LANES)
    v, up, down, yup, ydown = call(
        bottom_kernel, [t, xs, xs, ys, ys], [f, c, w[3], vz, own, *got], [t], name="bottom"
    )
    xlo, xhi = both_ways(up, down, "gx")
    ydn, yun = both_ways(yup, ydown, "gy")
    t2 = tile_shape(2)
    xs = x_shape(2, 3, False)
    g, *msg = call(
        last_kernel,
        [t2, xs, xs, ys, ys],
        [f, c, w[3], vz, own, xlo, xhi, ydn, yun, v, saved[2][3]],
        [t],
        name="last",
    )
    for level in (2, 1, 0):
        f, c, got, _ = saved[level]
        ggot = exchange(level, 3, *msg)
        t = tile_shape(level)
        args = [f, c, w[level], vz, own, *got, g, *ggot]
        if level == 0:
            (out,) = call(post_kernel(0), [(NZ * 24, LANES)], args, [t], name="post0")
            return out.reshape(NZ, 24, LANES)
        xs = x_shape(level - 1, 3, False)
        g, *msg = call(
            post_kernel(level),
            [tile_shape(level - 1), xs, xs, ys, ys],
            args + [saved[level - 1][3]],
            [t, t],
            name=f"post{level}",
        )


def solution(mesh):
    placed = (P(None, "gx", "gy"), P(None, "gx", "gy"), P(), P(), P("gx", "gy", None))
    return jax.shard_map(
        on_device, mesh=mesh, in_specs=placed, out_specs=P(None, "gx", "gy"), check_vma=False
    )
```

profile of v0, /device:TPU:0, one launch (start us, length us, event | category | flops | bytes accessed | tf_op | source)
XLA Modules:
  0.0 145.0 jit_solution(13036104086424704645)
XLA Ops:
  4.7 1.7 %collective-permute-start = (f32[296,128]{1,0:T(8,128)S(1)}, f32[296,128]{1,0:T(8,128)S(1)}, u32[]{:S(2)}, u32[]{:S(2)}) collective-permute-start(f32[296,128]{1,0:T(8,128)S(1)} %get-tuple-element.68), channel_id=1, source_target_pairs={{0,16},{16,32},{32,48},{48,64},{64,80},{80,96},{96,112},{112,0},{1... | collective-permute-start | bytes 454664 | tf_op jit(solution)/shard_map/ppermute | solution.py:501
  6.4 2.5 %collective-permute-start.1 = (f32[296,128]{1,0:T(8,128)S(1)}, f32[296,128]{1,0:T(8,128)S(1)}, u32[]{:S(2)}, u32[]{:S(2)}) collective-permute-start(f32[296,128]{1,0:T(8,128)S(1)} %get-tuple-element.69), channel_id=1, source_target_pairs={{16,0},{32,16},{48,32},{64,48},{80,64},{96,80},{112,96},{0,112},{1... | collective-permute-start | bytes 454664 | tf_op jit(solution)/shard_map/ppermute | solution.py:501
  9.5 3.4 %collective-permute-done.xlo = f32[296,128]{1,0:T(8,128)S(1)} collective-permute-done((f32[296,128]{1,0:T(8,128)S(1)}, f32[296,128]{1,0:T(8,128)S(1)}, u32[]{:S(2)}, u32[]{:S(2)}) %collective-permute-start) | collective-permute-done | bytes 151584 | tf_op jit(solution)/shard_map/ppermute | solution.py:501
  12.8 2.2 %collective-permute-done.1.xhi = f32[296,128]{1,0:T(8,128)S(1)} collective-permute-done((f32[296,128]{1,0:T(8,128)S(1)}, f32[296,128]{1,0:T(8,128)S(1)}, u32[]{:S(2)}, u32[]{:S(2)}) %collective-permute-start.1) | collective-permute-done | bytes 151584 | tf_op jit(solution)/shard_map/ppermute | solution.py:501
  15.3 5.3 %collective-permute-start.3 = (f32[80,128]{1,0:T(8,128)S(1)}, f32[80,128]{1,0:T(8,128)S(1)}, u32[]{:S(2)}, u32[]{:S(2)}) collective-permute-start(f32[80,128]{1,0:T(8,128)S(1)} %get-tuple-element.73), channel_id=1, source_target_pairs={{1,0},{2,1},{3,2},{4,3},{5,4},{6,5},{7,6},{8,7},{9,8},{10,9},{11,1... | collective-permute-start | bytes 122888 | tf_op jit(solution)/shard_map/ppermute | solution.py:501
  22.3 6.5 %pre0.1 = (f32[24,72,128]{2,1,0:T(8,128)S(1)}, f32[6,72,128]{2,1,0:T(8,128)S(1)}, f32[6,72,128]{2,1,0:T(8,128)S(1)}, f32[152,128]{1,0:T(8,128)S(1)}, f32[152,128...) custom-call(f32[24,72,128]{2,1,0:T(8,128)S(1)} %get-tuple-element.66.f, ...), custom_call_target="tpu_custom_call" | custom-call | tf_op jit(solution)/shard_map/pre0/pallas_call | solution.py:366
  29.1 3.8 %collective-permute-start.5 = (f32[152,128]{1,0:T(8,128)S(1)}, f32[152,128]{1,0:T(8,128)S(1)}, u32[]{:S(2)}, u32[]{:S(2)}) collective-permute-start(f32[152,128]{1,0:T(8,128)S(1)} %get-tuple-element.77), channel_id=1, source_target_pairs={{16,0},{32,16},{48,32},{64,48},{80,64},{96,80},{112,96},{0,112},{1... | collective-permute-start | bytes 233480 | tf_op jit(solution)/shard_map/ppermute | solution.py:501
  33.0 2.5 %collective-permute-done.4.xlo = f32[152,128]{1,0:T(8,128)S(1)} collective-permute-done((f32[152,128]{1,0:T(8,128)S(1)}, f32[152,128]{1,0:T(8,128)S(1)}, u32[]{:S(2)}, u32[]{:S(2)}) %collective-permute-start.4) | collective-permute-done | bytes 77856 | tf_op jit(solution)/shard_map/ppermute | solution.py:501
  35.9 5.3 %collective-permute-start.7 = (f32[80,128]{1,0:T(8,128)S(1)}, f32[80,128]{1,0:T(8,128)S(1)}, u32[]{:S(2)}, u32[]{:S(2)}) collective-permute-start(f32[80,128]{1,0:T(8,128)S(1)} %get-tuple-element.81), channel_id=1, source_target_pairs={{1,0},{2,1},{3,2},{4,3},{5,4},{6,5},{7,6},{8,7},{9,8},{10,9},{11,1... | collective-permute-start | bytes 122888 | tf_op jit(solution)/shard_map/ppermute | solution.py:501
  43.0 3.0 %pre1.1 = (f32[6,72,128]{2,1,0:T(8,128)S(1)}, f32[6,72,128]{2,1,0:T(8,128)S(1)}, f32[6,72,128]{2,1,0:T(8,128)S(1)}, f32[80,128]{1,0:T(8,128)S(1)}, f32[80,128]{1...) custom-call(f32[6,72,128]{2,1,0:T(8,128)S(1)} %get-tuple-element.74.f, ...), custom_call_target="tpu_custom_call" | custom-call | tf_op jit(solution)/shard_map/pre1/pallas_call | solution.py:366
  45.9 2.3 %collective-permute-start.8 = (f32[80,128]{1,0:T(8,128)S(1)}, f32[80,128]{1,0:T(8,128)S(1)}, u32[]{:S(2)}, u32[]{:S(2)}) collective-permute-start(f32[80,128]{1,0:T(8,128)S(1)} %get-tuple-element.84), channel_id=1, source_target_pairs={{0,16},{16,32},{32,48},{48,64},{64,80},{80,96},{96,112},{112,0},{1... | collective-permute-start | bytes 122888 | tf_op jit(solution)/shard_map/ppermute | solution.py:501
  48.3 2.1 %collective-permute-start.9 = (f32[80,128]{1,0:T(8,128)S(1)}, f32[80,128]{1,0:T(8,128)S(1)}, u32[]{:S(2)}, u32[]{:S(2)}) collective-permute-start(f32[80,128]{1,0:T(8,128)S(1)} %get-tuple-element.85), channel_id=1, source_target_pairs={{16,0},{32,16},{48,32},{64,48},{80,64},{96,80},{112,96},{0,112},{1... | collective-permute-start | bytes 122888 | tf_op jit(solution)/shard_map/ppermute | solution.py:501
  50.4 2.0 %collective-permute-done.8.xlo = f32[80,128]{1,0:T(8,128)S(1)} collective-permute-done((f32[80,128]{1,0:T(8,128)S(1)}, f32[80,128]{1,0:T(8,128)S(1)}, u32[]{:S(2)}, u32[]{:S(2)}) %collective-permute-start.8) | collective-permute-done | bytes 40992 | tf_op jit(solution)/shard_map/ppermute | solution.py:501
  53.0 5.3 %collective-permute-start.11 = (f32[80,128]{1,0:T(8,128)S(1)}, f32[80,128]{1,0:T(8,128)S(1)}, u32[]{:S(2)}, u32[]{:S(2)}) collective-permute-start(f32[80,128]{1,0:T(8,128)S(1)} %get-tuple-element.89), channel_id=1, source_target_pairs={{1,0},{2,1},{3,2},{4,3},{5,4},{6,5},{7,6},{8,7},{9,8},{10,9},{11,1... | collective-permute-start | bytes 122888 | tf_op jit(solution)/shard_map/ppermute | solution.py:501
  60.0 2.0 %pre2.1 = (f32[6,72,128]{2,1,0:T(8,128)S(1)}, f32[3,72,128]{2,1,0:T(8,128)S(1)}, f32[3,72,128]{2,1,0:T(8,128)S(1)}, f32[80,128]{1,0:T(8,128)S(1)}, f32[80,128]{1...) custom-call(f32[6,72,128]{2,1,0:T(8,128)S(1)} %get-tuple-element.82.f, ...), custom_call_target="tpu_custom_call" | custom-call | tf_op jit(solution)/shard_map/pre2/pallas_call | solution.py:366
  63.3 3.0 %collective-permute-start.13 = (f32[80,128]{1,0:T(8,128)S(1)}, f32[80,128]{1,0:T(8,128)S(1)}, u32[]{:S(2)}, u32[]{:S(2)}) collective-permute-start(f32[80,128]{1,0:T(8,128)S(1)} %get-tuple-element.93), channel_id=1, source_target_pairs={{16,0},{32,16},{48,32},{64,48},{80,64},{96,80},{112,96},{0,112},{1... | collective-permute-start | bytes 122888 | tf_op jit(solution)/shard_map/ppermute | solution.py:501
  66.3 2.0 %collective-permute-done.12.xlo = f32[80,128]{1,0:T(8,128)S(1)} collective-permute-done((f32[80,128]{1,0:T(8,128)S(1)}, f32[80,128]{1,0:T(8,128)S(1)}, u32[]{:S(2)}, u32[]{:S(2)}) %collective-permute-start.12) | collective-permute-done | bytes 40992 | tf_op jit(solution)/shard_map/ppermute | solution.py:501
  68.6 5.3 %collective-permute-start.15 = (f32[80,128]{1,0:T(8,128)S(1)}, f32[80,128]{1,0:T(8,128)S(1)}, u32[]{:S(2)}, u32[]{:S(2)}) collective-permute-start(f32[80,128]{1,0:T(8,128)S(1)} %get-tuple-element.97), channel_id=1, source_target_pairs={{1,0},{2,1},{3,2},{4,3},{5,4},{6,5},{7,6},{8,7},{9,8},{10,9},{11,1... | collective-permute-start | bytes 122888 | tf_op jit(solution)/shard_map/ppermute | solution.py:501
  79.0 2.6 %collective-permute-start.17 = (f32[72,128]{1,0:T(8,128)S(1)}, f32[72,128]{1,0:T(8,128)S(1)}, u32[]{:S(2)}, u32[]{:S(2)}) collective-permute-start(f32[72,128]{1,0:T(8,128)S(1)} %get-tuple-element.99), channel_id=1, source_target_pairs={{16,0},{32,16},{48,32},{64,48},{80,64},{96,80},{112,96},{0,112},{1... | collective-permute-start | bytes 110600 | tf_op jit(solution)/shard_map/ppermute | solution.py:501
  81.6 5.7 %collective-permute-start.19 = (f32[72,128]{1,0:T(8,128)S(1)}, f32[72,128]{1,0:T(8,128)S(1)}, u32[]{:S(2)}, u32[]{:S(2)}) collective-permute-start(f32[72,128]{1,0:T(8,128)S(1)} %get-tuple-element.101), channel_id=1, source_target_pairs={{1,0},{2,1},{3,2},{4,3},{5,4},{6,5},{7,6},{8,7},{9,8},{10,9},{11,1... | collective-permute-start | bytes 110600 | tf_op jit(solution)/shard_map/ppermute | solution.py:501
  90.1 4.1 %collective-permute-start.21 = (f32[72,128]{1,0:T(8,128)S(1)}, f32[72,128]{1,0:T(8,128)S(1)}, u32[]{:S(2)}, u32[]{:S(2)}) collective-permute-start(f32[72,128]{1,0:T(8,128)S(1)} %get-tuple-element.106), channel_id=1, source_target_pairs={{16,0},{32,16},{48,32},{64,48},{80,64},{96,80},{112,96},{0,112},{1... | collective-permute-start | bytes 110600 | tf_op jit(solution)/shard_map/ppermute | solution.py:501
  94.2 1.9 %collective-permute-done.20.xlo.glo = f32[72,128]{1,0:T(8,128)S(1)} collective-permute-done((f32[72,128]{1,0:T(8,128)S(1)}, f32[72,128]{1,0:T(8,128)S(1)}, u32[]{:S(2)}, u32[]{:S(2)}) %collective-permute-start.20) | collective-permute-done | bytes 36896 | tf_op jit(solution)/shard_map/ppermute | solution.py:501
  96.7 5.3 %collective-permute-start.23 = (f32[72,128]{1,0:T(8,128)S(1)}, f32[72,128]{1,0:T(8,128)S(1)}, u32[]{:S(2)}, u32[]{:S(2)}) collective-permute-start(f32[72,128]{1,0:T(8,128)S(1)} %get-tuple-element.110), channel_id=1, source_target_pairs={{1,0},{2,1},{3,2},{4,3},{5,4},{6,5},{7,6},{8,7},{9,8},{10,9},{11,1... | collective-permute-start | bytes 110600 | tf_op jit(solution)/shard_map/ppermute | solution.py:501
  103.7 2.5 %post2.1 = (f32[6,72,128]{2,1,0:T(8,128)S(1)}, f32[144,128]{1,0:T(8,128)S(1)}, f32[144,128]{1,0:T(8,128)S(1)}, f32[72,128]{1,0:T(8,128)S(1)}, f32[72,128]{1,0:T(8,128)S(1)}) custom-call(f32[6,72,128]{2,1,0:T(8,128)S(1)} %get-tuple-element.82.f, f32[6,72,128]{2,1,0:T(8,128)S(1)} %get-tuple-element.83.c, f32[72,216]{1,0:T(8,128)S(1)} %get-tuple-element.128.w, ...), custom_call_target="tpu_custom_call" | custom-call | tf_op jit(solution)/shard_map/post2/pallas_call | solution.py:366
  106.3 4.3 %collective-permute-start.25 = (f32[144,128]{1,0:T(8,128)S(1)}, f32[144,128]{1,0:T(8,128)S(1)}, u32[]{:S(2)}, u32[]{:S(2)}) collective-permute-start(f32[144,128]{1,0:T(8,128)S(1)} %get-tuple-element.114), channel_id=1, source_target_pairs={{16,0},{32,16},{48,32},{64,48},{80,64},{96,80},{112,96},{0,112},{1... | collective-permute-start | bytes 221192 | tf_op jit(solution)/shard_map/ppermute | solution.py:501
  110.7 2.2 %collective-permute-done.24.xlo.glo = f32[144,128]{1,0:T(8,128)S(1)} collective-permute-done((f32[144,128]{1,0:T(8,128)S(1)}, f32[144,128]{1,0:T(8,128)S(1)}, u32[]{:S(2)}, u32[]{:S(2)}) %collective-permute-start.24) | collective-permute-done | bytes 73760 | tf_op jit(solution)/shard_map/ppermute | solution.py:501
  113.2 5.3 %collective-permute-start.27 = (f32[72,128]{1,0:T(8,128)S(1)}, f32[72,128]{1,0:T(8,128)S(1)}, u32[]{:S(2)}, u32[]{:S(2)}) collective-permute-start(f32[72,128]{1,0:T(8,128)S(1)} %get-tuple-element.118), channel_id=1, source_target_pairs={{1,0},{2,1},{3,2},{4,3},{5,4},{6,5},{7,6},{8,7},{9,8},{10,9},{11,1... | collective-permute-start | bytes 110600 | tf_op jit(solution)/shard_map/ppermute | solution.py:501
  120.7 3.6 %post1.1 = (f32[24,72,128]{2,1,0:T(8,128)S(1)}, f32[216,128]{1,0:T(8,128)S(1)}, f32[216,128]{1,0:T(8,128)S(1)}, f32[72,128]{1,0:T(8,128)S(1)}, f32[72,128]{1,0:T(8,128)S(1)}) custom-call(f32[6,72,128]{2,1,0:T(8,128)S(1)} %get-tuple-element.74.f, f32[6,72,128]{2,1,0:T(8,128)S(1)} %get-tuple-element.75.c, f32[72,216]{1,0:T(8,128)S(1)} %get-tuple-element.129.w, ...), custom_call_target="tpu_custom_call" | custom-call | tf_op jit(solution)/shard_map/post1/pallas_call | solution.py:366
  124.4 4.5 %collective-permute-start.29 = (f32[216,128]{1,0:T(8,128)S(1)}, f32[216,128]{1,0:T(8,128)S(1)}, u32[]{:S(2)}, u32[]{:S(2)}) collective-permute-start(f32[216,128]{1,0:T(8,128)S(1)} %get-tuple-element.122), channel_id=1, source_target_pairs={{16,0},{32,16},{48,32},{64,48},{80,64},{96,80},{112,96},{0,112},{1... | collective-permute-start | bytes 331784 | tf_op jit(solution)/shard_map/ppermute | solution.py:501
  128.8 2.6 %collective-permute-done.28.xlo.glo = f32[216,128]{1,0:T(8,128)S(1)} collective-permute-done((f32[216,128]{1,0:T(8,128)S(1)}, f32[216,128]{1,0:T(8,128)S(1)}, u32[]{:S(2)}, u32[]{:S(2)}) %collective-permute-start.28) | collective-permute-done | bytes 110624 | tf_op jit(solution)/shard_map/ppermute | solution.py:501
  131.7 5.7 %collective-permute-start.31 = (f32[72,128]{1,0:T(8,128)S(1)}, f32[72,128]{1,0:T(8,128)S(1)}, u32[]{:S(2)}, u32[]{:S(2)}) collective-permute-start(f32[72,128]{1,0:T(8,128)S(1)} %get-tuple-element.126), channel_id=1, source_target_pairs={{1,0},{2,1},{3,2},{4,3},{5,4},{6,5},{7,6},{8,7},{9,8},{10,9},{11,1... | collective-permute-start | bytes 110600 | tf_op jit(solution)/shard_map/ppermute | solution.py:501
  139.1 5.9 %post0.1 = f32[1680,128]{1,0:T(8,128)} custom-call(f32[24,72,128]{2,1,0:T(8,128)S(1)} %get-tuple-element.66.f, f32[24,72,128]{2,1,0:T(8,128)S(1)} %get-tuple-element.67.c, f32[72,216]{1,0:T(8,128)S(1)} %get-tuple-element.130.w, f32[72,128]{1,0:T(8,128)S(1)} %pad.39.vz, f32[8,128]{1,0:T(8,128)S(1)} %pad.33.flags.own, ...), custom_call_target="tpu_custom_call" | custom-call | tf_op jit(solution)/shard_map/post0/pallas_call | solution.py:366
  (72 shorter events, 27.9 us)
Async XLA Ops:
  4.7 8.2 %collective-permute-start = (f32[296,128]{1,0:T(8,128)S(1)}, f32[296,128]{1,0:T(8,128)S(1)}, u32[]{:S(2)}, u32[]{:S(2)}) collective-permute-start(f32[296,128]{1,0:T(8,128)S(1)} %get-tuple-element.68), channel_id=1, source_target_pairs={{0,16},{16,32},{32,48},{48,64},{64,80},{80,96},{96,112},{112,0},{1... | collective-permute-start | bytes 454664 | tf_op jit(solution)/shard_map/ppermute | solution.py:501
  6.4 8.6 %collective-permute-start.1 = (f32[296,128]{1,0:T(8,128)S(1)}, f32[296,128]{1,0:T(8,128)S(1)}, u32[]{:S(2)}, u32[]{:S(2)}) collective-permute-start(f32[296,128]{1,0:T(8,128)S(1)} %get-tuple-element.69), channel_id=1, source_target_pairs={{16,0},{32,16},{48,32},{64,48},{80,64},{96,80},{112,96},{0,112},{1... | collective-permute-start | bytes 454664 | tf_op jit(solution)/shard_map/ppermute | solution.py:501
  15.2 7.1 %collective-permute-start.2 = (f32[80,128]{1,0:T(8,128)S(1)}, f32[80,128]{1,0:T(8,128)S(1)}, u32[]{:S(2)}, u32[]{:S(2)}) collective-permute-start(f32[80,128]{1,0:T(8,128)S(1)} %get-tuple-element.72), channel_id=1, source_target_pairs={{0,1},{1,2},{2,3},{3,4},{4,5},{5,6},{6,7},{7,8},{8,9},{9,10},{10,1... | collective-permute-start | bytes 122888 | tf_op jit(solution)/shard_map/ppermute | solution.py:501
  15.3 7.0 %collective-permute-start.3 = (f32[80,128]{1,0:T(8,128)S(1)}, f32[80,128]{1,0:T(8,128)S(1)}, u32[]{:S(2)}, u32[]{:S(2)}) collective-permute-start(f32[80,128]{1,0:T(8,128)S(1)} %get-tuple-element.73), channel_id=1, source_target_pairs={{1,0},{2,1},{3,2},{4,3},{5,4},{6,5},{7,6},{8,7},{9,8},{10,9},{11,1... | collective-permute-start | bytes 122888 | tf_op jit(solution)/shard_map/ppermute | solution.py:501
  28.8 6.7 %collective-permute-start.4 = (f32[152,128]{1,0:T(8,128)S(1)}, f32[152,128]{1,0:T(8,128)S(1)}, u32[]{:S(2)}, u32[]{:S(2)}) collective-permute-start(f32[152,128]{1,0:T(8,128)S(1)} %get-tuple-element.76), channel_id=1, source_target_pairs={{0,16},{16,32},{32,48},{48,64},{64,80},{80,96},{96,112},{112,0},{1... | collective-permute-start | bytes 233480 | tf_op jit(solution)/shard_map/ppermute | solution.py:501
  29.1 6.5 %collective-permute-start.5 = (f32[152,128]{1,0:T(8,128)S(1)}, f32[152,128]{1,0:T(8,128)S(1)}, u32[]{:S(2)}, u32[]{:S(2)}) collective-permute-start(f32[152,128]{1,0:T(8,128)S(1)} %get-tuple-element.77), channel_id=1, source_target_pairs={{16,0},{32,16},{48,32},{64,48},{80,64},{96,80},{112,96},{0,112},{1... | collective-permute-start | bytes 233480 | tf_op jit(solution)/shard_map/ppermute | solution.py:501
  35.8 7.1 %collective-permute-start.6 = (f32[80,128]{1,0:T(8,128)S(1)}, f32[80,128]{1,0:T(8,128)S(1)}, u32[]{:S(2)}, u32[]{:S(2)}) collective-permute-start(f32[80,128]{1,0:T(8,128)S(1)} %get-tuple-element.80), channel_id=1, source_target_pairs={{0,1},{1,2},{2,3},{3,4},{4,5},{5,6},{6,7},{7,8},{8,9},{9,10},{10,1... | collective-permute-start | bytes 122888 | tf_op jit(solution)/shard_map/ppermute | solution.py:501
  35.9 7.0 %collective-permute-start.7 = (f32[80,128]{1,0:T(8,128)S(1)}, f32[80,128]{1,0:T(8,128)S(1)}, u32[]{:S(2)}, u32[]{:S(2)}) collective-permute-start(f32[80,128]{1,0:T(8,128)S(1)} %get-tuple-element.81), channel_id=1, source_target_pairs={{1,0},{2,1},{3,2},{4,3},{5,4},{6,5},{7,6},{8,7},{9,8},{10,9},{11,1... | collective-permute-start | bytes 122888 | tf_op jit(solution)/shard_map/ppermute | solution.py:501
  45.9 6.5 %collective-permute-start.8 = (f32[80,128]{1,0:T(8,128)S(1)}, f32[80,128]{1,0:T(8,128)S(1)}, u32[]{:S(2)}, u32[]{:S(2)}) collective-permute-start(f32[80,128]{1,0:T(8,128)S(1)} %get-tuple-element.84), channel_id=1, source_target_pairs={{0,16},{16,32},{32,48},{48,64},{64,80},{80,96},{96,112},{112,0},{1... | collective-permute-start | bytes 122888 | tf_op jit(solution)/shard_map/ppermute | solution.py:501
  48.3 4.4 %collective-permute-start.9 = (f32[80,128]{1,0:T(8,128)S(1)}, f32[80,128]{1,0:T(8,128)S(1)}, u32[]{:S(2)}, u32[]{:S(2)}) collective-permute-start(f32[80,128]{1,0:T(8,128)S(1)} %get-tuple-element.85), channel_id=1, source_target_pairs={{16,0},{32,16},{48,32},{64,48},{80,64},{96,80},{112,96},{0,112},{1... | collective-permute-start | bytes 122888 | tf_op jit(solution)/shard_map/ppermute | solution.py:501
  52.9 7.1 %collective-permute-start.10 = (f32[80,128]{1,0:T(8,128)S(1)}, f32[80,128]{1,0:T(8,128)S(1)}, u32[]{:S(2)}, u32[]{:S(2)}) collective-permute-start(f32[80,128]{1,0:T(8,128)S(1)} %get-tuple-element.88), channel_id=1, source_target_pairs={{0,1},{1,2},{2,3},{3,4},{4,5},{5,6},{6,7},{7,8},{8,9},{9,10},{10,1... | collective-permute-start | bytes 122888 | tf_op jit(solution)/shard_map/ppermute | solution.py:501
  53.0 7.0 %collective-permute-start.11 = (f32[80,128]{1,0:T(8,128)S(1)}, f32[80,128]{1,0:T(8,128)S(1)}, u32[]{:S(2)}, u32[]{:S(2)}) collective-permute-start(f32[80,128]{1,0:T(8,128)S(1)} %get-tuple-element.89), channel_id=1, source_target_pairs={{1,0},{2,1},{3,2},{4,3},{5,4},{6,5},{7,6},{8,7},{9,8},{10,9},{11,1... | collective-permute-start | bytes 122888 | tf_op jit(solution)/shard_map/ppermute | solution.py:501
  62.1 6.2 %collective-permute-start.12 = (f32[80,128]{1,0:T(8,128)S(1)}, f32[80,128]{1,0:T(8,128)S(1)}, u32[]{:S(2)}, u32[]{:S(2)}) collective-permute-start(f32[80,128]{1,0:T(8,128)S(1)} %get-tuple-element.92), channel_id=1, source_target_pairs={{0,16},{16,32},{32,48},{48,64},{64,80},{80,96},{96,112},{112,0},{1... | collective-permute-start | bytes 122888 | tf_op jit(solution)/shard_map/ppermute | solution.py:501
  63.3 5.0 %collective-permute-start.13 = (f32[80,128]{1,0:T(8,128)S(1)}, f32[80,128]{1,0:T(8,128)S(1)}, u32[]{:S(2)}, u32[]{:S(2)}) collective-permute-start(f32[80,128]{1,0:T(8,128)S(1)} %get-tuple-element.93), channel_id=1, source_target_pairs={{16,0},{32,16},{48,32},{64,48},{80,64},{96,80},{112,96},{0,112},{1... | collective-permute-start | bytes 122888 | tf_op jit(solution)/shard_map/ppermute | solution.py:501
  68.5 7.1 %collective-permute-start.14 = (f32[80,128]{1,0:T(8,128)S(1)}, f32[80,128]{1,0:T(8,128)S(1)}, u32[]{:S(2)}, u32[]{:S(2)}) collective-permute-start(f32[80,128]{1,0:T(8,128)S(1)} %get-tuple-element.96), channel_id=1, source_target_pairs={{0,1},{1,2},{2,3},{3,4},{4,5},{5,6},{6,7},{7,8},{8,9},{9,10},{10,1... | collective-permute-start | bytes 122888 | tf_op jit(solution)/shard_map/ppermute | solution.py:501
  68.6 7.0 %collective-permute-start.15 = (f32[80,128]{1,0:T(8,128)S(1)}, f32[80,128]{1,0:T(8,128)S(1)}, u32[]{:S(2)}, u32[]{:S(2)}) collective-permute-start(f32[80,128]{1,0:T(8,128)S(1)} %get-tuple-element.97), channel_id=1, source_target_pairs={{1,0},{2,1},{3,2},{4,3},{5,4},{6,5},{7,6},{8,7},{9,8},{10,9},{11,1... | collective-permute-start | bytes 122888 | tf_op jit(solution)/shard_map/ppermute | solution.py:501
  77.3 9.9 %collective-permute-start.16 = (f32[72,128]{1,0:T(8,128)S(1)}, f32[72,128]{1,0:T(8,128)S(1)}, u32[]{:S(2)}, u32[]{:S(2)}) collective-permute-start(f32[72,128]{1,0:T(8,128)S(1)} %get-tuple-element.98), channel_id=1, source_target_pairs={{0,16},{16,32},{32,48},{48,64},{64,80},{80,96},{96,112},{112,0},{1... | collective-permute-start | bytes 110600 | tf_op jit(solution)/shard_map/ppermute | solution.py:501
  79.0 8.2 %collective-permute-start.17 = (f32[72,128]{1,0:T(8,128)S(1)}, f32[72,128]{1,0:T(8,128)S(1)}, u32[]{:S(2)}, u32[]{:S(2)}) collective-permute-start(f32[72,128]{1,0:T(8,128)S(1)} %get-tuple-element.99), channel_id=1, source_target_pairs={{16,0},{32,16},{48,32},{64,48},{80,64},{96,80},{112,96},{0,112},{1... | collective-permute-start | bytes 110600 | tf_op jit(solution)/shard_map/ppermute | solution.py:501
  81.6 7.3 %collective-permute-start.18 = (f32[72,128]{1,0:T(8,128)S(1)}, f32[72,128]{1,0:T(8,128)S(1)}, u32[]{:S(2)}, u32[]{:S(2)}) collective-permute-start(f32[72,128]{1,0:T(8,128)S(1)} %get-tuple-element.100), channel_id=1, source_target_pairs={{0,1},{1,2},{2,3},{3,4},{4,5},{5,6},{6,7},{7,8},{8,9},{9,10},{10,1... | collective-permute-start | bytes 110600 | tf_op jit(solution)/shard_map/ppermute | solution.py:501
  81.6 7.3 %collective-permute-start.19 = (f32[72,128]{1,0:T(8,128)S(1)}, f32[72,128]{1,0:T(8,128)S(1)}, u32[]{:S(2)}, u32[]{:S(2)}) collective-permute-start(f32[72,128]{1,0:T(8,128)S(1)} %get-tuple-element.101), channel_id=1, source_target_pairs={{1,0},{2,1},{3,2},{4,3},{5,4},{6,5},{7,6},{8,7},{9,8},{10,9},{11,1... | collective-permute-start | bytes 110600 | tf_op jit(solution)/shard_map/ppermute | solution.py:501
  90.1 6.1 %collective-permute-start.20 = (f32[72,128]{1,0:T(8,128)S(1)}, f32[72,128]{1,0:T(8,128)S(1)}, u32[]{:S(2)}, u32[]{:S(2)}) collective-permute-start(f32[72,128]{1,0:T(8,128)S(1)} %get-tuple-element.105), channel_id=1, source_target_pairs={{0,16},{16,32},{32,48},{48,64},{64,80},{80,96},{96,112},{112,0},{1... | collective-permute-start | bytes 110600 | tf_op jit(solution)/shard_map/ppermute | solution.py:501
  90.1 6.1 %collective-permute-start.21 = (f32[72,128]{1,0:T(8,128)S(1)}, f32[72,128]{1,0:T(8,128)S(1)}, u32[]{:S(2)}, u32[]{:S(2)}) collective-permute-start(f32[72,128]{1,0:T(8,128)S(1)} %get-tuple-element.106), channel_id=1, source_target_pairs={{16,0},{32,16},{48,32},{64,48},{80,64},{96,80},{112,96},{0,112},{1... | collective-permute-start | bytes 110600 | tf_op jit(solution)/shard_map/ppermute | solution.py:501
  96.4 7.3 %collective-permute-start.22 = (f32[72,128]{1,0:T(8,128)S(1)}, f32[72,128]{1,0:T(8,128)S(1)}, u32[]{:S(2)}, u32[]{:S(2)}) collective-permute-start(f32[72,128]{1,0:T(8,128)S(1)} %get-tuple-element.109), channel_id=1, source_target_pairs={{0,1},{1,2},{2,3},{3,4},{4,5},{5,6},{6,7},{7,8},{8,9},{9,10},{10,1... | collective-permute-start | bytes 110600 | tf_op jit(solution)/shard_map/ppermute | solution.py:501
  96.7 7.0 %collective-permute-start.23 = (f32[72,128]{1,0:T(8,128)S(1)}, f32[72,128]{1,0:T(8,128)S(1)}, u32[]{:S(2)}, u32[]{:S(2)}) collective-permute-start(f32[72,128]{1,0:T(8,128)S(1)} %get-tuple-element.110), channel_id=1, source_target_pairs={{1,0},{2,1},{3,2},{4,3},{5,4},{6,5},{7,6},{8,7},{9,8},{10,9},{11,1... | collective-permute-start | bytes 110600 | tf_op jit(solution)/shard_map/ppermute | solution.py:501
  106.2 6.7 %collective-permute-start.24 = (f32[144,128]{1,0:T(8,128)S(1)}, f32[144,128]{1,0:T(8,128)S(1)}, u32[]{:S(2)}, u32[]{:S(2)}) collective-permute-start(f32[144,128]{1,0:T(8,128)S(1)} %get-tuple-element.113), channel_id=1, source_target_pairs={{0,16},{16,32},{32,48},{48,64},{64,80},{80,96},{96,112},{112,0},{1... | collective-permute-start | bytes 221192 | tf_op jit(solution)/shard_map/ppermute | solution.py:501
  106.3 6.6 %collective-permute-start.25 = (f32[144,128]{1,0:T(8,128)S(1)}, f32[144,128]{1,0:T(8,128)S(1)}, u32[]{:S(2)}, u32[]{:S(2)}) collective-permute-start(f32[144,128]{1,0:T(8,128)S(1)} %get-tuple-element.114), channel_id=1, source_target_pairs={{16,0},{32,16},{48,32},{64,48},{80,64},{96,80},{112,96},{0,112},{1... | collective-permute-start | bytes 221192 | tf_op jit(solution)/shard_map/ppermute | solution.py:501
  113.1 7.1 %collective-permute-start.26 = (f32[72,128]{1,0:T(8,128)S(1)}, f32[72,128]{1,0:T(8,128)S(1)}, u32[]{:S(2)}, u32[]{:S(2)}) collective-permute-start(f32[72,128]{1,0:T(8,128)S(1)} %get-tuple-element.117), channel_id=1, source_target_pairs={{0,1},{1,2},{2,3},{3,4},{4,5},{5,6},{6,7},{7,8},{8,9},{9,10},{10,1... | collective-permute-start | bytes 110600 | tf_op jit(solution)/shard_map/ppermute | solution.py:501
  113.2 7.6 %collective-permute-start.27 = (f32[72,128]{1,0:T(8,128)S(1)}, f32[72,128]{1,0:T(8,128)S(1)}, u32[]{:S(2)}, u32[]{:S(2)}) collective-permute-start(f32[72,128]{1,0:T(8,128)S(1)} %get-tuple-element.118), channel_id=1, source_target_pairs={{1,0},{2,1},{3,2},{4,3},{5,4},{6,5},{7,6},{8,7},{9,8},{10,9},{11,1... | collective-permute-start | bytes 110600 | tf_op jit(solution)/shard_map/ppermute | solution.py:501
  124.3 7.2 %collective-permute-start.28 = (f32[216,128]{1,0:T(8,128)S(1)}, f32[216,128]{1,0:T(8,128)S(1)}, u32[]{:S(2)}, u32[]{:S(2)}) collective-permute-start(f32[216,128]{1,0:T(8,128)S(1)} %get-tuple-element.121), channel_id=1, source_target_pairs={{0,16},{16,32},{32,48},{48,64},{64,80},{80,96},{96,112},{112,0},{1... | collective-permute-start | bytes 331784 | tf_op jit(solution)/shard_map/ppermute | solution.py:501
  124.4 7.1 %collective-permute-start.29 = (f32[216,128]{1,0:T(8,128)S(1)}, f32[216,128]{1,0:T(8,128)S(1)}, u32[]{:S(2)}, u32[]{:S(2)}) collective-permute-start(f32[216,128]{1,0:T(8,128)S(1)} %get-tuple-element.122), channel_id=1, source_target_pairs={{16,0},{32,16},{48,32},{64,48},{80,64},{96,80},{112,96},{0,112},{1... | collective-permute-start | bytes 331784 | tf_op jit(solution)/shard_map/ppermute | solution.py:501
  131.7 7.1 %collective-permute-start.30 = (f32[72,128]{1,0:T(8,128)S(1)}, f32[72,128]{1,0:T(8,128)S(1)}, u32[]{:S(2)}, u32[]{:S(2)}) collective-permute-start(f32[72,128]{1,0:T(8,128)S(1)} %get-tuple-element.125), channel_id=1, source_target_pairs={{0,1},{1,2},{2,3},{3,4},{4,5},{5,6},{6,7},{7,8},{8,9},{9,10},{10,1... | collective-permute-start | bytes 110600 | tf_op jit(solution)/shard_map/ppermute | solution.py:501
  131.7 7.4 %collective-permute-start.31 = (f32[72,128]{1,0:T(8,128)S(1)}, f32[72,128]{1,0:T(8,128)S(1)}, u32[]{:S(2)}, u32[]{:S(2)}) collective-permute-start(f32[72,128]{1,0:T(8,128)S(1)} %get-tuple-element.126), channel_id=1, source_target_pairs={{1,0},{2,1},{3,2},{4,3},{5,4},{6,5},{7,6},{8,7},{9,8},{10,9},{11,1... | collective-permute-start | bytes 110600 | tf_op jit(solution)/shard_map/ppermute | solution.py:501
  (4 other events, 12.5 us)
where the time goes:
time: 146 us; the launch traced here: 145 us
  starting transfers between devices  78.7 us (54%)
  waiting for transfers between devices  33.1 us (23%)
  Pallas kernels  29.3 us (20%)
  local copies, waits for them, and re-layouts  2.64 us (2%)
    ppermute x32, starting transfers between devices, both_ways(): return (lax.ppermute(up, axis, fwd), lax.ppermute(down, axis, back))  78.7 us
    ppermute x32, waiting for transfers between devices, both_ways(): return (lax.ppermute(up, axis, fwd), lax.ppermute(down, axis, back))  33.1 us
    pallas_call x16, Pallas kernels, call(): pl.pallas_call(kernel, out_shape=[jax.ShapeDtypeStruct(s, F32) for s in o...  29.3 us
  transfers between devices with their start and end apart: 32, of which 20 were waited for; matrix products, arithmetic and copies ran while one was open for 0% of the time, Pallas kernels for 0%

commit v1 on v0

--- a/solution.py
+++ b/solution.py
@@ -50,13 +50,9 @@
     return jnp.dot(winv, parts, preferred_element_type=F32)
 
 
-def reverse_matrix(width, blocks=(0,)):
+def reverse_matrix(width):
     a, b = iota2(LANES, LANES)
-    out = jnp.zeros((LANES, LANES), F32)
-    for base in blocks:
-        inside = (b >= base) & (b < base + width)
-        out = jnp.where(inside & (a == 2 * base + width - 1 - b), 1.0, out)
-    return out
+    return jnp.where((b < width) & (a == width - 1 - b), 1.0, 0.0)
 
 
 def flag_row(flags, k):
@@ -64,10 +60,10 @@
 
 
 class Coef:
-    def __init__(self, ref):
-        self.mid = jnp.broadcast_to(ref[:, 0:1], (Z, LANES))
-        self.up = jnp.broadcast_to(ref[:, 1:2], (Z, LANES))
-        self.down = jnp.broadcast_to(ref[:, 2:3], (Z, LANES))
+    def __init__(self, ref, width=LANES):
+        self.mid = jnp.broadcast_to(ref[:, 0:1], (Z, width))
+        self.up = jnp.broadcast_to(ref[:, 1:2], (Z, width))
+        self.down = jnp.broadcast_to(ref[:, 2:3], (Z, width))
 
 
 def residual(co, f, c, v, beside):
@@ -93,13 +89,25 @@
     return jnp.where(lane == 3, col(last, base + ty - 1), out)
 
 
-def place_col(geom, v, y, offset, out):
+def whole_rows(geom):
+    return geom[1] == 1 and geom[2] == LANES
+
+
+def tile_rows(geom):
     m_rows, groups, ty = geom
+    return [(q * m_rows + m, m, q * ty) for m in range(m_rows) for q in range(groups)]
+
+
+def own_columns(geom, v):
+    ty = geom[2]
     lane = zl()
-    for m in range(m_rows):
+    out = jnp.zeros((Z, LANES), F32)
+    for r, m, base in tile_rows(geom):
         row = v[m]
-        for q in range(groups):
-            out = jnp.where(lane == offset + q * m_rows + m, col(row, q * ty + y), out)
+        first = roll(row, 2 * r + 1 - base)
+        out = jnp.where(lane == 2 * r + 1, first, out)
+        last = first if whole_rows(geom) else roll(row, 2 * r - (base + ty - 1))
+        out = jnp.where(lane == 2 * r, last, out)
     return out
 
 
@@ -145,12 +153,22 @@
 
 def put_y(geom, v, c, up, down):
     ty = geom[2]
-    for ref, edge, second in ((up, ty - 1, ty - 2), (down, 0, 1)):
-        out = place_col(geom, v, edge, 0, jnp.zeros((Z, LANES), F32))
-        out = place_col(geom, v, second, 32, out)
+    lane = zl()
+    out_up = jnp.zeros((Z, LANES), F32)
+    out_down = out_up
+    for r, m, base in tile_rows(geom):
+        row = v[m]
+        mine = lane // 2 == r
+        last = roll(row, 2 * r + 1 - (base + ty - 1))
+        first = roll(row, 2 * r - base)
+        out_up = jnp.where(mine, last, out_up)
+        out_down = jnp.where(mine, first, out_down)
         if c is not None:
-            out = place_col(geom, c, edge, 64, out)
-        ref[0:Z, :] = out
+            row = c[m]
+            out_up = jnp.where(lane == 65 + 2 * r, roll(row, 65 + 2 * r - (base + ty - 1)), out_up)
+            out_down = jnp.where(lane == 64 + 2 * r, roll(row, 64 + 2 * r - base), out_down)
+    up[0:Z, :] = out_up
+    down[0:Z, :] = out_down
 
 
 def merge_y(lo_extra, hi_extra, flags, up, down):
@@ -159,7 +177,7 @@
 
     def fill(part, values):
         for k, value in enumerate(values):
-            part = jnp.where(lane == 96 + k, value, part)
+            part = jnp.where(lane == 112 + k, value, part)
         return part
 
     lo = [col(lo_extra, k) for k in range(4)]
@@ -169,15 +187,19 @@
     return up_new, down_new
 
 
+def odd_lanes():
+    return zl() % 2 == 1
+
+
 class Halo:
     def __init__(self, lo, lo2, hi, hi2, dn, un):
         self.lo, self.lo2, self.hi, self.hi2, self.dn, self.un = lo, lo2, hi, hi2, dn, un
 
     def sides(self):
-        return jnp.where(zl() < 64, self.dn, roll(self.un, 64))
+        return jnp.where(odd_lanes(), self.dn, self.un)
 
     def seconds(self):
-        return jnp.where(zl() < 64, roll(self.dn, -32), roll(self.un, 32))
+        return jnp.where(odd_lanes(), roll(self.dn, 1), roll(self.un, -1))
 
 
 class Flags:
@@ -191,8 +213,10 @@
 
 def turn_sides(geom, sides, flag_dn, flag_un):
     tx = geom[0] * geom[1]
-    flag = jnp.where(zl() < 64, flag_dn, flag_un)
-    return jnp.where(flag > 0.5, lane_dot(sides, reverse_matrix(tx, (0, 64))), sides)
+    flag = jnp.where(odd_lanes(), flag_dn, flag_un)
+    a, b = iota2(LANES, LANES)
+    mat = jnp.where((b < 2 * tx) & (a == 2 * (tx - 1 - b // 2) + b % 2), 1.0, 0.0)
+    return jnp.where(flag > 0.5, lane_dot(sides, mat), sides)
 
 
 def frame(geom, fl, lo, hi, sides):
@@ -221,24 +245,21 @@
         halo.lo,
         halo.lo2,
         turn_row(geom, row_of(geom, v, 0), flag_row(fl.lo, 1)),
-        choose(fl.lo, 2, col(dn, 96), col(dn, 97)),
-        choose(fl.lo, 3, col(un, 96), col(un, 97)),
+        choose(fl.lo, 2, col(dn, 112), col(dn, 113)),
+        choose(fl.lo, 3, col(un, 112), col(un, 113)),
     )
     b_hi = beside_row(
         halo.hi,
         halo.hi2,
         turn_row(geom, row_of(geom, v, tx - 1), flag_row(fl.hi, 0)),
-        choose(fl.hi, 2, col(dn, 98), col(dn, 99)),
-        choose(fl.hi, 3, col(un, 98), col(un, 99)),
+        choose(fl.hi, 2, col(dn, 114), col(dn, 115)),
+        choose(fl.hi, 3, col(un, 114), col(un, 115)),
     )
     edge = halo.sides()
-    mine = place_col(geom, v, 0, 0, jnp.zeros((Z, LANES), F32))
-    mine = place_col(geom, v, ty - 1, 64, mine)
-    mine = turn_sides(geom, mine, flag_row(fl.dn, 3), flag_row(fl.un, 2))
-    below = jnp.where(lane == 0, col(dn, 100), roll(edge, 1))
-    below = jnp.where(lane == 64, col(un, 100), below)
-    above = jnp.where(lane == tx - 1, col(dn, 101), roll(edge, -1))
-    above = jnp.where(lane == 64 + tx - 1, col(un, 101), above)
+    mine = turn_sides(geom, own_columns(geom, v), flag_row(fl.dn, 3), flag_row(fl.un, 2))
+    below = jnp.where(lane == 1, col(dn, 116), jnp.where(lane == 0, col(un, 116), roll(edge, 2)))
+    last = 2 * (tx - 1)
+    above = jnp.where(lane == last + 1, col(dn, 117), jnp.where(lane == last, col(un, 117), roll(edge, -2)))
     b_sides = halo.seconds() + mine + below + above
     r_lo = residual(co, f_lo, c_lo, halo.lo, b_lo)
     r_hi = residual(co, f_hi, c_hi, halo.hi, b_hi)
@@ -264,8 +285,10 @@
     low_y, high_y = roll(here, 1), roll(here, -1)
     for q in range(groups):
         row = q * m_rows + m
-        low_y = jnp.where(lane == q * ty, col(sides, row), low_y)
-        high_y = jnp.where(lane == q * ty + ty - 1, col(sides, 64 + row), high_y)
+        low = roll(sides, q * ty - 2 * row - 1)
+        high = low if whole_rows(geom) else roll(sides, q * ty + ty - 1 - 2 * row)
+        low_y = jnp.where(lane == q * ty, low, low_y)
+        high_y = jnp.where(lane == q * ty + ty - 1, high, high_y)
     return residual(co, f[m], c[m], here, low_x + high_x + low_y + high_y)
 
 
@@ -334,10 +357,9 @@
 
 
 def own_data(geom, xlo, xhi, ydn, yun):
-    lane = zl()
     dn, un = ydn[0:Z, :], yun[0:Z, :]
-    f_sides = jnp.where(lane < 64, dn, roll(un, 64))
-    c_sides = jnp.where(lane < 64, roll(dn, -64), un)
+    f_sides = jnp.where(odd_lanes(), dn, un)
+    c_sides = roll(f_sides, -64)
     return (
         part_of(geom, xlo, 0),
         part_of(geom, xlo, 2),
@@ -359,6 +381,240 @@
         dst[x, NZ:Z, :] = jnp.zeros((Z - NZ, LANES), F32)
 
 
+STRIPS = {2: (6, 32, 256), 3: (3, 16, 128)}
+
+
+def in_tile(strip):
+    _, ty, width = strip
+    return lane_ids((Z, width)) % ty
+
+
+def group_dot(x, mat):
+    parts = [lane_dot(x[:, k : k + LANES], mat) for k in range(0, x.shape[1], LANES)]
+    return parts[0] if len(parts) == 1 else jnp.concatenate(parts, axis=1)
+
+
+def turn_groups(strip, x, flags, k, count):
+    _, ty, width = strip
+    a, b = iota2(LANES, LANES)
+    mat = jnp.where((a // ty == b // ty) & (b % ty < count) & (a % ty == count - 1 - b % ty), 1.0, 0.0)
+    flag = jnp.broadcast_to(flags[k : k + 1, :], (Z, width))
+    return jnp.where(flag > 0.5, group_dot(x, mat), x)
+
+
+def strip_ends(strip, v, flags):
+    m_rows, ty, _ = strip
+    low = turn_groups(strip, roll(v[m_rows - 1], ty), flags, 0, ty)
+    high = turn_groups(strip, roll(v[0], -ty), flags, 1, ty)
+    return low, high
+
+
+def strip_column(strip, v, y, offset, out):
+    lt = in_tile(strip)
+    for m in range(strip[0]):
+        out = jnp.where(lt == offset + m, roll(v[m], offset + m - y), out)
+    return out
+
+
+def strip_message(strip, v, c, ends, up, down):
+    m_rows, ty, width = strip
+    lt = in_tile(strip)
+    for ref, edge, second in ((up, ty - 1, ty - 2), (down, 0, 1)):
+        out = strip_column(strip, v, edge, 0, jnp.zeros((Z, width), F32))
+        out = strip_column(strip, v, second, m_rows, out)
+        if c is not None:
+            out = strip_column(strip, c, edge, 2 * m_rows, out)
+        for k, end in enumerate(ends):
+            out = jnp.where(lt == 3 * m_rows + k, roll(end, 3 * m_rows + k - edge), out)
+        ref[0:Z, :] = out
+
+
+def strip_edges(strip, winv, co, v, sides):
+    m_rows, _, width = strip
+    lt = in_tile(strip)
+    r = []
+    for x, raw, flags, k, y in sides:
+        mine = strip_column(strip, v, y, 0, jnp.zeros((Z, width), F32))
+        mine = turn_groups(strip, mine, flags, k, m_rows)
+        low = jnp.where(lt == 0, roll(x, -3 * m_rows), roll(x, 1))
+        high = jnp.where(lt == m_rows - 1, roll(x, -2 * m_rows - 2), roll(x, -1))
+        r.append(residual(co, raw, roll(raw, -2 * m_rows), x, roll(x, -m_rows) + mine + low + high))
+    d = block_dot(winv, jnp.concatenate(r, axis=1))
+    return [side[0] + d[:, k * width : (k + 1) * width] for k, side in enumerate(sides)]
+
+
+def strip_frame(strip, flags, low, high):
+    return turn_groups(strip, low, flags, 2, strip[0]), turn_groups(strip, high, flags, 3, strip[0])
+
+
+def strip_residual(strip, co, v, f, c, ends, sides, m):
+    m_rows, ty, _ = strip
+    lt = in_tile(strip)
+    low_x = v[m - 1] if m > 0 else ends[0]
+    high_x = v[m + 1] if m < m_rows - 1 else ends[1]
+    low_y = jnp.where(lt == 0, roll(sides[0], -m), roll(v[m], 1))
+    high_y = jnp.where(lt == ty - 1, roll(sides[1], ty - 1 - m), roll(v[m], -1))
+    return residual(co, f[m], c[m], v[m], low_x + high_x + low_y + high_y)
+
+
+def strip_relax(strip, winv, co, v, f, c, flags, sides, store):
+    ends = strip_ends(strip, v, flags)
+    for m in range(strip[0]):
+        r = strip_residual(strip, co, v, f, c, ends, sides, m)
+        store(m, v[m] + block_dot(winv, r))
+
+
+def strip_restrict(v, out):
+    a, b = iota2(LANES, LANES)
+    for m in range(3):
+        both = v[2 * m] + v[2 * m + 1]
+        out[m] = lane_dot(both[:, :LANES], jnp.where(a // 2 == b, 0.25, 0.0)) + lane_dot(
+            both[:, LANES:], jnp.where(a // 2 == b - 64, 0.25, 0.0)
+        )
+
+
+def open_strip_kernel(chunks, f, c, flags, up, down):
+    strip = STRIPS[2]
+    group = lane_ids((Z, LANES)) // 32
+    for m in range(6):
+        for ref, k in ((f, m), (c, 6 + m)):
+            part = (k // 4) * Z
+            halves = []
+            for h in range(2):
+                acc = None
+                for g in range(4):
+                    x = roll(chunks[4 * h + g, part : part + Z, :], (g - k % 4) * 32)
+                    acc = x if acc is None else jnp.where(group == g, x, acc)
+                halves.append(acc)
+            ref[m] = jnp.concatenate(halves, axis=1)
+    group = lane_ids((8, LANES)) // 32
+    for h in range(2):
+        acc = None
+        for g in range(4):
+            x = chunks[4 * h + g, 3 * Z : 3 * Z + 8, :]
+            acc = x if acc is None else jnp.where(group == g, x, acc)
+        flags[:, h * LANES : (h + 1) * LANES] = acc
+    strip_message(strip, f, c, strip_ends(strip, f, flags), up, down)
+    up[Z : Z + 8, :] = flags[...]
+    down[Z : Z + 8, :] = flags[...]
+
+
+def strip_sides(values, raws, dn, un, ty):
+    return (
+        (values[0], raws[0], dn[Z : Z + 8, :], 3, 0),
+        (values[1], raws[1], un[Z : Z + 8, :], 2, ty - 1),
+    )
+
+
+def pre_strip_kernel(f, c, w, vz, flags, dn, un, v_out, f_next, c_next, fl_next, up, down, one, res):
+    strip = STRIPS[2]
+    width = strip[2]
+    winv = w[...].astype(BF16)
+    co = Coef(vz, width)
+    for m in range(6):
+        one[m] = block_dot(winv, f[m])
+    raws = [dn[0:Z, :], un[0:Z, :]]
+    values = [block_dot(winv, x) for x in raws]
+    edges = strip_edges(strip, winv, co, one, strip_sides(values, raws, dn, un, strip[1]))
+    strip_relax(strip, winv, co, one, f, c, flags, strip_frame(strip, flags, *values), Setter(v_out))
+    ends = strip_ends(strip, v_out, flags)
+    sides = strip_frame(strip, flags, *edges)
+    for m in range(6):
+        res[m] = strip_residual(strip, co, v_out, f, c, ends, sides, m)
+    strip_restrict(res, f_next)
+    strip_restrict(c, c_next)
+    a, b = iota2(LANES, LANES)
+    fl_next[...] = lane_dot(flags[:, :LANES], jnp.where((b < 64) & (a == (b // 16) * 32), 1.0, 0.0)) + lane_dot(
+        flags[:, LANES:], jnp.where((b >= 64) & (a == (b // 16 - 4) * 32), 1.0, 0.0)
+    )
+    small = STRIPS[3]
+    strip_message(small, f_next, c_next, strip_ends(small, f_next, fl_next), up, down)
+    up[Z : Z + 8, :] = fl_next[...]
+    down[Z : Z + 8, :] = fl_next[...]
+
+
+def bottom_strip_kernel(f, c, w, vz, flags, dn, un, v_out, up, down, one):
+    strip = STRIPS[3]
+    winv = w[...].astype(BF16)
+    co = Coef(vz)
+    for m in range(3):
+        v_out[m] = block_dot(winv, f[m])
+    raws = [dn[0:Z, :], un[0:Z, :]]
+    values = [block_dot(winv, x) for x in raws]
+    edges = strip_edges(strip, winv, co, v_out, strip_sides(values, raws, dn, un, strip[1]))
+    strip_relax(strip, winv, co, v_out, f, c, flags, strip_frame(strip, flags, *values), Setter(one))
+    strip_relax(strip, winv, co, one, f, c, flags, strip_frame(strip, flags, *edges), Setter(v_out))
+    strip_message(strip, v_out, None, (), up, down)
+
+
+def last_strip_kernel(f, c, w, vz, flags, dn, un, v, fine_v, fine_flags, g, up, down, e):
+    strip, fine = STRIPS[3], STRIPS[2]
+    winv = w[...].astype(BF16)
+    strip_relax(strip, winv, Coef(vz), v, f, c, flags, strip_frame(strip, flags, dn[...], un[...]), Setter(e))
+    a, b = iota2(LANES, LANES)
+    for m in range(3):
+        add = jnp.concatenate([lane_dot(e[m], jnp.where(a == 64 * h + b // 2, 1.0, 0.0)) for h in range(2)], axis=1)
+        g[2 * m] = fine_v[2 * m] + add
+        g[2 * m + 1] = fine_v[2 * m + 1] + add
+    strip_message(fine, g, None, strip_ends(fine, g, fine_flags), up, down)
+
+
+def post_strip_kernel(
+    f, c, w, vz, flags, dn, un, g, gdn, gun, fine_v, xlo, xhi, own, g_out, lo_out, hi_out, up, down, one, e, tile, yup, ydown
+):
+    strip = STRIPS[2]
+    fine, geom = GEOM[1], GEOM[2]
+    winv = w[...].astype(BF16)
+    co = Coef(vz, strip[2])
+    raws = [dn[0:Z, :], un[0:Z, :]]
+    values = [gdn[...], gun[...]]
+    edges = strip_edges(strip, winv, co, g, strip_sides(values, raws, dn, un, strip[1]))
+    strip_relax(strip, winv, co, g, f, c, flags, strip_frame(strip, flags, *values), Setter(one))
+    strip_relax(strip, winv, co, one, f, c, flags, strip_frame(strip, flags, *edges), Setter(e))
+
+    place = lax.axis_index("gx")
+
+    def tile_row(m, step):
+        t = lax.rem(place + (step + 8), 8)
+        return pltpu.roll(e[m], lax.rem(8 - t, 8) * 32, axis=1)[:, :LANES]
+
+    for m in range(6):
+        tile[m] = tile_row(m, 0)
+    prolong_add(fine, geom, tile, fine_v, g_out)
+    a, b = iota2(LANES, LANES)
+    spread = jnp.where((b < 64) & (a == b // 2), 1.0, 0.0)
+    lane = zl()
+    extras = []
+    for ref, out, step, near in ((xlo, lo_out, -1, 5), (xhi, hi_out, 1, 0)):
+        first, last = tile_row(0, step), tile_row(5, step)
+        add = lane_dot(last if near else first, spread)
+        extra = part_of(fine, ref, 2)
+        for k, value in enumerate((col(first, 0), col(first, 31), col(last, 0), col(last, 31))):
+            extra = extra + jnp.where(lane == k, value, 0.0)
+        extras.append(extra)
+        for k, part in enumerate(pack(fine, [part_of(fine, ref, 0) + add, part_of(fine, ref, 1) + add, extra])):
+            out[k * Z : (k + 1) * Z, :] = part
+    put_y(fine, g_out, None, yup, ydown)
+    up[...], down[...] = merge_y(*extras, own, yup[...], ydown[...])
+
+
+def strip_ring(up, down):
+    nx, ny = lax.axis_size("gx"), lax.axis_size("gy")
+
+    def pairs(step):
+        out = []
+        for i in range(nx):
+            for j in range(ny):
+                to = (j + step) % ny
+                other = i ^ 1 if (2 * j // ny) != (2 * to // ny) else i
+                out.append((i * ny + j, other * ny + to))
+        return out
+
+    both = ("gx", "gy")
+    return lax.ppermute(up, both, pairs(1)), lax.ppermute(down, both, pairs(-1))
+
+
+LIMIT = 14 * 1024 * 1024
 VMEM = pl.BlockSpec(memory_space=pltpu.VMEM)
 
 
@@ -369,7 +625,7 @@
         in_specs=[VMEM] * len(args),
         out_specs=[VMEM] * len(outs),
         scratch_shapes=[pltpu.VMEM(s, F32) for s in scratch],
-        compiler_params=pltpu.CompilerParams(vmem_limit_bytes=48 * 1024 * 1024),
+        compiler_params=pltpu.CompilerParams(vmem_limit_bytes=LIMIT),
         name=name,
     )(*args)
 
@@ -385,13 +641,66 @@
 Y_FULL = (Z + 8, LANES)
 
 
-def open_kernel(f_in, c_in, flags, f, c, up, down, yup, ydown):
-    load_top(f_in, f)
-    load_top(c_in, c)
-    put_x(GEOM[0], f, c, up, down, flags[...])
+PARTS = 5
+
+
+def open_kernel(f_in, c_in, vert_in, flip_in, f, c, up, down, own, vz, f_raw, c_raw, vert, flip, sems, small):
+    rows = NZ * 24 // PARTS
+    copies = []
+    for k in range(PARTS):
+        for i, (src, dst) in enumerate(((f_in, f_raw), (c_in, c_raw))):
+            part = pl.ds(k * rows, rows)
+            copies.append(pltpu.make_async_copy(src.at[part, :], dst.at[part, :], sems.at[i, k]))
+    few = [pltpu.make_async_copy(vert_in, vert, small.at[0]), pltpu.make_async_copy(flip_in, flip, small.at[1])]
+    for copy in few + copies:
+        copy.start()
+    for copy in few:
+        copy.wait()
+    a, b = iota2(8, 4)
+    flags = jnp.broadcast_to(flip[...].astype(F32), (8, 4))
+    flags = jnp.broadcast_to(jnp.sum(jnp.where(a == b, flags, 0.0), axis=1, keepdims=True), (8, LANES))
+    own[...] = flags
+    a, b = iota2(Z, NZ + 1)
+    coef = jnp.broadcast_to(vert[...], (Z, NZ + 1))
+    high = jnp.sum(jnp.where((b == a + 1) & (a < NZ), coef, 0.0), axis=1, keepdims=True)
+    low = jnp.sum(jnp.where((b == a) & (a < NZ), coef, 0.0), axis=1, keepdims=True)
+    columns = [jnp.broadcast_to(x * 0.0625, (Z, LANES)) for x in (4.0 + high + low, high, low)]
+    lane = zl()
+    vz[...] = jnp.where(lane == 0, columns[0], jnp.where(lane == 1, columns[1], columns[2]))
+    for copy in copies:
+        copy.wait()
+    load_top(f_raw, f)
+    load_top(c_raw, c)
+    put_x(GEOM[0], f, c, up, down, flags)
+
+
+def block_matrix(inv):
+    width = 3 * Z
+    a, b = iota2(BLK, width)
+    b = b % Z
+    spread = jnp.where((b % BLK == a) & (b < NZ), 1.0, 0.0).astype(BF16)
+    whole = jnp.zeros((NZ, width), F32)
+    left = inv
+    for _ in range(3):
+        part = left.astype(BF16)
+        whole = whole + jnp.dot(part, spread, preferred_element_type=F32)
+        left = left - part.astype(F32)
+    a, b = iota2(NZ, width)
+    whole = jnp.where(a // BLK == (b % Z) // BLK, whole, 0.0)
+    high = whole.astype(BF16).astype(F32)
+    return jnp.where((b >= Z) & (b < 2 * Z), whole - high, high)
+
+
+def side_kernel(f, c, inv, own, w0, w1, w2, w3, one, c_next, c_tile, yup, ydown):
     put_y(GEOM[0], f, c, yup, ydown)
-    yup[Z : Z + 8, :] = flags[...]
-    ydown[Z : Z + 8, :] = flags[...]
+    yup[Z : Z + 8, :] = own[...]
+    ydown[Z : Z + 8, :] = own[...]
+    for level, w in enumerate((w0, w1, w2, w3)):
+        w[0:NZ, :] = block_matrix(inv[level])
+        w[NZ:Z, :] = jnp.zeros((Z - NZ, 3 * Z), F32)
+    start_tile(GEOM[0], w0[...].astype(BF16), f, Setter(one))
+    restrict(GEOM[0], GEOM[1], c, c_next)
+    restrict(GEOM[1], GEOM[2], c_next, c_tile)
 
 
 def merge_kernel(level, count):
@@ -408,55 +717,39 @@
     return kernel
 
 
-def pre_kernel(level):
-    geom, coarse = GEOM[level], GEOM[level + 1]
-
-    def kernel(f, c, w, vz, own, xlo, xhi, ydn, yun, v_out, f_next, c_next, up, down, yup, ydown, one, res):
-        winv = w[...].astype(BF16)
-        co = Coef(vz)
-        fl = flags_of(geom, own, xlo, xhi, ydn, yun)
-        start_tile(geom, winv, f, Setter(one))
-        halo, _ = messages(geom, xlo, xhi, ydn, yun, winv)
-        lo2, hi2, sides2 = relax_edges(geom, winv, co, one, halo, fl, *own_data(geom, xlo, xhi, ydn, yun))
-        relax_tile(geom, winv, co, one, f, c, frame(geom, fl, halo.lo, halo.hi, halo.sides()), Setter(v_out))
-        lo, hi, sides = frame(geom, fl, lo2, hi2, sides2)
-        for m in range(geom[0]):
-            res[m] = tile_residual(geom, co, v_out, f, c, lo, hi, sides, m)
-        restrict(geom, coarse, res, f_next)
-        restrict(geom, coarse, c, c_next)
-        put_x(coarse, f_next, c_next, up, down, own[...])
-        put_y(coarse, f_next, c_next, yup, ydown)
-        yup[Z : Z + 8, :] = own[...]
-        ydown[Z : Z + 8, :] = own[...]
-
-    return kernel
-
-
-def bottom_kernel(f, c, w, vz, own, xlo, xhi, ydn, yun, v_out, up, down, yup, ydown, one):
-    geom = GEOM[3]
+def pre_tile(level, f, c, w, vz, own, xlo, xhi, ydn, yun, one, v_out, res):
+    geom = GEOM[level]
     winv = w[...].astype(BF16)
     co = Coef(vz)
     fl = flags_of(geom, own, xlo, xhi, ydn, yun)
-    start_tile(geom, winv, f, Setter(v_out))
     halo, _ = messages(geom, xlo, xhi, ydn, yun, winv)
-    lo2, hi2, sides2 = relax_edges(geom, winv, co, v_out, halo, fl, *own_data(geom, xlo, xhi, ydn, yun))
-    relax_tile(geom, winv, co, v_out, f, c, frame(geom, fl, halo.lo, halo.hi, halo.sides()), Setter(one))
-    relax_tile(geom, winv, co, one, f, c, frame(geom, fl, lo2, hi2, sides2), Setter(v_out))
-    put_x(geom, v_out, None, up, down)
-    put_y(geom, v_out, None, yup, ydown)
-
-
-def last_kernel(f, c, w, vz, own, xlo, xhi, ydn, yun, v, fine_v, g, up, down, yup, ydown, e):
-    geom, fine = GEOM[3], GEOM[2]
-    winv = w[...].astype(BF16)
-    co = Coef(vz)
-    fl = Flags(own[...], None, None, None, None)
-    sides = jnp.where(zl() < 64, ydn[...], roll(yun[...], 64))
-    edges = frame(geom, fl, part_of(geom, xlo, 0), part_of(geom, xhi, 0), sides)
-    relax_tile(geom, winv, co, v, f, c, edges, Setter(e))
-    prolong_add(fine, geom, e, fine_v, g)
-    put_x(fine, g, None, up, down)
-    put_y(fine, g, None, yup, ydown)
+    lo2, hi2, sides2 = relax_edges(geom, winv, co, one, halo, fl, *own_data(geom, xlo, xhi, ydn, yun))
+    relax_tile(geom, winv, co, one, f, c, frame(geom, fl, halo.lo, halo.hi, halo.sides()), Setter(v_out))
+    lo, hi, sides = frame(geom, fl, lo2, hi2, sides2)
+    for m in range(geom[0]):
+        res[m] = tile_residual(geom, co, v_out, f, c, lo, hi, sides, m)
+
+
+def pre0_kernel(f, c, w, vz, own, xlo, xhi, ydn, yun, one, c_next, v_out, f_next, up, down, yup, ydown, res):
+    pre_tile(0, f, c, w, vz, own, xlo, xhi, ydn, yun, one, v_out, res)
+    coarse = GEOM[1]
+    restrict(GEOM[0], coarse, res, f_next)
+    put_x(coarse, f_next, c_next, up, down, own[...])
+    put_y(coarse, f_next, c_next, yup, ydown)
+    yup[Z : Z + 8, :] = own[...]
+    ydown[Z : Z + 8, :] = own[...]
+
+
+def pre1_kernel(f, c, w, vz, own, xlo, xhi, ydn, yun, c_tile, v_out, up, down, chunks, one, res, f_next):
+    start_tile(GEOM[1], w[...].astype(BF16), f, Setter(one))
+    pre_tile(1, f, c, w, vz, own, xlo, xhi, ydn, yun, one, v_out, res)
+    restrict(GEOM[1], GEOM[2], res, f_next)
+    put_x(GEOM[1], v_out, None, up, down)
+    whole = pack(GEOM[2], [f_next[m] for m in range(6)] + [c_tile[m] for m in range(6)])
+    for t in range(8):
+        for k, part in enumerate(whole):
+            chunks[t, k * Z : (k + 1) * Z, :] = part
+        chunks[t, 3 * Z : 3 * Z + 8, :] = own[...]
 
 
 def post_kernel(level):
@@ -501,91 +794,88 @@
     return lax.ppermute(up, axis, fwd), lax.ppermute(down, axis, back)
 
 
-def block_matrices(block_inverse):
-    levels = block_inverse.shape[0]
-    whole = jnp.zeros((levels, Z, Z), F32)
-    for k in range(NBLK):
-        lo, hi = k * BLK, Z - (k + 1) * BLK
-        whole = whole + jnp.pad(block_inverse[:, k], ((0, 0), (lo, hi), (lo, hi)))
-    high = lax.reduce_precision(whole, 8, 7)
-    low = lax.reduce_precision(whole - high, 8, 7)
-    return jnp.concatenate([high, low, high], axis=2)
-
-
-def vertical_columns(vert_coef):
-    zero = jnp.zeros((1,), F32)
-    up = jnp.concatenate([vert_coef[1:], zero, zero])
-    down = jnp.concatenate([vert_coef[:-1], zero, zero])
-    cols = jnp.stack([4.0 + up + down, up, down], axis=1) * 0.0625
-    return jnp.pad(cols, ((0, 0), (0, LANES - 3)))
-
-
 def on_device(right_side, helm_coef, vert_coef, block_inverse, edge_flip):
-    own = jnp.pad(jnp.broadcast_to(edge_flip.reshape(4, 1).astype(F32), (4, LANES)), ((0, 4), (0, 0)))
-    vz = vertical_columns(vert_coef)
-    w = block_matrices(block_inverse)
+    inv = block_inverse.reshape(4, NZ, BLK)
     f_in = right_side.reshape(NZ * 24, LANES)
     c_in = helm_coef.reshape(NZ * 24, LANES)
-
-    def exchange(level, count, up, down, yup, ydown):
-        xlo, xhi = both_ways(up, down, "gx")
+    vert = vert_coef.reshape(1, NZ + 1)
+    flip = edge_flip.reshape(1, 4)
+
+    ys = (Z, LANES)
+    t0, t1, t2 = tile_shape(0), tile_shape(1), tile_shape(2)
+    xs = x_shape(0, 4, True)
+    f, c, up, down, own, vz = pl.pallas_call(
+        open_kernel,
+        out_shape=[jax.ShapeDtypeStruct(x, F32) for x in (t0, t0, xs, xs, (8, LANES), ys)],
+        in_specs=[pl.BlockSpec(memory_space=pl.ANY)] * 4,
+        out_specs=[VMEM] * 6,
+        scratch_shapes=[pltpu.VMEM((NZ * 24, LANES), F32)] * 2
+        + [pltpu.VMEM((1, NZ + 1), F32), pltpu.VMEM((1, 4), jnp.int32)]
+        + [pltpu.SemaphoreType.DMA((2, PARTS)), pltpu.SemaphoreType.DMA((2,))],
+        compiler_params=pltpu.CompilerParams(vmem_limit_bytes=58 * 1024 * 1024),
+        name="open",
+    )(f_in, c_in, vert, flip)
+    xlo, xhi = both_ways(up, down, "gx")
+    ws = (Z, 3 * Z)
+    *w, one, c1, c_tile, yup, ydown = call(
+        side_kernel, [ws] * 4 + [t0, t1, t2, Y_FULL, Y_FULL], [f, c, inv, own], name="side"
+    )
+
+    def to_sides(level, count, xlo, xhi, yup, ydown):
         shape = yup.shape
         yup, ydown = call(merge_kernel(level, count), [shape, shape], [xlo, xhi, own, yup, ydown], name=f"merge{level}")
-        ydn, yun = both_ways(yup, ydown, "gy")
-        return xlo, xhi, ydn, yun
-
-    xs = x_shape(0, 4, True)
-    f, c, *msg = call(
-        open_kernel, [tile_shape(0)] * 2 + [xs, xs, Y_FULL, Y_FULL], [f_in, c_in, own], name="open"
-    )
-    saved = []
-    for level in range(3):
-        got = exchange(level, 4, *msg)
-        xs = x_shape(level + 1, 4, True)
-        t = tile_shape(level)
-        nxt = tile_shape(level + 1)
-        v, f_next, c_next, *msg = call(
-            pre_kernel(level),
-            [t, nxt, nxt, xs, xs, Y_FULL, Y_FULL],
-            [f, c, w[level], vz, own, *got],
-            [t, t],
-            name=f"pre{level}",
-        )
-        saved.append((f, c, got, v))
-        f, c = f_next, c_next
-    got = exchange(3, 4, *msg)
-    t = tile_shape(3)
-    xs, ys = x_shape(3, 3, False), (Z, LANES)
-    v, up, down, yup, ydown = call(
-        bottom_kernel, [t, xs, xs, ys, ys], [f, c, w[3], vz, own, *got], [t], name="bottom"
+        return both_ways(yup, ydown, "gy")
+
+    got0 = (xlo, xhi, *to_sides(0, 4, xlo, xhi, yup, ydown))
+    xs = x_shape(1, 4, True)
+    v0, f1, up, down, yup, ydown = call(
+        pre0_kernel, [t0, t1, xs, xs, Y_FULL, Y_FULL], [f, c, w[0], vz, own, *got0, one, c1], [t0], name="pre0"
     )
     xlo, xhi = both_ways(up, down, "gx")
-    ydn, yun = both_ways(yup, ydown, "gy")
-    t2 = tile_shape(2)
-    xs = x_shape(2, 3, False)
-    g, *msg = call(
-        last_kernel,
-        [t2, xs, xs, ys, ys],
-        [f, c, w[3], vz, own, xlo, xhi, ydn, yun, v, saved[2][3]],
-        [t],
-        name="last",
-    )
-    for level in (2, 1, 0):
-        f, c, got, _ = saved[level]
-        ggot = exchange(level, 3, *msg)
-        t = tile_shape(level)
-        args = [f, c, w[level], vz, own, *got, g, *ggot]
-        if level == 0:
-            (out,) = call(post_kernel(0), [(NZ * 24, LANES)], args, [t], name="post0")
-            return out.reshape(NZ, 24, LANES)
-        xs = x_shape(level - 1, 3, False)
-        g, *msg = call(
-            post_kernel(level),
-            [tile_shape(level - 1), xs, xs, ys, ys],
-            args + [saved[level - 1][3]],
-            [t, t],
-            name=f"post{level}",
-        )
+    got1 = (xlo, xhi, *to_sides(1, 4, xlo, xhi, yup, ydown))
+    xs = x_shape(1, 3, False)
+    v1, up, down, chunks = call(
+        pre1_kernel, [t1, xs, xs, (8, 3 * Z + 8, LANES)], [f1, c1, w[1], vz, own, *got1, c_tile], [t1, t1, t2], name="pre1"
+    )
+    v1_lo, v1_hi = both_ways(up, down, "gx")
+    chunks = lax.all_to_all(chunks, "gx", 0, 0)
+    s2, s3 = (6, Z, 256), (3, Z, 128)
+    m2, m3 = (Z, 256), (Z, 128)
+    full2, full3 = (Z + 8, 256), (Z + 8, 128)
+    f2, c2, fl2, up, down = call(open_strip_kernel, [s2, s2, (8, 256), full2, full2], [chunks], name="open2")
+    side2 = strip_ring(up, down)
+    v2, f3, c3, fl3, up, down = call(
+        pre_strip_kernel, [s2, s3, s3, (8, 128), full3, full3], [f2, c2, w[2], vz, fl2, *side2], [s2, s2], name="pre2"
+    )
+    side3 = strip_ring(up, down)
+    v3, up, down = call(bottom_strip_kernel, [s3, m3, m3], [f3, c3, w[3], vz, fl3, *side3], [s3], name="bottom")
+    side = strip_ring(up, down)
+    g2, up, down = call(
+        last_strip_kernel, [s2, m2, m2], [f3, c3, w[3], vz, fl3, *side, v3, v2, fl2], [s3], name="last"
+    )
+    side = strip_ring(up, down)
+    g1, lo, hi, up, down = call(
+        post_strip_kernel,
+        [t1, xs, xs, ys, ys],
+        [f2, c2, w[2], vz, fl2, *side2, g2, *side, v1, v1_lo, v1_hi, own],
+        [s2, s2, t2, ys, ys],
+        name="post2",
+    )
+    side = both_ways(up, down, "gy")
+    xs = x_shape(0, 3, False)
+    g0, up, down, yup, ydown = call(
+        post_kernel(1),
+        [t0, xs, xs, ys, ys],
+        [f1, c1, w[1], vz, own, *got1, g1, lo, hi, *side, v0],
+        [t1, t1],
+        name="post1",
+    )
+    xlo, xhi = both_ways(up, down, "gx")
+    got = (xlo, xhi, *to_sides(0, 3, xlo, xhi, yup, ydown))
+    (out,) = call(
+        post_kernel(0), [(NZ * 24, LANES)], [f, c, w[0], vz, own, *got0, g0, *got], [t0], name="post0"
+    )
+    return out.reshape(NZ, 24, LANES)
 
 
 def solution(mesh):

time: 146 us -> 128 us (0.88)
  starting transfers between devices: 78.7 us -> 59.1 us
  blocking collectives: 0 us -> 16 us
  waiting for transfers between devices: 33.1 us -> 20.8 us
    ppermute x32 -> x16, starting transfers between devices: 78.7 us -> 38.4 us  [both_ways(): return (lax.ppermute(up, axis, fwd), lax.ppermute(down, axis, back))]
    ppermute x0 -> x8, starting transfers between devices: none -> 20.7 us  [the longest x4 20.4 us: strip_ring(): lax.ppermute(down, both, pairs(-1))]
    ppermute x32 -> x16, waiting for transfers between devices: 33.1 us -> 14.9 us  [both_ways(): return (lax.ppermute(up, axis, fwd), lax.ppermute(down, axis, back))]
    all_to_all x0 -> x1, blocking collectives: none -> 16 us  [on_device(): chunks = lax.all_to_all(chunks, 'gx', 0, 0)]
    ppermute x0 -> x8, waiting for transfers between devices: none -> 5.83 us  [the longest x4 5.75 us: strip_ring(): lax.ppermute(up, both, pairs(1))]
    pallas_call x16 -> x13, Pallas kernels: 29.3 us -> 25.1 us  [call(): pl.pallas_call(kernel, out_shape=[jax.ShapeDtypeStruct(s, F32) for s in o...]
    pallas_call x0 -> x1, Pallas kernels: none -> 3.15 us  [on_device(): pl.pallas_call(open_kernel, out_shape=[jax.ShapeDtypeStruct(x, F32) for x...]
    unnamed x9 -> x14, local copies, waits for them, and re-layouts: 2.33 us -> 3.03 us
  transfers between devices with their start and end apart: 32 -> 24, of which waited for: 20 -> 14; matrix products, arithmetic and copies ran while one was open for 0% -> 0% of each run, Pallas kernels for 0% -> 2%
where the time goes in v1:
time: 128 us; the launch traced here: 127 us
  starting transfers between devices  59.1 us (46%)
  Pallas kernels  28.3 us (22%)
  waiting for transfers between devices  20.8 us (16%)
  blocking collectives  16 us (12%)
  local copies, waits for them, and re-layouts  3.04 us (2%)
    ppermute x16, starting transfers between devices, both_ways(): return (lax.ppermute(up, axis, fwd), lax.ppermute(down, axis, back))  38.4 us
    pallas_call x13, Pallas kernels, call(): pl.pallas_call(kernel, out_shape=[jax.ShapeDtypeStruct(s, F32) for s in o...  25.1 us
    ppermute x4, starting transfers between devices, strip_ring(): lax.ppermute(down, both, pairs(-1))  20.4 us
    all_to_all x1, blocking collectives, on_device(): chunks = lax.all_to_all(chunks, 'gx', 0, 0)  16 us
    ppermute x16, waiting for transfers between devices, both_ways(): return (lax.ppermute(up, axis, fwd), lax.ppermute(down, axis, back))  14.9 us
    ppermute x4, waiting for transfers between devices, strip_ring(): lax.ppermute(up, both, pairs(1))  5.75 us
    pallas_call x1, Pallas kernels, on_device(): pl.pallas_call(open_kernel, out_shape=[jax.ShapeDtypeStruct(x, F32) for x...  3.15 us
    unnamed x14, local copies, waits for them, and re-layouts  3.03 us
  transfers between devices with their start and end apart: 24, of which 14 were waited for; matrix products, arithmetic and copies ran while one was open for 0% of the time, Pallas kernels for 2%

profile of v1, /device:TPU:0, one launch (start us, length us, event | category | flops | bytes accessed | tf_op | source)
XLA Modules:
  0.0 127.4 jit_solution(10154836647808382948)
XLA Ops:
  0.0 3.2 %open.1 = (f32[24,72,128]{2,1,0:T(8,128)}, f32[24,72,128]{2,1,0:T(8,128)}, f32[296,128]{1,0:T(8,128)}, f32[296,128]{1,0:T(8,128)}, f32[8,128]{1,0:T(8,128)}, /*index=5*/f32[72,128]{1,0:T(8,128)}) custom-call(f32[1680,128]{1,0:T(8,128)} %bitcast.6, f32[1680,128]{1,0:T(8,128)} %bitcast.7, f32[1,71]{1,0:T(1,128)} %bitcast.9, s32[1,4]{1,0:T(1,128)} %bitcast.10), custom_call_target="tpu_custom_call" | custom-call | tf_op jit(solution)/shard_map/open/pallas_call | solution.py:807
  3.2 1.7 %collective-permute-start = (f32[296,128]{1,0:T(8,128)}, f32[296,128]{1,0:T(8,128)S(1)}, u32[]{:S(2)}, u32[]{:S(2)}) collective-permute-start(f32[296,128]{1,0:T(8,128)} %get-tuple-element.68), channel_id=1, source_target_pairs={{0,16},{16,32},{32,48},{48,64},{64,80},{80,96},{96,112},{112,0},{1... | collective-permute-start | bytes 454664 | tf_op jit(solution)/shard_map/ppermute | solution.py:794
  4.9 2.5 %collective-permute-start.1 = (f32[296,128]{1,0:T(8,128)}, f32[296,128]{1,0:T(8,128)S(1)}, u32[]{:S(2)}, u32[]{:S(2)}) collective-permute-start(f32[296,128]{1,0:T(8,128)} %get-tuple-element.69), channel_id=1, source_target_pairs={{16,0},{32,16},{48,32},{64,48},{80,64},{96,80},{112,96},{0,112},{1... | collective-permute-start | bytes 454664 | tf_op jit(solution)/shard_map/ppermute | solution.py:794
  11.6 2.1 %collective-permute-done.1.xhi = f32[296,128]{1,0:T(8,128)S(1)} collective-permute-done((f32[296,128]{1,0:T(8,128)}, f32[296,128]{1,0:T(8,128)S(1)}, u32[]{:S(2)}, u32[]{:S(2)}) %collective-permute-start.1) | collective-permute-done | bytes 151584 | tf_op jit(solution)/shard_map/ppermute | solution.py:794
  14.0 5.3 %collective-permute-start.3 = (f32[80,128]{1,0:T(8,128)S(1)}, f32[80,128]{1,0:T(8,128)S(1)}, u32[]{:S(2)}, u32[]{:S(2)}) collective-permute-start(f32[80,128]{1,0:T(8,128)S(1)} %get-tuple-element.73), channel_id=1, source_target_pairs={{1,0},{2,1},{3,2},{4,3},{5,4},{6,5},{7,6},{8,7},{9,8},{10,9},{11,1... | collective-permute-start | bytes 122888 | tf_op jit(solution)/shard_map/ppermute | solution.py:794
  19.3 1.7 %collective-permute-done.2.ydn = f32[80,128]{1,0:T(8,128)S(1)} collective-permute-done((f32[80,128]{1,0:T(8,128)S(1)}, f32[80,128]{1,0:T(8,128)S(1)}, u32[]{:S(2)}, u32[]{:S(2)}) %collective-permute-start.2) | collective-permute-done | bytes 40992 | tf_op jit(solution)/shard_map/ppermute | solution.py:794
  21.0 3.8 %pre0.1 = (f32[24,72,128]{2,1,0:T(8,128)S(1)}, f32[6,72,128]{2,1,0:T(8,128)S(1)}, f32[152,128]{1,0:T(8,128)S(1)}, f32[152,128]{1,0:T(8,128)S(1)}, f32[80,128]{1,0:T(8,128)S(1)}, /*index=5*/f32[80,128]{1,0:T(8,128)S(1)}) custom-call(f32[24,72,128]{2,1,0:T(8,128)S(1)} %copy-done.1, f32[24,72,128]{2,1,0:T(8,128)S(1)} %copy-done.2, ...), custom_call_target="tpu_custom_call" | custom-call | tf_op jit(solution)/shard_map/pre0/pallas_call | solution.py:622
  25.2 3.9 %collective-permute-start.5 = (f32[152,128]{1,0:T(8,128)S(1)}, f32[152,128]{1,0:T(8,128)S(1)}, u32[]{:S(2)}, u32[]{:S(2)}) collective-permute-start(f32[152,128]{1,0:T(8,128)S(1)} %get-tuple-element.79), channel_id=1, source_target_pairs={{16,0},{32,16},{48,32},{64,48},{80,64},{96,80},{112,96},{0,112},{1... | collective-permute-start | bytes 233480 | tf_op jit(solution)/shard_map/ppermute | solution.py:794
  29.0 2.5 %collective-permute-done.4.xlo = f32[152,128]{1,0:T(8,128)S(1)} collective-permute-done((f32[152,128]{1,0:T(8,128)S(1)}, f32[152,128]{1,0:T(8,128)S(1)}, u32[]{:S(2)}, u32[]{:S(2)}) %collective-permute-start.4) | collective-permute-done | bytes 77856 | tf_op jit(solution)/shard_map/ppermute | solution.py:794
  32.0 5.3 %collective-permute-start.7 = (f32[80,128]{1,0:T(8,128)S(1)}, f32[80,128]{1,0:T(8,128)S(1)}, u32[]{:S(2)}, u32[]{:S(2)}) collective-permute-start(f32[80,128]{1,0:T(8,128)S(1)} %get-tuple-element.83), channel_id=1, source_target_pairs={{1,0},{2,1},{3,2},{4,3},{5,4},{6,5},{7,6},{8,7},{9,8},{10,9},{11,1... | collective-permute-start | bytes 122888 | tf_op jit(solution)/shard_map/ppermute | solution.py:794
  37.3 1.7 %collective-permute-done.6.ydn = f32[80,128]{1,0:T(8,128)S(1)} collective-permute-done((f32[80,128]{1,0:T(8,128)S(1)}, f32[80,128]{1,0:T(8,128)S(1)}, u32[]{:S(2)}, u32[]{:S(2)}) %collective-permute-start.6) | collective-permute-done | bytes 40992 | tf_op jit(solution)/shard_map/ppermute | solution.py:794
  39.0 2.3 %pre1.1 = (f32[6,72,128]{2,1,0:T(8,128)S(1)}, f32[144,128]{1,0:T(8,128)S(1)}, f32[144,128]{1,0:T(8,128)S(1)}, f32[8,224,128]{2,1,0:T(8,128)S(1)}) custom-call(f32[6,72,128]{2,1,0:T(8,128)S(1)} %get-tuple-element.76.f, f32[6,72,128]{2,1,0:T(8,128)S(1)} %get-tuple-element.75.c_next.c, f32[72,216]{1,0:T(8,128)S(1)} %get-tuple-element.77.w, ...), custom_call_target="tpu_custom_call" | custom-call | tf_op jit(solution)/shard_map/pre1/pallas_call | solution.py:622
  41.3 16.0 %all_to_all.5.chunks = f32[8,224,128]{2,1,0:T(8,128)S(1)} all-to-all(f32[8,224,128]{2,1,0:T(8,128)S(1)} %get-tuple-element.85), channel_id=1, replica_groups=mesh['gx'=8,'gy'=16] {'gx'}, dimensions={0} | all-to-all | bytes 1835008 | tf_op jit(solution)/shard_map/all_to_all | solution.py:841
  57.2 1.6 %open2.1 = (f32[6,72,256]{2,1,0:T(8,128)S(1)}, f32[6,72,256]{2,1,0:T(8,128)S(1)}, f32[8,256]{1,0:T(8,128)S(1)}, f32[80,256]{1,0:T(8,128)S(1)}, f32[80,256]{1,0:T(8,128)S(1)}) custom-call(f32[8,224,128]{2,1,0:T(8,128)S(1)} %all_to_all.5.chunks), custom_call_target="tpu_custom_call" | custom-call | tf_op jit(solution)/shard_map/open2/pallas_call | solution.py:622
  58.9 5.1 %collective-permute-start.9 = (f32[80,256]{1,0:T(8,128)S(1)}, f32[80,256]{1,0:T(8,128)S(1)}, u32[]{:S(2)}, u32[]{:S(2)}) collective-permute-start(f32[80,256]{1,0:T(8,128)S(1)} %get-tuple-element.91), channel_id=1, source_target_pairs={{0,31},{1,0},{2,1},{3,2},{4,3},{5,4},{6,5},{7,6},{8,23},{9,8},{10,... | collective-permute-start | bytes 245768 | tf_op jit(solution)/shard_map/ppermute | solution.py:614
  64.0 2.1 %collective-permute-done.8.dn = f32[80,256]{1,0:T(8,128)S(1)} collective-permute-done((f32[80,256]{1,0:T(8,128)S(1)}, f32[80,256]{1,0:T(8,128)S(1)}, u32[]{:S(2)}, u32[]{:S(2)}) %collective-permute-start.8) | collective-permute-done | bytes 81952 | tf_op jit(solution)/shard_map/ppermute | solution.py:614
  66.1 2.9 %pre2.1 = (f32[6,72,256]{2,1,0:T(8,128)S(1)}, f32[3,72,128]{2,1,0:T(8,128)S(1)}, f32[3,72,128]{2,1,0:T(8,128)S(1)}, f32[8,128]{1,0:T(8,128)S(1)}, f32[80,128]{1,0:T(8,128)S(1)}, /*index=5*/f32[80,128]{1,0:T(8,128)S(1)}) custom-call(f32[6,72,256]{2,1,0:T(8,128)S(1)} %get-tuple-element.86.f, f32[6,72,256]{2,1,0:T(8,128)S(1)} %get-tuple-element.87.c, ...), custom_call_target="tpu_custom_call" | custom-call | tf_op jit(solution)/shard_map/pre2/pallas_call | solution.py:622
  69.0 5.1 %collective-permute-start.11 = (f32[80,128]{1,0:T(8,128)S(1)}, f32[80,128]{1,0:T(8,128)S(1)}, u32[]{:S(2)}, u32[]{:S(2)}) collective-permute-start(f32[80,128]{1,0:T(8,128)S(1)} %get-tuple-element.97), channel_id=1, source_target_pairs={{0,31},{1,0},{2,1},{3,2},{4,3},{5,4},{6,5},{7,6},{8,23},{9,8},{10,... | collective-permute-start | bytes 122888 | tf_op jit(solution)/shard_map/ppermute | solution.py:614
  74.2 1.6 %collective-permute-done.10.dn = f32[80,128]{1,0:T(8,128)S(1)} collective-permute-done((f32[80,128]{1,0:T(8,128)S(1)}, f32[80,128]{1,0:T(8,128)S(1)}, u32[]{:S(2)}, u32[]{:S(2)}) %collective-permute-start.10) | collective-permute-done | bytes 40992 | tf_op jit(solution)/shard_map/ppermute | solution.py:614
  77.3 5.1 %collective-permute-start.13 = (f32[72,128]{1,0:T(8,128)S(1)}, f32[72,128]{1,0:T(8,128)S(1)}, u32[]{:S(2)}, u32[]{:S(2)}) collective-permute-start(f32[72,128]{1,0:T(8,128)S(1)} %get-tuple-element.99), channel_id=1, source_target_pairs={{0,31},{1,0},{2,1},{3,2},{4,3},{5,4},{6,5},{7,6},{8,23},{9,8},{10,... | collective-permute-start | bytes 110600 | tf_op jit(solution)/shard_map/ppermute | solution.py:614
  82.5 4.1 %collective-permute-start.17 = (f32[144,128]{1,0:T(8,128)S(1)}, f32[144,128]{1,0:T(8,128)S(1)}, u32[]{:S(2)}, u32[]{:S(2)}) collective-permute-start(f32[144,128]{1,0:T(8,128)S(1)} %get-tuple-element.107), channel_id=1, source_target_pairs={{16,0},{32,16},{48,32},{64,48},{80,64},{96,80},{112,96},{0,112},{1... | collective-permute-start | bytes 221192 | tf_op jit(solution)/shard_map/ppermute | solution.py:794
  88.0 5.1 %collective-permute-start.15 = (f32[72,256]{1,0:T(8,128)S(1)}, f32[72,256]{1,0:T(8,128)S(1)}, u32[]{:S(2)}, u32[]{:S(2)}) collective-permute-start(f32[72,256]{1,0:T(8,128)S(1)} %get-tuple-element.104), channel_id=1, source_target_pairs={{0,31},{1,0},{2,1},{3,2},{4,3},{5,4},{6,5},{7,6},{8,23},{9,8},{10,... | collective-permute-start | bytes 221192 | tf_op jit(solution)/shard_map/ppermute | solution.py:614
  93.0 2.0 %collective-permute-done.14.gdn = f32[72,256]{1,0:T(8,128)S(1)} collective-permute-done((f32[72,256]{1,0:T(8,128)S(1)}, f32[72,256]{1,0:T(8,128)S(1)}, u32[]{:S(2)}, u32[]{:S(2)}) %collective-permute-start.14) | collective-permute-done | bytes 73760 | tf_op jit(solution)/shard_map/ppermute | solution.py:614
  95.1 3.6 %post2.1 = (f32[6,72,128]{2,1,0:T(8,128)S(1)}, f32[144,128]{1,0:T(8,128)S(1)}, f32[144,128]{1,0:T(8,128)S(1)}, f32[72,128]{1,0:T(8,128)S(1)}, f32[72,128]{1,0:T(8,128)S(1)}) custom-call(f32[6,72,256]{2,1,0:T(8,128)S(1)} %get-tuple-element.86.f, f32[6,72,256]{2,1,0:T(8,128)S(1)} %get-tuple-element.87.c, f32[72,216]{1,0:T(8,128)S(1)} %get-tuple-element.88.w, ...), custom_call_target="tpu_custom_call" | custom-call | tf_op jit(solution)/shard_map/post2/pallas_call | solution.py:622
  98.7 5.3 %collective-permute-start.19 = (f32[72,128]{1,0:T(8,128)S(1)}, f32[72,128]{1,0:T(8,128)S(1)}, u32[]{:S(2)}, u32[]{:S(2)}) collective-permute-start(f32[72,128]{1,0:T(8,128)S(1)} %get-tuple-element.112), channel_id=1, source_target_pairs={{1,0},{2,1},{3,2},{4,3},{5,4},{6,5},{7,6},{8,7},{9,8},{10,9},{11,1... | collective-permute-start | bytes 110600 | tf_op jit(solution)/shard_map/ppermute | solution.py:794
  104.1 1.6 %collective-permute-done.18.gdn = f32[72,128]{1,0:T(8,128)S(1)} collective-permute-done((f32[72,128]{1,0:T(8,128)S(1)}, f32[72,128]{1,0:T(8,128)S(1)}, u32[]{:S(2)}, u32[]{:S(2)}) %collective-permute-start.18) | collective-permute-done | bytes 36896 | tf_op jit(solution)/shard_map/ppermute | solution.py:794
  106.5 2.8 %post1.1 = (f32[24,72,128]{2,1,0:T(8,128)S(1)}, f32[216,128]{1,0:T(8,128)S(1)}, f32[216,128]{1,0:T(8,128)S(1)}, f32[72,128]{1,0:T(8,128)S(1)}, f32[72,128]{1,0:T(8,128)S(1)}) custom-call(f32[6,72,128]{2,1,0:T(8,128)S(1)} %get-tuple-element.76.f, f32[6,72,128]{2,1,0:T(8,128)S(1)} %get-tuple-element.75.c_next.c, f32[72,216]{1,0:T(8,128)S(1)} %get-tuple-element.77.w, ...), custom_call_target="tpu_custom_call" | custom-call | tf_op jit(solution)/shard_map/post1/pallas_call | solution.py:622
  109.6 3.9 %collective-permute-start.21 = (f32[216,128]{1,0:T(8,128)S(1)}, f32[216,128]{1,0:T(8,128)S(1)}, u32[]{:S(2)}, u32[]{:S(2)}) collective-permute-start(f32[216,128]{1,0:T(8,128)S(1)} %get-tuple-element.116), channel_id=1, source_target_pairs={{16,0},{32,16},{48,32},{64,48},{80,64},{96,80},{112,96},{0,112},{1... | collective-permute-start | bytes 331784 | tf_op jit(solution)/shard_map/ppermute | solution.py:794
  113.5 2.7 %collective-permute-done.20.xlo.glo = f32[216,128]{1,0:T(8,128)S(1)} collective-permute-done((f32[216,128]{1,0:T(8,128)S(1)}, f32[216,128]{1,0:T(8,128)S(1)}, u32[]{:S(2)}, u32[]{:S(2)}) %collective-permute-start.20) | collective-permute-done | bytes 110624 | tf_op jit(solution)/shard_map/ppermute | solution.py:794
  116.5 5.3 %collective-permute-start.23 = (f32[72,128]{1,0:T(8,128)S(1)}, f32[72,128]{1,0:T(8,128)S(1)}, u32[]{:S(2)}, u32[]{:S(2)}) collective-permute-start(f32[72,128]{1,0:T(8,128)S(1)} %get-tuple-element.120), channel_id=1, source_target_pairs={{1,0},{2,1},{3,2},{4,3},{5,4},{6,5},{7,6},{8,7},{9,8},{10,9},{11,1... | collective-permute-start | bytes 110600 | tf_op jit(solution)/shard_map/ppermute | solution.py:794
  121.8 1.6 %collective-permute-done.22.gdn = f32[72,128]{1,0:T(8,128)S(1)} collective-permute-done((f32[72,128]{1,0:T(8,128)S(1)}, f32[72,128]{1,0:T(8,128)S(1)}, u32[]{:S(2)}, u32[]{:S(2)}) %collective-permute-start.22) | collective-permute-done | bytes 36896 | tf_op jit(solution)/shard_map/ppermute | solution.py:794
  123.5 3.9 %post0.1 = f32[1680,128]{1,0:T(8,128)} custom-call(f32[24,72,128]{2,1,0:T(8,128)S(1)} %copy-done.1, f32[24,72,128]{2,1,0:T(8,128)S(1)} %copy-done.3, f32[72,216]{1,0:T(8,128)S(1)} %get-tuple-element.66.w, f32[72,128]{1,0:T(8,128)S(1)} %copy-done.4, f32[8,128]{1,0:T(8,128)S(1)} %copy-done.5, f32[296,128]{1,0:T(8,128)S(1)} %collective-permute-done.xlo, ...), custom_call_target="tpu_custom_call" | custom-call | tf_op jit(solution)/shard_map/post0/pallas_call | solution.py:622
  (46 shorter events, 9.8 us)
Async XLA Ops:
  0.0 7.4 %copy-start.6 = (f32[4,5,14,14]{3,0,2,1:T(4,128)S(1)}, f32[4,5,14,14]{3,0,2,1:T(4,128)}, u32[]{:S(2)}) copy-start(f32[4,5,14,14]{3,0,2,1:T(4,128)} %param.8) | copy-start | bytes 47044
  3.2 8.5 %collective-permute-start = (f32[296,128]{1,0:T(8,128)}, f32[296,128]{1,0:T(8,128)S(1)}, u32[]{:S(2)}, u32[]{:S(2)}) collective-permute-start(f32[296,128]{1,0:T(8,128)} %get-tuple-element.68), channel_id=1, source_target_pairs={{0,16},{16,32},{32,48},{48,64},{64,80},{80,96},{96,112},{112,0},{1... | collective-permute-start | bytes 454664 | tf_op jit(solution)/shard_map/ppermute | solution.py:794
  4.9 8.9 %collective-permute-start.1 = (f32[296,128]{1,0:T(8,128)}, f32[296,128]{1,0:T(8,128)S(1)}, u32[]{:S(2)}, u32[]{:S(2)}) collective-permute-start(f32[296,128]{1,0:T(8,128)} %get-tuple-element.69), channel_id=1, source_target_pairs={{16,0},{32,16},{48,32},{64,48},{80,64},{96,80},{112,96},{0,112},{1... | collective-permute-start | bytes 454664 | tf_op jit(solution)/shard_map/ppermute | solution.py:794
  7.4 0.7 copy-start.5
  8.1 1.2 copy-start
  9.2 1.2 copy-start.2
  10.4 10.6 %copy-start.1 = (f32[24,72,128]{2,1,0:T(8,128)S(1)}, f32[24,72,128]{2,1,0:T(8,128)}, u32[]{:S(2)}) copy-start(f32[24,72,128]{2,1,0:T(8,128)} %get-tuple-element.63.f) | copy-start | bytes 2654212
  13.7 7.3 %copy-start.4 = (f32[72,128]{1,0:T(8,128)S(1)}, f32[72,128]{1,0:T(8,128)}, u32[]{:S(2)}) copy-start(f32[72,128]{1,0:T(8,128)} %get-tuple-element.67.vz) | copy-start | bytes 110596
  13.9 7.1 %collective-permute-start.2 = (f32[80,128]{1,0:T(8,128)S(1)}, f32[80,128]{1,0:T(8,128)S(1)}, u32[]{:S(2)}, u32[]{:S(2)}) collective-permute-start(f32[80,128]{1,0:T(8,128)S(1)} %get-tuple-element.72), channel_id=1, source_target_pairs={{0,1},{1,2},{2,3},{3,4},{4,5},{5,6},{6,7},{7,8},{8,9},{9,10},{10,1... | collective-permute-start | bytes 122888 | tf_op jit(solution)/shard_map/ppermute | solution.py:794
  14.0 7.0 %collective-permute-start.3 = (f32[80,128]{1,0:T(8,128)S(1)}, f32[80,128]{1,0:T(8,128)S(1)}, u32[]{:S(2)}, u32[]{:S(2)}) collective-permute-start(f32[80,128]{1,0:T(8,128)S(1)} %get-tuple-element.73), channel_id=1, source_target_pairs={{1,0},{2,1},{3,2},{4,3},{5,4},{6,5},{7,6},{8,7},{9,8},{10,9},{11,1... | collective-permute-start | bytes 122888 | tf_op jit(solution)/shard_map/ppermute | solution.py:794
  24.8 6.7 %collective-permute-start.4 = (f32[152,128]{1,0:T(8,128)S(1)}, f32[152,128]{1,0:T(8,128)S(1)}, u32[]{:S(2)}, u32[]{:S(2)}) collective-permute-start(f32[152,128]{1,0:T(8,128)S(1)} %get-tuple-element.78), channel_id=1, source_target_pairs={{0,16},{16,32},{32,48},{48,64},{64,80},{80,96},{96,112},{112,0},{1... | collective-permute-start | bytes 233480 | tf_op jit(solution)/shard_map/ppermute | solution.py:794
  25.2 6.5 %collective-permute-start.5 = (f32[152,128]{1,0:T(8,128)S(1)}, f32[152,128]{1,0:T(8,128)S(1)}, u32[]{:S(2)}, u32[]{:S(2)}) collective-permute-start(f32[152,128]{1,0:T(8,128)S(1)} %get-tuple-element.79), channel_id=1, source_target_pairs={{16,0},{32,16},{48,32},{64,48},{80,64},{96,80},{112,96},{0,112},{1... | collective-permute-start | bytes 233480 | tf_op jit(solution)/shard_map/ppermute | solution.py:794
  31.9 7.1 %collective-permute-start.6 = (f32[80,128]{1,0:T(8,128)S(1)}, f32[80,128]{1,0:T(8,128)S(1)}, u32[]{:S(2)}, u32[]{:S(2)}) collective-permute-start(f32[80,128]{1,0:T(8,128)S(1)} %get-tuple-element.82), channel_id=1, source_target_pairs={{0,1},{1,2},{2,3},{3,4},{4,5},{5,6},{6,7},{7,8},{8,9},{9,10},{10,1... | collective-permute-start | bytes 122888 | tf_op jit(solution)/shard_map/ppermute | solution.py:794
  32.0 7.0 %collective-permute-start.7 = (f32[80,128]{1,0:T(8,128)S(1)}, f32[80,128]{1,0:T(8,128)S(1)}, u32[]{:S(2)}, u32[]{:S(2)}) collective-permute-start(f32[80,128]{1,0:T(8,128)S(1)} %get-tuple-element.83), channel_id=1, source_target_pairs={{1,0},{2,1},{3,2},{4,3},{5,4},{6,5},{7,6},{8,7},{9,8},{10,9},{11,1... | collective-permute-start | bytes 122888 | tf_op jit(solution)/shard_map/ppermute | solution.py:794
  58.8 7.3 %collective-permute-start.8 = (f32[80,256]{1,0:T(8,128)S(1)}, f32[80,256]{1,0:T(8,128)S(1)}, u32[]{:S(2)}, u32[]{:S(2)}) collective-permute-start(f32[80,256]{1,0:T(8,128)S(1)} %get-tuple-element.90), channel_id=1, source_target_pairs={{0,1},{1,2},{2,3},{3,4},{4,5},{5,6},{6,7},{7,24},{8,9},{9,10},{10,... | collective-permute-start | bytes 245768 | tf_op jit(solution)/shard_map/ppermute | solution.py:614
  58.9 7.2 %collective-permute-start.9 = (f32[80,256]{1,0:T(8,128)S(1)}, f32[80,256]{1,0:T(8,128)S(1)}, u32[]{:S(2)}, u32[]{:S(2)}) collective-permute-start(f32[80,256]{1,0:T(8,128)S(1)} %get-tuple-element.91), channel_id=1, source_target_pairs={{0,31},{1,0},{2,1},{3,2},{4,3},{5,4},{6,5},{7,6},{8,23},{9,8},{10,... | collective-permute-start | bytes 245768 | tf_op jit(solution)/shard_map/ppermute | solution.py:614
  68.9 6.8 %collective-permute-start.10 = (f32[80,128]{1,0:T(8,128)S(1)}, f32[80,128]{1,0:T(8,128)S(1)}, u32[]{:S(2)}, u32[]{:S(2)}) collective-permute-start(f32[80,128]{1,0:T(8,128)S(1)} %get-tuple-element.96), channel_id=1, source_target_pairs={{0,1},{1,2},{2,3},{3,4},{4,5},{5,6},{6,7},{7,24},{8,9},{9,10},{10,... | collective-permute-start | bytes 122888 | tf_op jit(solution)/shard_map/ppermute | solution.py:614
  69.0 6.8 %collective-permute-start.11 = (f32[80,128]{1,0:T(8,128)S(1)}, f32[80,128]{1,0:T(8,128)S(1)}, u32[]{:S(2)}, u32[]{:S(2)}) collective-permute-start(f32[80,128]{1,0:T(8,128)S(1)} %get-tuple-element.97), channel_id=1, source_target_pairs={{0,31},{1,0},{2,1},{3,2},{4,3},{5,4},{6,5},{7,6},{8,23},{9,8},{10,... | collective-permute-start | bytes 122888 | tf_op jit(solution)/shard_map/ppermute | solution.py:614
  77.3 9.4 %collective-permute-start.12 = (f32[72,128]{1,0:T(8,128)S(1)}, f32[72,128]{1,0:T(8,128)S(1)}, u32[]{:S(2)}, u32[]{:S(2)}) collective-permute-start(f32[72,128]{1,0:T(8,128)S(1)} %get-tuple-element.98), channel_id=1, source_target_pairs={{0,1},{1,2},{2,3},{3,4},{4,5},{5,6},{6,7},{7,24},{8,9},{9,10},{10,... | collective-permute-start | bytes 110600 | tf_op jit(solution)/shard_map/ppermute | solution.py:614
  77.3 9.3 %collective-permute-start.13 = (f32[72,128]{1,0:T(8,128)S(1)}, f32[72,128]{1,0:T(8,128)S(1)}, u32[]{:S(2)}, u32[]{:S(2)}) collective-permute-start(f32[72,128]{1,0:T(8,128)S(1)} %get-tuple-element.99), channel_id=1, source_target_pairs={{0,31},{1,0},{2,1},{3,2},{4,3},{5,4},{6,5},{7,6},{8,23},{9,8},{10,... | collective-permute-start | bytes 110600 | tf_op jit(solution)/shard_map/ppermute | solution.py:614
  82.5 10.6 %collective-permute-start.16 = (f32[144,128]{1,0:T(8,128)S(1)}, f32[144,128]{1,0:T(8,128)S(1)}, u32[]{:S(2)}, u32[]{:S(2)}) collective-permute-start(f32[144,128]{1,0:T(8,128)S(1)} %get-tuple-element.106), channel_id=1, source_target_pairs={{0,16},{16,32},{32,48},{48,64},{64,80},{80,96},{96,112},{112,0},{1... | collective-permute-start | bytes 221192 | tf_op jit(solution)/shard_map/ppermute | solution.py:794
  82.5 10.6 %collective-permute-start.17 = (f32[144,128]{1,0:T(8,128)S(1)}, f32[144,128]{1,0:T(8,128)S(1)}, u32[]{:S(2)}, u32[]{:S(2)}) collective-permute-start(f32[144,128]{1,0:T(8,128)S(1)} %get-tuple-element.107), channel_id=1, source_target_pairs={{16,0},{32,16},{48,32},{64,48},{80,64},{96,80},{112,96},{0,112},{1... | collective-permute-start | bytes 221192 | tf_op jit(solution)/shard_map/ppermute | solution.py:794
  87.9 7.2 %collective-permute-start.14 = (f32[72,256]{1,0:T(8,128)S(1)}, f32[72,256]{1,0:T(8,128)S(1)}, u32[]{:S(2)}, u32[]{:S(2)}) collective-permute-start(f32[72,256]{1,0:T(8,128)S(1)} %get-tuple-element.103), channel_id=1, source_target_pairs={{0,1},{1,2},{2,3},{3,4},{4,5},{5,6},{6,7},{7,24},{8,9},{9,10},{10,... | collective-permute-start | bytes 221192 | tf_op jit(solution)/shard_map/ppermute | solution.py:614
  88.0 7.1 %collective-permute-start.15 = (f32[72,256]{1,0:T(8,128)S(1)}, f32[72,256]{1,0:T(8,128)S(1)}, u32[]{:S(2)}, u32[]{:S(2)}) collective-permute-start(f32[72,256]{1,0:T(8,128)S(1)} %get-tuple-element.104), channel_id=1, source_target_pairs={{0,31},{1,0},{2,1},{3,2},{4,3},{5,4},{6,5},{7,6},{8,23},{9,8},{10,... | collective-permute-start | bytes 221192 | tf_op jit(solution)/shard_map/ppermute | solution.py:614
  98.6 7.1 %collective-permute-start.18 = (f32[72,128]{1,0:T(8,128)S(1)}, f32[72,128]{1,0:T(8,128)S(1)}, u32[]{:S(2)}, u32[]{:S(2)}) collective-permute-start(f32[72,128]{1,0:T(8,128)S(1)} %get-tuple-element.111), channel_id=1, source_target_pairs={{0,1},{1,2},{2,3},{3,4},{4,5},{5,6},{6,7},{7,8},{8,9},{9,10},{10,1... | collective-permute-start | bytes 110600 | tf_op jit(solution)/shard_map/ppermute | solution.py:794
  98.7 7.8 %collective-permute-start.19 = (f32[72,128]{1,0:T(8,128)S(1)}, f32[72,128]{1,0:T(8,128)S(1)}, u32[]{:S(2)}, u32[]{:S(2)}) collective-permute-start(f32[72,128]{1,0:T(8,128)S(1)} %get-tuple-element.112), channel_id=1, source_target_pairs={{1,0},{2,1},{3,2},{4,3},{5,4},{6,5},{7,6},{8,7},{9,8},{10,9},{11,1... | collective-permute-start | bytes 110600 | tf_op jit(solution)/shard_map/ppermute | solution.py:794
  106.5 17.0 %copy-start.3 = (f32[24,72,128]{2,1,0:T(8,128)S(1)}, f32[24,72,128]{2,1,0:T(8,128)}, u32[]{:S(2)}) copy-start(f32[24,72,128]{2,1,0:T(8,128)} %get-tuple-element.64.c) | copy-start | bytes 2654212
  109.3 6.9 %collective-permute-start.20 = (f32[216,128]{1,0:T(8,128)S(1)}, f32[216,128]{1,0:T(8,128)S(1)}, u32[]{:S(2)}, u32[]{:S(2)}) collective-permute-start(f32[216,128]{1,0:T(8,128)S(1)} %get-tuple-element.115), channel_id=1, source_target_pairs={{0,16},{16,32},{32,48},{48,64},{64,80},{80,96},{96,112},{112,0},{1... | collective-permute-start | bytes 331784 | tf_op jit(solution)/shard_map/ppermute | solution.py:794
  109.6 6.6 %collective-permute-start.21 = (f32[216,128]{1,0:T(8,128)S(1)}, f32[216,128]{1,0:T(8,128)S(1)}, u32[]{:S(2)}, u32[]{:S(2)}) collective-permute-start(f32[216,128]{1,0:T(8,128)S(1)} %get-tuple-element.116), channel_id=1, source_target_pairs={{16,0},{32,16},{48,32},{64,48},{80,64},{96,80},{112,96},{0,112},{1... | collective-permute-start | bytes 331784 | tf_op jit(solution)/shard_map/ppermute | solution.py:794
  116.4 7.1 %collective-permute-start.22 = (f32[72,128]{1,0:T(8,128)S(1)}, f32[72,128]{1,0:T(8,128)S(1)}, u32[]{:S(2)}, u32[]{:S(2)}) collective-permute-start(f32[72,128]{1,0:T(8,128)S(1)} %get-tuple-element.119), channel_id=1, source_target_pairs={{0,1},{1,2},{2,3},{3,4},{4,5},{5,6},{6,7},{7,8},{8,9},{9,10},{10,1... | collective-permute-start | bytes 110600 | tf_op jit(solution)/shard_map/ppermute | solution.py:794
  116.5 7.0 %collective-permute-start.23 = (f32[72,128]{1,0:T(8,128)S(1)}, f32[72,128]{1,0:T(8,128)S(1)}, u32[]{:S(2)}, u32[]{:S(2)}) collective-permute-start(f32[72,128]{1,0:T(8,128)S(1)} %get-tuple-element.120), channel_id=1, source_target_pairs={{1,0},{2,1},{3,2},{4,3},{5,4},{6,5},{7,6},{8,7},{9,8},{10,9},{11,1... | collective-permute-start | bytes 110600 | tf_op jit(solution)/shard_map/ppermute | solution.py:794

commit v2 on v1

--- a/solution.py
+++ b/solution.py
@@ -80,13 +80,22 @@
 
 def corners(geom, v):
     m_rows, groups, ty = geom
-    lane = zl()
     last = v[m_rows - 1]
     base = (groups - 1) * ty
-    out = jnp.where(lane == 0, col(v[0], 0), 0.0)
-    out = jnp.where(lane == 1, col(v[0], ty - 1), out)
-    out = jnp.where(lane == 2, col(last, base), out)
-    return jnp.where(lane == 3, col(last, base + ty - 1), out)
+    return corner_rows([col(v[0], 0), col(v[0], ty - 1), col(last, base), col(last, base + ty - 1)])
+
+
+def corner_rows(columns):
+    lane = zl()
+    out = jnp.zeros((Z, LANES), F32)
+    for k, column in enumerate(columns):
+        out = jnp.where(lane == 4 + k, column, out)
+    return jnp.concatenate([out, jnp.zeros((LANES - Z, LANES), F32)], axis=0).T[0:8, :]
+
+
+def corner_columns(rows):
+    out = jnp.concatenate([rows, jnp.zeros((LANES - 8, LANES), F32)], axis=0).T[0:Z, :]
+    return [col(out, 4 + k) for k in range(4)]
 
 
 def whole_rows(geom):
@@ -138,17 +147,26 @@
 def put_x(geom, v, c, up, down, flags=None):
     m_rows, groups, _ = geom
     tx = m_rows * groups
-    extra = corners(geom, v)
+    tail = corners(geom, v)
+    if flags is not None:
+        tail = tail + flags
     for ref, edge, second in ((up, tx - 1, tx - 2), (down, 0, 1)):
         parts = [row_of(geom, v, edge), row_of(geom, v, second)]
         if c is not None:
             parts.append(row_of(geom, c, edge))
-        parts.append(extra)
-        whole = pack(geom, parts)
-        for k, part in enumerate(whole):
-            ref[k * Z : (k + 1) * Z, :] = part
-        if flags is not None:
-            ref[len(whole) * Z : len(whole) * Z + 8, :] = flags
+        put_parts(geom, parts, tail, ref)
+
+
+def put_parts(geom, parts, tail, ref):
+    whole = pack(geom, parts)
+    for k, part in enumerate(whole):
+        ref[k * Z : (k + 1) * Z, :] = part
+    ref[len(whole) * Z : len(whole) * Z + 8, :] = tail
+
+
+def tail_of(geom, ref, count):
+    n = packed(geom, count) * Z
+    return ref[n : n + 8, :]
 
 
 def put_y(geom, v, c, up, down):
@@ -171,7 +189,7 @@
     down[0:Z, :] = out_down
 
 
-def merge_y(lo_extra, hi_extra, flags, up, down):
+def merge_y(lo, hi, flags, up, down):
     lane = zl()
     f0, f1 = flag_row(flags, 0) > 0.5, flag_row(flags, 1) > 0.5
 
@@ -180,8 +198,6 @@
             part = jnp.where(lane == 112 + k, value, part)
         return part
 
-    lo = [col(lo_extra, k) for k in range(4)]
-    hi = [col(hi_extra, k) for k in range(4)]
     up_new = fill(up, [lo[3], lo[1], hi[1], hi[3], jnp.where(f0, lo[2], lo[3]), jnp.where(f1, hi[0], hi[1])])
     down_new = fill(down, [lo[2], lo[0], hi[0], hi[2], jnp.where(f0, lo[3], lo[2]), jnp.where(f1, hi[1], hi[0])])
     return up_new, down_new
@@ -272,6 +288,8 @@
     m_rows, groups, ty = geom
     lane = zl()
     here = v[m]
+    if lo is None:
+        lo = hi = jnp.zeros((Z, LANES), F32)
     if m > 0:
         low_x = v[m - 1]
     else:
@@ -283,6 +301,10 @@
     else:
         high_x = jnp.where(lane < (groups - 1) * ty, roll(v[0], -ty), roll(hi, (groups - 1) * ty))
     low_y, high_y = roll(here, 1), roll(here, -1)
+    if sides is None:
+        low_y = jnp.where(lane % ty == 0, 0.0, low_y)
+        high_y = jnp.where(lane % ty == ty - 1, 0.0, high_y)
+        return residual(co, f[m], c[m], here, low_x + high_x + low_y + high_y)
     for q in range(groups):
         row = q * m_rows + m
         low = roll(sides, q * ty - 2 * row - 1)
@@ -300,6 +322,31 @@
         d = block_dot(winv, r[0] if len(r) == 1 else jnp.concatenate(r, axis=1))
         for i, k in enumerate(rows):
             store(k, v[k] + d[:, i * LANES : (i + 1) * LANES])
+
+
+ALONE = (None, None, None)
+
+
+def add_edges(geom, winv, part, edges, store):
+    m_rows, groups, ty = geom
+    lane = zl()
+    d = block_dot(winv, jnp.concatenate(edges, axis=1) * 0.0625)
+    low, high, sides = [d[:, k * LANES : (k + 1) * LANES] for k in range(3)]
+    if ty < LANES:
+        low = jnp.where(lane < ty, low, 0.0)
+        high = jnp.where(lane < ty, high, 0.0)
+    for m in range(m_rows):
+        x = part[m]
+        if m == 0:
+            x = x + low
+        if m == m_rows - 1:
+            x = x + roll(high, (groups - 1) * ty)
+        for q in range(groups):
+            row = q * m_rows + m
+            first = roll(sides, q * ty - 2 * row - 1)
+            last = first if whole_rows(geom) else roll(sides, q * ty + ty - 1 - 2 * row)
+            x = x + jnp.where(lane == q * ty, first, jnp.where(lane == q * ty + ty - 1, last, 0.0))
+        store(m, x)
 
 
 def start_tile(geom, winv, f, store):
@@ -349,11 +396,9 @@
 
 
 def messages(geom, xlo, xhi, ydn, yun, winv):
-    n = packed(geom, 4)
     raw = [part_of(geom, xlo, 0), part_of(geom, xlo, 1), part_of(geom, xhi, 0), part_of(geom, xhi, 1), ydn[0:Z, :], yun[0:Z, :]]
     d = block_dot(winv, jnp.concatenate(raw, axis=1))
-    halo = Halo(*[d[:, k * LANES : (k + 1) * LANES] for k in range(6)])
-    return halo, n
+    return Halo(*[d[:, k * LANES : (k + 1) * LANES] for k in range(6)])
 
 
 def own_data(geom, xlo, xhi, ydn, yun):
@@ -371,8 +416,7 @@
 
 
 def flags_of(geom, own, xlo, xhi, ydn, yun):
-    n = packed(geom, 4)
-    return Flags(own[...], xlo[n * Z : n * Z + 8, :], xhi[n * Z : n * Z + 8, :], ydn[Z : Z + 8, :], yun[Z : Z + 8, :])
+    return Flags(own[...], tail_of(geom, xlo, 3), tail_of(geom, xhi, 3), ydn[Z : Z + 8, :], yun[Z : Z + 8, :])
 
 
 def load_top(src, dst):
@@ -452,8 +496,10 @@
     lt = in_tile(strip)
     low_x = v[m - 1] if m > 0 else ends[0]
     high_x = v[m + 1] if m < m_rows - 1 else ends[1]
-    low_y = jnp.where(lt == 0, roll(sides[0], -m), roll(v[m], 1))
-    high_y = jnp.where(lt == ty - 1, roll(sides[1], ty - 1 - m), roll(v[m], -1))
+    low = 0.0 if sides is None else roll(sides[0], -m)
+    high = 0.0 if sides is None else roll(sides[1], ty - 1 - m)
+    low_y = jnp.where(lt == 0, low, roll(v[m], 1))
+    high_y = jnp.where(lt == ty - 1, high, roll(v[m], -1))
     return residual(co, f[m], c[m], v[m], low_x + high_x + low_y + high_y)
 
 
@@ -462,6 +508,15 @@
     for m in range(strip[0]):
         r = strip_residual(strip, co, v, f, c, ends, sides, m)
         store(m, v[m] + block_dot(winv, r))
+
+
+def strip_add_sides(strip, winv, part, sides, store):
+    m_rows, ty, width = strip
+    lt = in_tile(strip)
+    d = block_dot(winv, jnp.concatenate(sides, axis=1) * 0.0625)
+    for m in range(m_rows):
+        low, high = roll(d[:, :width], -m), roll(d[:, width:], ty - 1 - m)
+        store(m, part[m] + jnp.where(lt == 0, low, jnp.where(lt == ty - 1, high, 0.0)))
 
 
 def strip_restrict(v, out):
@@ -506,17 +561,15 @@
     )
 
 
-def pre_strip_kernel(f, c, w, vz, flags, dn, un, v_out, f_next, c_next, fl_next, up, down, one, res):
+def pre_strip_kernel(f, c, w, vz, flags, dn, un, one, part, v_out, f_next, c_next, fl_next, up, down, res):
     strip = STRIPS[2]
     width = strip[2]
     winv = w[...].astype(BF16)
     co = Coef(vz, width)
-    for m in range(6):
-        one[m] = block_dot(winv, f[m])
     raws = [dn[0:Z, :], un[0:Z, :]]
     values = [block_dot(winv, x) for x in raws]
     edges = strip_edges(strip, winv, co, one, strip_sides(values, raws, dn, un, strip[1]))
-    strip_relax(strip, winv, co, one, f, c, flags, strip_frame(strip, flags, *values), Setter(v_out))
+    strip_add_sides(strip, winv, part, strip_frame(strip, flags, *values), Setter(v_out))
     ends = strip_ends(strip, v_out, flags)
     sides = strip_frame(strip, flags, *edges)
     for m in range(6):
@@ -533,24 +586,22 @@
     down[Z : Z + 8, :] = fl_next[...]
 
 
-def bottom_strip_kernel(f, c, w, vz, flags, dn, un, v_out, up, down, one):
+def bottom_strip_kernel(f, c, w, vz, flags, dn, un, first, part, v_out, up, down, one):
     strip = STRIPS[3]
     winv = w[...].astype(BF16)
     co = Coef(vz)
-    for m in range(3):
-        v_out[m] = block_dot(winv, f[m])
     raws = [dn[0:Z, :], un[0:Z, :]]
     values = [block_dot(winv, x) for x in raws]
-    edges = strip_edges(strip, winv, co, v_out, strip_sides(values, raws, dn, un, strip[1]))
-    strip_relax(strip, winv, co, v_out, f, c, flags, strip_frame(strip, flags, *values), Setter(one))
+    edges = strip_edges(strip, winv, co, first, strip_sides(values, raws, dn, un, strip[1]))
+    strip_add_sides(strip, winv, part, strip_frame(strip, flags, *values), Setter(one))
     strip_relax(strip, winv, co, one, f, c, flags, strip_frame(strip, flags, *edges), Setter(v_out))
     strip_message(strip, v_out, None, (), up, down)
 
 
-def last_strip_kernel(f, c, w, vz, flags, dn, un, v, fine_v, fine_flags, g, up, down, e):
+def last_strip_kernel(w, flags, dn, un, part, fine_v, fine_flags, _lo, _hi, g, up, down, e):
     strip, fine = STRIPS[3], STRIPS[2]
     winv = w[...].astype(BF16)
-    strip_relax(strip, winv, Coef(vz), v, f, c, flags, strip_frame(strip, flags, dn[...], un[...]), Setter(e))
+    strip_add_sides(strip, winv, part, strip_frame(strip, flags, dn[...], un[...]), Setter(e))
     a, b = iota2(LANES, LANES)
     for m in range(3):
         add = jnp.concatenate([lane_dot(e[m], jnp.where(a == 64 * h + b // 2, 1.0, 0.0)) for h in range(2)], axis=1)
@@ -559,8 +610,29 @@
     strip_message(fine, g, None, strip_ends(fine, g, fine_flags), up, down)
 
 
+def alone_kernel(level, first):
+    def kernel(f, c, w, vz, *refs):
+        winv = w[...].astype(BF16)
+        flags = None
+        if level >= 2:
+            flags, *refs = refs
+        v, part = refs
+        if level < 2:
+            if first:
+                start_tile(GEOM[level], winv, f, Setter(v))
+            relax_tile(GEOM[level], winv, Coef(vz), v, f, c, ALONE, Setter(part))
+        else:
+            strip = STRIPS[level]
+            if first:
+                for m in range(strip[0]):
+                    v[m] = block_dot(winv, f[m])
+            strip_relax(strip, winv, Coef(vz, strip[2]), v, f, c, flags, None, Setter(part))
+
+    return kernel
+
+
 def post_strip_kernel(
-    f, c, w, vz, flags, dn, un, g, gdn, gun, fine_v, xlo, xhi, own, g_out, lo_out, hi_out, up, down, one, e, tile, yup, ydown
+    f, c, w, vz, flags, dn, un, g, part, gdn, gun, fine_v, xlo, xhi, own, g_out, lo_out, hi_out, up, down, one, e, tile, yup, ydown
 ):
     strip = STRIPS[2]
     fine, geom = GEOM[1], GEOM[2]
@@ -569,7 +641,7 @@
     raws = [dn[0:Z, :], un[0:Z, :]]
     values = [gdn[...], gun[...]]
     edges = strip_edges(strip, winv, co, g, strip_sides(values, raws, dn, un, strip[1]))
-    strip_relax(strip, winv, co, g, f, c, flags, strip_frame(strip, flags, *values), Setter(one))
+    strip_add_sides(strip, winv, part, strip_frame(strip, flags, *values), Setter(one))
     strip_relax(strip, winv, co, one, f, c, flags, strip_frame(strip, flags, *edges), Setter(e))
 
     place = lax.axis_index("gx")
@@ -583,17 +655,13 @@
     prolong_add(fine, geom, tile, fine_v, g_out)
     a, b = iota2(LANES, LANES)
     spread = jnp.where((b < 64) & (a == b // 2), 1.0, 0.0)
-    lane = zl()
     extras = []
     for ref, out, step, near in ((xlo, lo_out, -1, 5), (xhi, hi_out, 1, 0)):
         first, last = tile_row(0, step), tile_row(5, step)
         add = lane_dot(last if near else first, spread)
-        extra = part_of(fine, ref, 2)
-        for k, value in enumerate((col(first, 0), col(first, 31), col(last, 0), col(last, 31))):
-            extra = extra + jnp.where(lane == k, value, 0.0)
-        extras.append(extra)
-        for k, part in enumerate(pack(fine, [part_of(fine, ref, 0) + add, part_of(fine, ref, 1) + add, extra])):
-            out[k * Z : (k + 1) * Z, :] = part
+        adds = (col(first, 0), col(first, 31), col(last, 0), col(last, 31))
+        extras.append([x + y for x, y in zip(corner_columns(tail_of(fine, ref, 2)), adds)])
+        out[...] = pack(fine, [part_of(fine, ref, 0) + add, part_of(fine, ref, 1) + add])[0]
     put_y(fine, g_out, None, yup, ydown)
     up[...], down[...] = merge_y(*extras, own, yup[...], ydown[...])
 
@@ -614,15 +682,16 @@
     return lax.ppermute(up, both, pairs(1)), lax.ppermute(down, both, pairs(-1))
 
 
+ANY = pl.BlockSpec(memory_space=pl.ANY)
 LIMIT = 14 * 1024 * 1024
 VMEM = pl.BlockSpec(memory_space=pltpu.VMEM)
 
 
-def call(kernel, outs, args, scratch=(), name=None):
+def call(kernel, outs, args, scratch=(), name=None, after=0):
     return pl.pallas_call(
         kernel,
         out_shape=[jax.ShapeDtypeStruct(s, F32) for s in outs],
-        in_specs=[VMEM] * len(args),
+        in_specs=[VMEM] * (len(args) - after) + [ANY] * after,
         out_specs=[VMEM] * len(outs),
         scratch_shapes=[pltpu.VMEM(s, F32) for s in scratch],
         compiler_params=pltpu.CompilerParams(vmem_limit_bytes=LIMIT),
@@ -634,27 +703,26 @@
     return (GEOM[level][0], Z, LANES)
 
 
-def x_shape(level, count, flags):
-    return (packed(GEOM[level], count) * Z + (8 if flags else 0), LANES)
+def x_shape(level, count):
+    return (packed(GEOM[level], count) * Z + 8, LANES)
 
 
 Y_FULL = (Z + 8, LANES)
 
 
-PARTS = 5
-
-
-def open_kernel(f_in, c_in, vert_in, flip_in, f, c, up, down, own, vz, f_raw, c_raw, vert, flip, sems, small):
-    rows = NZ * 24 // PARTS
-    copies = []
-    for k in range(PARTS):
-        for i, (src, dst) in enumerate(((f_in, f_raw), (c_in, c_raw))):
-            part = pl.ds(k * rows, rows)
-            copies.append(pltpu.make_async_copy(src.at[part, :], dst.at[part, :], sems.at[i, k]))
-    few = [pltpu.make_async_copy(vert_in, vert, small.at[0]), pltpu.make_async_copy(flip_in, flip, small.at[1])]
-    for copy in few + copies:
+def open_kernel(f_in, c_in, vert_in, flip_in, up, down, own, vz, f_low, f_high, c_low, c_high, vert, flip, sems):
+    pairs = (
+        (vert_in, vert),
+        (flip_in, flip),
+        (f_in.at[:, 0:2, :], f_low),
+        (f_in.at[:, 22:24, :], f_high),
+        (c_in.at[:, 0:1, :], c_low),
+        (c_in.at[:, 23:24, :], c_high),
+    )
+    copies = [pltpu.make_async_copy(src, dst, sems.at[k]) for k, (src, dst) in enumerate(pairs)]
+    for copy in copies:
         copy.start()
-    for copy in few:
+    for copy in copies[:2]:
         copy.wait()
     a, b = iota2(8, 4)
     flags = jnp.broadcast_to(flip[...].astype(F32), (8, 4))
@@ -667,11 +735,20 @@
     columns = [jnp.broadcast_to(x * 0.0625, (Z, LANES)) for x in (4.0 + high + low, high, low)]
     lane = zl()
     vz[...] = jnp.where(lane == 0, columns[0], jnp.where(lane == 1, columns[1], columns[2]))
-    for copy in copies:
+    up[...] = jnp.zeros(up.shape, F32)
+    down[...] = jnp.zeros(down.shape, F32)
+    for copy in copies[2:]:
         copy.wait()
-    load_top(f_raw, f)
-    load_top(c_raw, c)
-    put_x(GEOM[0], f, c, up, down, flags)
+    up[0:NZ, :] = f_high[:, 1, :]
+    up[Z : Z + NZ, :] = f_high[:, 0, :]
+    up[2 * Z : 2 * Z + NZ, :] = c_high[:, 0, :]
+    down[0:NZ, :] = f_low[:, 0, :]
+    down[Z : Z + NZ, :] = f_low[:, 1, :]
+    down[2 * Z : 2 * Z + NZ, :] = c_low[:, 0, :]
+    first, last = down[0:Z, :], up[0:Z, :]
+    tail = flags + corner_rows([col(first, 0), col(first, LANES - 1), col(last, 0), col(last, LANES - 1)])
+    up[3 * Z : 3 * Z + 8, :] = tail
+    down[3 * Z : 3 * Z + 8, :] = tail
 
 
 def block_matrix(inv):
@@ -691,14 +768,18 @@
     return jnp.where((b >= Z) & (b < 2 * Z), whole - high, high)
 
 
-def side_kernel(f, c, inv, own, w0, w1, w2, w3, one, c_next, c_tile, yup, ydown):
+def side_kernel(f_in, c_in, inv, vz, own, f, c, w0, w1, w2, w3, one, part, c_next, c_tile, yup, ydown):
+    load_top(f_in, f)
+    load_top(c_in, c)
     put_y(GEOM[0], f, c, yup, ydown)
     yup[Z : Z + 8, :] = own[...]
     ydown[Z : Z + 8, :] = own[...]
     for level, w in enumerate((w0, w1, w2, w3)):
         w[0:NZ, :] = block_matrix(inv[level])
         w[NZ:Z, :] = jnp.zeros((Z - NZ, 3 * Z), F32)
-    start_tile(GEOM[0], w0[...].astype(BF16), f, Setter(one))
+    winv = w0[...].astype(BF16)
+    start_tile(GEOM[0], winv, f, Setter(one))
+    relax_tile(GEOM[0], winv, Coef(vz), one, f, c, ALONE, Setter(part))
     restrict(GEOM[0], GEOM[1], c, c_next)
     restrict(GEOM[1], GEOM[2], c_next, c_tile)
 
@@ -707,7 +788,7 @@
     geom = GEOM[level]
 
     def kernel(xlo, xhi, flags, yup, ydown, up, down):
-        lo, hi = part_of(geom, xlo, count - 1), part_of(geom, xhi, count - 1)
+        lo, hi = corner_columns(tail_of(geom, xlo, count)), corner_columns(tail_of(geom, xhi, count))
         up[...] = yup[...]
         down[...] = ydown[...]
         a, b = merge_y(lo, hi, flags, yup[0:Z, :], ydown[0:Z, :])
@@ -717,21 +798,21 @@
     return kernel
 
 
-def pre_tile(level, f, c, w, vz, own, xlo, xhi, ydn, yun, one, v_out, res):
+def pre_tile(level, f, c, w, vz, own, xlo, xhi, ydn, yun, one, part, v_out, res):
     geom = GEOM[level]
     winv = w[...].astype(BF16)
     co = Coef(vz)
     fl = flags_of(geom, own, xlo, xhi, ydn, yun)
-    halo, _ = messages(geom, xlo, xhi, ydn, yun, winv)
+    halo = messages(geom, xlo, xhi, ydn, yun, winv)
     lo2, hi2, sides2 = relax_edges(geom, winv, co, one, halo, fl, *own_data(geom, xlo, xhi, ydn, yun))
-    relax_tile(geom, winv, co, one, f, c, frame(geom, fl, halo.lo, halo.hi, halo.sides()), Setter(v_out))
+    add_edges(geom, winv, part, frame(geom, fl, halo.lo, halo.hi, halo.sides()), Setter(v_out))
     lo, hi, sides = frame(geom, fl, lo2, hi2, sides2)
     for m in range(geom[0]):
         res[m] = tile_residual(geom, co, v_out, f, c, lo, hi, sides, m)
 
 
-def pre0_kernel(f, c, w, vz, own, xlo, xhi, ydn, yun, one, c_next, v_out, f_next, up, down, yup, ydown, res):
-    pre_tile(0, f, c, w, vz, own, xlo, xhi, ydn, yun, one, v_out, res)
+def pre0_kernel(f, c, w, vz, own, xlo, xhi, ydn, yun, one, part, c_next, v_out, f_next, up, down, yup, ydown, res):
+    pre_tile(0, f, c, w, vz, own, xlo, xhi, ydn, yun, one, part, v_out, res)
     coarse = GEOM[1]
     restrict(GEOM[0], coarse, res, f_next)
     put_x(coarse, f_next, c_next, up, down, own[...])
@@ -740,9 +821,8 @@
     ydown[Z : Z + 8, :] = own[...]
 
 
-def pre1_kernel(f, c, w, vz, own, xlo, xhi, ydn, yun, c_tile, v_out, up, down, chunks, one, res, f_next):
-    start_tile(GEOM[1], w[...].astype(BF16), f, Setter(one))
-    pre_tile(1, f, c, w, vz, own, xlo, xhi, ydn, yun, one, v_out, res)
+def pre1_kernel(f, c, w, vz, own, xlo, xhi, ydn, yun, one, part, c_tile, v_out, up, down, chunks, res, f_next):
+    pre_tile(1, f, c, w, vz, own, xlo, xhi, ydn, yun, one, part, v_out, res)
     restrict(GEOM[1], GEOM[2], res, f_next)
     put_x(GEOM[1], v_out, None, up, down)
     whole = pack(GEOM[2], [f_next[m] for m in range(6)] + [c_tile[m] for m in range(6)])
@@ -755,7 +835,7 @@
 def post_kernel(level):
     geom = GEOM[level]
 
-    def sweeps(f, c, w, vz, own, xlo, xhi, ydn, yun, g, glo, ghi, gdn, gun, one, store):
+    def sweeps(f, c, w, vz, own, xlo, xhi, ydn, yun, g, part, glo, ghi, gdn, gun, one, store):
         winv = w[...].astype(BF16)
         co = Coef(vz)
         fl = flags_of(geom, own, xlo, xhi, ydn, yun)
@@ -763,23 +843,23 @@
             part_of(geom, glo, 0), part_of(geom, glo, 1), part_of(geom, ghi, 0), part_of(geom, ghi, 1), gdn[...], gun[...]
         )
         lo2, hi2, sides2 = relax_edges(geom, winv, co, g, halo, fl, *own_data(geom, xlo, xhi, ydn, yun))
-        relax_tile(geom, winv, co, g, f, c, frame(geom, fl, halo.lo, halo.hi, halo.sides()), Setter(one))
+        add_edges(geom, winv, part, frame(geom, fl, halo.lo, halo.hi, halo.sides()), Setter(one))
         relax_tile(geom, winv, co, one, f, c, frame(geom, fl, lo2, hi2, sides2), store)
 
     if level == 0:
 
-        def kernel(f, c, w, vz, own, xlo, xhi, ydn, yun, g, glo, ghi, gdn, gun, out, one):
+        def kernel(f, c, w, vz, own, xlo, xhi, ydn, yun, g, part, glo, ghi, gdn, gun, out, one):
             def store(x, value):
                 out[pl.ds(x, NZ, stride=24), :] = value[0:NZ, :]
 
-            sweeps(f, c, w, vz, own, xlo, xhi, ydn, yun, g, glo, ghi, gdn, gun, one, store)
+            sweeps(f, c, w, vz, own, xlo, xhi, ydn, yun, g, part, glo, ghi, gdn, gun, one, store)
 
         return kernel
 
     fine = GEOM[level - 1]
 
-    def kernel(f, c, w, vz, own, xlo, xhi, ydn, yun, g, glo, ghi, gdn, gun, fine_v, g_out, up, down, yup, ydown, one, e):
-        sweeps(f, c, w, vz, own, xlo, xhi, ydn, yun, g, glo, ghi, gdn, gun, one, Setter(e))
+    def kernel(f, c, w, vz, own, xlo, xhi, ydn, yun, g, part, glo, ghi, gdn, gun, fine_v, g_out, up, down, yup, ydown, one, e):
+        sweeps(f, c, w, vz, own, xlo, xhi, ydn, yun, g, part, glo, ghi, gdn, gun, one, Setter(e))
         prolong_add(fine, geom, e, fine_v, g_out)
         put_x(fine, g_out, None, up, down)
         put_y(fine, g_out, None, yup, ydown)
@@ -803,22 +883,25 @@
 
     ys = (Z, LANES)
     t0, t1, t2 = tile_shape(0), tile_shape(1), tile_shape(2)
-    xs = x_shape(0, 4, True)
-    f, c, up, down, own, vz = pl.pallas_call(
+    xs = x_shape(0, 3)
+    up, down, own, vz = pl.pallas_call(
         open_kernel,
-        out_shape=[jax.ShapeDtypeStruct(x, F32) for x in (t0, t0, xs, xs, (8, LANES), ys)],
-        in_specs=[pl.BlockSpec(memory_space=pl.ANY)] * 4,
-        out_specs=[VMEM] * 6,
-        scratch_shapes=[pltpu.VMEM((NZ * 24, LANES), F32)] * 2
-        + [pltpu.VMEM((1, NZ + 1), F32), pltpu.VMEM((1, 4), jnp.int32)]
-        + [pltpu.SemaphoreType.DMA((2, PARTS)), pltpu.SemaphoreType.DMA((2,))],
+        out_shape=[jax.ShapeDtypeStruct(x, F32) for x in (xs, xs, (8, LANES), ys)],
+        in_specs=[ANY] * 4,
+        out_specs=[VMEM] * 4,
+        scratch_shapes=[pltpu.VMEM((NZ, 2, LANES), F32)] * 2
+        + [pltpu.VMEM((NZ, 1, LANES), F32)] * 2
+        + [pltpu.VMEM((1, NZ + 1), F32), pltpu.VMEM((1, 4), jnp.int32), pltpu.SemaphoreType.DMA((6,))],
         compiler_params=pltpu.CompilerParams(vmem_limit_bytes=58 * 1024 * 1024),
         name="open",
-    )(f_in, c_in, vert, flip)
+    )(right_side, helm_coef, vert, flip)
     xlo, xhi = both_ways(up, down, "gx")
     ws = (Z, 3 * Z)
-    *w, one, c1, c_tile, yup, ydown = call(
-        side_kernel, [ws] * 4 + [t0, t1, t2, Y_FULL, Y_FULL], [f, c, inv, own], name="side"
+    f, c, *w, one, part, c1, c_tile, yup, ydown = call(
+        side_kernel,
+        [t0, t0] + [ws] * 4 + [t0, t0, t1, t2, Y_FULL, Y_FULL],
+        [f_in, c_in, inv, vz, own],
+        name="side",
     )
 
     def to_sides(level, count, xlo, xhi, yup, ydown):
@@ -826,54 +909,67 @@
         yup, ydown = call(merge_kernel(level, count), [shape, shape], [xlo, xhi, own, yup, ydown], name=f"merge{level}")
         return both_ways(yup, ydown, "gy")
 
-    got0 = (xlo, xhi, *to_sides(0, 4, xlo, xhi, yup, ydown))
-    xs = x_shape(1, 4, True)
+    got0 = (xlo, xhi, *to_sides(0, 3, xlo, xhi, yup, ydown))
+    xs = x_shape(1, 3)
     v0, f1, up, down, yup, ydown = call(
-        pre0_kernel, [t0, t1, xs, xs, Y_FULL, Y_FULL], [f, c, w[0], vz, own, *got0, one, c1], [t0], name="pre0"
+        pre0_kernel, [t0, t1, xs, xs, Y_FULL, Y_FULL], [f, c, w[0], vz, own, *got0, one, part, c1], [t0], name="pre0"
     )
     xlo, xhi = both_ways(up, down, "gx")
-    got1 = (xlo, xhi, *to_sides(1, 4, xlo, xhi, yup, ydown))
-    xs = x_shape(1, 3, False)
+    one, part = call(alone_kernel(1, True), [t1, t1], [f1, c1, w[1], vz], name="alone1")
+    got1 = (xlo, xhi, *to_sides(1, 3, xlo, xhi, yup, ydown))
+    xs = x_shape(1, 2)
     v1, up, down, chunks = call(
-        pre1_kernel, [t1, xs, xs, (8, 3 * Z + 8, LANES)], [f1, c1, w[1], vz, own, *got1, c_tile], [t1, t1, t2], name="pre1"
+        pre1_kernel,
+        [t1, xs, xs, (8, 3 * Z + 8, LANES)],
+        [f1, c1, w[1], vz, own, *got1, one, part, c_tile],
+        [t1, t2],
+        name="pre1",
     )
     v1_lo, v1_hi = both_ways(up, down, "gx")
     chunks = lax.all_to_all(chunks, "gx", 0, 0)
     s2, s3 = (6, Z, 256), (3, Z, 128)
     m2, m3 = (Z, 256), (Z, 128)
     full2, full3 = (Z + 8, 256), (Z + 8, 128)
-    f2, c2, fl2, up, down = call(open_strip_kernel, [s2, s2, (8, 256), full2, full2], [chunks], name="open2")
+    f2, c2, fl2, up, down = call(
+        open_strip_kernel, [s2, s2, (8, 256), full2, full2], [chunks], name="open2"
+    )
     side2 = strip_ring(up, down)
+    one, part = call(alone_kernel(2, True), [s2, s2], [f2, c2, w[2], vz, fl2], name="alone2")
     v2, f3, c3, fl3, up, down = call(
-        pre_strip_kernel, [s2, s3, s3, (8, 128), full3, full3], [f2, c2, w[2], vz, fl2, *side2], [s2, s2], name="pre2"
+        pre_strip_kernel, [s2, s3, s3, (8, 128), full3, full3], [f2, c2, w[2], vz, fl2, *side2, one, part], [s2], name="pre2"
     )
     side3 = strip_ring(up, down)
-    v3, up, down = call(bottom_strip_kernel, [s3, m3, m3], [f3, c3, w[3], vz, fl3, *side3], [s3], name="bottom")
+    one, part = call(alone_kernel(3, True), [s3, s3], [f3, c3, w[3], vz, fl3], name="alone3")
+    v3, up, down = call(
+        bottom_strip_kernel, [s3, m3, m3], [f3, c3, w[3], vz, fl3, *side3, one, part], [s3], name="bottom"
+    )
     side = strip_ring(up, down)
-    g2, up, down = call(
-        last_strip_kernel, [s2, m2, m2], [f3, c3, w[3], vz, fl3, *side, v3, v2, fl2], [s3], name="last"
-    )
+    (part,) = call(alone_kernel(3, False), [s3], [f3, c3, w[3], vz, fl3, v3], name="again3")
+    g2, up, down = call(last_strip_kernel, [s2, m2, m2], [w[3], fl3, *side, part, v2, fl2, v1_lo, v1_hi], [s3], name="last", after=2)
     side = strip_ring(up, down)
+    (part,) = call(alone_kernel(2, False), [s2], [f2, c2, w[2], vz, fl2, g2], name="again2")
     g1, lo, hi, up, down = call(
         post_strip_kernel,
-        [t1, xs, xs, ys, ys],
-        [f2, c2, w[2], vz, fl2, *side2, g2, *side, v1, v1_lo, v1_hi, own],
+        [t1, ys, ys, ys, ys],
+        [f2, c2, w[2], vz, fl2, *side2, g2, part, *side, v1, v1_lo, v1_hi, own],
         [s2, s2, t2, ys, ys],
         name="post2",
     )
     side = both_ways(up, down, "gy")
-    xs = x_shape(0, 3, False)
+    (part,) = call(alone_kernel(1, False), [t1], [f1, c1, w[1], vz, g1], name="again1")
+    xs = x_shape(0, 2)
     g0, up, down, yup, ydown = call(
         post_kernel(1),
         [t0, xs, xs, ys, ys],
-        [f1, c1, w[1], vz, own, *got1, g1, lo, hi, *side, v0],
+        [f1, c1, w[1], vz, own, *got1, g1, part, lo, hi, *side, v0],
         [t1, t1],
         name="post1",
     )
     xlo, xhi = both_ways(up, down, "gx")
-    got = (xlo, xhi, *to_sides(0, 3, xlo, xhi, yup, ydown))
+    (part,) = call(alone_kernel(0, False), [t0], [f, c, w[0], vz, g0], name="again0")
+    got = (xlo, xhi, *to_sides(0, 2, xlo, xhi, yup, ydown))
     (out,) = call(
-        post_kernel(0), [(NZ * 24, LANES)], [f, c, w[0], vz, own, *got0, g0, *got], [t0], name="post0"
+        post_kernel(0), [(NZ * 24, LANES)], [f, c, w[0], vz, own, *got0, g0, part, *got], [t0], name="post0"
     )
     return out.reshape(NZ, 24, LANES)
 

time: 128 us -> 123 us (0.961)
  waiting for transfers between devices: 20.8 us -> 13.9 us
  Pallas kernels: 28.3 us -> 30.8 us
  local copies, waits for them, and re-layouts: 3.04 us -> 1.58 us
    ppermute x16, waiting for transfers between devices: 14.9 us -> 10.2 us  [both_ways(): return (lax.ppermute(up, axis, fwd), lax.ppermute(down, axis, back))]
    pallas_call x13 -> x20, Pallas kernels: 25.1 us -> 28.8 us  [call(): pl.pallas_call(kernel, out_shape=[jax.ShapeDtypeStruct(s, F32) for s in o...]
    unnamed x14 -> x8, local copies, waits for them, and re-layouts: 3.03 us -> 0.66 us
    ppermute x4, waiting for transfers between devices: 5.75 us -> 3.43 us  [strip_ring(): lax.ppermute(up, both, pairs(1))]
  transfers between devices with their start and end apart: 24 -> 24, of which waited for: 14 -> 12; matrix products, arithmetic and copies ran while one was open for 0% -> 1% of each run, Pallas kernels for 2% -> 7%
where the time goes in v2:
time: 123 us; the launch traced here: 122 us
  starting transfers between devices  59.3 us (48%)
  Pallas kernels  30.8 us (25%)
  blocking collectives  15.9 us (13%)
  waiting for transfers between devices  13.9 us (11%)
  local copies, waits for them, and re-layouts  1.58 us (1%)
    ppermute x16, starting transfers between devices, both_ways(): return (lax.ppermute(up, axis, fwd), lax.ppermute(down, axis, back))  38.4 us
    pallas_call x20, Pallas kernels, call(): pl.pallas_call(kernel, out_shape=[jax.ShapeDtypeStruct(s, F32) for s in o...  28.8 us
    ppermute x4, starting transfers between devices, strip_ring(): lax.ppermute(down, both, pairs(-1))  20.6 us
    all_to_all x1, blocking collectives, on_device(): chunks = lax.all_to_all(chunks, 'gx', 0, 0)  15.9 us
    ppermute x16, waiting for transfers between devices, both_ways(): return (lax.ppermute(up, axis, fwd), lax.ppermute(down, axis, back))  10.2 us
    ppermute x4, waiting for transfers between devices, strip_ring(): lax.ppermute(up, both, pairs(1))  3.43 us
  transfers between devices with their start and end apart: 24, of which 12 were waited for; matrix products, arithmetic and copies ran while one was open for 1% of the time, Pallas kernels for 7%

profile of v2, /device:TPU:0, one launch (start us, length us, event | category | flops | bytes accessed | tf_op | source)
XLA Modules:
  0.0 121.9 jit_solution(14128372801125046098)
XLA Ops:
  0.0 2.0 %open.1 = (f32[224,128]{1,0:T(8,128)}, f32[224,128]{1,0:T(8,128)}, f32[8,128]{1,0:T(8,128)}, f32[72,128]{1,0:T(8,128)}) custom-call(f32[70,24,128]{2,1,0:T(8,128)} %f_in.1, f32[70,24,128]{2,1,0:T(8,128)} %c_in.1, f32[1,71]{1,0:T(1,128)} %bitcast.9, s32[1,4]{1,0:T(1,128)} %bitcast.10), custom_call_target="tpu_custom_call" | custom-call | tf_op jit(solution)/shard_map/open/pallas_call | solution.py:887
  2.0 1.7 %collective-permute-start = (f32[224,128]{1,0:T(8,128)}, f32[224,128]{1,0:T(8,128)S(1)}, u32[]{:S(2)}, u32[]{:S(2)}) collective-permute-start(f32[224,128]{1,0:T(8,128)} %get-tuple-element.75), channel_id=1, source_target_pairs={{0,16},{16,32},{32,48},{48,64},{64,80},{80,96},{96,112},{112,0},{1... | collective-permute-start | bytes 344072 | tf_op jit(solution)/shard_map/ppermute | solution.py:874
  3.7 2.5 %collective-permute-start.1 = (f32[224,128]{1,0:T(8,128)}, f32[224,128]{1,0:T(8,128)S(1)}, u32[]{:S(2)}, u32[]{:S(2)}) collective-permute-start(f32[224,128]{1,0:T(8,128)} %get-tuple-element.76), channel_id=1, source_target_pairs={{16,0},{32,16},{48,32},{64,48},{80,64},{96,80},{112,96},{0,112},{1... | collective-permute-start | bytes 344072 | tf_op jit(solution)/shard_map/ppermute | solution.py:874
  7.8 2.5 %side.1 = (f32[24,72,128]{2,1,0:T(8,128)S(1)}, f32[24,72,128]{2,1,0:T(8,128)S(1)}, f32[72,216]{1,0:T(8,128)S(1)}, f32[72,216]{1,0:T(8,128)S(1)}, f32[72,216]{1,0...) custom-call(f32[1680,128]{1,0:T(8,128)S(1)} %bitcast.6, ...), custom_call_target="tpu_custom_call" | custom-call | tf_op jit(solution)/shard_map/side/pallas_call | solution.py:691
  11.3 5.3 %collective-permute-start.3 = (f32[80,128]{1,0:T(8,128)S(1)}, f32[80,128]{1,0:T(8,128)S(1)}, u32[]{:S(2)}, u32[]{:S(2)}) collective-permute-start(f32[80,128]{1,0:T(8,128)S(1)} %get-tuple-element.80), channel_id=1, source_target_pairs={{1,0},{2,1},{3,2},{4,3},{5,4},{6,5},{7,6},{8,7},{9,8},{10,9},{11,1... | collective-permute-start | bytes 122888 | tf_op jit(solution)/shard_map/ppermute | solution.py:874
  16.7 1.7 %collective-permute-done.2.ydn = f32[80,128]{1,0:T(8,128)S(1)} collective-permute-done((f32[80,128]{1,0:T(8,128)S(1)}, f32[80,128]{1,0:T(8,128)S(1)}, u32[]{:S(2)}, u32[]{:S(2)}) %collective-permute-start.2) | collective-permute-done | bytes 40992 | tf_op jit(solution)/shard_map/ppermute | solution.py:874
  18.4 3.1 %pre0.1 = (f32[24,72,128]{2,1,0:T(8,128)S(1)}, f32[6,72,128]{2,1,0:T(8,128)S(1)}, f32[152,128]{1,0:T(8,128)S(1)}, f32[152,128]{1,0:T(8,128)S(1)}, f32[80,128]{1,0:T(8,128)S(1)}, /*index=5*/f32[80,128]{1,0:T(8,128)S(1)}) custom-call(f32[24,72,128]{2,1,0:T(8,128)S(1)} %get-tuple-element.72.f, f32[24,72,128]{2,1,0:T(8,128)S(1)} %get-tuple-element.73.c, ...), custom_call_target="tpu_custom_call" | custom-call | tf_op jit(solution)/shard_map/pre0/pallas_call | solution.py:691
  21.8 3.9 %collective-permute-start.5 = (f32[152,128]{1,0:T(8,128)S(1)}, f32[152,128]{1,0:T(8,128)S(1)}, u32[]{:S(2)}, u32[]{:S(2)}) collective-permute-start(f32[152,128]{1,0:T(8,128)S(1)} %get-tuple-element.87), channel_id=1, source_target_pairs={{16,0},{32,16},{48,32},{64,48},{80,64},{96,80},{112,96},{0,112},{1... | collective-permute-start | bytes 233480 | tf_op jit(solution)/shard_map/ppermute | solution.py:874
  25.6 2.5 %collective-permute-done.4.xlo = f32[152,128]{1,0:T(8,128)S(1)} collective-permute-done((f32[152,128]{1,0:T(8,128)S(1)}, f32[152,128]{1,0:T(8,128)S(1)}, u32[]{:S(2)}, u32[]{:S(2)}) %collective-permute-start.4) | collective-permute-done | bytes 77856 | tf_op jit(solution)/shard_map/ppermute | solution.py:874
  28.6 5.3 %collective-permute-start.7 = (f32[80,128]{1,0:T(8,128)S(1)}, f32[80,128]{1,0:T(8,128)S(1)}, u32[]{:S(2)}, u32[]{:S(2)}) collective-permute-start(f32[80,128]{1,0:T(8,128)S(1)} %get-tuple-element.91), channel_id=1, source_target_pairs={{1,0},{2,1},{3,2},{4,3},{5,4},{6,5},{7,6},{8,7},{9,8},{10,9},{11,1... | collective-permute-start | bytes 122888 | tf_op jit(solution)/shard_map/ppermute | solution.py:874
  34.5 1.1 collective-permute-done.6.ydn
  35.6 2.1 %pre1.1 = (f32[6,72,128]{2,1,0:T(8,128)S(1)}, f32[80,128]{1,0:T(8,128)S(1)}, f32[80,128]{1,0:T(8,128)S(1)}, f32[8,224,128]{2,1,0:T(8,128)S(1)}) custom-call(f32[6,72,128]{2,1,0:T(8,128)S(1)} %get-tuple-element.84.f, f32[6,72,128]{2,1,0:T(8,128)S(1)} %get-tuple-element.83.c_next.c, f32[72,216]{1,0:T(8,128)S(1)} %get-tuple-element.85.w, ...), custom_call_target="tpu_custom_call" | custom-call | tf_op jit(solution)/shard_map/pre1/pallas_call | solution.py:691
  37.8 15.9 %all_to_all.5.chunks = f32[8,224,128]{2,1,0:T(8,128)S(1)} all-to-all(f32[8,224,128]{2,1,0:T(8,128)S(1)} %get-tuple-element.95), channel_id=1, replica_groups=mesh['gx'=8,'gy'=16] {'gx'}, dimensions={0} | all-to-all | bytes 1835008 | tf_op jit(solution)/shard_map/all_to_all | solution.py:929
  53.7 1.6 %open2.1 = (f32[6,72,256]{2,1,0:T(8,128)S(1)}, f32[6,72,256]{2,1,0:T(8,128)S(1)}, f32[8,256]{1,0:T(8,128)S(1)}, f32[80,256]{1,0:T(8,128)S(1)}, f32[80,256]{1,0:T(8,128)S(1)}) custom-call(f32[8,224,128]{2,1,0:T(8,128)S(1)} %all_to_all.5.chunks), custom_call_target="tpu_custom_call" | custom-call | tf_op jit(solution)/shard_map/open2/pallas_call | solution.py:691
  55.4 5.1 %collective-permute-start.9 = (f32[80,256]{1,0:T(8,128)S(1)}, f32[80,256]{1,0:T(8,128)S(1)}, u32[]{:S(2)}, u32[]{:S(2)}) collective-permute-start(f32[80,256]{1,0:T(8,128)S(1)} %get-tuple-element.101), channel_id=1, source_target_pairs={{0,31},{1,0},{2,1},{3,2},{4,3},{5,4},{6,5},{7,6},{8,23},{9,8},{10,... | collective-permute-start | bytes 245768 | tf_op jit(solution)/shard_map/ppermute | solution.py:682
  61.3 1.2 %collective-permute-done.8.dn = f32[80,256]{1,0:T(8,128)S(1)} collective-permute-done((f32[80,256]{1,0:T(8,128)S(1)}, f32[80,256]{1,0:T(8,128)S(1)}, u32[]{:S(2)}, u32[]{:S(2)}) %collective-permute-start.8) | collective-permute-done | bytes 81952 | tf_op jit(solution)/shard_map/ppermute | solution.py:682
  62.6 2.5 %pre2.1 = (f32[6,72,256]{2,1,0:T(8,128)S(1)}, f32[3,72,128]{2,1,0:T(8,128)S(1)}, f32[3,72,128]{2,1,0:T(8,128)S(1)}, f32[8,128]{1,0:T(8,128)S(1)}, f32[80,128]{1,0:T(8,128)S(1)}, /*index=5*/f32[80,128]{1,0:T(8,128)S(1)}) custom-call(f32[6,72,256]{2,1,0:T(8,128)S(1)} %get-tuple-element.96.f, f32[6,72,256]{2,1,0:T(8,128)S(1)} %get-tuple-element.97.c, ...), custom_call_target="tpu_custom_call" | custom-call | tf_op jit(solution)/shard_map/pre2/pallas_call | solution.py:691
  65.2 5.1 %collective-permute-start.11 = (f32[80,128]{1,0:T(8,128)S(1)}, f32[80,128]{1,0:T(8,128)S(1)}, u32[]{:S(2)}, u32[]{:S(2)}) collective-permute-start(f32[80,128]{1,0:T(8,128)S(1)} %get-tuple-element.109), channel_id=1, source_target_pairs={{0,31},{1,0},{2,1},{3,2},{4,3},{5,4},{6,5},{7,6},{8,23},{9,8},{10,... | collective-permute-start | bytes 122888 | tf_op jit(solution)/shard_map/ppermute | solution.py:682
  70.3 4.1 %collective-permute-start.15 = (f32[80,128]{1,0:T(8,128)S(1)}, f32[80,128]{1,0:T(8,128)S(1)}, u32[]{:S(2)}, u32[]{:S(2)}) collective-permute-start(f32[80,128]{1,0:T(8,128)S(1)} %get-tuple-element.117), channel_id=1, source_target_pairs={{16,0},{32,16},{48,32},{64,48},{80,64},{96,80},{112,96},{0,112},{1... | collective-permute-start | bytes 122888 | tf_op jit(solution)/shard_map/ppermute | solution.py:874
  75.1 1.2 %bottom.1 = (f32[3,72,128]{2,1,0:T(8,128)S(1)}, f32[72,128]{1,0:T(8,128)S(1)}, f32[72,128]{1,0:T(8,128)S(1)}) custom-call(f32[3,72,128]{2,1,0:T(8,128)S(1)} %get-tuple-element.106.f, f32[3,72,128]{2,1,0:T(8,128)S(1)} %get-tuple-element.107.c, f32[72,216]{1,0:T(8,128)S(1)} %get-tuple-element.102.w, f32[72,128]{1,0:T(8,128)S(1)} %copy-done, ...), custom_call_target="tpu_custom_call" | custom-call | tf_op jit(solution)/shard_map/bottom/pallas_call | solution.py:691
  76.4 5.1 %collective-permute-start.13 = (f32[72,128]{1,0:T(8,128)S(1)}, f32[72,128]{1,0:T(8,128)S(1)}, u32[]{:S(2)}, u32[]{:S(2)}) collective-permute-start(f32[72,128]{1,0:T(8,128)S(1)} %get-tuple-element.113), channel_id=1, source_target_pairs={{0,31},{1,0},{2,1},{3,2},{4,3},{5,4},{6,5},{7,6},{8,23},{9,8},{10,... | collective-permute-start | bytes 110600 | tf_op jit(solution)/shard_map/ppermute | solution.py:682
  81.9 1.2 collective-permute-done.12.dn
  83.1 1.2 %last.1 = (f32[6,72,256]{2,1,0:T(8,128)S(1)}, f32[72,256]{1,0:T(8,128)S(1)}, f32[72,256]{1,0:T(8,128)S(1)}) custom-call(f32[72,216]{1,0:T(8,128)S(1)} %get-tuple-element.102.w, f32[8,128]{1,0:T(8,128)S(1)} %get-tuple-element.105.refs_0_.flags, f32[72,128]{1,0:T(8,128)S(1)} %collective-permute-done.12.dn, f32[72,128]{1,0:T(8,128)S(1)} %collective-permute-done.13.un, ...), custom_call_target="tpu_custom_call" | custom-call | tf_op jit(solution)/shard_map/last/pallas_call | solution.py:691
  84.4 5.3 %collective-permute-start.17 = (f32[72,256]{1,0:T(8,128)S(1)}, f32[72,256]{1,0:T(8,128)S(1)}, u32[]{:S(2)}, u32[]{:S(2)}) collective-permute-start(f32[72,256]{1,0:T(8,128)S(1)} %get-tuple-element.120), channel_id=1, source_target_pairs={{0,31},{1,0},{2,1},{3,2},{4,3},{5,4},{6,5},{7,6},{8,23},{9,8},{10,... | collective-permute-start | bytes 221192 | tf_op jit(solution)/shard_map/ppermute | solution.py:682
  91.7 3.3 %post2.1 = (f32[6,72,128]{2,1,0:T(8,128)S(1)}, f32[72,128]{1,0:T(8,128)S(1)}, f32[72,128]{1,0:T(8,128)S(1)}, f32[72,128]{1,0:T(8,128)S(1)}, f32[72,128]{1,0:T(8,128)S(1)}) custom-call(f32[6,72,256]{2,1,0:T(8,128)S(1)} %get-tuple-element.96.f, f32[6,72,256]{2,1,0:T(8,128)S(1)} %get-tuple-element.97.c, f32[72,216]{1,0:T(8,128)S(1)} %get-tuple-element.98.w, ...), custom_call_target="tpu_custom_call" | custom-call | tf_op jit(solution)/shard_map/post2/pallas_call | solution.py:691
  95.1 5.3 %collective-permute-start.19 = (f32[72,128]{1,0:T(8,128)S(1)}, f32[72,128]{1,0:T(8,128)S(1)}, u32[]{:S(2)}, u32[]{:S(2)}) collective-permute-start(f32[72,128]{1,0:T(8,128)S(1)} %get-tuple-element.126), channel_id=1, source_target_pairs={{1,0},{2,1},{3,2},{4,3},{5,4},{6,5},{7,6},{8,7},{9,8},{10,9},{11,1... | collective-permute-start | bytes 110600 | tf_op jit(solution)/shard_map/ppermute | solution.py:874
  100.9 1.2 collective-permute-done.18.gdn
  102.1 2.7 %post1.1 = (f32[24,72,128]{2,1,0:T(8,128)S(1)}, f32[152,128]{1,0:T(8,128)S(1)}, f32[152,128]{1,0:T(8,128)S(1)}, f32[72,128]{1,0:T(8,128)S(1)}, f32[72,128]{1,0:T(8,128)S(1)}) custom-call(f32[6,72,128]{2,1,0:T(8,128)S(1)} %get-tuple-element.84.f, f32[6,72,128]{2,1,0:T(8,128)S(1)} %get-tuple-element.83.c_next.c, f32[72,216]{1,0:T(8,128)S(1)} %get-tuple-element.85.w, ...), custom_call_target="tpu_custom_call" | custom-call | tf_op jit(solution)/shard_map/post1/pallas_call | solution.py:691
  105.6 3.4 %collective-permute-start.21 = (f32[152,128]{1,0:T(8,128)S(1)}, f32[152,128]{1,0:T(8,128)S(1)}, u32[]{:S(2)}, u32[]{:S(2)}) collective-permute-start(f32[152,128]{1,0:T(8,128)S(1)} %get-tuple-element.130), channel_id=1, source_target_pairs={{16,0},{32,16},{48,32},{64,48},{80,64},{96,80},{112,96},{0,112},{1... | collective-permute-start | bytes 233480 | tf_op jit(solution)/shard_map/ppermute | solution.py:874
  109.0 2.4 %collective-permute-done.20.xlo.glo = f32[152,128]{1,0:T(8,128)S(1)} collective-permute-done((f32[152,128]{1,0:T(8,128)S(1)}, f32[152,128]{1,0:T(8,128)S(1)}, u32[]{:S(2)}, u32[]{:S(2)}) %collective-permute-start.20) | collective-permute-done | bytes 77856 | tf_op jit(solution)/shard_map/ppermute | solution.py:874
  111.7 5.3 %collective-permute-start.23 = (f32[72,128]{1,0:T(8,128)S(1)}, f32[72,128]{1,0:T(8,128)S(1)}, u32[]{:S(2)}, u32[]{:S(2)}) collective-permute-start(f32[72,128]{1,0:T(8,128)S(1)} %get-tuple-element.134), channel_id=1, source_target_pairs={{1,0},{2,1},{3,2},{4,3},{5,4},{6,5},{7,6},{8,7},{9,8},{10,9},{11,1... | collective-permute-start | bytes 110600 | tf_op jit(solution)/shard_map/ppermute | solution.py:874
  118.7 3.2 %post0.1 = f32[1680,128]{1,0:T(8,128)} custom-call(f32[24,72,128]{2,1,0:T(8,128)S(1)} %get-tuple-element.72.f, f32[24,72,128]{2,1,0:T(8,128)S(1)} %get-tuple-element.73.c, f32[72,216]{1,0:T(8,128)S(1)} %get-tuple-element.74.w, f32[72,128]{1,0:T(8,128)S(1)} %copy-done, f32[8,128]{1,0:T(8,128)S(1)} %copy-done.3, f32[224,128]{1,0:T(8,128)S(1)} %collective-permute-done.xlo, ...), custom_call_target="tpu_custom_call" | custom-call | tf_op jit(solution)/shard_map/post0/pallas_call | solution.py:691
  (47 shorter events, 11.3 us)
Async XLA Ops:
  0.0 7.2 %copy-start.1 = (f32[70,24,128]{2,1,0:T(8,128)S(1)}, f32[70,24,128]{2,1,0:T(8,128)}, u32[]{:S(2)}) copy-start(f32[70,24,128]{2,1,0:T(8,128)} %f_in.1) | copy-start | bytes 2580484
  0.0 7.2 %copy-start.2 = (f32[70,24,128]{2,1,0:T(8,128)S(1)}, f32[70,24,128]{2,1,0:T(8,128)}, u32[]{:S(2)}) copy-start(f32[70,24,128]{2,1,0:T(8,128)} %c_in.1) | copy-start | bytes 2580484
  2.0 8.4 %collective-permute-start = (f32[224,128]{1,0:T(8,128)}, f32[224,128]{1,0:T(8,128)S(1)}, u32[]{:S(2)}, u32[]{:S(2)}) collective-permute-start(f32[224,128]{1,0:T(8,128)} %get-tuple-element.75), channel_id=1, source_target_pairs={{0,16},{16,32},{32,48},{48,64},{64,80},{80,96},{96,112},{112,0},{1... | collective-permute-start | bytes 344072 | tf_op jit(solution)/shard_map/ppermute | solution.py:874
  3.7 7.3 %collective-permute-start.1 = (f32[224,128]{1,0:T(8,128)}, f32[224,128]{1,0:T(8,128)S(1)}, u32[]{:S(2)}, u32[]{:S(2)}) collective-permute-start(f32[224,128]{1,0:T(8,128)} %get-tuple-element.76), channel_id=1, source_target_pairs={{16,0},{32,16},{48,32},{64,48},{80,64},{96,80},{112,96},{0,112},{1... | collective-permute-start | bytes 344072 | tf_op jit(solution)/shard_map/ppermute | solution.py:874
  6.2 1.0 copy-start
  7.2 0.7 copy-start.3
  11.3 7.1 %collective-permute-start.2 = (f32[80,128]{1,0:T(8,128)S(1)}, f32[80,128]{1,0:T(8,128)S(1)}, u32[]{:S(2)}, u32[]{:S(2)}) collective-permute-start(f32[80,128]{1,0:T(8,128)S(1)} %get-tuple-element.79), channel_id=1, source_target_pairs={{0,1},{1,2},{2,3},{3,4},{4,5},{5,6},{6,7},{7,8},{8,9},{9,10},{10,1... | collective-permute-start | bytes 122888 | tf_op jit(solution)/shard_map/ppermute | solution.py:874
  11.3 7.0 %collective-permute-start.3 = (f32[80,128]{1,0:T(8,128)S(1)}, f32[80,128]{1,0:T(8,128)S(1)}, u32[]{:S(2)}, u32[]{:S(2)}) collective-permute-start(f32[80,128]{1,0:T(8,128)S(1)} %get-tuple-element.80), channel_id=1, source_target_pairs={{1,0},{2,1},{3,2},{4,3},{5,4},{6,5},{7,6},{8,7},{9,8},{10,9},{11,1... | collective-permute-start | bytes 122888 | tf_op jit(solution)/shard_map/ppermute | solution.py:874
  21.4 6.7 %collective-permute-start.4 = (f32[152,128]{1,0:T(8,128)S(1)}, f32[152,128]{1,0:T(8,128)S(1)}, u32[]{:S(2)}, u32[]{:S(2)}) collective-permute-start(f32[152,128]{1,0:T(8,128)S(1)} %get-tuple-element.86), channel_id=1, source_target_pairs={{0,16},{16,32},{32,48},{48,64},{64,80},{80,96},{96,112},{112,0},{1... | collective-permute-start | bytes 233480 | tf_op jit(solution)/shard_map/ppermute | solution.py:874
  21.8 6.5 %collective-permute-start.5 = (f32[152,128]{1,0:T(8,128)S(1)}, f32[152,128]{1,0:T(8,128)S(1)}, u32[]{:S(2)}, u32[]{:S(2)}) collective-permute-start(f32[152,128]{1,0:T(8,128)S(1)} %get-tuple-element.87), channel_id=1, source_target_pairs={{16,0},{32,16},{48,32},{64,48},{80,64},{96,80},{112,96},{0,112},{1... | collective-permute-start | bytes 233480 | tf_op jit(solution)/shard_map/ppermute | solution.py:874
  28.5 7.1 %collective-permute-start.6 = (f32[80,128]{1,0:T(8,128)S(1)}, f32[80,128]{1,0:T(8,128)S(1)}, u32[]{:S(2)}, u32[]{:S(2)}) collective-permute-start(f32[80,128]{1,0:T(8,128)S(1)} %get-tuple-element.90), channel_id=1, source_target_pairs={{0,1},{1,2},{2,3},{3,4},{4,5},{5,6},{6,7},{7,8},{8,9},{9,10},{10,1... | collective-permute-start | bytes 122888 | tf_op jit(solution)/shard_map/ppermute | solution.py:874
  28.6 7.0 %collective-permute-start.7 = (f32[80,128]{1,0:T(8,128)S(1)}, f32[80,128]{1,0:T(8,128)S(1)}, u32[]{:S(2)}, u32[]{:S(2)}) collective-permute-start(f32[80,128]{1,0:T(8,128)S(1)} %get-tuple-element.91), channel_id=1, source_target_pairs={{1,0},{2,1},{3,2},{4,3},{5,4},{6,5},{7,6},{8,7},{9,8},{10,9},{11,1... | collective-permute-start | bytes 122888 | tf_op jit(solution)/shard_map/ppermute | solution.py:874
  55.3 7.3 %collective-permute-start.8 = (f32[80,256]{1,0:T(8,128)S(1)}, f32[80,256]{1,0:T(8,128)S(1)}, u32[]{:S(2)}, u32[]{:S(2)}) collective-permute-start(f32[80,256]{1,0:T(8,128)S(1)} %get-tuple-element.100), channel_id=1, source_target_pairs={{0,1},{1,2},{2,3},{3,4},{4,5},{5,6},{6,7},{7,24},{8,9},{9,10},{10,... | collective-permute-start | bytes 245768 | tf_op jit(solution)/shard_map/ppermute | solution.py:682
  55.4 7.2 %collective-permute-start.9 = (f32[80,256]{1,0:T(8,128)S(1)}, f32[80,256]{1,0:T(8,128)S(1)}, u32[]{:S(2)}, u32[]{:S(2)}) collective-permute-start(f32[80,256]{1,0:T(8,128)S(1)} %get-tuple-element.101), channel_id=1, source_target_pairs={{0,31},{1,0},{2,1},{3,2},{4,3},{5,4},{6,5},{7,6},{8,23},{9,8},{10,... | collective-permute-start | bytes 245768 | tf_op jit(solution)/shard_map/ppermute | solution.py:682
  65.1 9.9 %collective-permute-start.10 = (f32[80,128]{1,0:T(8,128)S(1)}, f32[80,128]{1,0:T(8,128)S(1)}, u32[]{:S(2)}, u32[]{:S(2)}) collective-permute-start(f32[80,128]{1,0:T(8,128)S(1)} %get-tuple-element.108), channel_id=1, source_target_pairs={{0,1},{1,2},{2,3},{3,4},{4,5},{5,6},{6,7},{7,24},{8,9},{9,10},{10,... | collective-permute-start | bytes 122888 | tf_op jit(solution)/shard_map/ppermute | solution.py:682
  65.2 9.9 %collective-permute-start.11 = (f32[80,128]{1,0:T(8,128)S(1)}, f32[80,128]{1,0:T(8,128)S(1)}, u32[]{:S(2)}, u32[]{:S(2)}) collective-permute-start(f32[80,128]{1,0:T(8,128)S(1)} %get-tuple-element.109), channel_id=1, source_target_pairs={{0,31},{1,0},{2,1},{3,2},{4,3},{5,4},{6,5},{7,6},{8,23},{9,8},{10,... | collective-permute-start | bytes 122888 | tf_op jit(solution)/shard_map/ppermute | solution.py:682
  70.3 11.5 %collective-permute-start.14 = (f32[80,128]{1,0:T(8,128)S(1)}, f32[80,128]{1,0:T(8,128)S(1)}, u32[]{:S(2)}, u32[]{:S(2)}) collective-permute-start(f32[80,128]{1,0:T(8,128)S(1)} %get-tuple-element.116), channel_id=1, source_target_pairs={{0,16},{16,32},{32,48},{48,64},{64,80},{80,96},{96,112},{112,0},{1... | collective-permute-start | bytes 122888 | tf_op jit(solution)/shard_map/ppermute | solution.py:874
  70.3 11.6 %collective-permute-start.15 = (f32[80,128]{1,0:T(8,128)S(1)}, f32[80,128]{1,0:T(8,128)S(1)}, u32[]{:S(2)}, u32[]{:S(2)}) collective-permute-start(f32[80,128]{1,0:T(8,128)S(1)} %get-tuple-element.117), channel_id=1, source_target_pairs={{16,0},{32,16},{48,32},{64,48},{80,64},{96,80},{112,96},{0,112},{1... | collective-permute-start | bytes 122888 | tf_op jit(solution)/shard_map/ppermute | solution.py:874
  76.3 6.8 %collective-permute-start.12 = (f32[72,128]{1,0:T(8,128)S(1)}, f32[72,128]{1,0:T(8,128)S(1)}, u32[]{:S(2)}, u32[]{:S(2)}) collective-permute-start(f32[72,128]{1,0:T(8,128)S(1)} %get-tuple-element.112), channel_id=1, source_target_pairs={{0,1},{1,2},{2,3},{3,4},{4,5},{5,6},{6,7},{7,24},{8,9},{9,10},{10,... | collective-permute-start | bytes 110600 | tf_op jit(solution)/shard_map/ppermute | solution.py:682
  76.4 6.7 %collective-permute-start.13 = (f32[72,128]{1,0:T(8,128)S(1)}, f32[72,128]{1,0:T(8,128)S(1)}, u32[]{:S(2)}, u32[]{:S(2)}) collective-permute-start(f32[72,128]{1,0:T(8,128)S(1)} %get-tuple-element.113), channel_id=1, source_target_pairs={{0,31},{1,0},{2,1},{3,2},{4,3},{5,4},{6,5},{7,6},{8,23},{9,8},{10,... | collective-permute-start | bytes 110600 | tf_op jit(solution)/shard_map/ppermute | solution.py:682
  84.3 7.2 %collective-permute-start.16 = (f32[72,256]{1,0:T(8,128)S(1)}, f32[72,256]{1,0:T(8,128)S(1)}, u32[]{:S(2)}, u32[]{:S(2)}) collective-permute-start(f32[72,256]{1,0:T(8,128)S(1)} %get-tuple-element.119), channel_id=1, source_target_pairs={{0,1},{1,2},{2,3},{3,4},{4,5},{5,6},{6,7},{7,24},{8,9},{9,10},{10,... | collective-permute-start | bytes 221192 | tf_op jit(solution)/shard_map/ppermute | solution.py:682
  84.4 7.3 %collective-permute-start.17 = (f32[72,256]{1,0:T(8,128)S(1)}, f32[72,256]{1,0:T(8,128)S(1)}, u32[]{:S(2)}, u32[]{:S(2)}) collective-permute-start(f32[72,256]{1,0:T(8,128)S(1)} %get-tuple-element.120), channel_id=1, source_target_pairs={{0,31},{1,0},{2,1},{3,2},{4,3},{5,4},{6,5},{7,6},{8,23},{9,8},{10,... | collective-permute-start | bytes 221192 | tf_op jit(solution)/shard_map/ppermute | solution.py:682
  95.0 7.1 %collective-permute-start.18 = (f32[72,128]{1,0:T(8,128)S(1)}, f32[72,128]{1,0:T(8,128)S(1)}, u32[]{:S(2)}, u32[]{:S(2)}) collective-permute-start(f32[72,128]{1,0:T(8,128)S(1)} %get-tuple-element.125), channel_id=1, source_target_pairs={{0,1},{1,2},{2,3},{3,4},{4,5},{5,6},{6,7},{7,8},{8,9},{9,10},{10,1... | collective-permute-start | bytes 110600 | tf_op jit(solution)/shard_map/ppermute | solution.py:874
  95.1 7.0 %collective-permute-start.19 = (f32[72,128]{1,0:T(8,128)S(1)}, f32[72,128]{1,0:T(8,128)S(1)}, u32[]{:S(2)}, u32[]{:S(2)}) collective-permute-start(f32[72,128]{1,0:T(8,128)S(1)} %get-tuple-element.126), channel_id=1, source_target_pairs={{1,0},{2,1},{3,2},{4,3},{5,4},{6,5},{7,6},{8,7},{9,8},{10,9},{11,1... | collective-permute-start | bytes 110600 | tf_op jit(solution)/shard_map/ppermute | solution.py:874
  104.8 6.6 %collective-permute-start.20 = (f32[152,128]{1,0:T(8,128)S(1)}, f32[152,128]{1,0:T(8,128)S(1)}, u32[]{:S(2)}, u32[]{:S(2)}) collective-permute-start(f32[152,128]{1,0:T(8,128)S(1)} %get-tuple-element.129), channel_id=1, source_target_pairs={{0,16},{16,32},{32,48},{48,64},{64,80},{80,96},{96,112},{112,0},{1... | collective-permute-start | bytes 233480 | tf_op jit(solution)/shard_map/ppermute | solution.py:874
  105.6 5.8 %collective-permute-start.21 = (f32[152,128]{1,0:T(8,128)S(1)}, f32[152,128]{1,0:T(8,128)S(1)}, u32[]{:S(2)}, u32[]{:S(2)}) collective-permute-start(f32[152,128]{1,0:T(8,128)S(1)} %get-tuple-element.130), channel_id=1, source_target_pairs={{16,0},{32,16},{48,32},{64,48},{80,64},{96,80},{112,96},{0,112},{1... | collective-permute-start | bytes 233480 | tf_op jit(solution)/shard_map/ppermute | solution.py:874
  111.6 7.1 %collective-permute-start.22 = (f32[72,128]{1,0:T(8,128)S(1)}, f32[72,128]{1,0:T(8,128)S(1)}, u32[]{:S(2)}, u32[]{:S(2)}) collective-permute-start(f32[72,128]{1,0:T(8,128)S(1)} %get-tuple-element.133), channel_id=1, source_target_pairs={{0,1},{1,2},{2,3},{3,4},{4,5},{5,6},{6,7},{7,8},{8,9},{9,10},{10,1... | collective-permute-start | bytes 110600 | tf_op jit(solution)/shard_map/ppermute | solution.py:874
  111.7 7.0 %collective-permute-start.23 = (f32[72,128]{1,0:T(8,128)S(1)}, f32[72,128]{1,0:T(8,128)S(1)}, u32[]{:S(2)}, u32[]{:S(2)}) collective-permute-start(f32[72,128]{1,0:T(8,128)S(1)} %get-tuple-element.134), channel_id=1, source_target_pairs={{1,0},{2,1},{3,2},{4,3},{5,4},{6,5},{7,6},{8,7},{9,8},{10,9},{11,1... | collective-permute-start | bytes 110600 | tf_op jit(solution)/shard_map/ppermute | solution.py:874

commit v3 on v2

--- a/solution.py
+++ b/solution.py
@@ -243,7 +243,7 @@
     )
 
 
-def relax_edges(geom, winv, co, v, halo, fl, f_lo, c_lo, f_hi, c_hi, f_sides, c_sides):
+def relax_edges(geom, winv, co, v, columns, halo, fl, f_lo, c_lo, f_hi, c_hi, f_sides, c_sides):
     m_rows, groups, ty = geom
     tx = m_rows * groups
     lane = zl()
@@ -272,7 +272,7 @@
         choose(fl.hi, 3, col(un, 114), col(un, 115)),
     )
     edge = halo.sides()
-    mine = turn_sides(geom, own_columns(geom, v), flag_row(fl.dn, 3), flag_row(fl.un, 2))
+    mine = turn_sides(geom, columns, flag_row(fl.dn, 3), flag_row(fl.un, 2))
     below = jnp.where(lane == 1, col(dn, 116), jnp.where(lane == 0, col(un, 116), roll(edge, 2)))
     last = 2 * (tx - 1)
     above = jnp.where(lane == last + 1, col(dn, 117), jnp.where(lane == last, col(un, 117), roll(edge, -2)))
@@ -327,26 +327,37 @@
 ALONE = (None, None, None)
 
 
-def add_edges(geom, winv, part, edges, store):
-    m_rows, groups, ty = geom
+def edge_terms(geom, winv, edges):
+    ty = geom[2]
     lane = zl()
     d = block_dot(winv, jnp.concatenate(edges, axis=1) * 0.0625)
     low, high, sides = [d[:, k * LANES : (k + 1) * LANES] for k in range(3)]
     if ty < LANES:
         low = jnp.where(lane < ty, low, 0.0)
         high = jnp.where(lane < ty, high, 0.0)
-    for m in range(m_rows):
-        x = part[m]
-        if m == 0:
-            x = x + low
-        if m == m_rows - 1:
-            x = x + roll(high, (groups - 1) * ty)
-        for q in range(groups):
-            row = q * m_rows + m
-            first = roll(sides, q * ty - 2 * row - 1)
-            last = first if whole_rows(geom) else roll(sides, q * ty + ty - 1 - 2 * row)
-            x = x + jnp.where(lane == q * ty, first, jnp.where(lane == q * ty + ty - 1, last, 0.0))
-        store(m, x)
+    return low, high, sides
+
+
+def with_terms(geom, x, terms, m):
+    m_rows, groups, ty = geom
+    low, high, sides = terms
+    lane = zl()
+    if m == 0:
+        x = x + low
+    if m == m_rows - 1:
+        x = x + roll(high, (groups - 1) * ty)
+    for q in range(groups):
+        row = q * m_rows + m
+        first = roll(sides, q * ty - 2 * row - 1)
+        last = first if whole_rows(geom) else roll(sides, q * ty + ty - 1 - 2 * row)
+        x = x + jnp.where(lane == q * ty, first, jnp.where(lane == q * ty + ty - 1, last, 0.0))
+    return x
+
+
+def add_edges(geom, winv, part, edges, store):
+    terms = edge_terms(geom, winv, edges)
+    for m in range(geom[0]):
+        store(m, with_terms(geom, part[m], terms, m))
 
 
 def start_tile(geom, winv, f, store):
@@ -358,25 +369,28 @@
             store(k, d[:, i * LANES : (i + 1) * LANES])
 
 
-def restrict(fine, coarse, v, out):
+def restrict(fine, coarse, v, out, wanted=None):
     m_rows, _, ty = fine
     cm, cq, cty = coarse
     a, b = iota2(LANES, LANES)
     for mc in range(cm):
         acc = None
         for qc in range(cq):
+            if wanted is not None and qc * cm + mc not in wanted:
+                continue
             q, m = divmod(2 * (qc * cm + mc), m_rows)
             inside = (b >= qc * cty) & (b < (qc + 1) * cty) & (a // 2 == b - qc * cty + q * (ty // 2))
             term = lane_dot(v[m] + v[m + 1], jnp.where(inside, 0.25, 0.0))
             acc = term if acc is None else acc + term
-        out[mc] = acc
-
-
-def prolong_add(fine, coarse, e, v, out):
+        if acc is not None:
+            out[mc] = acc
+
+
+def prolong_add(fine, coarse, e, v, out, rows=None):
     m_rows, groups, ty = fine
     cm, _, cty = coarse
     a, b = iota2(LANES, LANES)
-    for m in range(0, m_rows, 2):
+    for m in range(0, m_rows, 2) if rows is None else rows:
         acc = None
         for q in range(groups):
             qc, mc = divmod((q * m_rows + m) // 2, cm)
@@ -473,12 +487,11 @@
         ref[0:Z, :] = out
 
 
-def strip_edges(strip, winv, co, v, sides):
+def strip_edges(strip, winv, co, sides):
     m_rows, _, width = strip
     lt = in_tile(strip)
     r = []
-    for x, raw, flags, k, y in sides:
-        mine = strip_column(strip, v, y, 0, jnp.zeros((Z, width), F32))
+    for x, raw, flags, k, mine in sides:
         mine = turn_groups(strip, mine, flags, k, m_rows)
         low = jnp.where(lt == 0, roll(x, -3 * m_rows), roll(x, 1))
         high = jnp.where(lt == m_rows - 1, roll(x, -2 * m_rows - 2), roll(x, -1))
@@ -538,9 +551,9 @@
             for h in range(2):
                 acc = None
                 for g in range(4):
-                    x = roll(chunks[4 * h + g, part : part + Z, :], (g - k % 4) * 32)
-                    acc = x if acc is None else jnp.where(group == g, x, acc)
-                halves.append(acc)
+                    x = chunks[4 * h + g, part : part + Z, :]
+                    acc = x if acc is None else jnp.where(group == (g + k) % 4, x, acc)
+                halves.append(roll(acc, -(k % 4) * 32))
             ref[m] = jnp.concatenate(halves, axis=1)
     group = lane_ids((8, LANES)) // 32
     for h in range(2):
@@ -554,132 +567,178 @@
     down[Z : Z + 8, :] = flags[...]
 
 
-def strip_sides(values, raws, dn, un, ty):
+def strip_sides(values, raws, dn, un, first, last):
     return (
-        (values[0], raws[0], dn[Z : Z + 8, :], 3, 0),
-        (values[1], raws[1], un[Z : Z + 8, :], 2, ty - 1),
-    )
-
-
-def pre_strip_kernel(f, c, w, vz, flags, dn, un, one, part, v_out, f_next, c_next, fl_next, up, down, res):
+        (values[0], raws[0], dn[Z : Z + 8, :], 3, first[...]),
+        (values[1], raws[1], un[Z : Z + 8, :], 2, last[...]),
+    )
+
+
+def pre_strip_kernel(f, c, w, vz, flags, dn, un, part, first, last, fl_next, c_up, c_down, v_out, f_next, up, down, res):
     strip = STRIPS[2]
     width = strip[2]
     winv = w[...].astype(BF16)
     co = Coef(vz, width)
     raws = [dn[0:Z, :], un[0:Z, :]]
     values = [block_dot(winv, x) for x in raws]
-    edges = strip_edges(strip, winv, co, one, strip_sides(values, raws, dn, un, strip[1]))
+    edges = strip_edges(strip, winv, co, strip_sides(values, raws, dn, un, first, last))
     strip_add_sides(strip, winv, part, strip_frame(strip, flags, *values), Setter(v_out))
     ends = strip_ends(strip, v_out, flags)
     sides = strip_frame(strip, flags, *edges)
     for m in range(6):
         res[m] = strip_residual(strip, co, v_out, f, c, ends, sides, m)
     strip_restrict(res, f_next)
+    small = STRIPS[3]
+    strip_message(small, f_next, None, strip_ends(small, f_next, fl_next), up, down)
+    up[0:Z, :] = up[0:Z, :] + c_up[...]
+    down[0:Z, :] = down[0:Z, :] + c_down[...]
+    up[Z : Z + 8, :] = fl_next[...]
+    down[Z : Z + 8, :] = fl_next[...]
+
+
+def next_coef_kernel(c, flags, c_next, fl_next, up, down):
     strip_restrict(c, c_next)
     a, b = iota2(LANES, LANES)
     fl_next[...] = lane_dot(flags[:, :LANES], jnp.where((b < 64) & (a == (b // 16) * 32), 1.0, 0.0)) + lane_dot(
         flags[:, LANES:], jnp.where((b >= 64) & (a == (b // 16 - 4) * 32), 1.0, 0.0)
     )
     small = STRIPS[3]
-    strip_message(small, f_next, c_next, strip_ends(small, f_next, fl_next), up, down)
-    up[Z : Z + 8, :] = fl_next[...]
-    down[Z : Z + 8, :] = fl_next[...]
-
-
-def bottom_strip_kernel(f, c, w, vz, flags, dn, un, first, part, v_out, up, down, one):
+    zero = jnp.zeros((Z, LANES), F32)
+    up[...] = strip_column(small, c_next, small[1] - 1, 2 * small[0], zero)
+    down[...] = strip_column(small, c_next, 0, 2 * small[0], zero)
+
+
+def bottom_strip_kernel(f, c, w, vz, flags, dn, un, part, first, last, v_out, up, down, one):
     strip = STRIPS[3]
     winv = w[...].astype(BF16)
     co = Coef(vz)
     raws = [dn[0:Z, :], un[0:Z, :]]
     values = [block_dot(winv, x) for x in raws]
-    edges = strip_edges(strip, winv, co, first, strip_sides(values, raws, dn, un, strip[1]))
+    edges = strip_edges(strip, winv, co, strip_sides(values, raws, dn, un, first, last))
     strip_add_sides(strip, winv, part, strip_frame(strip, flags, *values), Setter(one))
     strip_relax(strip, winv, co, one, f, c, flags, strip_frame(strip, flags, *edges), Setter(v_out))
     strip_message(strip, v_out, None, (), up, down)
 
 
-def last_strip_kernel(w, flags, dn, un, part, fine_v, fine_flags, _lo, _hi, g, up, down, e):
+def last_strip_kernel(w, flags, dn, un, part, base_up, base_down, _lo, _hi, e, up, down, small_up, small_down):
     strip, fine = STRIPS[3], STRIPS[2]
     winv = w[...].astype(BF16)
     strip_add_sides(strip, winv, part, strip_frame(strip, flags, dn[...], un[...]), Setter(e))
+    strip_message(strip, e, None, strip_ends(strip, e, flags), small_up, small_down)
+    a, b = iota2(LANES, LANES)
+    for h in range(2):
+        lt = b % 32
+        source = jnp.where(lt < 12, (lt % 6) // 2, jnp.where((lt == 18) | (lt == 19), lt - 9, 15))
+        spread = jnp.where((lt != 15) & (a == 64 * h + (b // 32) * 16 + source) & (source < 15), 1.0, 0.0)
+        half = slice(h * LANES, (h + 1) * LANES)
+        up[:, half] = base_up[:, half] + lane_dot(small_up[...], spread)
+        down[:, half] = base_down[:, half] + lane_dot(small_down[...], spread)
+
+
+def base_message_kernel(v, flags, up, down):
+    strip_message(STRIPS[2], v, None, strip_ends(STRIPS[2], v, flags), up, down)
+
+
+def again2_kernel(f, c, w, vz, flags, v, e, tile_v, g, part, low, high, yup, ydown):
+    strip = STRIPS[2]
     a, b = iota2(LANES, LANES)
     for m in range(3):
         add = jnp.concatenate([lane_dot(e[m], jnp.where(a == 64 * h + b // 2, 1.0, 0.0)) for h in range(2)], axis=1)
-        g[2 * m] = fine_v[2 * m] + add
-        g[2 * m + 1] = fine_v[2 * m + 1] + add
-    strip_message(fine, g, None, strip_ends(fine, g, fine_flags), up, down)
-
-
-def alone_kernel(level, first):
-    def kernel(f, c, w, vz, *refs):
+        g[2 * m] = v[2 * m] + add
+        g[2 * m + 1] = v[2 * m + 1] + add
+    strip_relax(strip, w[...].astype(BF16), Coef(vz, strip[2]), g, f, c, flags, None, Setter(part))
+    zero = jnp.zeros((Z, strip[2]), F32)
+    low[...] = strip_column(strip, g, 0, 0, zero)
+    high[...] = strip_column(strip, g, strip[1] - 1, 0, zero)
+    put_y(GEOM[1], tile_v, None, yup, ydown)
+
+
+def alone_kernel(level):
+    strip = STRIPS[level]
+
+    def kernel(f, c, w, vz, flags, part, low, high, v):
         winv = w[...].astype(BF16)
-        flags = None
-        if level >= 2:
-            flags, *refs = refs
-        v, part = refs
-        if level < 2:
-            if first:
-                start_tile(GEOM[level], winv, f, Setter(v))
-            relax_tile(GEOM[level], winv, Coef(vz), v, f, c, ALONE, Setter(part))
-        else:
-            strip = STRIPS[level]
-            if first:
-                for m in range(strip[0]):
-                    v[m] = block_dot(winv, f[m])
-            strip_relax(strip, winv, Coef(vz, strip[2]), v, f, c, flags, None, Setter(part))
+        for m in range(strip[0]):
+            v[m] = block_dot(winv, f[m])
+        strip_relax(strip, winv, Coef(vz, strip[2]), v, f, c, flags, None, Setter(part))
+        zero = jnp.zeros((Z, strip[2]), F32)
+        low[...] = strip_column(strip, v, 0, 0, zero)
+        high[...] = strip_column(strip, v, strip[1] - 1, 0, zero)
 
     return kernel
 
 
+def again3_kernel(f, c, w, vz, flags, v, part):
+    strip_relax(STRIPS[3], w[...].astype(BF16), Coef(vz), v, f, c, flags, None, Setter(part))
+
+
+def tile_row(e, m, step):
+    t = lax.rem(lax.axis_index("gx") + (step + 8), 8)
+    half = jnp.where(t < 4, e[m, :, :LANES], e[m, :, LANES:])
+    return pltpu.roll(half, lax.rem(8 - t, 4) * 32, axis=1)
+
+
 def post_strip_kernel(
-    f, c, w, vz, flags, dn, un, g, part, gdn, gun, fine_v, xlo, xhi, own, g_out, lo_out, hi_out, up, down, one, e, tile, yup, ydown
+    f, c, w, vz, flags, dn, un, part, first_column, last_column, gdn, gun, xlo, xhi, own, yup, ydown, e, up, down, one
 ):
     strip = STRIPS[2]
-    fine, geom = GEOM[1], GEOM[2]
+    fine = GEOM[1]
     winv = w[...].astype(BF16)
     co = Coef(vz, strip[2])
     raws = [dn[0:Z, :], un[0:Z, :]]
     values = [gdn[...], gun[...]]
-    edges = strip_edges(strip, winv, co, g, strip_sides(values, raws, dn, un, strip[1]))
+    edges = strip_edges(strip, winv, co, strip_sides(values, raws, dn, un, first_column, last_column))
     strip_add_sides(strip, winv, part, strip_frame(strip, flags, *values), Setter(one))
     strip_relax(strip, winv, co, one, f, c, flags, strip_frame(strip, flags, *edges), Setter(e))
-
-    place = lax.axis_index("gx")
-
-    def tile_row(m, step):
-        t = lax.rem(place + (step + 8), 8)
-        return pltpu.roll(e[m], lax.rem(8 - t, 8) * 32, axis=1)[:, :LANES]
-
+    extras = []
+    for ref, step in ((xlo, -1), (xhi, 1)):
+        first, last = tile_row(e, 0, step), tile_row(e, 5, step)
+        adds = (col(first, 0), col(first, 31), col(last, 0), col(last, 31))
+        extras.append([x + y for x, y in zip(corner_columns(tail_of(fine, ref, 2)), adds)])
+    group = zl() // 4
+    add_up = add_down = jnp.zeros((Z, LANES), F32)
     for m in range(6):
-        tile[m] = tile_row(m, 0)
-    prolong_add(fine, geom, tile, fine_v, g_out)
+        row = tile_row(e, m, 0)
+        add_up = jnp.where(group == m, col(row, 31), add_up)
+        add_down = jnp.where(group == m, col(row, 0), add_down)
+    up[...], down[...] = merge_y(*extras, own, yup[...] + add_up, ydown[...] + add_down)
+
+
+def again1_kernel(f, c, w, vz, v, e, xlo, xhi, g, part, columns, lo_out, hi_out, tile):
+    fine, geom = GEOM[1], GEOM[2]
+    for m in range(6):
+        tile[m] = tile_row(e, m, 0)
+    prolong_add(fine, geom, tile, v, g)
     a, b = iota2(LANES, LANES)
     spread = jnp.where((b < 64) & (a == b // 2), 1.0, 0.0)
-    extras = []
-    for ref, out, step, near in ((xlo, lo_out, -1, 5), (xhi, hi_out, 1, 0)):
-        first, last = tile_row(0, step), tile_row(5, step)
-        add = lane_dot(last if near else first, spread)
-        adds = (col(first, 0), col(first, 31), col(last, 0), col(last, 31))
-        extras.append([x + y for x, y in zip(corner_columns(tail_of(fine, ref, 2)), adds)])
+    for ref, out, row in ((xlo, lo_out, tile_row(e, 5, -1)), (xhi, hi_out, tile_row(e, 0, 1))):
+        add = lane_dot(row, spread)
         out[...] = pack(fine, [part_of(fine, ref, 0) + add, part_of(fine, ref, 1) + add])[0]
-    put_y(fine, g_out, None, yup, ydown)
-    up[...], down[...] = merge_y(*extras, own, yup[...], ydown[...])
-
-
-def strip_ring(up, down):
-    nx, ny = lax.axis_size("gx"), lax.axis_size("gy")
-
-    def pairs(step):
-        out = []
-        for i in range(nx):
-            for j in range(ny):
-                to = (j + step) % ny
-                other = i ^ 1 if (2 * j // ny) != (2 * to // ny) else i
-                out.append((i * ny + j, other * ny + to))
-        return out
-
+    columns[...] = own_columns(fine, g)
+    relax_tile(fine, w[...].astype(BF16), Coef(vz), g, f, c, ALONE, Setter(part))
+
+
+def swap_pairs(axis, which, nearest=False):
+    sizes = lax.axis_size("gx"), lax.axis_size("gy")
+    out = []
+    for i in range(sizes[0]):
+        for j in range(sizes[1]):
+            at = [i, j]
+            dim = 0 if axis == "gx" else 1
+            n = sizes[dim]
+            at[dim] = (at[dim] ^ 1) if which == 0 else (at[dim] + (1 if at[dim] % 2 else n - 1)) % n
+            if nearest and 2 * j // n != 2 * at[1] // n:
+                at[0] = i ^ 1
+            out.append((i * sizes[1] + j, at[0] * sizes[1] + at[1]))
+    return out
+
+
+def swap(first, second, axis, nearest=False):
     both = ("gx", "gy")
-    return lax.ppermute(up, both, pairs(1)), lax.ppermute(down, both, pairs(-1))
+    return (
+        lax.ppermute(first, both, swap_pairs(axis, 0, nearest)),
+        lax.ppermute(second, both, swap_pairs(axis, 1, nearest)),
+    )
 
 
 ANY = pl.BlockSpec(memory_space=pl.ANY)
@@ -687,13 +746,50 @@
 VMEM = pl.BlockSpec(memory_space=pltpu.VMEM)
 
 
-def call(kernel, outs, args, scratch=(), name=None, after=0):
+class Either:
+    def __init__(self, first, a, b):
+        self.first, self.a, self.b = first, a, b
+
+    def __getitem__(self, index):
+        return jnp.where(self.first, self.a[index], self.b[index])
+
+
+def is_even(axis):
+    return lax.rem(lax.axis_index(axis), 2) == 0
+
+
+def by_swaps(kernel, n_in, n_out, got, send):
+    def wrapped(*refs):
+        refs = list(refs)
+        for place, axis in got:
+            a, b = refs[place], refs[place + 1]
+            refs[place], refs[place + 1] = Either(is_even(axis), b, a), Either(is_even(axis), a, b)
+        extra = refs[len(refs) - 2 * len(send) :]
+        refs = refs[: len(refs) - 2 * len(send)]
+        outs = []
+        for k, (place, axis) in enumerate(send):
+            place += n_in
+            outs.append((refs[place], refs[place + 1], extra[2 * k], extra[2 * k + 1], axis))
+            refs[place], refs[place + 1] = extra[2 * k], extra[2 * k + 1]
+        kernel(*refs)
+        for first, second, up, down, axis in outs:
+            even = is_even(axis)
+            up, down = up[...], down[...]
+            first[...] = jnp.where(even, up, down)
+            second[...] = jnp.where(even, down, up)
+
+    return wrapped
+
+
+def call(kernel, outs, args, scratch=(), name=None, after=0, got=(), send=()):
+    scratch = [pltpu.VMEM(s, F32) for s in scratch]
+    scratch += [pltpu.VMEM(outs[place], F32) for place, _ in send for _ in range(2)]
     return pl.pallas_call(
-        kernel,
+        by_swaps(kernel, len(args), len(outs), got, send),
         out_shape=[jax.ShapeDtypeStruct(s, F32) for s in outs],
         in_specs=[VMEM] * (len(args) - after) + [ANY] * after,
         out_specs=[VMEM] * len(outs),
-        scratch_shapes=[pltpu.VMEM(s, F32) for s in scratch],
+        scratch_shapes=scratch,
         compiler_params=pltpu.CompilerParams(vmem_limit_bytes=LIMIT),
         name=name,
     )(*args)
@@ -768,7 +864,7 @@
     return jnp.where((b >= Z) & (b < 2 * Z), whole - high, high)
 
 
-def side_kernel(f_in, c_in, inv, vz, own, f, c, w0, w1, w2, w3, one, part, c_next, c_tile, yup, ydown):
+def side_kernel(f_in, c_in, inv, vz, own, f, c, w0, w1, w2, w3, one, part, columns, c_next, c_tile, yup, ydown):
     load_top(f_in, f)
     load_top(c_in, c)
     put_y(GEOM[0], f, c, yup, ydown)
@@ -780,6 +876,7 @@
     winv = w0[...].astype(BF16)
     start_tile(GEOM[0], winv, f, Setter(one))
     relax_tile(GEOM[0], winv, Coef(vz), one, f, c, ALONE, Setter(part))
+    columns[...] = own_columns(GEOM[0], one)
     restrict(GEOM[0], GEOM[1], c, c_next)
     restrict(GEOM[1], GEOM[2], c_next, c_tile)
 
@@ -798,80 +895,100 @@
     return kernel
 
 
-def pre_tile(level, f, c, w, vz, own, xlo, xhi, ydn, yun, one, part, v_out, res):
-    geom = GEOM[level]
+def pre_edges(geom, f, c, w, vz, own, xlo, xhi, ydn, yun, one, columns):
+    winv = w[...].astype(BF16)
+    fl = flags_of(geom, own, xlo, xhi, ydn, yun)
+    halo = messages(geom, xlo, xhi, ydn, yun, winv)
+    relaxed = relax_edges(geom, winv, Coef(vz), one, columns[...], halo, fl, *own_data(geom, xlo, xhi, ydn, yun))
+    terms = edge_terms(geom, winv, frame(geom, fl, halo.lo, halo.hi, halo.sides()))
+    return terms, frame(geom, fl, *relaxed)
+
+
+def pre0_kernel(f, c, w, vz, own, xlo, xhi, ydn, yun, one, part, columns, c_next, up, down, terms_out, edges_out, v, res, f_next):
+    geom, coarse = GEOM[0], GEOM[1]
+    terms, edges = pre_edges(geom, f, c, w, vz, own, xlo, xhi, ydn, yun, one, columns)
+    for k in range(3):
+        terms_out[k] = terms[k]
+        edges_out[k] = edges[k]
+    co = Coef(vz)
+    for m in (*range(5), *range(19, 24)):
+        v[m] = with_terms(geom, part[m], terms, m)
+    for m in (*range(4), *range(20, 24)):
+        res[m] = tile_residual(geom, co, v, f, c, *edges, m)
+    restrict(geom, coarse, res, f_next, (0, 1, 10, 11))
+    put_x(coarse, f_next, c_next, up, down, own[...])
+
+
+def mid1_kernel(f, c, part, terms_in, edges_in, vz, w, c_next, own, v, f_next, one, part_next, columns, yup, ydown, res):
+    geom, coarse = GEOM[0], GEOM[1]
+    co = Coef(vz)
+    terms = [terms_in[k] for k in range(3)]
+    edges = [edges_in[k] for k in range(3)]
+    for m in range(24):
+        v[m] = with_terms(geom, part[m], terms, m)
+    for m in range(24):
+        res[m] = tile_residual(geom, co, v, f, c, *edges, m)
+    restrict(geom, coarse, res, f_next)
+    put_y(coarse, f_next, c_next, yup, ydown)
+    yup[Z : Z + 8, :] = own[...]
+    ydown[Z : Z + 8, :] = own[...]
+    winv = w[...].astype(BF16)
+    start_tile(coarse, winv, f_next, Setter(one))
+    relax_tile(coarse, winv, co, one, f_next, c_next, ALONE, Setter(part_next))
+    columns[...] = own_columns(coarse, one)
+
+
+def pre1_kernel(f, c, w, vz, own, xlo, xhi, ydn, yun, one, part, columns, c_tile, v_out, up, down, chunks, res, f_next):
+    geom = GEOM[1]
+    terms, edges = pre_edges(geom, f, c, w, vz, own, xlo, xhi, ydn, yun, one, columns)
+    for m in range(6):
+        v_out[m] = with_terms(geom, part[m], terms, m)
+    co = Coef(vz)
+    for m in range(6):
+        res[m] = tile_residual(geom, co, v_out, f, c, *edges, m)
+    restrict(geom, GEOM[2], res, f_next)
+    put_x(geom, v_out, None, up, down)
+    whole = pack(GEOM[2], [f_next[m] for m in range(6)] + [c_tile[m] for m in range(6)])
+    turn = lax.rem(lax.axis_index("gx"), 4) * 32
+    whole = [pltpu.roll(x, turn, axis=1) for x in whole]
+    for t in range(8):
+        for k, x in enumerate(whole):
+            chunks[t, k * Z : (k + 1) * Z, :] = x
+        chunks[t, 3 * Z : 3 * Z + 8, :] = own[...]
+
+
+def again0_kernel(f, c, w, vz, e, v, g, part, columns, yup, ydown):
+    prolong_add(GEOM[0], GEOM[1], e, v, g)
+    put_y(GEOM[0], g, None, yup, ydown)
+    columns[...] = own_columns(GEOM[0], g)
+    relax_tile(GEOM[0], w[...].astype(BF16), Coef(vz), g, f, c, ALONE, Setter(part))
+
+
+def post_sweeps(geom, f, c, w, vz, own, xlo, xhi, ydn, yun, g, part, columns, glo, ghi, gdn, gun, one, store):
     winv = w[...].astype(BF16)
     co = Coef(vz)
     fl = flags_of(geom, own, xlo, xhi, ydn, yun)
-    halo = messages(geom, xlo, xhi, ydn, yun, winv)
-    lo2, hi2, sides2 = relax_edges(geom, winv, co, one, halo, fl, *own_data(geom, xlo, xhi, ydn, yun))
-    add_edges(geom, winv, part, frame(geom, fl, halo.lo, halo.hi, halo.sides()), Setter(v_out))
-    lo, hi, sides = frame(geom, fl, lo2, hi2, sides2)
-    for m in range(geom[0]):
-        res[m] = tile_residual(geom, co, v_out, f, c, lo, hi, sides, m)
-
-
-def pre0_kernel(f, c, w, vz, own, xlo, xhi, ydn, yun, one, part, c_next, v_out, f_next, up, down, yup, ydown, res):
-    pre_tile(0, f, c, w, vz, own, xlo, xhi, ydn, yun, one, part, v_out, res)
-    coarse = GEOM[1]
-    restrict(GEOM[0], coarse, res, f_next)
-    put_x(coarse, f_next, c_next, up, down, own[...])
-    put_y(coarse, f_next, c_next, yup, ydown)
-    yup[Z : Z + 8, :] = own[...]
-    ydown[Z : Z + 8, :] = own[...]
-
-
-def pre1_kernel(f, c, w, vz, own, xlo, xhi, ydn, yun, one, part, c_tile, v_out, up, down, chunks, res, f_next):
-    pre_tile(1, f, c, w, vz, own, xlo, xhi, ydn, yun, one, part, v_out, res)
-    restrict(GEOM[1], GEOM[2], res, f_next)
-    put_x(GEOM[1], v_out, None, up, down)
-    whole = pack(GEOM[2], [f_next[m] for m in range(6)] + [c_tile[m] for m in range(6)])
-    for t in range(8):
-        for k, part in enumerate(whole):
-            chunks[t, k * Z : (k + 1) * Z, :] = part
-        chunks[t, 3 * Z : 3 * Z + 8, :] = own[...]
-
-
-def post_kernel(level):
-    geom = GEOM[level]
-
-    def sweeps(f, c, w, vz, own, xlo, xhi, ydn, yun, g, part, glo, ghi, gdn, gun, one, store):
-        winv = w[...].astype(BF16)
-        co = Coef(vz)
-        fl = flags_of(geom, own, xlo, xhi, ydn, yun)
-        halo = Halo(
-            part_of(geom, glo, 0), part_of(geom, glo, 1), part_of(geom, ghi, 0), part_of(geom, ghi, 1), gdn[...], gun[...]
-        )
-        lo2, hi2, sides2 = relax_edges(geom, winv, co, g, halo, fl, *own_data(geom, xlo, xhi, ydn, yun))
-        add_edges(geom, winv, part, frame(geom, fl, halo.lo, halo.hi, halo.sides()), Setter(one))
-        relax_tile(geom, winv, co, one, f, c, frame(geom, fl, lo2, hi2, sides2), store)
-
-    if level == 0:
-
-        def kernel(f, c, w, vz, own, xlo, xhi, ydn, yun, g, part, glo, ghi, gdn, gun, out, one):
-            def store(x, value):
-                out[pl.ds(x, NZ, stride=24), :] = value[0:NZ, :]
-
-            sweeps(f, c, w, vz, own, xlo, xhi, ydn, yun, g, part, glo, ghi, gdn, gun, one, store)
-
-        return kernel
-
-    fine = GEOM[level - 1]
-
-    def kernel(f, c, w, vz, own, xlo, xhi, ydn, yun, g, part, glo, ghi, gdn, gun, fine_v, g_out, up, down, yup, ydown, one, e):
-        sweeps(f, c, w, vz, own, xlo, xhi, ydn, yun, g, part, glo, ghi, gdn, gun, one, Setter(e))
-        prolong_add(fine, geom, e, fine_v, g_out)
-        put_x(fine, g_out, None, up, down)
-        put_y(fine, g_out, None, yup, ydown)
-
-    return kernel
-
-
-def both_ways(up, down, axis):
-    n = lax.axis_size(axis)
-    fwd = [(i, (i + 1) % n) for i in range(n)]
-    back = [((i + 1) % n, i) for i in range(n)]
-    return lax.ppermute(up, axis, fwd), lax.ppermute(down, axis, back)
+    halo = Halo(
+        part_of(geom, glo, 0), part_of(geom, glo, 1), part_of(geom, ghi, 0), part_of(geom, ghi, 1), gdn[...], gun[...]
+    )
+    relaxed = relax_edges(geom, winv, co, g, columns[...], halo, fl, *own_data(geom, xlo, xhi, ydn, yun))
+    add_edges(geom, winv, part, frame(geom, fl, halo.lo, halo.hi, halo.sides()), Setter(one))
+    relax_tile(geom, winv, co, one, f, c, frame(geom, fl, *relaxed), store)
+
+
+def post0_kernel(f, c, w, vz, own, xlo, xhi, ydn, yun, g, part, columns, glo, ghi, gdn, gun, out, one):
+    def store(x, value):
+        out[pl.ds(x, NZ, stride=24), :] = value[0:NZ, :]
+
+    post_sweeps(GEOM[0], f, c, w, vz, own, xlo, xhi, ydn, yun, g, part, columns, glo, ghi, gdn, gun, one, store)
+
+
+def post1_kernel(
+    f, c, w, vz, own, xlo, xhi, ydn, yun, g, part, columns, glo, ghi, gdn, gun, fine_v, e, up, down, one, fine_g
+):
+    post_sweeps(GEOM[1], f, c, w, vz, own, xlo, xhi, ydn, yun, g, part, columns, glo, ghi, gdn, gun, one, Setter(e))
+    prolong_add(GEOM[0], GEOM[1], e, fine_v, fine_g, (0, 22))
+    put_x(GEOM[0], fine_g, None, up, down)
 
 
 def on_device(right_side, helm_coef, vert_coef, block_inverse, edge_flip):
@@ -885,91 +1002,135 @@
     t0, t1, t2 = tile_shape(0), tile_shape(1), tile_shape(2)
     xs = x_shape(0, 3)
     up, down, own, vz = pl.pallas_call(
-        open_kernel,
+        by_swaps(open_kernel, 4, 4, (), ((0, "gx"),)),
         out_shape=[jax.ShapeDtypeStruct(x, F32) for x in (xs, xs, (8, LANES), ys)],
         in_specs=[ANY] * 4,
         out_specs=[VMEM] * 4,
         scratch_shapes=[pltpu.VMEM((NZ, 2, LANES), F32)] * 2
         + [pltpu.VMEM((NZ, 1, LANES), F32)] * 2
-        + [pltpu.VMEM((1, NZ + 1), F32), pltpu.VMEM((1, 4), jnp.int32), pltpu.SemaphoreType.DMA((6,))],
+        + [pltpu.VMEM((1, NZ + 1), F32), pltpu.VMEM((1, 4), jnp.int32), pltpu.SemaphoreType.DMA((6,))]
+        + [pltpu.VMEM(xs, F32)] * 2,
         compiler_params=pltpu.CompilerParams(vmem_limit_bytes=58 * 1024 * 1024),
         name="open",
     )(right_side, helm_coef, vert, flip)
-    xlo, xhi = both_ways(up, down, "gx")
+    xlo, xhi = swap(up, down, "gx")
     ws = (Z, 3 * Z)
-    f, c, *w, one, part, c1, c_tile, yup, ydown = call(
+    f, c, *w, one, part, columns, c1, c_tile, yup, ydown = call(
         side_kernel,
-        [t0, t0] + [ws] * 4 + [t0, t0, t1, t2, Y_FULL, Y_FULL],
+        [t0, t0] + [ws] * 4 + [t0, t0, ys, t1, t2, Y_FULL, Y_FULL],
         [f_in, c_in, inv, vz, own],
         name="side",
     )
 
     def to_sides(level, count, xlo, xhi, yup, ydown):
         shape = yup.shape
-        yup, ydown = call(merge_kernel(level, count), [shape, shape], [xlo, xhi, own, yup, ydown], name=f"merge{level}")
-        return both_ways(yup, ydown, "gy")
+        yup, ydown = call(merge_kernel(level, count), [shape, shape], [xlo, xhi, own, yup, ydown], name=f"merge{level}", got=((0, "gx"),), send=((0, "gy"),))
+        return swap(yup, ydown, "gy")
 
     got0 = (xlo, xhi, *to_sides(0, 3, xlo, xhi, yup, ydown))
     xs = x_shape(1, 3)
-    v0, f1, up, down, yup, ydown = call(
-        pre0_kernel, [t0, t1, xs, xs, Y_FULL, Y_FULL], [f, c, w[0], vz, own, *got0, one, part, c1], [t0], name="pre0"
-    )
-    xlo, xhi = both_ways(up, down, "gx")
-    one, part = call(alone_kernel(1, True), [t1, t1], [f1, c1, w[1], vz], name="alone1")
+    three = (3, Z, LANES)
+    up, down, terms, edges = call(
+        pre0_kernel,
+        [xs, xs, three, three],
+        [f, c, w[0], vz, own, *got0, one, part, columns, c1],
+        [t0, t0, t1],
+        name="pre0",
+        got=((5, "gx"), (7, "gy")),
+        send=((0, "gx"),),
+    )
+    xlo, xhi = swap(up, down, "gx")
+    v0, f1, one, part, columns, yup, ydown = call(
+        mid1_kernel,
+        [t0, t1, t1, t1, ys, Y_FULL, Y_FULL],
+        [f, c, part, terms, edges, vz, w[1], c1, own],
+        [t0],
+        name="mid1",
+    )
     got1 = (xlo, xhi, *to_sides(1, 3, xlo, xhi, yup, ydown))
     xs = x_shape(1, 2)
     v1, up, down, chunks = call(
         pre1_kernel,
         [t1, xs, xs, (8, 3 * Z + 8, LANES)],
-        [f1, c1, w[1], vz, own, *got1, one, part, c_tile],
+        [f1, c1, w[1], vz, own, *got1, one, part, columns, c_tile],
         [t1, t2],
         name="pre1",
-    )
-    v1_lo, v1_hi = both_ways(up, down, "gx")
+        got=((5, "gx"), (7, "gy")),
+        send=((1, "gx"),),
+    )
+    v1_lo, v1_hi = swap(up, down, "gx")
     chunks = lax.all_to_all(chunks, "gx", 0, 0)
     s2, s3 = (6, Z, 256), (3, Z, 128)
     m2, m3 = (Z, 256), (Z, 128)
     full2, full3 = (Z + 8, 256), (Z + 8, 128)
     f2, c2, fl2, up, down = call(
-        open_strip_kernel, [s2, s2, (8, 256), full2, full2], [chunks], name="open2"
-    )
-    side2 = strip_ring(up, down)
-    one, part = call(alone_kernel(2, True), [s2, s2], [f2, c2, w[2], vz, fl2], name="alone2")
-    v2, f3, c3, fl3, up, down = call(
-        pre_strip_kernel, [s2, s3, s3, (8, 128), full3, full3], [f2, c2, w[2], vz, fl2, *side2, one, part], [s2], name="pre2"
-    )
-    side3 = strip_ring(up, down)
-    one, part = call(alone_kernel(3, True), [s3, s3], [f3, c3, w[3], vz, fl3], name="alone3")
+        open_strip_kernel, [s2, s2, (8, 256), full2, full2], [chunks], name="open2", send=((3, "gy"),)
+    )
+    side2 = swap(up, down, "gy", True)
+    alone = call(alone_kernel(2), [s2, m2, m2], [f2, c2, w[2], vz, fl2], [s2], name="alone2")
+    c3, fl3, c_up, c_down = call(next_coef_kernel, [s3, (8, 128), m3, m3], [c2, fl2], name="coef3")
+    v2, f3, up, down = call(
+        pre_strip_kernel,
+        [s2, s3, full3, full3],
+        [f2, c2, w[2], vz, fl2, *side2, *alone, fl3, c_up, c_down],
+        [s2],
+        name="pre2",
+        got=((5, "gy"),),
+        send=((2, "gy"),),
+    )
+    side3 = swap(up, down, "gy", True)
+    alone = call(alone_kernel(3), [s3, m3, m3], [f3, c3, w[3], vz, fl3], [s3], name="alone3")
     v3, up, down = call(
-        bottom_strip_kernel, [s3, m3, m3], [f3, c3, w[3], vz, fl3, *side3, one, part], [s3], name="bottom"
-    )
-    side = strip_ring(up, down)
-    (part,) = call(alone_kernel(3, False), [s3], [f3, c3, w[3], vz, fl3, v3], name="again3")
-    g2, up, down = call(last_strip_kernel, [s2, m2, m2], [w[3], fl3, *side, part, v2, fl2, v1_lo, v1_hi], [s3], name="last", after=2)
-    side = strip_ring(up, down)
-    (part,) = call(alone_kernel(2, False), [s2], [f2, c2, w[2], vz, fl2, g2], name="again2")
-    g1, lo, hi, up, down = call(
+        bottom_strip_kernel, [s3, m3, m3], [f3, c3, w[3], vz, fl3, *side3, *alone], [s3], name="bottom", got=((5, "gy"),), send=((1, "gy"),)
+    )
+    side = swap(up, down, "gy", True)
+    (part,) = call(again3_kernel, [s3], [f3, c3, w[3], vz, fl3, v3], name="again3")
+    base_up, base_down = call(base_message_kernel, [m2, m2], [v2, fl2], name="base2")
+    e3, up, down = call(
+        last_strip_kernel,
+        [s3, m2, m2],
+        [w[3], fl3, *side, part, base_up, base_down, v1_lo, v1_hi],
+        [m3, m3],
+        name="last",
+        after=2,
+        got=((2, "gy"),),
+        send=((1, "gy"),),
+    )
+    side = swap(up, down, "gy", True)
+    g2, *alone, yup, ydown = call(
+        again2_kernel, [s2, s2, m2, m2, ys, ys], [f2, c2, w[2], vz, fl2, v2, e3, v1], name="again2"
+    )
+    e2, up, down = call(
         post_strip_kernel,
-        [t1, ys, ys, ys, ys],
-        [f2, c2, w[2], vz, fl2, *side2, g2, part, *side, v1, v1_lo, v1_hi, own],
-        [s2, s2, t2, ys, ys],
+        [s2, ys, ys],
+        [f2, c2, w[2], vz, fl2, *side2, *alone, *side, v1_lo, v1_hi, own, yup, ydown],
+        [s2],
         name="post2",
-    )
-    side = both_ways(up, down, "gy")
-    (part,) = call(alone_kernel(1, False), [t1], [f1, c1, w[1], vz, g1], name="again1")
+        got=((5, "gy"), (10, "gy"), (12, "gx")),
+        send=((1, "gy"),),
+    )
+    side = swap(up, down, "gy")
+    g1, part, columns, lo, hi = call(
+        again1_kernel, [t1, t1, ys, ys, ys], [f1, c1, w[1], vz, v1, e2, v1_lo, v1_hi], [t2], name="again1", got=((6, "gx"),)
+    )
     xs = x_shape(0, 2)
-    g0, up, down, yup, ydown = call(
-        post_kernel(1),
-        [t0, xs, xs, ys, ys],
-        [f1, c1, w[1], vz, own, *got1, g1, part, lo, hi, *side, v0],
-        [t1, t1],
+    e1, up, down = call(
+        post1_kernel,
+        [t1, xs, xs],
+        [f1, c1, w[1], vz, own, *got1, g1, part, columns, lo, hi, *side, v0],
+        [t1, t0],
         name="post1",
-    )
-    xlo, xhi = both_ways(up, down, "gx")
-    (part,) = call(alone_kernel(0, False), [t0], [f, c, w[0], vz, g0], name="again0")
+        got=((5, "gx"), (7, "gy"), (14, "gy")),
+        send=((1, "gx"),),
+    )
+    xlo, xhi = swap(up, down, "gx")
+    g0, part, columns, yup, ydown = call(
+        again0_kernel, [t0, t0, ys, ys, ys], [f, c, w[0], vz, e1, v0], name="again0"
+    )
     got = (xlo, xhi, *to_sides(0, 2, xlo, xhi, yup, ydown))
     (out,) = call(
-        post_kernel(0), [(NZ * 24, LANES)], [f, c, w[0], vz, own, *got0, g0, part, *got], [t0], name="post0"
+        post0_kernel, [(NZ * 24, LANES)], [f, c, w[0], vz, own, *got0, g0, part, columns, *got], [t0], name="post0",
+        got=((5, "gx"), (7, "gy"), (12, "gx"), (14, "gy")),
     )
     return out.reshape(NZ, 24, LANES)
 

time: 123 us -> 117 us (0.951)
  starting transfers between devices: 59.3 us -> 43.8 us
  waiting for transfers between devices: 13.9 us -> 23.8 us
    ppermute x24, starting transfers between devices: 59.3 us -> 43.8 us  [the longest x12 41.2 us: swap(): lax.ppermute(second, both, swap_pairs(axis, 1, nearest))]
    ppermute x24, waiting for transfers between devices: 13.9 us -> 23.8 us  [the longest x12 23.1 us: swap(): lax.ppermute(second, both, swap_pairs(axis, 1, nearest))]
    pallas_call x21 -> x23, Pallas kernels: 30.8 us -> 31.9 us  [the longest x22 29.9 us: call(): pl.pallas_call(by_swaps(kernel, len(args), len(outs), got, send), out_sha...]
  transfers between devices with their start and end apart: 24 -> 24, of which waited for: 12 -> 11; matrix products, arithmetic and copies ran while one was open for 1% -> 1% of each run, Pallas kernels for 7% -> 12%
where the time goes in v3:
time: 117 us
  starting transfers between devices  43.8 us (37%)
  Pallas kernels  31.9 us (27%)
  waiting for transfers between devices  23.8 us (20%)
  blocking collectives  15.5 us (13%)
  local copies, waits for them, and re-layouts  1.57 us (1%)
    ppermute x12, starting transfers between devices, swap(): lax.ppermute(second, both, swap_pairs(axis, 1, nearest))  41.2 us
    pallas_call x22, Pallas kernels, call(): pl.pallas_call(by_swaps(kernel, len(args), len(outs), got, send), out_sha...  29.9 us
    ppermute x12, waiting for transfers between devices, swap(): lax.ppermute(second, both, swap_pairs(axis, 1, nearest))  23.1 us
    all_to_all x1, blocking collectives, on_device(): chunks = lax.all_to_all(chunks, 'gx', 0, 0)  15.5 us
    ppermute x12, starting transfers between devices, swap(): lax.ppermute(first, both, swap_pairs(axis, 0, nearest))  2.55 us
  transfers between devices with their start and end apart: 24, of which 11 were waited for; matrix products, arithmetic and copies ran while one was open for 1% of the time, Pallas kernels for 12%

profile of v3, /device:TPU:0, one launch (start us, length us, event | category | flops | bytes accessed | tf_op | source)
XLA Modules:
  0.0 116.9 jit_solution(1882920415427772648)
XLA Ops:
  0.0 2.0 %open.1 = (f32[224,128]{1,0:T(8,128)}, f32[224,128]{1,0:T(8,128)}, f32[8,128]{1,0:T(8,128)}, f32[72,128]{1,0:T(8,128)}) custom-call(f32[70,24,128]{2,1,0:T(8,128)} %refs_0_.1, f32[70,24,128]{2,1,0:T(8,128)} %refs_1_.1, f32[1,71]{1,0:T(1,128)} %bitcast.9, s32[1,4]{1,0:T(1,128)} %bitcast.10), custom_call_target="tpu_custom_call" | custom-call | tf_op jit(solution)/shard_map/open/pallas_call | solution.py:1004
  2.0 1.7 %collective-permute-start = (f32[224,128]{1,0:T(8,128)}, f32[224,128]{1,0:T(8,128)S(1)}, u32[]{:S(2)}, u32[]{:S(2)}) collective-permute-start(f32[224,128]{1,0:T(8,128)} %get-tuple-element.96), channel_id=1, source_target_pairs={{0,16},{1,17},{2,18},{3,19},{4,20},{5,21},{6,22},{7,23},{8,24},{9,... | collective-permute-start | bytes 344072 | tf_op jit(solution)/shard_map/ppermute | solution.py:739
  3.8 2.6 %collective-permute-start.1 = (f32[224,128]{1,0:T(8,128)}, f32[224,128]{1,0:T(8,128)S(1)}, u32[]{:S(2)}, u32[]{:S(2)}) collective-permute-start(f32[224,128]{1,0:T(8,128)} %get-tuple-element.97), channel_id=1, source_target_pairs={{0,112},{1,113},{2,114},{3,115},{4,116},{5,117},{6,118},{7,119},{8... | collective-permute-start | bytes 344072 | tf_op jit(solution)/shard_map/ppermute | solution.py:740
  8.0 2.6 %side.1 = (f32[24,72,128]{2,1,0:T(8,128)S(1)}, f32[24,72,128]{2,1,0:T(8,128)S(1)}, f32[72,216]{1,0:T(8,128)S(1)}, f32[72,216]{1,0:T(8,128)S(1)}, f32[72,216]{1,0...) custom-call(f32[1680,128]{1,0:T(8,128)S(1)} %bitcast.6, ...), custom_call_target="tpu_custom_call" | custom-call | tf_op jit(solution)/shard_map/side/pallas_call | solution.py:787
  11.2 6.6 %collective-permute-start.3 = (f32[80,128]{1,0:T(8,128)S(1)}, f32[80,128]{1,0:T(8,128)S(1)}, u32[]{:S(2)}, u32[]{:S(2)}) collective-permute-start(f32[80,128]{1,0:T(8,128)S(1)} %get-tuple-element.101), channel_id=1, source_target_pairs={{0,15},{1,2},{2,1},{3,4},{4,3},{5,6},{6,5},{7,8},{8,7},{9,10},{10,... | collective-permute-start | bytes 122888 | tf_op jit(solution)/shard_map/ppermute | solution.py:740
  17.8 1.7 %collective-permute-done.3.refs_8_ = f32[80,128]{1,0:T(8,128)S(1)} collective-permute-done((f32[80,128]{1,0:T(8,128)S(1)}, f32[80,128]{1,0:T(8,128)S(1)}, u32[]{:S(2)}, u32[]{:S(2)}) %collective-permute-start.3) | collective-permute-done | bytes 40992 | tf_op jit(solution)/shard_map/ppermute | solution.py:740
  19.5 1.6 %pre0.1 = (f32[152,128]{1,0:T(8,128)S(1)}, f32[152,128]{1,0:T(8,128)S(1)}, f32[3,72,128]{2,1,0:T(8,128)S(1)}, f32[3,72,128]{2,1,0:T(8,128)S(1)}) custom-call(f32[24,72,128]{2,1,0:T(8,128)S(1)} %get-tuple-element.93.refs_0_, f32[24,72,128]{2,1,0:T(8,128)S(1)} %get-tuple-element.94.refs_1_, f32[72,216]{1,0:T(8,128)S(1)} %get-tuple-element.95.refs_2_, ...), custom_call_target="tpu_custom_call" | custom-call | tf_op jit(solution)/shard_map/pre0/pallas_call | solution.py:787
  21.2 3.4 %collective-permute-start.5 = (f32[152,128]{1,0:T(8,128)S(1)}, f32[152,128]{1,0:T(8,128)S(1)}, u32[]{:S(2)}, u32[]{:S(2)}) collective-permute-start(f32[152,128]{1,0:T(8,128)S(1)} %get-tuple-element.111), channel_id=1, source_target_pairs={{0,112},{1,113},{2,114},{3,115},{4,116},{5,117},{6,118},{7,119},{8... | collective-permute-start | bytes 233480 | tf_op jit(solution)/shard_map/ppermute | solution.py:740
  24.6 2.2 %mid1.1 = (f32[24,72,128]{2,1,0:T(8,128)S(1)}, f32[6,72,128]{2,1,0:T(8,128)S(1)}, f32[6,72,128]{2,1,0:T(8,128)S(1)}, f32[6,72,128]{2,1,0:T(8,128)S(1)}, f32[72,1...) custom-call(f32[24,72,128]{2,1,0:T(8,128)S(1)} %get-tuple-element.93.refs_0_, ...), custom_call_target="tpu_custom_call" | custom-call | tf_op jit(solution)/shard_map/mid1/pallas_call | solution.py:787
  28.1 4.4 %collective-permute-start.7 = (f32[80,128]{1,0:T(8,128)S(1)}, f32[80,128]{1,0:T(8,128)S(1)}, u32[]{:S(2)}, u32[]{:S(2)}) collective-permute-start(f32[80,128]{1,0:T(8,128)S(1)} %get-tuple-element.115), channel_id=1, source_target_pairs={{0,15},{1,2},{2,1},{3,4},{4,3},{5,6},{6,5},{7,8},{8,7},{9,10},{10,... | collective-permute-start | bytes 122888 | tf_op jit(solution)/shard_map/ppermute | solution.py:740
  32.5 2.7 %collective-permute-done.7.refs_8_ = f32[80,128]{1,0:T(8,128)S(1)} collective-permute-done((f32[80,128]{1,0:T(8,128)S(1)}, f32[80,128]{1,0:T(8,128)S(1)}, u32[]{:S(2)}, u32[]{:S(2)}) %collective-permute-start.7) | collective-permute-done | bytes 40992 | tf_op jit(solution)/shard_map/ppermute | solution.py:740
  35.2 2.0 %pre1.1 = (f32[6,72,128]{2,1,0:T(8,128)S(1)}, f32[80,128]{1,0:T(8,128)S(1)}, f32[80,128]{1,0:T(8,128)S(1)}, f32[8,224,128]{2,1,0:T(8,128)S(1)}) custom-call(f32[6,72,128]{2,1,0:T(8,128)S(1)} %get-tuple-element.109.refs_0_, f32[6,72,128]{2,1,0:T(8,128)S(1)} %get-tuple-element.105.refs_12_.refs_7_.refs_1_, f32[72,216]{1,0:T(8,128)S(1)} %get-tuple-element.108.refs_6_.refs_2_, ...), custom_call_target="tpu_custom_call" | custom-call | tf_op jit(solution)/shard_map/pre1/pallas_call | solution.py:787
  37.3 15.5 %all_to_all.5.refs_0_ = f32[8,224,128]{2,1,0:T(8,128)S(1)} all-to-all(f32[8,224,128]{2,1,0:T(8,128)S(1)} %get-tuple-element.121), channel_id=1, replica_groups=mesh['gx'=8,'gy'=16] {'gx'}, dimensions={0} | all-to-all | bytes 1835008 | tf_op jit(solution)/shard_map/all_to_all | solution.py:1062
  54.0 4.5 %collective-permute-start.9 = (f32[80,256]{1,0:T(8,128)S(1)}, f32[80,256]{1,0:T(8,128)S(1)}, u32[]{:S(2)}, u32[]{:S(2)}) collective-permute-start(f32[80,256]{1,0:T(8,128)S(1)} %get-tuple-element.127), channel_id=1, source_target_pairs={{0,31},{1,2},{2,1},{3,4},{4,3},{5,6},{6,5},{7,24},{8,23},{9,10},{1... | collective-permute-start | bytes 245768 | tf_op jit(solution)/shard_map/ppermute | solution.py:740
  59.7 1.7 %collective-permute-done.9.refs_6_ = f32[80,256]{1,0:T(8,128)S(1)} collective-permute-done((f32[80,256]{1,0:T(8,128)S(1)}, f32[80,256]{1,0:T(8,128)S(1)}, u32[]{:S(2)}, u32[]{:S(2)}) %collective-permute-start.9) | collective-permute-done | bytes 81952 | tf_op jit(solution)/shard_map/ppermute | solution.py:740
  61.4 2.5 %pre2.1 = (f32[6,72,256]{2,1,0:T(8,128)S(1)}, f32[3,72,128]{2,1,0:T(8,128)S(1)}, f32[80,128]{1,0:T(8,128)S(1)}, f32[80,128]{1,0:T(8,128)S(1)}) custom-call(f32[6,72,256]{2,1,0:T(8,128)S(1)} %get-tuple-element.122.refs_0_, f32[6,72,256]{2,1,0:T(8,128)S(1)} %get-tuple-element.123.refs_1_.refs_0_, f32[72,216]{1,0:T(8,128)S(1)} %get-tuple-element.124.refs_2_, ...), custom_call_target="tpu_custom_call" | custom-call | tf_op jit(solution)/shard_map/pre2/pallas_call | solution.py:787
  64.0 4.3 %collective-permute-start.11 = (f32[80,128]{1,0:T(8,128)S(1)}, f32[80,128]{1,0:T(8,128)S(1)}, u32[]{:S(2)}, u32[]{:S(2)}) collective-permute-start(f32[80,128]{1,0:T(8,128)S(1)} %get-tuple-element.139), channel_id=1, source_target_pairs={{0,31},{1,2},{2,1},{3,4},{4,3},{5,6},{6,5},{7,24},{8,23},{9,10},{1... | collective-permute-start | bytes 122888 | tf_op jit(solution)/shard_map/ppermute | solution.py:740
  68.3 2.6 %collective-permute-start.15 = (f32[80,128]{1,0:T(8,128)S(1)}, f32[80,128]{1,0:T(8,128)S(1)}, u32[]{:S(2)}, u32[]{:S(2)}) collective-permute-start(f32[80,128]{1,0:T(8,128)S(1)} %get-tuple-element.149), channel_id=1, source_target_pairs={{0,112},{1,113},{2,114},{3,115},{4,116},{5,117},{6,118},{7,119},{8... | collective-permute-start | bytes 122888 | tf_op jit(solution)/shard_map/ppermute | solution.py:740
  72.9 3.6 %collective-permute-start.13 = (f32[72,128]{1,0:T(8,128)S(1)}, f32[72,128]{1,0:T(8,128)S(1)}, u32[]{:S(2)}, u32[]{:S(2)}) collective-permute-start(f32[72,128]{1,0:T(8,128)S(1)} %get-tuple-element.144), channel_id=1, source_target_pairs={{0,31},{1,2},{2,1},{3,4},{4,3},{5,6},{6,5},{7,24},{8,23},{9,10},{1... | collective-permute-start | bytes 110600 | tf_op jit(solution)/shard_map/ppermute | solution.py:740
  77.5 2.1 %collective-permute-done.13.refs_3_ = f32[72,128]{1,0:T(8,128)S(1)} collective-permute-done((f32[72,128]{1,0:T(8,128)S(1)}, f32[72,128]{1,0:T(8,128)S(1)}, u32[]{:S(2)}, u32[]{:S(2)}) %collective-permute-start.13) | collective-permute-done | bytes 36896 | tf_op jit(solution)/shard_map/ppermute | solution.py:740
  80.6 3.6 %collective-permute-start.17 = (f32[72,256]{1,0:T(8,128)S(1)}, f32[72,256]{1,0:T(8,128)S(1)}, u32[]{:S(2)}, u32[]{:S(2)}) collective-permute-start(f32[72,256]{1,0:T(8,128)S(1)} %get-tuple-element.155), channel_id=1, source_target_pairs={{0,31},{1,2},{2,1},{3,4},{4,3},{5,6},{6,5},{7,24},{8,23},{9,10},{1... | collective-permute-start | bytes 221192 | tf_op jit(solution)/shard_map/ppermute | solution.py:740
  84.1 1.7 %again2.1 = (f32[6,72,256]{2,1,0:T(8,128)}, f32[6,72,256]{2,1,0:T(8,128)S(1)}, f32[72,256]{1,0:T(8,128)S(1)}, f32[72,256]{1,0:T(8,128)S(1)}, f32[72,128]{1,0:T(8,128)S(1)}, /*index=5*/f32[72,128]{1,0:T(8,128)S(1)}) custom-call(f32[6,72,256]{2,1,0:T(8,128)S(1)} %get-tuple-element.122.refs_0_, f32[6,72,256]{2,1,0:T(8,128)S(1)} %get-tuple-element.123.refs_1_.refs_0_, ...), custom_call_target="tpu_custom_call" | custom-call | tf_op jit(solution)/shard_map/again2/pallas_call | solution.py:787
  85.8 1.9 %collective-permute-done.17.refs_11_ = f32[72,256]{1,0:T(8,128)S(1)} collective-permute-done((f32[72,256]{1,0:T(8,128)S(1)}, f32[72,256]{1,0:T(8,128)S(1)}, u32[]{:S(2)}, u32[]{:S(2)}) %collective-permute-start.17) | collective-permute-done | bytes 73760 | tf_op jit(solution)/shard_map/ppermute | solution.py:740
  87.7 2.8 %post2.1 = (f32[6,72,256]{2,1,0:T(8,128)S(1)}, f32[72,128]{1,0:T(8,128)S(1)}, f32[72,128]{1,0:T(8,128)S(1)}) custom-call(f32[6,72,256]{2,1,0:T(8,128)S(1)} %get-tuple-element.122.refs_0_, f32[6,72,256]{2,1,0:T(8,128)S(1)} %get-tuple-element.123.refs_1_.refs_0_, f32[72,216]{1,0:T(8,128)S(1)} %get-tuple-element.124.refs_2_, f32[72,128]{1,0:T(8,128)S(1)} %copy-done, ...), custom_call_target="tpu_custom_call" | custom-call | tf_op jit(solution)/shard_map/post2/pallas_call | solution.py:787
  92.0 6.0 %collective-permute-done.19.refs_15_ = f32[72,128]{1,0:T(8,128)S(1)} collective-permute-done((f32[72,128]{1,0:T(8,128)S(1)}, f32[72,128]{1,0:T(8,128)S(1)}, u32[]{:S(2)}, u32[]{:S(2)}) %collective-permute-start.19) | collective-permute-done | bytes 36896 | tf_op jit(solution)/shard_map/ppermute | solution.py:740
  98.0 1.8 %post1.1 = (f32[6,72,128]{2,1,0:T(8,128)S(1)}, f32[152,128]{1,0:T(8,128)S(1)}, f32[152,128]{1,0:T(8,128)S(1)}) custom-call(f32[6,72,128]{2,1,0:T(8,128)S(1)} %get-tuple-element.109.refs_0_, f32[6,72,128]{2,1,0:T(8,128)S(1)} %get-tuple-element.105.refs_12_.refs_7_.refs_1_, f32[72,216]{1,0:T(8,128)S(1)} %get-tuple-element.108.refs_6_.refs_2_, ...), custom_call_target="tpu_custom_call" | custom-call | tf_op jit(solution)/shard_map/post1/pallas_call | solution.py:787
  99.8 1.8 %collective-permute-start.21 = (f32[152,128]{1,0:T(8,128)S(1)}, f32[152,128]{1,0:T(8,128)S(1)}, u32[]{:S(2)}, u32[]{:S(2)}) collective-permute-start(f32[152,128]{1,0:T(8,128)S(1)} %get-tuple-element.172), channel_id=1, source_target_pairs={{0,112},{1,113},{2,114},{3,115},{4,116},{5,117},{6,118},{7,119},{8... | collective-permute-start | bytes 233480 | tf_op jit(solution)/shard_map/ppermute | solution.py:740
  101.7 1.9 %again0.1 = (f32[24,72,128]{2,1,0:T(8,128)S(1)}, f32[24,72,128]{2,1,0:T(8,128)S(1)}, f32[72,128]{1,0:T(8,128)S(1)}, f32[72,128]{1,0:T(8,128)S(1)}, f32[72,128]{1,0:T(8,128)S(1)}) custom-call(f32[24,72,128]{2,1,0:T(8,128)S(1)} %get-tuple-element.93.refs_0_, f32[24,72,128]{2,1,0:T(8,128)S(1)} %get-tuple-element.94.refs_1_, ...), custom_call_target="tpu_custom_call" | custom-call | tf_op jit(solution)/shard_map/again0/pallas_call | solution.py:787
  104.2 2.2 %collective-permute-done.21.refs_1_.refs_13_ = f32[152,128]{1,0:T(8,128)S(1)} collective-permute-done((f32[152,128]{1,0:T(8,128)S(1)}, f32[152,128]{1,0:T(8,128)S(1)}, u32[]{:S(2)}, u32[]{:S(2)}) %collective-permute-start.21) | collective-permute-done | bytes 77856 | tf_op jit(solution)/shard_map/ppermute | solution.py:740
  106.8 3.5 %collective-permute-start.23 = (f32[72,128]{1,0:T(8,128)S(1)}, f32[72,128]{1,0:T(8,128)S(1)}, u32[]{:S(2)}, u32[]{:S(2)}) collective-permute-start(f32[72,128]{1,0:T(8,128)S(1)} %get-tuple-element.176), channel_id=1, source_target_pairs={{0,15},{1,2},{2,1},{3,4},{4,3},{5,6},{6,5},{7,8},{8,7},{9,10},{10,... | collective-permute-start | bytes 110600 | tf_op jit(solution)/shard_map/ppermute | solution.py:740
  110.3 3.6 %collective-permute-done.23.refs_15_ = f32[72,128]{1,0:T(8,128)S(1)} collective-permute-done((f32[72,128]{1,0:T(8,128)S(1)}, f32[72,128]{1,0:T(8,128)S(1)}, u32[]{:S(2)}, u32[]{:S(2)}) %collective-permute-start.23) | collective-permute-done | bytes 36896 | tf_op jit(solution)/shard_map/ppermute | solution.py:740
  113.8 3.1 %post0.1 = f32[1680,128]{1,0:T(8,128)} custom-call(f32[24,72,128]{2,1,0:T(8,128)S(1)} %get-tuple-element.93.refs_0_, f32[24,72,128]{2,1,0:T(8,128)S(1)} %get-tuple-element.94.refs_1_, f32[72,216]{1,0:T(8,128)S(1)} %get-tuple-element.95.refs_2_, f32[72,128]{1,0:T(8,128)S(1)} %copy-done, f32[8,128]{1,0:T(8,128)S(1)} %copy-done.3, ...), custom_call_target="tpu_custom_call" | custom-call | tf_op jit(solution)/shard_map/post0/pallas_call | solution.py:787
  (49 shorter events, 12.2 us)
Async XLA Ops:
  0.0 7.4 %copy-start.1 = (f32[70,24,128]{2,1,0:T(8,128)S(1)}, f32[70,24,128]{2,1,0:T(8,128)}, u32[]{:S(2)}) copy-start(f32[70,24,128]{2,1,0:T(8,128)} %refs_0_.1) | copy-start | bytes 2580484
  0.0 7.4 %copy-start.2 = (f32[70,24,128]{2,1,0:T(8,128)S(1)}, f32[70,24,128]{2,1,0:T(8,128)}, u32[]{:S(2)}) copy-start(f32[70,24,128]{2,1,0:T(8,128)} %refs_1_.1) | copy-start | bytes 2580484
  2.0 8.6 %collective-permute-start = (f32[224,128]{1,0:T(8,128)}, f32[224,128]{1,0:T(8,128)S(1)}, u32[]{:S(2)}, u32[]{:S(2)}) collective-permute-start(f32[224,128]{1,0:T(8,128)} %get-tuple-element.96), channel_id=1, source_target_pairs={{0,16},{1,17},{2,18},{3,19},{4,20},{5,21},{6,22},{7,23},{8,24},{9,... | collective-permute-start | bytes 344072 | tf_op jit(solution)/shard_map/ppermute | solution.py:739
  3.8 7.1 %collective-permute-start.1 = (f32[224,128]{1,0:T(8,128)}, f32[224,128]{1,0:T(8,128)S(1)}, u32[]{:S(2)}, u32[]{:S(2)}) collective-permute-start(f32[224,128]{1,0:T(8,128)} %get-tuple-element.97), channel_id=1, source_target_pairs={{0,112},{1,113},{2,114},{3,115},{4,116},{5,117},{6,118},{7,119},{8... | collective-permute-start | bytes 344072 | tf_op jit(solution)/shard_map/ppermute | solution.py:740
  6.4 1.0 copy-start
  7.3 0.7 copy-start.3
  11.1 6.7 %collective-permute-start.2 = (f32[80,128]{1,0:T(8,128)S(1)}, f32[80,128]{1,0:T(8,128)S(1)}, u32[]{:S(2)}, u32[]{:S(2)}) collective-permute-start(f32[80,128]{1,0:T(8,128)S(1)} %get-tuple-element.100), channel_id=1, source_target_pairs={{0,1},{1,0},{2,3},{3,2},{4,5},{5,4},{6,7},{7,6},{8,9},{9,8},{10,11... | collective-permute-start | bytes 122888 | tf_op jit(solution)/shard_map/ppermute | solution.py:739
  11.2 8.3 %collective-permute-start.3 = (f32[80,128]{1,0:T(8,128)S(1)}, f32[80,128]{1,0:T(8,128)S(1)}, u32[]{:S(2)}, u32[]{:S(2)}) collective-permute-start(f32[80,128]{1,0:T(8,128)S(1)} %get-tuple-element.101), channel_id=1, source_target_pairs={{0,15},{1,2},{2,1},{3,4},{4,3},{5,6},{6,5},{7,8},{8,7},{9,10},{10,... | collective-permute-start | bytes 122888 | tf_op jit(solution)/shard_map/ppermute | solution.py:740
  21.1 5.7 %collective-permute-start.4 = (f32[152,128]{1,0:T(8,128)S(1)}, f32[152,128]{1,0:T(8,128)S(1)}, u32[]{:S(2)}, u32[]{:S(2)}) collective-permute-start(f32[152,128]{1,0:T(8,128)S(1)} %get-tuple-element.110), channel_id=1, source_target_pairs={{0,16},{1,17},{2,18},{3,19},{4,20},{5,21},{6,22},{7,23},{8,24},{9,... | collective-permute-start | bytes 233480 | tf_op jit(solution)/shard_map/ppermute | solution.py:739
  21.2 6.6 %collective-permute-start.5 = (f32[152,128]{1,0:T(8,128)S(1)}, f32[152,128]{1,0:T(8,128)S(1)}, u32[]{:S(2)}, u32[]{:S(2)}) collective-permute-start(f32[152,128]{1,0:T(8,128)S(1)} %get-tuple-element.111), channel_id=1, source_target_pairs={{0,112},{1,113},{2,114},{3,115},{4,116},{5,117},{6,118},{7,119},{8... | collective-permute-start | bytes 233480 | tf_op jit(solution)/shard_map/ppermute | solution.py:740
  28.0 4.5 %collective-permute-start.6 = (f32[80,128]{1,0:T(8,128)S(1)}, f32[80,128]{1,0:T(8,128)S(1)}, u32[]{:S(2)}, u32[]{:S(2)}) collective-permute-start(f32[80,128]{1,0:T(8,128)S(1)} %get-tuple-element.114), channel_id=1, source_target_pairs={{0,1},{1,0},{2,3},{3,2},{4,5},{5,4},{6,7},{7,6},{8,9},{9,8},{10,11... | collective-permute-start | bytes 122888 | tf_op jit(solution)/shard_map/ppermute | solution.py:739
  28.1 7.1 %collective-permute-start.7 = (f32[80,128]{1,0:T(8,128)S(1)}, f32[80,128]{1,0:T(8,128)S(1)}, u32[]{:S(2)}, u32[]{:S(2)}) collective-permute-start(f32[80,128]{1,0:T(8,128)S(1)} %get-tuple-element.115), channel_id=1, source_target_pairs={{0,15},{1,2},{2,1},{3,4},{4,3},{5,6},{6,5},{7,8},{8,7},{9,10},{10,... | collective-permute-start | bytes 122888 | tf_op jit(solution)/shard_map/ppermute | solution.py:740
  53.9 5.8 %collective-permute-start.8 = (f32[80,256]{1,0:T(8,128)S(1)}, f32[80,256]{1,0:T(8,128)S(1)}, u32[]{:S(2)}, u32[]{:S(2)}) collective-permute-start(f32[80,256]{1,0:T(8,128)S(1)} %get-tuple-element.126), channel_id=1, source_target_pairs={{0,1},{1,0},{2,3},{3,2},{4,5},{5,4},{6,7},{7,6},{8,9},{9,8},{10,11... | collective-permute-start | bytes 245768 | tf_op jit(solution)/shard_map/ppermute | solution.py:739
  54.0 7.4 %collective-permute-start.9 = (f32[80,256]{1,0:T(8,128)S(1)}, f32[80,256]{1,0:T(8,128)S(1)}, u32[]{:S(2)}, u32[]{:S(2)}) collective-permute-start(f32[80,256]{1,0:T(8,128)S(1)} %get-tuple-element.127), channel_id=1, source_target_pairs={{0,31},{1,2},{2,1},{3,4},{4,3},{5,6},{6,5},{7,24},{8,23},{9,10},{1... | collective-permute-start | bytes 245768 | tf_op jit(solution)/shard_map/ppermute | solution.py:740
  63.9 7.6 %collective-permute-start.10 = (f32[80,128]{1,0:T(8,128)S(1)}, f32[80,128]{1,0:T(8,128)S(1)}, u32[]{:S(2)}, u32[]{:S(2)}) collective-permute-start(f32[80,128]{1,0:T(8,128)S(1)} %get-tuple-element.138), channel_id=1, source_target_pairs={{0,1},{1,0},{2,3},{3,2},{4,5},{5,4},{6,7},{7,6},{8,9},{9,8},{10,11... | collective-permute-start | bytes 122888 | tf_op jit(solution)/shard_map/ppermute | solution.py:739
  64.0 7.5 %collective-permute-start.11 = (f32[80,128]{1,0:T(8,128)S(1)}, f32[80,128]{1,0:T(8,128)S(1)}, u32[]{:S(2)}, u32[]{:S(2)}) collective-permute-start(f32[80,128]{1,0:T(8,128)S(1)} %get-tuple-element.139), channel_id=1, source_target_pairs={{0,31},{1,2},{2,1},{3,4},{4,3},{5,6},{6,5},{7,24},{8,23},{9,10},{1... | collective-permute-start | bytes 122888 | tf_op jit(solution)/shard_map/ppermute | solution.py:740
  68.3 9.2 %collective-permute-start.14 = (f32[80,128]{1,0:T(8,128)S(1)}, f32[80,128]{1,0:T(8,128)S(1)}, u32[]{:S(2)}, u32[]{:S(2)}) collective-permute-start(f32[80,128]{1,0:T(8,128)S(1)} %get-tuple-element.148), channel_id=1, source_target_pairs={{0,16},{1,17},{2,18},{3,19},{4,20},{5,21},{6,22},{7,23},{8,24},{9,... | collective-permute-start | bytes 122888 | tf_op jit(solution)/shard_map/ppermute | solution.py:739
  68.3 9.2 %collective-permute-start.15 = (f32[80,128]{1,0:T(8,128)S(1)}, f32[80,128]{1,0:T(8,128)S(1)}, u32[]{:S(2)}, u32[]{:S(2)}) collective-permute-start(f32[80,128]{1,0:T(8,128)S(1)} %get-tuple-element.149), channel_id=1, source_target_pairs={{0,112},{1,113},{2,114},{3,115},{4,116},{5,117},{6,118},{7,119},{8... | collective-permute-start | bytes 122888 | tf_op jit(solution)/shard_map/ppermute | solution.py:740
  72.8 4.8 %collective-permute-start.12 = (f32[72,128]{1,0:T(8,128)S(1)}, f32[72,128]{1,0:T(8,128)S(1)}, u32[]{:S(2)}, u32[]{:S(2)}) collective-permute-start(f32[72,128]{1,0:T(8,128)S(1)} %get-tuple-element.143), channel_id=1, source_target_pairs={{0,1},{1,0},{2,3},{3,2},{4,5},{5,4},{6,7},{7,6},{8,9},{9,8},{10,11... | collective-permute-start | bytes 110600 | tf_op jit(solution)/shard_map/ppermute | solution.py:739
  72.9 6.8 %collective-permute-start.13 = (f32[72,128]{1,0:T(8,128)S(1)}, f32[72,128]{1,0:T(8,128)S(1)}, u32[]{:S(2)}, u32[]{:S(2)}) collective-permute-start(f32[72,128]{1,0:T(8,128)S(1)} %get-tuple-element.144), channel_id=1, source_target_pairs={{0,31},{1,2},{2,1},{3,4},{4,3},{5,6},{6,5},{7,24},{8,23},{9,10},{1... | collective-permute-start | bytes 110600 | tf_op jit(solution)/shard_map/ppermute | solution.py:740
  80.5 5.3 %collective-permute-start.16 = (f32[72,256]{1,0:T(8,128)S(1)}, f32[72,256]{1,0:T(8,128)S(1)}, u32[]{:S(2)}, u32[]{:S(2)}) collective-permute-start(f32[72,256]{1,0:T(8,128)S(1)} %get-tuple-element.154), channel_id=1, source_target_pairs={{0,1},{1,0},{2,3},{3,2},{4,5},{5,4},{6,7},{7,6},{8,9},{9,8},{10,11... | collective-permute-start | bytes 221192 | tf_op jit(solution)/shard_map/ppermute | solution.py:739
  80.6 7.2 %collective-permute-start.17 = (f32[72,256]{1,0:T(8,128)S(1)}, f32[72,256]{1,0:T(8,128)S(1)}, u32[]{:S(2)}, u32[]{:S(2)}) collective-permute-start(f32[72,256]{1,0:T(8,128)S(1)} %get-tuple-element.155), channel_id=1, source_target_pairs={{0,31},{1,2},{2,1},{3,4},{4,3},{5,6},{6,5},{7,24},{8,23},{9,10},{1... | collective-permute-start | bytes 221192 | tf_op jit(solution)/shard_map/ppermute | solution.py:740
  90.6 1.4 %collective-permute-start.18 = (f32[72,128]{1,0:T(8,128)S(1)}, f32[72,128]{1,0:T(8,128)S(1)}, u32[]{:S(2)}, u32[]{:S(2)}) collective-permute-start(f32[72,128]{1,0:T(8,128)S(1)} %get-tuple-element.164), channel_id=1, source_target_pairs={{0,1},{1,0},{2,3},{3,2},{4,5},{5,4},{6,7},{7,6},{8,9},{9,8},{10,11... | collective-permute-start | bytes 110600 | tf_op jit(solution)/shard_map/ppermute | solution.py:739
  90.7 7.3 %collective-permute-start.19 = (f32[72,128]{1,0:T(8,128)S(1)}, f32[72,128]{1,0:T(8,128)S(1)}, u32[]{:S(2)}, u32[]{:S(2)}) collective-permute-start(f32[72,128]{1,0:T(8,128)S(1)} %get-tuple-element.165), channel_id=1, source_target_pairs={{0,15},{1,2},{2,1},{3,4},{4,3},{5,6},{6,5},{7,8},{8,7},{9,10},{10,... | collective-permute-start | bytes 110600 | tf_op jit(solution)/shard_map/ppermute | solution.py:740
  99.8 4.5 %collective-permute-start.20 = (f32[152,128]{1,0:T(8,128)S(1)}, f32[152,128]{1,0:T(8,128)S(1)}, u32[]{:S(2)}, u32[]{:S(2)}) collective-permute-start(f32[152,128]{1,0:T(8,128)S(1)} %get-tuple-element.171), channel_id=1, source_target_pairs={{0,16},{1,17},{2,18},{3,19},{4,20},{5,21},{6,22},{7,23},{8,24},{9,... | collective-permute-start | bytes 233480 | tf_op jit(solution)/shard_map/ppermute | solution.py:739
  99.8 6.6 %collective-permute-start.21 = (f32[152,128]{1,0:T(8,128)S(1)}, f32[152,128]{1,0:T(8,128)S(1)}, u32[]{:S(2)}, u32[]{:S(2)}) collective-permute-start(f32[152,128]{1,0:T(8,128)S(1)} %get-tuple-element.172), channel_id=1, source_target_pairs={{0,112},{1,113},{2,114},{3,115},{4,116},{5,117},{6,118},{7,119},{8... | collective-permute-start | bytes 233480 | tf_op jit(solution)/shard_map/ppermute | solution.py:740
  106.7 3.6 %collective-permute-start.22 = (f32[72,128]{1,0:T(8,128)S(1)}, f32[72,128]{1,0:T(8,128)S(1)}, u32[]{:S(2)}, u32[]{:S(2)}) collective-permute-start(f32[72,128]{1,0:T(8,128)S(1)} %get-tuple-element.175), channel_id=1, source_target_pairs={{0,1},{1,0},{2,3},{3,2},{4,5},{5,4},{6,7},{7,6},{8,9},{9,8},{10,11... | collective-permute-start | bytes 110600 | tf_op jit(solution)/shard_map/ppermute | solution.py:739
  106.8 7.1 %collective-permute-start.23 = (f32[72,128]{1,0:T(8,128)S(1)}, f32[72,128]{1,0:T(8,128)S(1)}, u32[]{:S(2)}, u32[]{:S(2)}) collective-permute-start(f32[72,128]{1,0:T(8,128)S(1)} %get-tuple-element.176), channel_id=1, source_target_pairs={{0,15},{1,2},{2,1},{3,4},{4,3},{5,6},{6,5},{7,8},{8,7},{9,10},{10,... | collective-permute-start | bytes 110600 | tf_op jit(solution)/shard_map/ppermute | solution.py:740

commit v4 on v3

--- a/solution.py
+++ b/solution.py
@@ -532,6 +532,23 @@
         store(m, part[m] + jnp.where(lt == 0, low, jnp.where(lt == ty - 1, high, 0.0)))
 
 
+def strip_side_terms(strip, winv, co, flags, c_columns, sides, sides_next):
+    m_rows, ty, width = strip
+    lt = in_tile(strip)
+    d = block_dot(winv, jnp.concatenate(sides, axis=1) * 0.0625)
+    first, last = d[:, :width], d[:, width:]
+    turned = [jnp.broadcast_to(flags[k : k + 1, :], (Z, width)) > 0.5 for k in range(2)]
+    step = ty - m_rows + 1
+    r = []
+    for mine, other, c, beyond in ((first, last, c_columns[0], sides_next[0]), (last, first, c_columns[1], sides_next[1])):
+        low = jnp.where(turned[0], roll(other, step), roll(mine, step))
+        high = jnp.where(turned[1], roll(other, -step), roll(mine, -step))
+        low = jnp.where(lt == 0, low, roll(mine, 1))
+        high = jnp.where(lt == m_rows - 1, high, roll(mine, -1))
+        r.append(residual(co, beyond * 0.0625, c, mine, low + high))
+    return first, last, r
+
+
 def strip_restrict(v, out):
     a, b = iota2(LANES, LANES)
     for m in range(3):
@@ -574,50 +591,109 @@
     )
 
 
-def pre_strip_kernel(f, c, w, vz, flags, dn, un, part, first, last, fl_next, c_up, c_down, v_out, f_next, up, down, res):
-    strip = STRIPS[2]
-    width = strip[2]
+def column_restrict(strip, x):
+    a, b = iota2(LANES, LANES)
+    out = None
+    for h in range(2):
+        inside = (b // 16 == 4 * h + a // 32) & ((a % 32) // 2 == b % 16) & (a % 32 < strip[0])
+        term = lane_dot(x[:, h * LANES : (h + 1) * LANES], jnp.where(inside, 0.25, 0.0))
+        out = term if out is None else out + term
+    return out
+
+
+def pre_strip_kernel(
+    w, vz, flags, dn, un, first_column, last_column, c_low, c_high, f_part, fl_next, base_up, base_down, terms, f_next, up, down
+):
+    strip, small = STRIPS[2], STRIPS[3]
     winv = w[...].astype(BF16)
-    co = Coef(vz, width)
+    co = Coef(vz, strip[2])
     raws = [dn[0:Z, :], un[0:Z, :]]
-    values = [block_dot(winv, x) for x in raws]
-    edges = strip_edges(strip, winv, co, strip_sides(values, raws, dn, un, first, last))
-    strip_add_sides(strip, winv, part, strip_frame(strip, flags, *values), Setter(v_out))
-    ends = strip_ends(strip, v_out, flags)
-    sides = strip_frame(strip, flags, *edges)
-    for m in range(6):
-        res[m] = strip_residual(strip, co, v_out, f, c, ends, sides, m)
-    strip_restrict(res, f_next)
-    small = STRIPS[3]
-    strip_message(small, f_next, None, strip_ends(small, f_next, fl_next), up, down)
-    up[0:Z, :] = up[0:Z, :] + c_up[...]
-    down[0:Z, :] = down[0:Z, :] + c_down[...]
-    up[Z : Z + 8, :] = fl_next[...]
-    down[Z : Z + 8, :] = fl_next[...]
-
-
-def next_coef_kernel(c, flags, c_next, fl_next, up, down):
+    values = block_dot(winv, jnp.concatenate(raws, axis=1))
+    values = [values[:, : strip[2]], values[:, strip[2] :]]
+    edges = strip_edges(strip, winv, co, strip_sides(values, raws, dn, un, first_column, last_column))
+    first, last, r = strip_side_terms(
+        strip, winv, co, flags, (c_low[...], c_high[...]), strip_frame(strip, flags, *values), strip_frame(strip, flags, *edges)
+    )
+    terms[0] = first
+    terms[1] = last
+    low = column_restrict(strip, r[0] + first * 0.0625)
+    high = column_restrict(strip, r[1] + last * 0.0625)
+    m_rows, ty, width = small
+    lt = in_tile(small)
+    for m in range(m_rows):
+        x = jnp.where(lt == 0, roll(low, -m), 0.0)
+        f_next[m] = f_part[m] + jnp.where(lt == ty - 1, roll(high, ty - 1 - m), x)
+    turned = [jnp.broadcast_to(fl_next[k : k + 1, :], (Z, width)) > 0.5 for k in range(2)]
+    for ref, base, mine, other in ((up, base_up, high, low), (down, base_down, low, high)):
+        before, after = 3 * m_rows + ty - m_rows + 1, 3 * m_rows + 1 - ty
+        end_low = jnp.where(turned[0], roll(other, before), roll(mine, before))
+        end_high = jnp.where(turned[1], roll(other, after), roll(mine, after))
+        add = jnp.where(lt < m_rows, mine, 0.0)
+        add = jnp.where(lt == 3 * m_rows, end_low, add)
+        add = jnp.where(lt == 3 * m_rows + 1, end_high, add)
+        ref[0:Z, :] = base[...] + add
+        ref[Z : Z + 8, :] = fl_next[...]
+
+
+def next_coef_kernel(c, flags, c_next, fl_next, low, high, low_next, high_next):
     strip_restrict(c, c_next)
     a, b = iota2(LANES, LANES)
     fl_next[...] = lane_dot(flags[:, :LANES], jnp.where((b < 64) & (a == (b // 16) * 32), 1.0, 0.0)) + lane_dot(
         flags[:, LANES:], jnp.where((b >= 64) & (a == (b // 16 - 4) * 32), 1.0, 0.0)
     )
-    small = STRIPS[3]
-    zero = jnp.zeros((Z, LANES), F32)
-    up[...] = strip_column(small, c_next, small[1] - 1, 2 * small[0], zero)
-    down[...] = strip_column(small, c_next, 0, 2 * small[0], zero)
-
-
-def bottom_strip_kernel(f, c, w, vz, flags, dn, un, part, first, last, v_out, up, down, one):
+    for strip, ref, first, last in ((STRIPS[2], c, low, high), (STRIPS[3], c_next, low_next, high_next)):
+        zero = jnp.zeros((Z, strip[2]), F32)
+        first[...] = strip_column(strip, ref, 0, 0, zero)
+        last[...] = strip_column(strip, ref, strip[1] - 1, 0, zero)
+
+
+def alone2_kernel(f, c, w, vz, flags, c_next, fl_next, part, low, high, f_part, up, down, v, res):
+    strip, small = STRIPS[2], STRIPS[3]
+    winv = w[...].astype(BF16)
+    co = Coef(vz, strip[2])
+    for m in range(6):
+        v[m] = block_dot(winv, f[m])
+    zero = jnp.zeros((Z, strip[2]), F32)
+    low[...] = strip_column(strip, v, 0, 0, zero)
+    high[...] = strip_column(strip, v, strip[1] - 1, 0, zero)
+    strip_relax(strip, winv, co, v, f, c, flags, None, Setter(part))
+    ends = strip_ends(strip, part, flags)
+    for m in range(6):
+        res[m] = strip_residual(strip, co, part, f, c, ends, None, m)
+    strip_restrict(res, f_part)
+    strip_message(small, f_part, c_next, strip_ends(small, f_part, fl_next), up, down)
+
+
+def bottom_strip_kernel(
+    w, vz, flags, dn, un, first_column, last_column, c_low, c_high, part_low, part_high, terms, up, down
+):
     strip = STRIPS[3]
+    width = strip[2]
     winv = w[...].astype(BF16)
     co = Coef(vz)
     raws = [dn[0:Z, :], un[0:Z, :]]
-    values = [block_dot(winv, x) for x in raws]
-    edges = strip_edges(strip, winv, co, strip_sides(values, raws, dn, un, first, last))
-    strip_add_sides(strip, winv, part, strip_frame(strip, flags, *values), Setter(one))
-    strip_relax(strip, winv, co, one, f, c, flags, strip_frame(strip, flags, *edges), Setter(v_out))
-    strip_message(strip, v_out, None, (), up, down)
+    values = block_dot(winv, jnp.concatenate(raws, axis=1))
+    values = [values[:, :width], values[:, width:]]
+    edges = strip_edges(strip, winv, co, strip_sides(values, raws, dn, un, first_column, last_column))
+    first, last, r = strip_side_terms(
+        strip, winv, co, flags, (c_low[...], c_high[...]), strip_frame(strip, flags, *values), strip_frame(strip, flags, *edges)
+    )
+    d = block_dot(winv, jnp.concatenate([r[0], first * 0.0625, last * 0.0625, r[1]], axis=1))
+    d = [d[:, k * width : (k + 1) * width] for k in range(4)]
+    d[0] = first + d[0]
+    d[3] = last + d[3]
+    for k in range(4):
+        terms[k] = d[k]
+    up[...] = part_high[...] + d[3]
+    down[...] = part_low[...] + d[0]
+
+
+def with_columns(strip, x, terms, m):
+    ty = strip[1]
+    lt = in_tile(strip)
+    for k, y in enumerate((0, 1, ty - 2, ty - 1)):
+        x = x + jnp.where(lt == y, roll(terms[k], y - m), 0.0)
+    return x
 
 
 def last_strip_kernel(w, flags, dn, un, part, base_up, base_down, _lo, _hi, e, up, down, small_up, small_down):
@@ -635,83 +711,106 @@
         down[:, half] = base_down[:, half] + lane_dot(small_down[...], spread)
 
 
-def base_message_kernel(v, flags, up, down):
-    strip_message(STRIPS[2], v, None, strip_ends(STRIPS[2], v, flags), up, down)
-
-
-def again2_kernel(f, c, w, vz, flags, v, e, tile_v, g, part, low, high, yup, ydown):
+def base_message_kernel(part, flags, terms, v, up, down):
+    strip = STRIPS[2]
+    lt = in_tile(strip)
+    for m in range(6):
+        x = jnp.where(lt == 0, roll(terms[0], -m), 0.0)
+        v[m] = part[m] + jnp.where(lt == strip[1] - 1, roll(terms[1], strip[1] - 1 - m), x)
+    strip_message(strip, v, None, strip_ends(strip, v, flags), up, down)
+
+
+def again2_kernel(f, c, w, vz, flags, v, e, tile_v, low, high, part_low, part_high, yup, ydown, twice, g, part):
     strip = STRIPS[2]
     a, b = iota2(LANES, LANES)
     for m in range(3):
         add = jnp.concatenate([lane_dot(e[m], jnp.where(a == 64 * h + b // 2, 1.0, 0.0)) for h in range(2)], axis=1)
         g[2 * m] = v[2 * m] + add
         g[2 * m + 1] = v[2 * m + 1] + add
-    strip_relax(strip, w[...].astype(BF16), Coef(vz, strip[2]), g, f, c, flags, None, Setter(part))
     zero = jnp.zeros((Z, strip[2]), F32)
     low[...] = strip_column(strip, g, 0, 0, zero)
     high[...] = strip_column(strip, g, strip[1] - 1, 0, zero)
+    winv = w[...].astype(BF16)
+    co = Coef(vz, strip[2])
+    strip_relax(strip, winv, co, g, f, c, flags, None, Setter(part))
+    strip_relax(strip, winv, co, part, f, c, flags, None, Setter(twice))
+    part_low[...] = strip_column(strip, twice, 0, 0, zero)
+    part_high[...] = strip_column(strip, twice, strip[1] - 1, 0, zero)
     put_y(GEOM[1], tile_v, None, yup, ydown)
 
 
-def alone_kernel(level):
-    strip = STRIPS[level]
-
-    def kernel(f, c, w, vz, flags, part, low, high, v):
-        winv = w[...].astype(BF16)
-        for m in range(strip[0]):
-            v[m] = block_dot(winv, f[m])
-        strip_relax(strip, winv, Coef(vz, strip[2]), v, f, c, flags, None, Setter(part))
-        zero = jnp.zeros((Z, strip[2]), F32)
-        low[...] = strip_column(strip, v, 0, 0, zero)
-        high[...] = strip_column(strip, v, strip[1] - 1, 0, zero)
-
-    return kernel
-
-
-def again3_kernel(f, c, w, vz, flags, v, part):
-    strip_relax(STRIPS[3], w[...].astype(BF16), Coef(vz), v, f, c, flags, None, Setter(part))
-
-
-def tile_row(e, m, step):
+def alone3_kernel(f, c, w, vz, flags, low, high, part_low, part_high, twice, v, part):
+    strip = STRIPS[3]
+    winv = w[...].astype(BF16)
+    co = Coef(vz)
+    for m in range(3):
+        v[m] = block_dot(winv, f[m])
+    strip_relax(strip, winv, co, v, f, c, flags, None, Setter(part))
+    strip_relax(strip, winv, co, part, f, c, flags, None, Setter(twice))
+    zero = jnp.zeros((Z, LANES), F32)
+    for ref, first, last in ((v, low, high), (twice, part_low, part_high)):
+        first[...] = strip_column(strip, ref, 0, 0, zero)
+        last[...] = strip_column(strip, ref, strip[1] - 1, 0, zero)
+
+
+def again3_kernel(f, c, w, vz, flags, twice, terms, part, v):
+    strip = STRIPS[3]
+    for m in range(3):
+        v[m] = with_columns(strip, twice[m], terms, m)
+    strip_relax(strip, w[...].astype(BF16), Coef(vz), v, f, c, flags, None, Setter(part))
+
+
+def tile_lanes(x, step):
     t = lax.rem(lax.axis_index("gx") + (step + 8), 8)
-    half = jnp.where(t < 4, e[m, :, :LANES], e[m, :, LANES:])
+    half = jnp.where(t < 4, x[:, :LANES], x[:, LANES:])
     return pltpu.roll(half, lax.rem(8 - t, 4) * 32, axis=1)
 
 
 def post_strip_kernel(
-    f, c, w, vz, flags, dn, un, part, first_column, last_column, gdn, gun, xlo, xhi, own, yup, ydown, e, up, down, one
+    w, vz, flags, dn, un, first_column, last_column, c_low, c_high, part_low, part_high, gdn, gun, xlo, xhi, own, yup, ydown, terms, up, down
 ):
     strip = STRIPS[2]
     fine = GEOM[1]
+    width = strip[2]
     winv = w[...].astype(BF16)
-    co = Coef(vz, strip[2])
+    co = Coef(vz, width)
     raws = [dn[0:Z, :], un[0:Z, :]]
     values = [gdn[...], gun[...]]
     edges = strip_edges(strip, winv, co, strip_sides(values, raws, dn, un, first_column, last_column))
-    strip_add_sides(strip, winv, part, strip_frame(strip, flags, *values), Setter(one))
-    strip_relax(strip, winv, co, one, f, c, flags, strip_frame(strip, flags, *edges), Setter(e))
+    first, last, r = strip_side_terms(
+        strip, winv, co, flags, (c_low[...], c_high[...]), strip_frame(strip, flags, *values), strip_frame(strip, flags, *edges)
+    )
+    d = block_dot(winv, jnp.concatenate([r[0], first * 0.0625, last * 0.0625, r[1]], axis=1))
+    d = [d[:, k * width : (k + 1) * width] for k in range(4)]
+    d[0] = first + d[0]
+    d[3] = last + d[3]
+    for k in range(4):
+        terms[k] = d[k]
+    low, high = part_low[...] + d[0], part_high[...] + d[3]
     extras = []
     for ref, step in ((xlo, -1), (xhi, 1)):
-        first, last = tile_row(e, 0, step), tile_row(e, 5, step)
-        adds = (col(first, 0), col(first, 31), col(last, 0), col(last, 31))
+        near, far = tile_lanes(low, step), tile_lanes(high, step)
+        adds = (col(near, 0), col(far, 0), col(near, 5), col(far, 5))
         extras.append([x + y for x, y in zip(corner_columns(tail_of(fine, ref, 2)), adds)])
     group = zl() // 4
+    near, far = tile_lanes(low, 0), tile_lanes(high, 0)
     add_up = add_down = jnp.zeros((Z, LANES), F32)
     for m in range(6):
-        row = tile_row(e, m, 0)
-        add_up = jnp.where(group == m, col(row, 31), add_up)
-        add_down = jnp.where(group == m, col(row, 0), add_down)
+        add_up = jnp.where(group == m, col(far, m), add_up)
+        add_down = jnp.where(group == m, col(near, m), add_down)
     up[...], down[...] = merge_y(*extras, own, yup[...] + add_up, ydown[...] + add_down)
 
 
-def again1_kernel(f, c, w, vz, v, e, xlo, xhi, g, part, columns, lo_out, hi_out, tile):
+def again1_kernel(f, c, w, vz, v, twice, terms, xlo, xhi, g, part, columns, lo_out, hi_out, tile):
     fine, geom = GEOM[1], GEOM[2]
+    rows = []
     for m in range(6):
-        tile[m] = tile_row(e, m, 0)
+        rows.append(with_columns(STRIPS[2], twice[m], terms, m))
+        tile[m] = tile_lanes(rows[m], 0)
     prolong_add(fine, geom, tile, v, g)
     a, b = iota2(LANES, LANES)
     spread = jnp.where((b < 64) & (a == b // 2), 1.0, 0.0)
-    for ref, out, row in ((xlo, lo_out, tile_row(e, 5, -1)), (xhi, hi_out, tile_row(e, 0, 1))):
+    for ref, out, row in ((xlo, lo_out, tile_lanes(rows[5], -1)), (xhi, hi_out, tile_lanes(rows[0], 1))):
         add = lane_dot(row, spread)
         out[...] = pack(fine, [part_of(fine, ref, 0) + add, part_of(fine, ref, 1) + add])[0]
     columns[...] = own_columns(fine, g)
@@ -957,36 +1056,73 @@
         chunks[t, 3 * Z : 3 * Z + 8, :] = own[...]
 
 
-def again0_kernel(f, c, w, vz, e, v, g, part, columns, yup, ydown):
+def again0_kernel(f, c, w, vz, e, v, g, part, columns, c_columns, yup, ydown):
     prolong_add(GEOM[0], GEOM[1], e, v, g)
     put_y(GEOM[0], g, None, yup, ydown)
     columns[...] = own_columns(GEOM[0], g)
+    c_columns[...] = own_columns(GEOM[0], c)
     relax_tile(GEOM[0], w[...].astype(BF16), Coef(vz), g, f, c, ALONE, Setter(part))
 
 
-def post_sweeps(geom, f, c, w, vz, own, xlo, xhi, ydn, yun, g, part, columns, glo, ghi, gdn, gun, one, store):
-    winv = w[...].astype(BF16)
-    co = Coef(vz)
+def twice0_kernel(f, c, w, vz, part, _after, twice):
+    relax_tile(GEOM[0], w[...].astype(BF16), Coef(vz), part, f, c, ALONE, Setter(twice))
+
+
+def post_edges(geom, f, c, w, vz, own, xlo, xhi, ydn, yun, g, columns, glo, ghi, gdn, gun):
     fl = flags_of(geom, own, xlo, xhi, ydn, yun)
     halo = Halo(
         part_of(geom, glo, 0), part_of(geom, glo, 1), part_of(geom, ghi, 0), part_of(geom, ghi, 1), gdn[...], gun[...]
     )
-    relaxed = relax_edges(geom, winv, co, g, columns[...], halo, fl, *own_data(geom, xlo, xhi, ydn, yun))
-    add_edges(geom, winv, part, frame(geom, fl, halo.lo, halo.hi, halo.sides()), Setter(one))
-    relax_tile(geom, winv, co, one, f, c, frame(geom, fl, *relaxed), store)
-
-
-def post0_kernel(f, c, w, vz, own, xlo, xhi, ydn, yun, g, part, columns, glo, ghi, gdn, gun, out, one):
-    def store(x, value):
-        out[pl.ds(x, NZ, stride=24), :] = value[0:NZ, :]
-
-    post_sweeps(GEOM[0], f, c, w, vz, own, xlo, xhi, ydn, yun, g, part, columns, glo, ghi, gdn, gun, one, store)
+    winv = w[...].astype(BF16)
+    relaxed = relax_edges(geom, winv, Coef(vz), g, columns[...], halo, fl, *own_data(geom, xlo, xhi, ydn, yun))
+    return frame(geom, fl, halo.lo, halo.hi, halo.sides()), frame(geom, fl, *relaxed)
+
+
+def post0_kernel(f, c, w, vz, own, xlo, xhi, ydn, yun, g, columns, c_columns, twice, glo, ghi, gdn, gun, out):
+    geom = GEOM[0]
+    rows = geom[0]
+    winv = w[...].astype(BF16)
+    co = Coef(vz)
+    lane = zl()
+    edges, edges_next = post_edges(geom, f, c, w, vz, own, xlo, xhi, ydn, yun, g, columns, glo, ghi, gdn, gun)
+    low, high, sides = edge_terms(geom, winv, edges)
+
+    def row_residual(v, c_row, beyond):
+        beside = jnp.where(lane == 0, 0.0, roll(v, 1)) + jnp.where(lane == LANES - 1, 0.0, roll(v, -1))
+        return residual(co, beyond * 0.0625, c_row, v, beside)
+
+    beside = jnp.where(lane < 2, 0.0, roll(sides, 2)) + jnp.where(lane >= 2 * rows - 2, 0.0, roll(sides, -2))
+    r = [
+        row_residual(low, c[0], edges_next[0]),
+        low * 0.0625,
+        high * 0.0625,
+        row_residual(high, c[rows - 1], edges_next[1]),
+        residual(co, edges_next[2] * 0.0625, c_columns[...], sides, beside),
+        sides * 0.0625,
+    ]
+    d = block_dot(winv, jnp.concatenate(r, axis=1))
+    d = [d[:, k * LANES : (k + 1) * LANES] for k in range(6)]
+    a, b = iota2(LANES, LANES)
+    outer = jnp.where((b % 4 == 1) | (b % 4 == 2), 1.0, 0.0) * jnp.where(a == 2 * (b // 4) + b % 4 - 1, 1.0, 0.0)
+    inner = jnp.where((b % 4 == 0) | (b % 4 == 3), 1.0, 0.0) * jnp.where(a == 2 * (b // 4) + b % 4 // 3, 1.0, 0.0)
+    four = lane_dot(sides + d[4], outer) + lane_dot(d[5], inner)
+    inside = (lane < 2) | (lane >= LANES - 2)
+    row_terms = {0: low + d[0], 1: d[1], rows - 2: d[2], rows - 1: high + d[3]}
+    for m in range(rows):
+        x = twice[m] + jnp.where(inside, roll(four, -4 * m - 2), 0.0)
+        if m in row_terms:
+            x = x + row_terms[m]
+        out[pl.ds(m, NZ, stride=24), :] = x[0:NZ, :]
 
 
 def post1_kernel(
     f, c, w, vz, own, xlo, xhi, ydn, yun, g, part, columns, glo, ghi, gdn, gun, fine_v, e, up, down, one, fine_g
 ):
-    post_sweeps(GEOM[1], f, c, w, vz, own, xlo, xhi, ydn, yun, g, part, columns, glo, ghi, gdn, gun, one, Setter(e))
+    geom = GEOM[1]
+    edges, edges_next = post_edges(geom, f, c, w, vz, own, xlo, xhi, ydn, yun, g, columns, glo, ghi, gdn, gun)
+    winv = w[...].astype(BF16)
+    add_edges(geom, winv, part, edges, Setter(one))
+    relax_tile(geom, winv, Coef(vz), one, f, c, edges_next, Setter(e))
     prolong_add(GEOM[0], GEOM[1], e, fine_v, fine_g, (0, 22))
     put_x(GEOM[0], fine_g, None, up, down)
 
@@ -1067,25 +1203,31 @@
         open_strip_kernel, [s2, s2, (8, 256), full2, full2], [chunks], name="open2", send=((3, "gy"),)
     )
     side2 = swap(up, down, "gy", True)
-    alone = call(alone_kernel(2), [s2, m2, m2], [f2, c2, w[2], vz, fl2], [s2], name="alone2")
-    c3, fl3, c_up, c_down = call(next_coef_kernel, [s3, (8, 128), m3, m3], [c2, fl2], name="coef3")
-    v2, f3, up, down = call(
+    c3, fl3, *c_sides = call(next_coef_kernel, [s3, (8, 128), m2, m2, m3, m3], [c2, fl2], name="coef3")
+    part2, first, last, f_part, base_up, base_down = call(
+        alone2_kernel, [s2, m2, m2, s3, m3, m3], [f2, c2, w[2], vz, fl2, c3, fl3], [s2, s2], name="alone2"
+    )
+    terms2, f3, up, down = call(
         pre_strip_kernel,
-        [s2, s3, full3, full3],
-        [f2, c2, w[2], vz, fl2, *side2, *alone, fl3, c_up, c_down],
-        [s2],
+        [(2, *m2), s3, full3, full3],
+        [w[2], vz, fl2, *side2, first, last, *c_sides[:2], f_part, fl3, base_up, base_down],
         name="pre2",
-        got=((5, "gy"),),
+        got=((3, "gy"),),
         send=((2, "gy"),),
     )
     side3 = swap(up, down, "gy", True)
-    alone = call(alone_kernel(3), [s3, m3, m3], [f3, c3, w[3], vz, fl3], [s3], name="alone3")
-    v3, up, down = call(
-        bottom_strip_kernel, [s3, m3, m3], [f3, c3, w[3], vz, fl3, *side3, *alone], [s3], name="bottom", got=((5, "gy"),), send=((1, "gy"),)
+    *alone, twice = call(alone3_kernel, [m3] * 4 + [s3], [f3, c3, w[3], vz, fl3], [s3, s3], name="alone3")
+    terms, up, down = call(
+        bottom_strip_kernel,
+        [(4, *m3), m3, m3],
+        [w[3], vz, fl3, *side3, *alone[:2], *c_sides[2:], *alone[2:]],
+        name="bottom",
+        got=((3, "gy"),),
+        send=((1, "gy"),),
     )
     side = swap(up, down, "gy", True)
-    (part,) = call(again3_kernel, [s3], [f3, c3, w[3], vz, fl3, v3], name="again3")
-    base_up, base_down = call(base_message_kernel, [m2, m2], [v2, fl2], name="base2")
+    (part,) = call(again3_kernel, [s3], [f3, c3, w[3], vz, fl3, twice, terms], [s3], name="again3")
+    v2, base_up, base_down = call(base_message_kernel, [s2, m2, m2], [part2, fl2, terms2], name="base2")
     e3, up, down = call(
         last_strip_kernel,
         [s3, m2, m2],
@@ -1097,21 +1239,20 @@
         send=((1, "gy"),),
     )
     side = swap(up, down, "gy", True)
-    g2, *alone, yup, ydown = call(
-        again2_kernel, [s2, s2, m2, m2, ys, ys], [f2, c2, w[2], vz, fl2, v2, e3, v1], name="again2"
-    )
-    e2, up, down = call(
+    first, last, part_low, part_high, yup, ydown, twice = call(
+        again2_kernel, [m2] * 4 + [ys, ys, s2], [f2, c2, w[2], vz, fl2, v2, e3, v1], [s2, s2], name="again2"
+    )
+    terms, up, down = call(
         post_strip_kernel,
-        [s2, ys, ys],
-        [f2, c2, w[2], vz, fl2, *side2, *alone, *side, v1_lo, v1_hi, own, yup, ydown],
-        [s2],
+        [(4, *m2), ys, ys],
+        [w[2], vz, fl2, *side2, first, last, *c_sides[:2], part_low, part_high, *side, v1_lo, v1_hi, own, yup, ydown],
         name="post2",
-        got=((5, "gy"), (10, "gy"), (12, "gx")),
+        got=((3, "gy"), (11, "gy"), (13, "gx")),
         send=((1, "gy"),),
     )
     side = swap(up, down, "gy")
     g1, part, columns, lo, hi = call(
-        again1_kernel, [t1, t1, ys, ys, ys], [f1, c1, w[1], vz, v1, e2, v1_lo, v1_hi], [t2], name="again1", got=((6, "gx"),)
+        again1_kernel, [t1, t1, ys, ys, ys], [f1, c1, w[1], vz, v1, twice, terms, v1_lo, v1_hi], [t2], name="again1", got=((7, "gx"),)
     )
     xs = x_shape(0, 2)
     e1, up, down = call(
@@ -1124,13 +1265,20 @@
         send=((1, "gx"),),
     )
     xlo, xhi = swap(up, down, "gx")
-    g0, part, columns, yup, ydown = call(
-        again0_kernel, [t0, t0, ys, ys, ys], [f, c, w[0], vz, e1, v0], name="again0"
-    )
-    got = (xlo, xhi, *to_sides(0, 2, xlo, xhi, yup, ydown))
+    g0, part, columns, c_columns, yup, ydown = call(
+        again0_kernel, [t0, t0, ys, ys, ys, ys], [f, c, w[0], vz, e1, v0], name="again0"
+    )
+    up, down = call(
+        merge_kernel(0, 2), [ys, ys], [xlo, xhi, own, yup, ydown], name="merge0", got=((0, "gx"),), send=((0, "gy"),)
+    )
+    side = swap(up, down, "gy")
+    (twice,) = call(twice0_kernel, [t0], [f, c, w[0], vz, part, up], name="twice0", after=1)
     (out,) = call(
-        post0_kernel, [(NZ * 24, LANES)], [f, c, w[0], vz, own, *got0, g0, part, columns, *got], [t0], name="post0",
-        got=((5, "gx"), (7, "gy"), (12, "gx"), (14, "gy")),
+        post0_kernel,
+        [(NZ * 24, LANES)],
+        [f, c, w[0], vz, own, *got0, g0, columns, c_columns, twice, xlo, xhi, *side],
+        name="post0",
+        got=((5, "gx"), (7, "gy"), (13, "gx"), (15, "gy")),
     )
     return out.reshape(NZ, 24, LANES)
 

time: 117 us -> 114 us (0.974)
  waiting for transfers between devices: 23.8 us -> 21 us
  starting transfers between devices: 43.8 us -> 42.2 us
  Pallas kernels: 31.9 us -> 33.3 us
    ppermute x12, waiting for transfers between devices: 23.1 us -> 20.6 us  [swap(): lax.ppermute(second, both, swap_pairs(axis, 1, nearest))]
    ppermute x12, starting transfers between devices: 41.2 us -> 39.7 us  [swap(): lax.ppermute(second, both, swap_pairs(axis, 1, nearest))]
    pallas_call x22 -> x23, Pallas kernels: 29.9 us -> 31.3 us  [call(): pl.pallas_call(by_swaps(kernel, len(args), len(outs), got, send), out_sha...]
  transfers between devices with their start and end apart: 24 -> 24, of which waited for: 11 -> 11; matrix products, arithmetic and copies ran while one was open for 1% -> 1% of each run, Pallas kernels for 12% -> 16%
where the time goes in v4:
time: 114 us
  starting transfers between devices  42.2 us (37%)
  Pallas kernels  33.3 us (29%)
  waiting for transfers between devices  21 us (18%)
  blocking collectives  15.5 us (14%)
  local copies, waits for them, and re-layouts  1.57 us (1%)
    ppermute x12, starting transfers between devices, swap(): lax.ppermute(second, both, swap_pairs(axis, 1, nearest))  39.7 us
    pallas_call x23, Pallas kernels, call(): pl.pallas_call(by_swaps(kernel, len(args), len(outs), got, send), out_sha...  31.3 us
    ppermute x12, waiting for transfers between devices, swap(): lax.ppermute(second, both, swap_pairs(axis, 1, nearest))  20.6 us
    all_to_all x1, blocking collectives, on_device(): chunks = lax.all_to_all(chunks, 'gx', 0, 0)  15.5 us
    ppermute x12, starting transfers between devices, swap(): lax.ppermute(first, both, swap_pairs(axis, 0, nearest))  2.52 us
  transfers between devices with their start and end apart: 24, of which 11 were waited for; matrix products, arithmetic and copies ran while one was open for 1% of the time, Pallas kernels for 16%

profile of v4, /device:TPU:0, one launch (start us, length us, event | category | flops | bytes accessed | tf_op | source)
XLA Modules:
  0.0 114.0 jit_solution(2940166324649040862)
XLA Ops:
  0.0 2.0 %open.1 = (f32[224,128]{1,0:T(8,128)}, f32[224,128]{1,0:T(8,128)}, f32[8,128]{1,0:T(8,128)}, f32[72,128]{1,0:T(8,128)}) custom-call(f32[70,24,128]{2,1,0:T(8,128)} %refs_0_.1, f32[70,24,128]{2,1,0:T(8,128)} %refs_1_.1, f32[1,71]{1,0:T(1,128)} %bitcast.9, s32[1,4]{1,0:T(1,128)} %bitcast.10), custom_call_target="tpu_custom_call" | custom-call | tf_op jit(solution)/shard_map/open/pallas_call | solution.py:1140
  2.0 1.7 %collective-permute-start = (f32[224,128]{1,0:T(8,128)}, f32[224,128]{1,0:T(8,128)S(1)}, u32[]{:S(2)}, u32[]{:S(2)}) collective-permute-start(f32[224,128]{1,0:T(8,128)} %get-tuple-element.107), channel_id=1, source_target_pairs={{0,16},{1,17},{2,18},{3,19},{4,20},{5,21},{6,22},{7,23},{8,24},{9,... | collective-permute-start | bytes 344072 | tf_op jit(solution)/shard_map/ppermute | solution.py:838
  3.8 2.6 %collective-permute-start.1 = (f32[224,128]{1,0:T(8,128)}, f32[224,128]{1,0:T(8,128)S(1)}, u32[]{:S(2)}, u32[]{:S(2)}) collective-permute-start(f32[224,128]{1,0:T(8,128)} %get-tuple-element.108), channel_id=1, source_target_pairs={{0,112},{1,113},{2,114},{3,115},{4,116},{5,117},{6,118},{7,119},{8... | collective-permute-start | bytes 344072 | tf_op jit(solution)/shard_map/ppermute | solution.py:839
  8.0 2.6 %side.1 = (f32[24,72,128]{2,1,0:T(8,128)S(1)}, f32[24,72,128]{2,1,0:T(8,128)S(1)}, f32[72,216]{1,0:T(8,128)S(1)}, f32[72,216]{1,0:T(8,128)S(1)}, f32[72,216]{1,0...) custom-call(f32[1680,128]{1,0:T(8,128)S(1)} %bitcast.6, ...), custom_call_target="tpu_custom_call" | custom-call | tf_op jit(solution)/shard_map/side/pallas_call | solution.py:886
  11.2 6.5 %collective-permute-start.3 = (f32[80,128]{1,0:T(8,128)S(1)}, f32[80,128]{1,0:T(8,128)S(1)}, u32[]{:S(2)}, u32[]{:S(2)}) collective-permute-start(f32[80,128]{1,0:T(8,128)S(1)} %get-tuple-element.112), channel_id=1, source_target_pairs={{0,15},{1,2},{2,1},{3,4},{4,3},{5,6},{6,5},{7,8},{8,7},{9,10},{10,... | collective-permute-start | bytes 122888 | tf_op jit(solution)/shard_map/ppermute | solution.py:839
  17.8 1.7 %collective-permute-done.3.refs_8_ = f32[80,128]{1,0:T(8,128)S(1)} collective-permute-done((f32[80,128]{1,0:T(8,128)S(1)}, f32[80,128]{1,0:T(8,128)S(1)}, u32[]{:S(2)}, u32[]{:S(2)}) %collective-permute-start.3) | collective-permute-done | bytes 40992 | tf_op jit(solution)/shard_map/ppermute | solution.py:839
  19.4 1.6 %pre0.1 = (f32[152,128]{1,0:T(8,128)S(1)}, f32[152,128]{1,0:T(8,128)S(1)}, f32[3,72,128]{2,1,0:T(8,128)S(1)}, f32[3,72,128]{2,1,0:T(8,128)S(1)}) custom-call(f32[24,72,128]{2,1,0:T(8,128)S(1)} %get-tuple-element.104.refs_0_, f32[24,72,128]{2,1,0:T(8,128)S(1)} %get-tuple-element.105.refs_1_, f32[72,216]{1,0:T(8,128)S(1)} %get-tuple-element.106.refs_2_, ...), custom_call_target="tpu_custom_call" | custom-call | tf_op jit(solution)/shard_map/pre0/pallas_call | solution.py:886
  21.2 3.4 %collective-permute-start.5 = (f32[152,128]{1,0:T(8,128)S(1)}, f32[152,128]{1,0:T(8,128)S(1)}, u32[]{:S(2)}, u32[]{:S(2)}) collective-permute-start(f32[152,128]{1,0:T(8,128)S(1)} %get-tuple-element.122), channel_id=1, source_target_pairs={{0,112},{1,113},{2,114},{3,115},{4,116},{5,117},{6,118},{7,119},{8... | collective-permute-start | bytes 233480 | tf_op jit(solution)/shard_map/ppermute | solution.py:839
  24.6 2.1 %mid1.1 = (f32[24,72,128]{2,1,0:T(8,128)S(1)}, f32[6,72,128]{2,1,0:T(8,128)S(1)}, f32[6,72,128]{2,1,0:T(8,128)S(1)}, f32[6,72,128]{2,1,0:T(8,128)S(1)}, f32[72,1...) custom-call(f32[24,72,128]{2,1,0:T(8,128)S(1)} %get-tuple-element.104.refs_0_, ...), custom_call_target="tpu_custom_call" | custom-call | tf_op jit(solution)/shard_map/mid1/pallas_call | solution.py:886
  28.1 4.5 %collective-permute-start.7 = (f32[80,128]{1,0:T(8,128)S(1)}, f32[80,128]{1,0:T(8,128)S(1)}, u32[]{:S(2)}, u32[]{:S(2)}) collective-permute-start(f32[80,128]{1,0:T(8,128)S(1)} %get-tuple-element.126), channel_id=1, source_target_pairs={{0,15},{1,2},{2,1},{3,4},{4,3},{5,6},{6,5},{7,8},{8,7},{9,10},{10,... | collective-permute-start | bytes 122888 | tf_op jit(solution)/shard_map/ppermute | solution.py:839
  32.5 2.7 %collective-permute-done.7.refs_8_ = f32[80,128]{1,0:T(8,128)S(1)} collective-permute-done((f32[80,128]{1,0:T(8,128)S(1)}, f32[80,128]{1,0:T(8,128)S(1)}, u32[]{:S(2)}, u32[]{:S(2)}) %collective-permute-start.7) | collective-permute-done | bytes 40992 | tf_op jit(solution)/shard_map/ppermute | solution.py:839
  35.2 2.1 %pre1.1 = (f32[6,72,128]{2,1,0:T(8,128)S(1)}, f32[80,128]{1,0:T(8,128)S(1)}, f32[80,128]{1,0:T(8,128)S(1)}, f32[8,224,128]{2,1,0:T(8,128)S(1)}) custom-call(f32[6,72,128]{2,1,0:T(8,128)S(1)} %get-tuple-element.120.refs_0_, f32[6,72,128]{2,1,0:T(8,128)S(1)} %get-tuple-element.116.refs_12_.refs_7_.refs_1_, f32[72,216]{1,0:T(8,128)S(1)} %get-tuple-element.119.refs_6_.refs_2_, ...), custom_call_target="tpu_custom_call" | custom-call | tf_op jit(solution)/shard_map/pre1/pallas_call | solution.py:886
  37.3 15.5 %all_to_all.5.refs_0_ = f32[8,224,128]{2,1,0:T(8,128)S(1)} all-to-all(f32[8,224,128]{2,1,0:T(8,128)S(1)} %get-tuple-element.132), channel_id=1, replica_groups=mesh['gx'=8,'gy'=16] {'gx'}, dimensions={0} | all-to-all | bytes 1835008 | tf_op jit(solution)/shard_map/all_to_all | solution.py:1198
  54.0 4.5 %collective-permute-start.9 = (f32[80,256]{1,0:T(8,128)S(1)}, f32[80,256]{1,0:T(8,128)S(1)}, u32[]{:S(2)}, u32[]{:S(2)}) collective-permute-start(f32[80,256]{1,0:T(8,128)S(1)} %get-tuple-element.141), channel_id=1, source_target_pairs={{0,31},{1,2},{2,1},{3,4},{4,3},{5,6},{6,5},{7,24},{8,23},{9,10},{1... | collective-permute-start | bytes 245768 | tf_op jit(solution)/shard_map/ppermute | solution.py:839
  58.8 1.9 %alone2.1 = (f32[6,72,256]{2,1,0:T(8,128)S(1)}, f32[72,256]{1,0:T(8,128)S(1)}, f32[72,256]{1,0:T(8,128)S(1)}, f32[3,72,128]{2,1,0:T(8,128)S(1)}, f32[72,128]{1,0:T(8,128)S(1)}, /*index=5*/f32[72,128]{1,0:T(8,128)S(1)}) custom-call(f32[6,72,256]{2,1,0:T(8,128)S(1)} %get-tuple-element.133.refs_0_, f32[6,72,256]{2,1,0:T(8,128)S(1)} %get-tuple-element.134.refs_0_.refs_1_, ...), custom_call_target="tpu_custom_call" | custom-call | tf_op jit(solution)/shard_map/alone2/pallas_call | solution.py:886
  62.9 4.3 %collective-permute-start.11 = (f32[80,128]{1,0:T(8,128)S(1)}, f32[80,128]{1,0:T(8,128)S(1)}, u32[]{:S(2)}, u32[]{:S(2)}) collective-permute-start(f32[80,128]{1,0:T(8,128)S(1)} %get-tuple-element.153), channel_id=1, source_target_pairs={{0,31},{1,2},{2,1},{3,4},{4,3},{5,6},{6,5},{7,24},{8,23},{9,10},{1... | collective-permute-start | bytes 122888 | tf_op jit(solution)/shard_map/ppermute | solution.py:839
  67.2 2.6 %collective-permute-start.15 = (f32[80,128]{1,0:T(8,128)S(1)}, f32[80,128]{1,0:T(8,128)S(1)}, u32[]{:S(2)}, u32[]{:S(2)}) collective-permute-start(f32[80,128]{1,0:T(8,128)S(1)} %get-tuple-element.168), channel_id=1, source_target_pairs={{0,112},{1,113},{2,114},{3,115},{4,116},{5,117},{6,118},{7,119},{8... | collective-permute-start | bytes 122888 | tf_op jit(solution)/shard_map/ppermute | solution.py:839
  72.0 3.1 %collective-permute-start.13 = (f32[72,128]{1,0:T(8,128)S(1)}, f32[72,128]{1,0:T(8,128)S(1)}, u32[]{:S(2)}, u32[]{:S(2)}) collective-permute-start(f32[72,128]{1,0:T(8,128)S(1)} %get-tuple-element.162), channel_id=1, source_target_pairs={{0,31},{1,2},{2,1},{3,4},{4,3},{5,6},{6,5},{7,24},{8,23},{9,10},{1... | collective-permute-start | bytes 110600 | tf_op jit(solution)/shard_map/ppermute | solution.py:839
  76.6 2.2 %collective-permute-done.13.refs_3_ = f32[72,128]{1,0:T(8,128)S(1)} collective-permute-done((f32[72,128]{1,0:T(8,128)S(1)}, f32[72,128]{1,0:T(8,128)S(1)}, u32[]{:S(2)}, u32[]{:S(2)}) %collective-permute-start.13) | collective-permute-done | bytes 36896 | tf_op jit(solution)/shard_map/ppermute | solution.py:839
  79.7 3.1 %collective-permute-start.17 = (f32[72,256]{1,0:T(8,128)S(1)}, f32[72,256]{1,0:T(8,128)S(1)}, u32[]{:S(2)}, u32[]{:S(2)}) collective-permute-start(f32[72,256]{1,0:T(8,128)S(1)} %get-tuple-element.176), channel_id=1, source_target_pairs={{0,31},{1,2},{2,1},{3,4},{4,3},{5,6},{6,5},{7,24},{8,23},{9,10},{1... | collective-permute-start | bytes 221192 | tf_op jit(solution)/shard_map/ppermute | solution.py:839
  82.8 2.3 %again2.1 = (f32[72,256]{1,0:T(8,128)S(1)}, f32[72,256]{1,0:T(8,128)S(1)}, f32[72,256]{1,0:T(8,128)S(1)}, f32[72,256]{1,0:T(8,128)S(1)}, f32[72,128]{1,0:T(8,128...) custom-call(f32[6,72,256]{2,1,0:T(8,128)S(1)} %get-tuple-element.133.refs_0_, ...), custom_call_target="tpu_custom_call" | custom-call | tf_op jit(solution)/shard_map/again2/pallas_call | solution.py:886
  85.1 1.8 %collective-permute-done.17.refs_12_ = f32[72,256]{1,0:T(8,128)S(1)} collective-permute-done((f32[72,256]{1,0:T(8,128)S(1)}, f32[72,256]{1,0:T(8,128)S(1)}, u32[]{:S(2)}, u32[]{:S(2)}) %collective-permute-start.17) | collective-permute-done | bytes 73760 | tf_op jit(solution)/shard_map/ppermute | solution.py:839
  86.9 1.5 %post2.1 = (f32[4,72,256]{2,1,0:T(8,128)S(1)}, f32[72,128]{1,0:T(8,128)S(1)}, f32[72,128]{1,0:T(8,128)S(1)}) custom-call(f32[72,216]{1,0:T(8,128)S(1)} %get-tuple-element.135.refs_2_.refs_0_, f32[72,128]{1,0:T(8,128)S(1)} %copy-done, f32[8,256]{1,0:T(8,128)S(1)} %get-tuple-element.136.refs_1_.refs_4_.refs_2_, f32[80,256]{1,0:T(8,128)S(1)} %collective-permute-done.8.refs_3_, ...), custom_call_target="tpu_custom_call" | custom-call | tf_op jit(solution)/shard_map/post2/pallas_call | solution.py:886
  88.8 1.8 %again1.1 = (f32[6,72,128]{2,1,0:T(8,128)S(1)}, f32[6,72,128]{2,1,0:T(8,128)S(1)}, f32[72,128]{1,0:T(8,128)S(1)}, f32[72,128]{1,0:T(8,128)S(1)}, f32[72,128]{1,0:T(8,128)S(1)}) custom-call(f32[6,72,128]{2,1,0:T(8,128)S(1)} %get-tuple-element.120.refs_0_, f32[6,72,128]{2,1,0:T(8,128)S(1)} %get-tuple-element.116.refs_12_.refs_7_.refs_1_, ...), custom_call_target="tpu_custom_call" | custom-call | tf_op jit(solution)/shard_map/again1/pallas_call | solution.py:886
  90.7 5.2 %collective-permute-done.19.refs_15_ = f32[72,128]{1,0:T(8,128)S(1)} collective-permute-done((f32[72,128]{1,0:T(8,128)S(1)}, f32[72,128]{1,0:T(8,128)S(1)}, u32[]{:S(2)}, u32[]{:S(2)}) %collective-permute-start.19) | collective-permute-done | bytes 36896 | tf_op jit(solution)/shard_map/ppermute | solution.py:839
  95.8 1.8 %post1.1 = (f32[6,72,128]{2,1,0:T(8,128)S(1)}, f32[152,128]{1,0:T(8,128)S(1)}, f32[152,128]{1,0:T(8,128)S(1)}) custom-call(f32[6,72,128]{2,1,0:T(8,128)S(1)} %get-tuple-element.120.refs_0_, f32[6,72,128]{2,1,0:T(8,128)S(1)} %get-tuple-element.116.refs_12_.refs_7_.refs_1_, f32[72,216]{1,0:T(8,128)S(1)} %get-tuple-element.119.refs_6_.refs_2_, ...), custom_call_target="tpu_custom_call" | custom-call | tf_op jit(solution)/shard_map/post1/pallas_call | solution.py:886
  97.6 1.7 %collective-permute-start.21 = (f32[152,128]{1,0:T(8,128)S(1)}, f32[152,128]{1,0:T(8,128)S(1)}, u32[]{:S(2)}, u32[]{:S(2)}) collective-permute-start(f32[152,128]{1,0:T(8,128)S(1)} %get-tuple-element.194), channel_id=1, source_target_pairs={{0,112},{1,113},{2,114},{3,115},{4,116},{5,117},{6,118},{7,119},{8... | collective-permute-start | bytes 233480 | tf_op jit(solution)/shard_map/ppermute | solution.py:839
  99.3 2.3 %again0.1 = (f32[24,72,128]{2,1,0:T(8,128)S(1)}, f32[24,72,128]{2,1,0:T(8,128)S(1)}, f32[72,128]{1,0:T(8,128)S(1)}, f32[72,128]{1,0:T(8,128)S(1)}, f32[72,128]{1,0:T(8,128)S(1)}, /*index=5*/f32[72,128]{1,0:T(8,128)S(1)}) custom-call(f32[24,72,128]{2,1,0:T(8,128)S(1)} %get-tuple-element.104.refs_0_, f32[24,72,128]{2,1,0:T(8,128)S(1)} %get-tuple-element.105.refs_1_, ...), custom_call_target="tpu_custom_call" | custom-call | tf_op jit(solution)/shard_map/again0/pallas_call | solution.py:886
  102.0 2.2 %collective-permute-done.21.refs_1_.refs_14_ = f32[152,128]{1,0:T(8,128)S(1)} collective-permute-done((f32[152,128]{1,0:T(8,128)S(1)}, f32[152,128]{1,0:T(8,128)S(1)}, u32[]{:S(2)}, u32[]{:S(2)}) %collective-permute-start.21) | collective-permute-done | bytes 77856 | tf_op jit(solution)/shard_map/ppermute | solution.py:839
  104.6 3.0 %collective-permute-start.23 = (f32[72,128]{1,0:T(8,128)S(1)}, f32[72,128]{1,0:T(8,128)S(1)}, u32[]{:S(2)}, u32[]{:S(2)}) collective-permute-start(f32[72,128]{1,0:T(8,128)S(1)} %get-tuple-element.198), channel_id=1, source_target_pairs={{0,15},{1,2},{2,1},{3,4},{4,3},{5,6},{6,5},{7,8},{8,7},{9,10},{10,... | collective-permute-start | bytes 110600 | tf_op jit(solution)/shard_map/ppermute | solution.py:839
  108.7 2.9 %collective-permute-done.23.refs_16_ = f32[72,128]{1,0:T(8,128)S(1)} collective-permute-done((f32[72,128]{1,0:T(8,128)S(1)}, f32[72,128]{1,0:T(8,128)S(1)}, u32[]{:S(2)}, u32[]{:S(2)}) %collective-permute-start.23) | collective-permute-done | bytes 36896 | tf_op jit(solution)/shard_map/ppermute | solution.py:839
  111.6 2.4 %post0.1 = f32[1680,128]{1,0:T(8,128)} custom-call(f32[24,72,128]{2,1,0:T(8,128)S(1)} %get-tuple-element.104.refs_0_, f32[24,72,128]{2,1,0:T(8,128)S(1)} %get-tuple-element.105.refs_1_, f32[72,216]{1,0:T(8,128)S(1)} %get-tuple-element.106.refs_2_, f32[72,128]{1,0:T(8,128)S(1)} %copy-done, f32[8,128]{1,0:T(8,128)S(1)} %copy-done.3, ...), custom_call_target="tpu_custom_call" | custom-call | tf_op jit(solution)/shard_map/post0/pallas_call | solution.py:886
  (50 shorter events, 14.1 us)
Async XLA Ops:
  0.0 7.4 %copy-start.1 = (f32[70,24,128]{2,1,0:T(8,128)S(1)}, f32[70,24,128]{2,1,0:T(8,128)}, u32[]{:S(2)}) copy-start(f32[70,24,128]{2,1,0:T(8,128)} %refs_0_.1) | copy-start | bytes 2580484
  0.0 7.4 %copy-start.2 = (f32[70,24,128]{2,1,0:T(8,128)S(1)}, f32[70,24,128]{2,1,0:T(8,128)}, u32[]{:S(2)}) copy-start(f32[70,24,128]{2,1,0:T(8,128)} %refs_1_.1) | copy-start | bytes 2580484
  2.0 8.6 %collective-permute-start = (f32[224,128]{1,0:T(8,128)}, f32[224,128]{1,0:T(8,128)S(1)}, u32[]{:S(2)}, u32[]{:S(2)}) collective-permute-start(f32[224,128]{1,0:T(8,128)} %get-tuple-element.107), channel_id=1, source_target_pairs={{0,16},{1,17},{2,18},{3,19},{4,20},{5,21},{6,22},{7,23},{8,24},{9,... | collective-permute-start | bytes 344072 | tf_op jit(solution)/shard_map/ppermute | solution.py:838
  3.8 7.1 %collective-permute-start.1 = (f32[224,128]{1,0:T(8,128)}, f32[224,128]{1,0:T(8,128)S(1)}, u32[]{:S(2)}, u32[]{:S(2)}) collective-permute-start(f32[224,128]{1,0:T(8,128)} %get-tuple-element.108), channel_id=1, source_target_pairs={{0,112},{1,113},{2,114},{3,115},{4,116},{5,117},{6,118},{7,119},{8... | collective-permute-start | bytes 344072 | tf_op jit(solution)/shard_map/ppermute | solution.py:839
  6.4 1.0 copy-start
  7.3 0.7 copy-start.3
  11.1 6.6 %collective-permute-start.2 = (f32[80,128]{1,0:T(8,128)S(1)}, f32[80,128]{1,0:T(8,128)S(1)}, u32[]{:S(2)}, u32[]{:S(2)}) collective-permute-start(f32[80,128]{1,0:T(8,128)S(1)} %get-tuple-element.111), channel_id=1, source_target_pairs={{0,1},{1,0},{2,3},{3,2},{4,5},{5,4},{6,7},{7,6},{8,9},{9,8},{10,11... | collective-permute-start | bytes 122888 | tf_op jit(solution)/shard_map/ppermute | solution.py:838
  11.2 8.2 %collective-permute-start.3 = (f32[80,128]{1,0:T(8,128)S(1)}, f32[80,128]{1,0:T(8,128)S(1)}, u32[]{:S(2)}, u32[]{:S(2)}) collective-permute-start(f32[80,128]{1,0:T(8,128)S(1)} %get-tuple-element.112), channel_id=1, source_target_pairs={{0,15},{1,2},{2,1},{3,4},{4,3},{5,6},{6,5},{7,8},{8,7},{9,10},{10,... | collective-permute-start | bytes 122888 | tf_op jit(solution)/shard_map/ppermute | solution.py:839
  21.1 5.7 %collective-permute-start.4 = (f32[152,128]{1,0:T(8,128)S(1)}, f32[152,128]{1,0:T(8,128)S(1)}, u32[]{:S(2)}, u32[]{:S(2)}) collective-permute-start(f32[152,128]{1,0:T(8,128)S(1)} %get-tuple-element.121), channel_id=1, source_target_pairs={{0,16},{1,17},{2,18},{3,19},{4,20},{5,21},{6,22},{7,23},{8,24},{9,... | collective-permute-start | bytes 233480 | tf_op jit(solution)/shard_map/ppermute | solution.py:838
  21.2 6.6 %collective-permute-start.5 = (f32[152,128]{1,0:T(8,128)S(1)}, f32[152,128]{1,0:T(8,128)S(1)}, u32[]{:S(2)}, u32[]{:S(2)}) collective-permute-start(f32[152,128]{1,0:T(8,128)S(1)} %get-tuple-element.122), channel_id=1, source_target_pairs={{0,112},{1,113},{2,114},{3,115},{4,116},{5,117},{6,118},{7,119},{8... | collective-permute-start | bytes 233480 | tf_op jit(solution)/shard_map/ppermute | solution.py:839
  28.0 4.6 %collective-permute-start.6 = (f32[80,128]{1,0:T(8,128)S(1)}, f32[80,128]{1,0:T(8,128)S(1)}, u32[]{:S(2)}, u32[]{:S(2)}) collective-permute-start(f32[80,128]{1,0:T(8,128)S(1)} %get-tuple-element.125), channel_id=1, source_target_pairs={{0,1},{1,0},{2,3},{3,2},{4,5},{5,4},{6,7},{7,6},{8,9},{9,8},{10,11... | collective-permute-start | bytes 122888 | tf_op jit(solution)/shard_map/ppermute | solution.py:838
  28.1 7.1 %collective-permute-start.7 = (f32[80,128]{1,0:T(8,128)S(1)}, f32[80,128]{1,0:T(8,128)S(1)}, u32[]{:S(2)}, u32[]{:S(2)}) collective-permute-start(f32[80,128]{1,0:T(8,128)S(1)} %get-tuple-element.126), channel_id=1, source_target_pairs={{0,15},{1,2},{2,1},{3,4},{4,3},{5,6},{6,5},{7,8},{8,7},{9,10},{10,... | collective-permute-start | bytes 122888 | tf_op jit(solution)/shard_map/ppermute | solution.py:839
  53.9 6.8 %collective-permute-start.8 = (f32[80,256]{1,0:T(8,128)S(1)}, f32[80,256]{1,0:T(8,128)S(1)}, u32[]{:S(2)}, u32[]{:S(2)}) collective-permute-start(f32[80,256]{1,0:T(8,128)S(1)} %get-tuple-element.140), channel_id=1, source_target_pairs={{0,1},{1,0},{2,3},{3,2},{4,5},{5,4},{6,7},{7,6},{8,9},{9,8},{10,11... | collective-permute-start | bytes 245768 | tf_op jit(solution)/shard_map/ppermute | solution.py:838
  54.0 7.4 %collective-permute-start.9 = (f32[80,256]{1,0:T(8,128)S(1)}, f32[80,256]{1,0:T(8,128)S(1)}, u32[]{:S(2)}, u32[]{:S(2)}) collective-permute-start(f32[80,256]{1,0:T(8,128)S(1)} %get-tuple-element.141), channel_id=1, source_target_pairs={{0,31},{1,2},{2,1},{3,4},{4,3},{5,6},{6,5},{7,24},{8,23},{9,10},{1... | collective-permute-start | bytes 245768 | tf_op jit(solution)/shard_map/ppermute | solution.py:839
  62.8 8.1 %collective-permute-start.10 = (f32[80,128]{1,0:T(8,128)S(1)}, f32[80,128]{1,0:T(8,128)S(1)}, u32[]{:S(2)}, u32[]{:S(2)}) collective-permute-start(f32[80,128]{1,0:T(8,128)S(1)} %get-tuple-element.152), channel_id=1, source_target_pairs={{0,1},{1,0},{2,3},{3,2},{4,5},{5,4},{6,7},{7,6},{8,9},{9,8},{10,11... | collective-permute-start | bytes 122888 | tf_op jit(solution)/shard_map/ppermute | solution.py:838
  62.9 8.0 %collective-permute-start.11 = (f32[80,128]{1,0:T(8,128)S(1)}, f32[80,128]{1,0:T(8,128)S(1)}, u32[]{:S(2)}, u32[]{:S(2)}) collective-permute-start(f32[80,128]{1,0:T(8,128)S(1)} %get-tuple-element.153), channel_id=1, source_target_pairs={{0,31},{1,2},{2,1},{3,4},{4,3},{5,6},{6,5},{7,24},{8,23},{9,10},{1... | collective-permute-start | bytes 122888 | tf_op jit(solution)/shard_map/ppermute | solution.py:839
  67.2 9.4 %collective-permute-start.14 = (f32[80,128]{1,0:T(8,128)S(1)}, f32[80,128]{1,0:T(8,128)S(1)}, u32[]{:S(2)}, u32[]{:S(2)}) collective-permute-start(f32[80,128]{1,0:T(8,128)S(1)} %get-tuple-element.167), channel_id=1, source_target_pairs={{0,16},{1,17},{2,18},{3,19},{4,20},{5,21},{6,22},{7,23},{8,24},{9,... | collective-permute-start | bytes 122888 | tf_op jit(solution)/shard_map/ppermute | solution.py:838
  67.2 9.4 %collective-permute-start.15 = (f32[80,128]{1,0:T(8,128)S(1)}, f32[80,128]{1,0:T(8,128)S(1)}, u32[]{:S(2)}, u32[]{:S(2)}) collective-permute-start(f32[80,128]{1,0:T(8,128)S(1)} %get-tuple-element.168), channel_id=1, source_target_pairs={{0,112},{1,113},{2,114},{3,115},{4,116},{5,117},{6,118},{7,119},{8... | collective-permute-start | bytes 122888 | tf_op jit(solution)/shard_map/ppermute | solution.py:839
  71.9 4.7 %collective-permute-start.12 = (f32[72,128]{1,0:T(8,128)S(1)}, f32[72,128]{1,0:T(8,128)S(1)}, u32[]{:S(2)}, u32[]{:S(2)}) collective-permute-start(f32[72,128]{1,0:T(8,128)S(1)} %get-tuple-element.161), channel_id=1, source_target_pairs={{0,1},{1,0},{2,3},{3,2},{4,5},{5,4},{6,7},{7,6},{8,9},{9,8},{10,11... | collective-permute-start | bytes 110600 | tf_op jit(solution)/shard_map/ppermute | solution.py:838
  72.0 6.8 %collective-permute-start.13 = (f32[72,128]{1,0:T(8,128)S(1)}, f32[72,128]{1,0:T(8,128)S(1)}, u32[]{:S(2)}, u32[]{:S(2)}) collective-permute-start(f32[72,128]{1,0:T(8,128)S(1)} %get-tuple-element.162), channel_id=1, source_target_pairs={{0,31},{1,2},{2,1},{3,4},{4,3},{5,6},{6,5},{7,24},{8,23},{9,10},{1... | collective-permute-start | bytes 110600 | tf_op jit(solution)/shard_map/ppermute | solution.py:839
  79.6 5.5 %collective-permute-start.16 = (f32[72,256]{1,0:T(8,128)S(1)}, f32[72,256]{1,0:T(8,128)S(1)}, u32[]{:S(2)}, u32[]{:S(2)}) collective-permute-start(f32[72,256]{1,0:T(8,128)S(1)} %get-tuple-element.175), channel_id=1, source_target_pairs={{0,1},{1,0},{2,3},{3,2},{4,5},{5,4},{6,7},{7,6},{8,9},{9,8},{10,11... | collective-permute-start | bytes 221192 | tf_op jit(solution)/shard_map/ppermute | solution.py:838
  79.7 7.2 %collective-permute-start.17 = (f32[72,256]{1,0:T(8,128)S(1)}, f32[72,256]{1,0:T(8,128)S(1)}, u32[]{:S(2)}, u32[]{:S(2)}) collective-permute-start(f32[72,256]{1,0:T(8,128)S(1)} %get-tuple-element.176), channel_id=1, source_target_pairs={{0,31},{1,2},{2,1},{3,4},{4,3},{5,6},{6,5},{7,24},{8,23},{9,10},{1... | collective-permute-start | bytes 221192 | tf_op jit(solution)/shard_map/ppermute | solution.py:839
  88.4 2.2 %collective-permute-start.18 = (f32[72,128]{1,0:T(8,128)S(1)}, f32[72,128]{1,0:T(8,128)S(1)}, u32[]{:S(2)}, u32[]{:S(2)}) collective-permute-start(f32[72,128]{1,0:T(8,128)S(1)} %get-tuple-element.185), channel_id=1, source_target_pairs={{0,1},{1,0},{2,3},{3,2},{4,5},{5,4},{6,7},{7,6},{8,9},{9,8},{10,11... | collective-permute-start | bytes 110600 | tf_op jit(solution)/shard_map/ppermute | solution.py:838
  88.5 7.3 %collective-permute-start.19 = (f32[72,128]{1,0:T(8,128)S(1)}, f32[72,128]{1,0:T(8,128)S(1)}, u32[]{:S(2)}, u32[]{:S(2)}) collective-permute-start(f32[72,128]{1,0:T(8,128)S(1)} %get-tuple-element.186), channel_id=1, source_target_pairs={{0,15},{1,2},{2,1},{3,4},{4,3},{5,6},{6,5},{7,8},{8,7},{9,10},{10,... | collective-permute-start | bytes 110600 | tf_op jit(solution)/shard_map/ppermute | solution.py:839
  97.6 4.4 %collective-permute-start.20 = (f32[152,128]{1,0:T(8,128)S(1)}, f32[152,128]{1,0:T(8,128)S(1)}, u32[]{:S(2)}, u32[]{:S(2)}) collective-permute-start(f32[152,128]{1,0:T(8,128)S(1)} %get-tuple-element.193), channel_id=1, source_target_pairs={{0,16},{1,17},{2,18},{3,19},{4,20},{5,21},{6,22},{7,23},{8,24},{9,... | collective-permute-start | bytes 233480 | tf_op jit(solution)/shard_map/ppermute | solution.py:838
  97.6 6.6 %collective-permute-start.21 = (f32[152,128]{1,0:T(8,128)S(1)}, f32[152,128]{1,0:T(8,128)S(1)}, u32[]{:S(2)}, u32[]{:S(2)}) collective-permute-start(f32[152,128]{1,0:T(8,128)S(1)} %get-tuple-element.194), channel_id=1, source_target_pairs={{0,112},{1,113},{2,114},{3,115},{4,116},{5,117},{6,118},{7,119},{8... | collective-permute-start | bytes 233480 | tf_op jit(solution)/shard_map/ppermute | solution.py:839
  104.5 4.2 %collective-permute-start.22 = (f32[72,128]{1,0:T(8,128)S(1)}, f32[72,128]{1,0:T(8,128)S(1)}, u32[]{:S(2)}, u32[]{:S(2)}) collective-permute-start(f32[72,128]{1,0:T(8,128)S(1)} %get-tuple-element.197.refs_5_), channel_id=1, source_target_pairs={{0,1},{1,0},{2,3},{3,2},{4,5},{5,4},{6,7},{7,6},{8,9},{9,8},{10,11... | collective-permute-start | bytes 110600 | tf_op jit(solution)/shard_map/ppermute | solution.py:838
  104.6 7.1 %collective-permute-start.23 = (f32[72,128]{1,0:T(8,128)S(1)}, f32[72,128]{1,0:T(8,128)S(1)}, u32[]{:S(2)}, u32[]{:S(2)}) collective-permute-start(f32[72,128]{1,0:T(8,128)S(1)} %get-tuple-element.198), channel_id=1, source_target_pairs={{0,15},{1,2},{2,1},{3,4},{4,3},{5,6},{6,5},{7,8},{8,7},{9,10},{10,... | collective-permute-start | bytes 110600 | tf_op jit(solution)/shard_map/ppermute | solution.py:839

commit v5 on v4

--- a/solution.py
+++ b/solution.py
@@ -157,7 +157,21 @@
         put_parts(geom, parts, tail, ref)
 
 
+SPLIT = 40
+
+
+def halved(geom, count):
+    return geom[2] == 64 and count == 3
+
+
 def put_parts(geom, parts, tail, ref):
+    if halved(geom, len(parts)):
+        lane = lane_ids((SPLIT, LANES))
+        rest = jnp.concatenate([parts[2][SPLIT:Z, :], jnp.zeros((2 * SPLIT - Z, LANES), F32)], axis=0)
+        ref[0:Z, :] = pack(geom, parts[:2])[0]
+        ref[Z : Z + SPLIT, :] = jnp.where(lane < 64, parts[2][0:SPLIT, :], roll(rest, 64))
+        ref[Z + SPLIT : Z + SPLIT + 8, :] = tail
+        return
     whole = pack(geom, parts)
     for k, part in enumerate(whole):
         ref[k * Z : (k + 1) * Z, :] = part
@@ -165,8 +179,12 @@
 
 
 def tail_of(geom, ref, count):
-    n = packed(geom, count) * Z
+    n = message_rows(geom, count)
     return ref[n : n + 8, :]
+
+
+def message_rows(geom, count):
+    return Z + SPLIT if halved(geom, count) else packed(geom, count) * Z
 
 
 def put_y(geom, v, c, up, down):
@@ -415,15 +433,22 @@
     return Halo(*[d[:, k * LANES : (k + 1) * LANES] for k in range(6)])
 
 
+def third_of(geom, ref):
+    if not halved(geom, 3):
+        return part_of(geom, ref, 2)
+    both = ref[Z : Z + SPLIT, :]
+    return jnp.concatenate([both, roll(both[0 : Z - SPLIT, :], 64)], axis=0)
+
+
 def own_data(geom, xlo, xhi, ydn, yun):
     dn, un = ydn[0:Z, :], yun[0:Z, :]
     f_sides = jnp.where(odd_lanes(), dn, un)
     c_sides = roll(f_sides, -64)
     return (
         part_of(geom, xlo, 0),
-        part_of(geom, xlo, 2),
+        third_of(geom, xlo),
         part_of(geom, xhi, 0),
-        part_of(geom, xhi, 2),
+        third_of(geom, xhi),
         f_sides,
         c_sides,
     )
@@ -899,7 +924,7 @@
 
 
 def x_shape(level, count):
-    return (packed(GEOM[level], count) * Z + 8, LANES)
+    return (message_rows(GEOM[level], count) + 8, LANES)
 
 
 Y_FULL = (Z + 8, LANES)
@@ -984,12 +1009,21 @@
     geom = GEOM[level]
 
     def kernel(xlo, xhi, flags, yup, ydown, up, down):
-        lo, hi = corner_columns(tail_of(geom, xlo, count)), corner_columns(tail_of(geom, xhi, count))
+        lo, hi = tail_of(geom, xlo, count), tail_of(geom, xhi, count)
+        lo = [lo[4 + k : 5 + k, :] for k in range(4)]
+        hi = [hi[4 + k : 5 + k, :] for k in range(4)]
+        f0, f1 = flags[0:1, :] > 0.5, flags[1:2, :] > 0.5
+        to_up = [lo[3], lo[1], hi[1], hi[3], jnp.where(f0, lo[2], lo[3]), jnp.where(f1, hi[0], hi[1])]
+        to_down = [lo[2], lo[0], hi[0], hi[2], jnp.where(f0, lo[3], lo[2]), jnp.where(f1, hi[1], hi[0])]
+        two = jnp.zeros((2, LANES), F32)
+        rows = [*to_down, two, jnp.zeros((104, LANES), F32), *to_up, two, jnp.zeros((8, LANES), F32)]
+        turned = jnp.concatenate(rows, axis=0).T[0:Z, :]
+        lane = zl()
+        inside = (lane >= 112) & (lane < 118)
         up[...] = yup[...]
         down[...] = ydown[...]
-        a, b = merge_y(lo, hi, flags, yup[0:Z, :], ydown[0:Z, :])
-        up[0:Z, :] = a
-        down[0:Z, :] = b
+        up[0:Z, :] = jnp.where(inside, turned, yup[0:Z, :])
+        down[0:Z, :] = jnp.where(inside, roll(turned, 112), ydown[0:Z, :])
 
     return kernel
 

time: 114 us -> 114 us (level)
  no operation moved by 1% of the time
where the time goes in v5:
time: 114 us; the launch traced here: 113 us
  starting transfers between devices  42 us (37%)
  Pallas kernels  33.2 us (29%)
  waiting for transfers between devices  21 us (18%)
  blocking collectives  15.4 us (14%)
  local copies, waits for them, and re-layouts  1.57 us (1%)
    ppermute x12, starting transfers between devices, swap(): lax.ppermute(second, both, swap_pairs(axis, 1, nearest))  39.5 us
    pallas_call x23, Pallas kernels, call(): pl.pallas_call(by_swaps(kernel, len(args), len(outs), got, send), out_sha...  31.1 us
    ppermute x12, waiting for transfers between devices, swap(): lax.ppermute(second, both, swap_pairs(axis, 1, nearest))  20.5 us
    all_to_all x1, blocking collectives, on_device(): chunks = lax.all_to_all(chunks, 'gx', 0, 0)  15.4 us
    ppermute x12, starting transfers between devices, swap(): lax.ppermute(first, both, swap_pairs(axis, 0, nearest))  2.51 us
  transfers between devices with their start and end apart: 24, of which 11 were waited for; matrix products, arithmetic and copies ran while one was open for 1% of the time, Pallas kernels for 16%

profile of v5, /device:TPU:0, one launch (start us, length us, event | category | flops | bytes accessed | tf_op | source)
XLA Modules:
  0.0 113.5 jit_solution(15587260398726426339)
XLA Ops:
  0.0 2.0 %open.1 = (f32[224,128]{1,0:T(8,128)}, f32[224,128]{1,0:T(8,128)}, f32[8,128]{1,0:T(8,128)}, f32[72,128]{1,0:T(8,128)}) custom-call(f32[70,24,128]{2,1,0:T(8,128)} %refs_0_.1, f32[70,24,128]{2,1,0:T(8,128)} %refs_1_.1, f32[1,71]{1,0:T(1,128)} %bitcast.9, s32[1,4]{1,0:T(1,128)} %bitcast.10), custom_call_target="tpu_custom_call" | custom-call | tf_op jit(solution)/shard_map/open/pallas_call | solution.py:1174
  2.0 1.7 %collective-permute-start = (f32[224,128]{1,0:T(8,128)}, f32[224,128]{1,0:T(8,128)S(1)}, u32[]{:S(2)}, u32[]{:S(2)}) collective-permute-start(f32[224,128]{1,0:T(8,128)} %get-tuple-element.107), channel_id=1, source_target_pairs={{0,16},{1,17},{2,18},{3,19},{4,20},{5,21},{6,22},{7,23},{8,24},{9,... | collective-permute-start | bytes 344072 | tf_op jit(solution)/shard_map/ppermute | solution.py:863
  3.8 2.6 %collective-permute-start.1 = (f32[224,128]{1,0:T(8,128)}, f32[224,128]{1,0:T(8,128)S(1)}, u32[]{:S(2)}, u32[]{:S(2)}) collective-permute-start(f32[224,128]{1,0:T(8,128)} %get-tuple-element.108), channel_id=1, source_target_pairs={{0,112},{1,113},{2,114},{3,115},{4,116},{5,117},{6,118},{7,119},{8... | collective-permute-start | bytes 344072 | tf_op jit(solution)/shard_map/ppermute | solution.py:864
  8.0 2.6 %side.1 = (f32[24,72,128]{2,1,0:T(8,128)S(1)}, f32[24,72,128]{2,1,0:T(8,128)S(1)}, f32[72,216]{1,0:T(8,128)S(1)}, f32[72,216]{1,0:T(8,128)S(1)}, f32[72,216]{1,0...) custom-call(f32[1680,128]{1,0:T(8,128)S(1)} %bitcast.6, ...), custom_call_target="tpu_custom_call" | custom-call | tf_op jit(solution)/shard_map/side/pallas_call | solution.py:911
  11.1 6.5 %collective-permute-start.3 = (f32[80,128]{1,0:T(8,128)S(1)}, f32[80,128]{1,0:T(8,128)S(1)}, u32[]{:S(2)}, u32[]{:S(2)}) collective-permute-start(f32[80,128]{1,0:T(8,128)S(1)} %get-tuple-element.112), channel_id=1, source_target_pairs={{0,15},{1,2},{2,1},{3,4},{4,3},{5,6},{6,5},{7,8},{8,7},{9,10},{10,... | collective-permute-start | bytes 122888 | tf_op jit(solution)/shard_map/ppermute | solution.py:864
  17.7 1.7 %collective-permute-done.3.refs_8_ = f32[80,128]{1,0:T(8,128)S(1)} collective-permute-done((f32[80,128]{1,0:T(8,128)S(1)}, f32[80,128]{1,0:T(8,128)S(1)}, u32[]{:S(2)}, u32[]{:S(2)}) %collective-permute-start.3) | collective-permute-done | bytes 40992 | tf_op jit(solution)/shard_map/ppermute | solution.py:864
  19.4 1.7 %pre0.1 = (f32[120,128]{1,0:T(8,128)S(1)}, f32[120,128]{1,0:T(8,128)S(1)}, f32[3,72,128]{2,1,0:T(8,128)S(1)}, f32[3,72,128]{2,1,0:T(8,128)S(1)}) custom-call(f32[24,72,128]{2,1,0:T(8,128)S(1)} %get-tuple-element.104.refs_0_, f32[24,72,128]{2,1,0:T(8,128)S(1)} %get-tuple-element.105.refs_1_, f32[72,216]{1,0:T(8,128)S(1)} %get-tuple-element.106.refs_2_, ...), custom_call_target="tpu_custom_call" | custom-call | tf_op jit(solution)/shard_map/pre0/pallas_call | solution.py:911
  21.1 3.3 %collective-permute-start.5 = (f32[120,128]{1,0:T(8,128)S(1)}, f32[120,128]{1,0:T(8,128)S(1)}, u32[]{:S(2)}, u32[]{:S(2)}) collective-permute-start(f32[120,128]{1,0:T(8,128)S(1)} %get-tuple-element.122), channel_id=1, source_target_pairs={{0,112},{1,113},{2,114},{3,115},{4,116},{5,117},{6,118},{7,119},{8... | collective-permute-start | bytes 184328 | tf_op jit(solution)/shard_map/ppermute | solution.py:864
  24.4 2.2 %mid1.1 = (f32[24,72,128]{2,1,0:T(8,128)S(1)}, f32[6,72,128]{2,1,0:T(8,128)S(1)}, f32[6,72,128]{2,1,0:T(8,128)S(1)}, f32[6,72,128]{2,1,0:T(8,128)S(1)}, f32[72,1...) custom-call(f32[24,72,128]{2,1,0:T(8,128)S(1)} %get-tuple-element.104.refs_0_, ...), custom_call_target="tpu_custom_call" | custom-call | tf_op jit(solution)/shard_map/mid1/pallas_call | solution.py:911
  27.8 4.5 %collective-permute-start.7 = (f32[80,128]{1,0:T(8,128)S(1)}, f32[80,128]{1,0:T(8,128)S(1)}, u32[]{:S(2)}, u32[]{:S(2)}) collective-permute-start(f32[80,128]{1,0:T(8,128)S(1)} %get-tuple-element.126), channel_id=1, source_target_pairs={{0,15},{1,2},{2,1},{3,4},{4,3},{5,6},{6,5},{7,8},{8,7},{9,10},{10,... | collective-permute-start | bytes 122888 | tf_op jit(solution)/shard_map/ppermute | solution.py:864
  32.2 2.7 %collective-permute-done.7.refs_8_ = f32[80,128]{1,0:T(8,128)S(1)} collective-permute-done((f32[80,128]{1,0:T(8,128)S(1)}, f32[80,128]{1,0:T(8,128)S(1)}, u32[]{:S(2)}, u32[]{:S(2)}) %collective-permute-start.7) | collective-permute-done | bytes 40992 | tf_op jit(solution)/shard_map/ppermute | solution.py:864
  34.9 2.1 %pre1.1 = (f32[6,72,128]{2,1,0:T(8,128)S(1)}, f32[80,128]{1,0:T(8,128)S(1)}, f32[80,128]{1,0:T(8,128)S(1)}, f32[8,224,128]{2,1,0:T(8,128)S(1)}) custom-call(f32[6,72,128]{2,1,0:T(8,128)S(1)} %get-tuple-element.120.refs_0_, f32[6,72,128]{2,1,0:T(8,128)S(1)} %get-tuple-element.116.refs_12_.refs_7_.refs_1_, f32[72,216]{1,0:T(8,128)S(1)} %get-tuple-element.119.refs_6_.refs_2_, ...), custom_call_target="tpu_custom_call" | custom-call | tf_op jit(solution)/shard_map/pre1/pallas_call | solution.py:911
  36.9 15.4 %all_to_all.5.refs_0_ = f32[8,224,128]{2,1,0:T(8,128)S(1)} all-to-all(f32[8,224,128]{2,1,0:T(8,128)S(1)} %get-tuple-element.132), channel_id=1, replica_groups=mesh['gx'=8,'gy'=16] {'gx'}, dimensions={0} | all-to-all | bytes 1835008 | tf_op jit(solution)/shard_map/all_to_all | solution.py:1232
  53.5 4.4 %collective-permute-start.9 = (f32[80,256]{1,0:T(8,128)S(1)}, f32[80,256]{1,0:T(8,128)S(1)}, u32[]{:S(2)}, u32[]{:S(2)}) collective-permute-start(f32[80,256]{1,0:T(8,128)S(1)} %get-tuple-element.141), channel_id=1, source_target_pairs={{0,31},{1,2},{2,1},{3,4},{4,3},{5,6},{6,5},{7,24},{8,23},{9,10},{1... | collective-permute-start | bytes 245768 | tf_op jit(solution)/shard_map/ppermute | solution.py:864
  58.3 1.9 %alone2.1 = (f32[6,72,256]{2,1,0:T(8,128)S(1)}, f32[72,256]{1,0:T(8,128)S(1)}, f32[72,256]{1,0:T(8,128)S(1)}, f32[3,72,128]{2,1,0:T(8,128)S(1)}, f32[72,128]{1,0:T(8,128)S(1)}, /*index=5*/f32[72,128]{1,0:T(8,128)S(1)}) custom-call(f32[6,72,256]{2,1,0:T(8,128)S(1)} %get-tuple-element.133.refs_0_, f32[6,72,256]{2,1,0:T(8,128)S(1)} %get-tuple-element.134.refs_0_.refs_1_, ...), custom_call_target="tpu_custom_call" | custom-call | tf_op jit(solution)/shard_map/alone2/pallas_call | solution.py:911
  62.5 4.3 %collective-permute-start.11 = (f32[80,128]{1,0:T(8,128)S(1)}, f32[80,128]{1,0:T(8,128)S(1)}, u32[]{:S(2)}, u32[]{:S(2)}) collective-permute-start(f32[80,128]{1,0:T(8,128)S(1)} %get-tuple-element.153), channel_id=1, source_target_pairs={{0,31},{1,2},{2,1},{3,4},{4,3},{5,6},{6,5},{7,24},{8,23},{9,10},{1... | collective-permute-start | bytes 122888 | tf_op jit(solution)/shard_map/ppermute | solution.py:864
  66.7 2.6 %collective-permute-start.15 = (f32[80,128]{1,0:T(8,128)S(1)}, f32[80,128]{1,0:T(8,128)S(1)}, u32[]{:S(2)}, u32[]{:S(2)}) collective-permute-start(f32[80,128]{1,0:T(8,128)S(1)} %get-tuple-element.168), channel_id=1, source_target_pairs={{0,112},{1,113},{2,114},{3,115},{4,116},{5,117},{6,118},{7,119},{8... | collective-permute-start | bytes 122888 | tf_op jit(solution)/shard_map/ppermute | solution.py:864
  71.5 3.1 %collective-permute-start.13 = (f32[72,128]{1,0:T(8,128)S(1)}, f32[72,128]{1,0:T(8,128)S(1)}, u32[]{:S(2)}, u32[]{:S(2)}) collective-permute-start(f32[72,128]{1,0:T(8,128)S(1)} %get-tuple-element.162), channel_id=1, source_target_pairs={{0,31},{1,2},{2,1},{3,4},{4,3},{5,6},{6,5},{7,24},{8,23},{9,10},{1... | collective-permute-start | bytes 110600 | tf_op jit(solution)/shard_map/ppermute | solution.py:864
  76.1 2.2 %collective-permute-done.13.refs_3_ = f32[72,128]{1,0:T(8,128)S(1)} collective-permute-done((f32[72,128]{1,0:T(8,128)S(1)}, f32[72,128]{1,0:T(8,128)S(1)}, u32[]{:S(2)}, u32[]{:S(2)}) %collective-permute-start.13) | collective-permute-done | bytes 36896 | tf_op jit(solution)/shard_map/ppermute | solution.py:864
  79.2 3.1 %collective-permute-start.17 = (f32[72,256]{1,0:T(8,128)S(1)}, f32[72,256]{1,0:T(8,128)S(1)}, u32[]{:S(2)}, u32[]{:S(2)}) collective-permute-start(f32[72,256]{1,0:T(8,128)S(1)} %get-tuple-element.176), channel_id=1, source_target_pairs={{0,31},{1,2},{2,1},{3,4},{4,3},{5,6},{6,5},{7,24},{8,23},{9,10},{1... | collective-permute-start | bytes 221192 | tf_op jit(solution)/shard_map/ppermute | solution.py:864
  82.3 2.3 %again2.1 = (f32[72,256]{1,0:T(8,128)S(1)}, f32[72,256]{1,0:T(8,128)S(1)}, f32[72,256]{1,0:T(8,128)S(1)}, f32[72,256]{1,0:T(8,128)S(1)}, f32[72,128]{1,0:T(8,128...) custom-call(f32[6,72,256]{2,1,0:T(8,128)S(1)} %get-tuple-element.133.refs_0_, ...), custom_call_target="tpu_custom_call" | custom-call | tf_op jit(solution)/shard_map/again2/pallas_call | solution.py:911
  84.6 1.8 %collective-permute-done.17.refs_12_ = f32[72,256]{1,0:T(8,128)S(1)} collective-permute-done((f32[72,256]{1,0:T(8,128)S(1)}, f32[72,256]{1,0:T(8,128)S(1)}, u32[]{:S(2)}, u32[]{:S(2)}) %collective-permute-start.17) | collective-permute-done | bytes 73760 | tf_op jit(solution)/shard_map/ppermute | solution.py:864
  86.4 1.5 %post2.1 = (f32[4,72,256]{2,1,0:T(8,128)S(1)}, f32[72,128]{1,0:T(8,128)S(1)}, f32[72,128]{1,0:T(8,128)S(1)}) custom-call(f32[72,216]{1,0:T(8,128)S(1)} %get-tuple-element.135.refs_2_.refs_0_, f32[72,128]{1,0:T(8,128)S(1)} %copy-done, f32[8,256]{1,0:T(8,128)S(1)} %get-tuple-element.136.refs_1_.refs_4_.refs_2_, f32[80,256]{1,0:T(8,128)S(1)} %collective-permute-done.8.refs_3_, ...), custom_call_target="tpu_custom_call" | custom-call | tf_op jit(solution)/shard_map/post2/pallas_call | solution.py:911
  88.4 1.8 %again1.1 = (f32[6,72,128]{2,1,0:T(8,128)S(1)}, f32[6,72,128]{2,1,0:T(8,128)S(1)}, f32[72,128]{1,0:T(8,128)S(1)}, f32[72,128]{1,0:T(8,128)S(1)}, f32[72,128]{1,0:T(8,128)S(1)}) custom-call(f32[6,72,128]{2,1,0:T(8,128)S(1)} %get-tuple-element.120.refs_0_, f32[6,72,128]{2,1,0:T(8,128)S(1)} %get-tuple-element.116.refs_12_.refs_7_.refs_1_, ...), custom_call_target="tpu_custom_call" | custom-call | tf_op jit(solution)/shard_map/again1/pallas_call | solution.py:911
  90.2 5.2 %collective-permute-done.19.refs_15_ = f32[72,128]{1,0:T(8,128)S(1)} collective-permute-done((f32[72,128]{1,0:T(8,128)S(1)}, f32[72,128]{1,0:T(8,128)S(1)}, u32[]{:S(2)}, u32[]{:S(2)}) %collective-permute-start.19) | collective-permute-done | bytes 36896 | tf_op jit(solution)/shard_map/ppermute | solution.py:864
  95.3 1.8 %post1.1 = (f32[6,72,128]{2,1,0:T(8,128)S(1)}, f32[152,128]{1,0:T(8,128)S(1)}, f32[152,128]{1,0:T(8,128)S(1)}) custom-call(f32[6,72,128]{2,1,0:T(8,128)S(1)} %get-tuple-element.120.refs_0_, f32[6,72,128]{2,1,0:T(8,128)S(1)} %get-tuple-element.116.refs_12_.refs_7_.refs_1_, f32[72,216]{1,0:T(8,128)S(1)} %get-tuple-element.119.refs_6_.refs_2_, ...), custom_call_target="tpu_custom_call" | custom-call | tf_op jit(solution)/shard_map/post1/pallas_call | solution.py:911
  97.2 1.7 %collective-permute-start.21 = (f32[152,128]{1,0:T(8,128)S(1)}, f32[152,128]{1,0:T(8,128)S(1)}, u32[]{:S(2)}, u32[]{:S(2)}) collective-permute-start(f32[152,128]{1,0:T(8,128)S(1)} %get-tuple-element.194), channel_id=1, source_target_pairs={{0,112},{1,113},{2,114},{3,115},{4,116},{5,117},{6,118},{7,119},{8... | collective-permute-start | bytes 233480 | tf_op jit(solution)/shard_map/ppermute | solution.py:864
  98.8 2.3 %again0.1 = (f32[24,72,128]{2,1,0:T(8,128)S(1)}, f32[24,72,128]{2,1,0:T(8,128)S(1)}, f32[72,128]{1,0:T(8,128)S(1)}, f32[72,128]{1,0:T(8,128)S(1)}, f32[72,128]{1,0:T(8,128)S(1)}, /*index=5*/f32[72,128]{1,0:T(8,128)S(1)}) custom-call(f32[24,72,128]{2,1,0:T(8,128)S(1)} %get-tuple-element.104.refs_0_, f32[24,72,128]{2,1,0:T(8,128)S(1)} %get-tuple-element.105.refs_1_, ...), custom_call_target="tpu_custom_call" | custom-call | tf_op jit(solution)/shard_map/again0/pallas_call | solution.py:911
  101.6 2.2 %collective-permute-done.21.refs_1_.refs_14_ = f32[152,128]{1,0:T(8,128)S(1)} collective-permute-done((f32[152,128]{1,0:T(8,128)S(1)}, f32[152,128]{1,0:T(8,128)S(1)}, u32[]{:S(2)}, u32[]{:S(2)}) %collective-permute-start.21) | collective-permute-done | bytes 77856 | tf_op jit(solution)/shard_map/ppermute | solution.py:864
  104.0 3.0 %collective-permute-start.23 = (f32[72,128]{1,0:T(8,128)S(1)}, f32[72,128]{1,0:T(8,128)S(1)}, u32[]{:S(2)}, u32[]{:S(2)}) collective-permute-start(f32[72,128]{1,0:T(8,128)S(1)} %get-tuple-element.198), channel_id=1, source_target_pairs={{0,15},{1,2},{2,1},{3,4},{4,3},{5,6},{6,5},{7,8},{8,7},{9,10},{10,... | collective-permute-start | bytes 110600 | tf_op jit(solution)/shard_map/ppermute | solution.py:864
  108.2 2.9 %collective-permute-done.23.refs_16_ = f32[72,128]{1,0:T(8,128)S(1)} collective-permute-done((f32[72,128]{1,0:T(8,128)S(1)}, f32[72,128]{1,0:T(8,128)S(1)}, u32[]{:S(2)}, u32[]{:S(2)}) %collective-permute-start.23) | collective-permute-done | bytes 36896 | tf_op jit(solution)/shard_map/ppermute | solution.py:864
  111.1 2.4 %post0.1 = f32[1680,128]{1,0:T(8,128)} custom-call(f32[24,72,128]{2,1,0:T(8,128)S(1)} %get-tuple-element.104.refs_0_, f32[24,72,128]{2,1,0:T(8,128)S(1)} %get-tuple-element.105.refs_1_, f32[72,216]{1,0:T(8,128)S(1)} %get-tuple-element.106.refs_2_, f32[72,128]{1,0:T(8,128)S(1)} %copy-done, f32[8,128]{1,0:T(8,128)S(1)} %copy-done.3, ...), custom_call_target="tpu_custom_call" | custom-call | tf_op jit(solution)/shard_map/post0/pallas_call | solution.py:911
  (50 shorter events, 13.8 us)
Async XLA Ops:
  0.0 7.4 %copy-start.1 = (f32[70,24,128]{2,1,0:T(8,128)S(1)}, f32[70,24,128]{2,1,0:T(8,128)}, u32[]{:S(2)}) copy-start(f32[70,24,128]{2,1,0:T(8,128)} %refs_0_.1) | copy-start | bytes 2580484
  0.0 7.4 %copy-start.2 = (f32[70,24,128]{2,1,0:T(8,128)S(1)}, f32[70,24,128]{2,1,0:T(8,128)}, u32[]{:S(2)}) copy-start(f32[70,24,128]{2,1,0:T(8,128)} %refs_1_.1) | copy-start | bytes 2580484
  2.0 8.6 %collective-permute-start = (f32[224,128]{1,0:T(8,128)}, f32[224,128]{1,0:T(8,128)S(1)}, u32[]{:S(2)}, u32[]{:S(2)}) collective-permute-start(f32[224,128]{1,0:T(8,128)} %get-tuple-element.107), channel_id=1, source_target_pairs={{0,16},{1,17},{2,18},{3,19},{4,20},{5,21},{6,22},{7,23},{8,24},{9,... | collective-permute-start | bytes 344072 | tf_op jit(solution)/shard_map/ppermute | solution.py:863
  3.8 7.1 %collective-permute-start.1 = (f32[224,128]{1,0:T(8,128)}, f32[224,128]{1,0:T(8,128)S(1)}, u32[]{:S(2)}, u32[]{:S(2)}) collective-permute-start(f32[224,128]{1,0:T(8,128)} %get-tuple-element.108), channel_id=1, source_target_pairs={{0,112},{1,113},{2,114},{3,115},{4,116},{5,117},{6,118},{7,119},{8... | collective-permute-start | bytes 344072 | tf_op jit(solution)/shard_map/ppermute | solution.py:864
  6.4 1.0 copy-start
  7.3 0.7 copy-start.3
  11.0 6.6 %collective-permute-start.2 = (f32[80,128]{1,0:T(8,128)S(1)}, f32[80,128]{1,0:T(8,128)S(1)}, u32[]{:S(2)}, u32[]{:S(2)}) collective-permute-start(f32[80,128]{1,0:T(8,128)S(1)} %get-tuple-element.111), channel_id=1, source_target_pairs={{0,1},{1,0},{2,3},{3,2},{4,5},{5,4},{6,7},{7,6},{8,9},{9,8},{10,11... | collective-permute-start | bytes 122888 | tf_op jit(solution)/shard_map/ppermute | solution.py:863
  11.1 8.2 %collective-permute-start.3 = (f32[80,128]{1,0:T(8,128)S(1)}, f32[80,128]{1,0:T(8,128)S(1)}, u32[]{:S(2)}, u32[]{:S(2)}) collective-permute-start(f32[80,128]{1,0:T(8,128)S(1)} %get-tuple-element.112), channel_id=1, source_target_pairs={{0,15},{1,2},{2,1},{3,4},{4,3},{5,6},{6,5},{7,8},{8,7},{9,10},{10,... | collective-permute-start | bytes 122888 | tf_op jit(solution)/shard_map/ppermute | solution.py:864
  21.0 5.5 %collective-permute-start.4 = (f32[120,128]{1,0:T(8,128)S(1)}, f32[120,128]{1,0:T(8,128)S(1)}, u32[]{:S(2)}, u32[]{:S(2)}) collective-permute-start(f32[120,128]{1,0:T(8,128)S(1)} %get-tuple-element.121), channel_id=1, source_target_pairs={{0,16},{1,17},{2,18},{3,19},{4,20},{5,21},{6,22},{7,23},{8,24},{9,... | collective-permute-start | bytes 184328 | tf_op jit(solution)/shard_map/ppermute | solution.py:863
  21.1 6.4 %collective-permute-start.5 = (f32[120,128]{1,0:T(8,128)S(1)}, f32[120,128]{1,0:T(8,128)S(1)}, u32[]{:S(2)}, u32[]{:S(2)}) collective-permute-start(f32[120,128]{1,0:T(8,128)S(1)} %get-tuple-element.122), channel_id=1, source_target_pairs={{0,112},{1,113},{2,114},{3,115},{4,116},{5,117},{6,118},{7,119},{8... | collective-permute-start | bytes 184328 | tf_op jit(solution)/shard_map/ppermute | solution.py:864
  27.7 4.6 %collective-permute-start.6 = (f32[80,128]{1,0:T(8,128)S(1)}, f32[80,128]{1,0:T(8,128)S(1)}, u32[]{:S(2)}, u32[]{:S(2)}) collective-permute-start(f32[80,128]{1,0:T(8,128)S(1)} %get-tuple-element.125), channel_id=1, source_target_pairs={{0,1},{1,0},{2,3},{3,2},{4,5},{5,4},{6,7},{7,6},{8,9},{9,8},{10,11... | collective-permute-start | bytes 122888 | tf_op jit(solution)/shard_map/ppermute | solution.py:863
  27.8 7.1 %collective-permute-start.7 = (f32[80,128]{1,0:T(8,128)S(1)}, f32[80,128]{1,0:T(8,128)S(1)}, u32[]{:S(2)}, u32[]{:S(2)}) collective-permute-start(f32[80,128]{1,0:T(8,128)S(1)} %get-tuple-element.126), channel_id=1, source_target_pairs={{0,15},{1,2},{2,1},{3,4},{4,3},{5,6},{6,5},{7,8},{8,7},{9,10},{10,... | collective-permute-start | bytes 122888 | tf_op jit(solution)/shard_map/ppermute | solution.py:864
  53.5 6.8 %collective-permute-start.8 = (f32[80,256]{1,0:T(8,128)S(1)}, f32[80,256]{1,0:T(8,128)S(1)}, u32[]{:S(2)}, u32[]{:S(2)}) collective-permute-start(f32[80,256]{1,0:T(8,128)S(1)} %get-tuple-element.140), channel_id=1, source_target_pairs={{0,1},{1,0},{2,3},{3,2},{4,5},{5,4},{6,7},{7,6},{8,9},{9,8},{10,11... | collective-permute-start | bytes 245768 | tf_op jit(solution)/shard_map/ppermute | solution.py:863
  53.5 7.4 %collective-permute-start.9 = (f32[80,256]{1,0:T(8,128)S(1)}, f32[80,256]{1,0:T(8,128)S(1)}, u32[]{:S(2)}, u32[]{:S(2)}) collective-permute-start(f32[80,256]{1,0:T(8,128)S(1)} %get-tuple-element.141), channel_id=1, source_target_pairs={{0,31},{1,2},{2,1},{3,4},{4,3},{5,6},{6,5},{7,24},{8,23},{9,10},{1... | collective-permute-start | bytes 245768 | tf_op jit(solution)/shard_map/ppermute | solution.py:864
  62.4 8.1 %collective-permute-start.10 = (f32[80,128]{1,0:T(8,128)S(1)}, f32[80,128]{1,0:T(8,128)S(1)}, u32[]{:S(2)}, u32[]{:S(2)}) collective-permute-start(f32[80,128]{1,0:T(8,128)S(1)} %get-tuple-element.152), channel_id=1, source_target_pairs={{0,1},{1,0},{2,3},{3,2},{4,5},{5,4},{6,7},{7,6},{8,9},{9,8},{10,11... | collective-permute-start | bytes 122888 | tf_op jit(solution)/shard_map/ppermute | solution.py:863
  62.5 8.0 %collective-permute-start.11 = (f32[80,128]{1,0:T(8,128)S(1)}, f32[80,128]{1,0:T(8,128)S(1)}, u32[]{:S(2)}, u32[]{:S(2)}) collective-permute-start(f32[80,128]{1,0:T(8,128)S(1)} %get-tuple-element.153), channel_id=1, source_target_pairs={{0,31},{1,2},{2,1},{3,4},{4,3},{5,6},{6,5},{7,24},{8,23},{9,10},{1... | collective-permute-start | bytes 122888 | tf_op jit(solution)/shard_map/ppermute | solution.py:864
  66.7 9.4 %collective-permute-start.14 = (f32[80,128]{1,0:T(8,128)S(1)}, f32[80,128]{1,0:T(8,128)S(1)}, u32[]{:S(2)}, u32[]{:S(2)}) collective-permute-start(f32[80,128]{1,0:T(8,128)S(1)} %get-tuple-element.167), channel_id=1, source_target_pairs={{0,16},{1,17},{2,18},{3,19},{4,20},{5,21},{6,22},{7,23},{8,24},{9,... | collective-permute-start | bytes 122888 | tf_op jit(solution)/shard_map/ppermute | solution.py:863
  66.7 9.4 %collective-permute-start.15 = (f32[80,128]{1,0:T(8,128)S(1)}, f32[80,128]{1,0:T(8,128)S(1)}, u32[]{:S(2)}, u32[]{:S(2)}) collective-permute-start(f32[80,128]{1,0:T(8,128)S(1)} %get-tuple-element.168), channel_id=1, source_target_pairs={{0,112},{1,113},{2,114},{3,115},{4,116},{5,117},{6,118},{7,119},{8... | collective-permute-start | bytes 122888 | tf_op jit(solution)/shard_map/ppermute | solution.py:864
  71.4 4.7 %collective-permute-start.12 = (f32[72,128]{1,0:T(8,128)S(1)}, f32[72,128]{1,0:T(8,128)S(1)}, u32[]{:S(2)}, u32[]{:S(2)}) collective-permute-start(f32[72,128]{1,0:T(8,128)S(1)} %get-tuple-element.161), channel_id=1, source_target_pairs={{0,1},{1,0},{2,3},{3,2},{4,5},{5,4},{6,7},{7,6},{8,9},{9,8},{10,11... | collective-permute-start | bytes 110600 | tf_op jit(solution)/shard_map/ppermute | solution.py:863
  71.5 6.8 %collective-permute-start.13 = (f32[72,128]{1,0:T(8,128)S(1)}, f32[72,128]{1,0:T(8,128)S(1)}, u32[]{:S(2)}, u32[]{:S(2)}) collective-permute-start(f32[72,128]{1,0:T(8,128)S(1)} %get-tuple-element.162), channel_id=1, source_target_pairs={{0,31},{1,2},{2,1},{3,4},{4,3},{5,6},{6,5},{7,24},{8,23},{9,10},{1... | collective-permute-start | bytes 110600 | tf_op jit(solution)/shard_map/ppermute | solution.py:864
  79.1 5.5 %collective-permute-start.16 = (f32[72,256]{1,0:T(8,128)S(1)}, f32[72,256]{1,0:T(8,128)S(1)}, u32[]{:S(2)}, u32[]{:S(2)}) collective-permute-start(f32[72,256]{1,0:T(8,128)S(1)} %get-tuple-element.175), channel_id=1, source_target_pairs={{0,1},{1,0},{2,3},{3,2},{4,5},{5,4},{6,7},{7,6},{8,9},{9,8},{10,11... | collective-permute-start | bytes 221192 | tf_op jit(solution)/shard_map/ppermute | solution.py:863
  79.2 7.2 %collective-permute-start.17 = (f32[72,256]{1,0:T(8,128)S(1)}, f32[72,256]{1,0:T(8,128)S(1)}, u32[]{:S(2)}, u32[]{:S(2)}) collective-permute-start(f32[72,256]{1,0:T(8,128)S(1)} %get-tuple-element.176), channel_id=1, source_target_pairs={{0,31},{1,2},{2,1},{3,4},{4,3},{5,6},{6,5},{7,24},{8,23},{9,10},{1... | collective-permute-start | bytes 221192 | tf_op jit(solution)/shard_map/ppermute | solution.py:864
  88.0 2.2 %collective-permute-start.18 = (f32[72,128]{1,0:T(8,128)S(1)}, f32[72,128]{1,0:T(8,128)S(1)}, u32[]{:S(2)}, u32[]{:S(2)}) collective-permute-start(f32[72,128]{1,0:T(8,128)S(1)} %get-tuple-element.185), channel_id=1, source_target_pairs={{0,1},{1,0},{2,3},{3,2},{4,5},{5,4},{6,7},{7,6},{8,9},{9,8},{10,11... | collective-permute-start | bytes 110600 | tf_op jit(solution)/shard_map/ppermute | solution.py:863
  88.0 7.3 %collective-permute-start.19 = (f32[72,128]{1,0:T(8,128)S(1)}, f32[72,128]{1,0:T(8,128)S(1)}, u32[]{:S(2)}, u32[]{:S(2)}) collective-permute-start(f32[72,128]{1,0:T(8,128)S(1)} %get-tuple-element.186), channel_id=1, source_target_pairs={{0,15},{1,2},{2,1},{3,4},{4,3},{5,6},{6,5},{7,8},{8,7},{9,10},{10,... | collective-permute-start | bytes 110600 | tf_op jit(solution)/shard_map/ppermute | solution.py:864
  97.1 4.4 %collective-permute-start.20 = (f32[152,128]{1,0:T(8,128)S(1)}, f32[152,128]{1,0:T(8,128)S(1)}, u32[]{:S(2)}, u32[]{:S(2)}) collective-permute-start(f32[152,128]{1,0:T(8,128)S(1)} %get-tuple-element.193), channel_id=1, source_target_pairs={{0,16},{1,17},{2,18},{3,19},{4,20},{5,21},{6,22},{7,23},{8,24},{9,... | collective-permute-start | bytes 233480 | tf_op jit(solution)/shard_map/ppermute | solution.py:863
  97.2 6.6 %collective-permute-start.21 = (f32[152,128]{1,0:T(8,128)S(1)}, f32[152,128]{1,0:T(8,128)S(1)}, u32[]{:S(2)}, u32[]{:S(2)}) collective-permute-start(f32[152,128]{1,0:T(8,128)S(1)} %get-tuple-element.194), channel_id=1, source_target_pairs={{0,112},{1,113},{2,114},{3,115},{4,116},{5,117},{6,118},{7,119},{8... | collective-permute-start | bytes 233480 | tf_op jit(solution)/shard_map/ppermute | solution.py:864
  103.9 4.2 %collective-permute-start.22 = (f32[72,128]{1,0:T(8,128)S(1)}, f32[72,128]{1,0:T(8,128)S(1)}, u32[]{:S(2)}, u32[]{:S(2)}) collective-permute-start(f32[72,128]{1,0:T(8,128)S(1)} %get-tuple-element.197.refs_5_), channel_id=1, source_target_pairs={{0,1},{1,0},{2,3},{3,2},{4,5},{5,4},{6,7},{7,6},{8,9},{9,8},{10,11... | collective-permute-start | bytes 110600 | tf_op jit(solution)/shard_map/ppermute | solution.py:863
  104.0 7.1 %collective-permute-start.23 = (f32[72,128]{1,0:T(8,128)S(1)}, f32[72,128]{1,0:T(8,128)S(1)}, u32[]{:S(2)}, u32[]{:S(2)}) collective-permute-start(f32[72,128]{1,0:T(8,128)S(1)} %get-tuple-element.198), channel_id=1, source_target_pairs={{0,15},{1,2},{2,1},{3,4},{4,3},{5,6},{6,5},{7,8},{8,7},{9,10},{10,... | collective-permute-start | bytes 110600 | tf_op jit(solution)/shard_map/ppermute | solution.py:864

commit v6 on v5

--- a/solution.py
+++ b/solution.py
@@ -61,9 +61,7 @@
 
 class Coef:
     def __init__(self, ref, width=LANES):
-        self.mid = jnp.broadcast_to(ref[:, 0:1], (Z, width))
-        self.up = jnp.broadcast_to(ref[:, 1:2], (Z, width))
-        self.down = jnp.broadcast_to(ref[:, 2:3], (Z, width))
+        self.mid, self.up, self.down = [jnp.concatenate([ref[k]] * (width // LANES), axis=1) for k in range(3)]
 
 
 def residual(co, f, c, v, beside):
@@ -207,18 +205,22 @@
     down[0:Z, :] = out_down
 
 
-def merge_y(lo, hi, flags, up, down):
+def relay_order(lo, hi, f0, f1):
+    up = [lo[3], lo[1], hi[1], hi[3], jnp.where(f0, lo[2], lo[3]), jnp.where(f1, hi[0], hi[1])]
+    down = [lo[2], lo[0], hi[0], hi[2], jnp.where(f0, lo[3], lo[2]), jnp.where(f1, hi[1], hi[0])]
+    return up, down
+
+
+def relayed(lo, hi, flags):
+    lo = [lo[4 + k : 5 + k, :] for k in range(4)]
+    hi = [hi[4 + k : 5 + k, :] for k in range(4)]
+    up, down = relay_order(lo, hi, flags[0:1, :] > 0.5, flags[1:2, :] > 0.5)
+    two = jnp.zeros((2, LANES), F32)
+    rows = [*down, two, jnp.zeros((104, LANES), F32), *up, two, jnp.zeros((8, LANES), F32)]
+    turned = jnp.concatenate(rows, axis=0).T[0:Z, :]
     lane = zl()
-    f0, f1 = flag_row(flags, 0) > 0.5, flag_row(flags, 1) > 0.5
-
-    def fill(part, values):
-        for k, value in enumerate(values):
-            part = jnp.where(lane == 112 + k, value, part)
-        return part
-
-    up_new = fill(up, [lo[3], lo[1], hi[1], hi[3], jnp.where(f0, lo[2], lo[3]), jnp.where(f1, hi[0], hi[1])])
-    down_new = fill(down, [lo[2], lo[0], hi[0], hi[2], jnp.where(f0, lo[3], lo[2]), jnp.where(f1, hi[1], hi[0])])
-    return up_new, down_new
+    inside = (lane >= 112) & (lane < 118)
+    return jnp.where(inside, turned, 0.0), jnp.where(inside, roll(turned, 112), 0.0)
 
 
 def odd_lanes():
@@ -268,32 +270,33 @@
     dn, un = halo.dn, halo.un
 
     def beside_row(edge, second, mine, low, high):
-        left = jnp.where(lane == 0, low, roll(edge, 1))
-        right = jnp.where(lane == ty - 1, high, roll(edge, -1))
+        left = jnp.where(lane == 0, roll(low, -112), roll(edge, 1))
+        right = jnp.where(lane == ty - 1, roll(high, ty - 113), roll(edge, -1))
         return second + mine + left + right
 
-    def choose(flags, k, first, other):
-        return jnp.where(flag_row(flags, k) > 0.5, other, first)
+    def choose(flags, k, x, place):
+        x = roll(x, 112 - place)
+        return jnp.where(flag_row(flags, k) > 0.5, roll(x, -1), x)
 
     b_lo = beside_row(
         halo.lo,
         halo.lo2,
         turn_row(geom, row_of(geom, v, 0), flag_row(fl.lo, 1)),
-        choose(fl.lo, 2, col(dn, 112), col(dn, 113)),
-        choose(fl.lo, 3, col(un, 112), col(un, 113)),
+        choose(fl.lo, 2, dn, 112),
+        choose(fl.lo, 3, un, 112),
     )
     b_hi = beside_row(
         halo.hi,
         halo.hi2,
         turn_row(geom, row_of(geom, v, tx - 1), flag_row(fl.hi, 0)),
-        choose(fl.hi, 2, col(dn, 114), col(dn, 115)),
-        choose(fl.hi, 3, col(un, 114), col(un, 115)),
+        choose(fl.hi, 2, dn, 114),
+        choose(fl.hi, 3, un, 114),
     )
     edge = halo.sides()
     mine = turn_sides(geom, columns, flag_row(fl.dn, 3), flag_row(fl.un, 2))
-    below = jnp.where(lane == 1, col(dn, 116), jnp.where(lane == 0, col(un, 116), roll(edge, 2)))
+    below = jnp.where(lane == 1, roll(dn, -115), jnp.where(lane == 0, roll(un, -116), roll(edge, 2)))
     last = 2 * (tx - 1)
-    above = jnp.where(lane == last + 1, col(dn, 117), jnp.where(lane == last, col(un, 117), roll(edge, -2)))
+    above = jnp.where(lane == last + 1, roll(dn, last - 116), jnp.where(lane == last, roll(un, last - 117), roll(edge, -2)))
     b_sides = halo.seconds() + mine + below + above
     r_lo = residual(co, f_lo, c_lo, halo.lo, b_lo)
     r_hi = residual(co, f_hi, c_hi, halo.hi, b_hi)
@@ -745,7 +748,7 @@
     strip_message(strip, v, None, strip_ends(strip, v, flags), up, down)
 
 
-def again2_kernel(f, c, w, vz, flags, v, e, tile_v, low, high, part_low, part_high, yup, ydown, twice, g, part):
+def again2_kernel(f, c, w, vz, flags, v, e, tile_v, xlo, xhi, own, low, high, part_low, part_high, yup, ydown, twice, g, part):
     strip = STRIPS[2]
     a, b = iota2(LANES, LANES)
     for m in range(3):
@@ -762,6 +765,9 @@
     part_low[...] = strip_column(strip, twice, 0, 0, zero)
     part_high[...] = strip_column(strip, twice, strip[1] - 1, 0, zero)
     put_y(GEOM[1], tile_v, None, yup, ydown)
+    add_up, add_down = relayed(tail_of(GEOM[1], xlo, 2), tail_of(GEOM[1], xhi, 2), own)
+    yup[...] = yup[...] + add_up
+    ydown[...] = ydown[...] + add_down
 
 
 def alone3_kernel(f, c, w, vz, flags, low, high, part_low, part_high, twice, v, part):
@@ -792,10 +798,9 @@
 
 
 def post_strip_kernel(
-    w, vz, flags, dn, un, first_column, last_column, c_low, c_high, part_low, part_high, gdn, gun, xlo, xhi, own, yup, ydown, terms, up, down
+    w, vz, flags, dn, un, first_column, last_column, c_low, c_high, part_low, part_high, gdn, gun, own, yup, ydown, terms, up, down
 ):
     strip = STRIPS[2]
-    fine = GEOM[1]
     width = strip[2]
     winv = w[...].astype(BF16)
     co = Coef(vz, width)
@@ -812,18 +817,23 @@
     for k in range(4):
         terms[k] = d[k]
     low, high = part_low[...] + d[0], part_high[...] + d[3]
-    extras = []
-    for ref, step in ((xlo, -1), (xhi, 1)):
-        near, far = tile_lanes(low, step), tile_lanes(high, step)
-        adds = (col(near, 0), col(far, 0), col(near, 5), col(far, 5))
-        extras.append([x + y for x, y in zip(corner_columns(tail_of(fine, ref, 2)), adds)])
-    group = zl() // 4
-    near, far = tile_lanes(low, 0), tile_lanes(high, 0)
-    add_up = add_down = jnp.zeros((Z, LANES), F32)
-    for m in range(6):
-        add_up = jnp.where(group == m, col(far, m), add_up)
-        add_down = jnp.where(group == m, col(near, m), add_down)
-    up[...], down[...] = merge_y(*extras, own, yup[...] + add_up, ydown[...] + add_down)
+    lane = zl()
+
+    def tile_corners(step):
+        first_lanes, last_lanes = tile_lanes(low, step), tile_lanes(high, step)
+        return [roll(x, 112 - place) for x, place in ((first_lanes, 0), (last_lanes, 0), (first_lanes, 5), (last_lanes, 5))]
+
+    f0, f1 = flag_row(own, 0) > 0.5, flag_row(own, 1) > 0.5
+    a, b = iota2(LANES, LANES)
+    spread = jnp.where((b < 24) & (a == b // 4), 1.0, 0.0)
+    add_up = lane_dot(tile_lanes(high, 0), spread)
+    add_down = lane_dot(tile_lanes(low, 0), spread)
+    to_up, to_down = relay_order(tile_corners(-1), tile_corners(1), f0, f1)
+    for k in range(6):
+        add_up = jnp.where(lane == 112 + k, roll(to_up[k], k), add_up)
+        add_down = jnp.where(lane == 112 + k, roll(to_down[k], k), add_down)
+    up[...] = yup[...] + add_up
+    down[...] = ydown[...] + add_down
 
 
 def again1_kernel(f, c, w, vz, v, twice, terms, xlo, xhi, g, part, columns, lo_out, hi_out, tile):
@@ -953,8 +963,8 @@
     high = jnp.sum(jnp.where((b == a + 1) & (a < NZ), coef, 0.0), axis=1, keepdims=True)
     low = jnp.sum(jnp.where((b == a) & (a < NZ), coef, 0.0), axis=1, keepdims=True)
     columns = [jnp.broadcast_to(x * 0.0625, (Z, LANES)) for x in (4.0 + high + low, high, low)]
-    lane = zl()
-    vz[...] = jnp.where(lane == 0, columns[0], jnp.where(lane == 1, columns[1], columns[2]))
+    for k in range(3):
+        vz[k] = columns[k]
     up[...] = jnp.zeros(up.shape, F32)
     down[...] = jnp.zeros(down.shape, F32)
     for copy in copies[2:]:
@@ -1009,21 +1019,11 @@
     geom = GEOM[level]
 
     def kernel(xlo, xhi, flags, yup, ydown, up, down):
-        lo, hi = tail_of(geom, xlo, count), tail_of(geom, xhi, count)
-        lo = [lo[4 + k : 5 + k, :] for k in range(4)]
-        hi = [hi[4 + k : 5 + k, :] for k in range(4)]
-        f0, f1 = flags[0:1, :] > 0.5, flags[1:2, :] > 0.5
-        to_up = [lo[3], lo[1], hi[1], hi[3], jnp.where(f0, lo[2], lo[3]), jnp.where(f1, hi[0], hi[1])]
-        to_down = [lo[2], lo[0], hi[0], hi[2], jnp.where(f0, lo[3], lo[2]), jnp.where(f1, hi[1], hi[0])]
-        two = jnp.zeros((2, LANES), F32)
-        rows = [*to_down, two, jnp.zeros((104, LANES), F32), *to_up, two, jnp.zeros((8, LANES), F32)]
-        turned = jnp.concatenate(rows, axis=0).T[0:Z, :]
-        lane = zl()
-        inside = (lane >= 112) & (lane < 118)
+        add_up, add_down = relayed(tail_of(geom, xlo, count), tail_of(geom, xhi, count), flags)
         up[...] = yup[...]
         down[...] = ydown[...]
-        up[0:Z, :] = jnp.where(inside, turned, yup[0:Z, :])
-        down[0:Z, :] = jnp.where(inside, roll(turned, 112), ydown[0:Z, :])
+        up[0:Z, :] = yup[0:Z, :] + add_up
+        down[0:Z, :] = ydown[0:Z, :] + add_down
 
     return kernel
 
@@ -1173,7 +1173,7 @@
     xs = x_shape(0, 3)
     up, down, own, vz = pl.pallas_call(
         by_swaps(open_kernel, 4, 4, (), ((0, "gx"),)),
-        out_shape=[jax.ShapeDtypeStruct(x, F32) for x in (xs, xs, (8, LANES), ys)],
+        out_shape=[jax.ShapeDtypeStruct(x, F32) for x in (xs, xs, (8, LANES), (3, Z, LANES))],
         in_specs=[ANY] * 4,
         out_specs=[VMEM] * 4,
         scratch_shapes=[pltpu.VMEM((NZ, 2, LANES), F32)] * 2
@@ -1274,14 +1274,14 @@
     )
     side = swap(up, down, "gy", True)
     first, last, part_low, part_high, yup, ydown, twice = call(
-        again2_kernel, [m2] * 4 + [ys, ys, s2], [f2, c2, w[2], vz, fl2, v2, e3, v1], [s2, s2], name="again2"
+        again2_kernel, [m2] * 4 + [ys, ys, s2], [f2, c2, w[2], vz, fl2, v2, e3, v1, v1_lo, v1_hi, own], [s2, s2], name="again2", got=((8, "gx"),)
     )
     terms, up, down = call(
         post_strip_kernel,
         [(4, *m2), ys, ys],
-        [w[2], vz, fl2, *side2, first, last, *c_sides[:2], part_low, part_high, *side, v1_lo, v1_hi, own, yup, ydown],
+        [w[2], vz, fl2, *side2, first, last, *c_sides[:2], part_low, part_high, *side, own, yup, ydown],
         name="post2",
-        got=((3, "gy"), (11, "gy"), (13, "gx")),
+        got=((3, "gy"), (11, "gy")),
         send=((1, "gy"),),
     )
     side = swap(up, down, "gy")

time: 114 us -> 113 us (level)
  transfers between devices with their start and end apart: 24 -> 24, of which waited for: 11 -> 11; matrix products, arithmetic and copies ran while one was open for 1% -> 1% of each run, Pallas kernels for 16% -> 15%
where the time goes in v6:
time: 113 us
  starting transfers between devices  42.1 us (37%)
  Pallas kernels  32.3 us (29%)
  waiting for transfers between devices  21.3 us (19%)
  blocking collectives  15.4 us (14%)
  local copies, waits for them, and re-layouts  1.6 us (1%)
    ppermute x12, starting transfers between devices, swap(): lax.ppermute(second, both, swap_pairs(axis, 1, nearest))  39.6 us
    pallas_call x23, Pallas kernels, call(): pl.pallas_call(by_swaps(kernel, len(args), len(outs), got, send), out_sha...  30.3 us
    ppermute x12, waiting for transfers between devices, swap(): lax.ppermute(second, both, swap_pairs(axis, 1, nearest))  20.7 us
    all_to_all x1, blocking collectives, on_device(): chunks = lax.all_to_all(chunks, 'gx', 0, 0)  15.4 us
    ppermute x12, starting transfers between devices, swap(): lax.ppermute(first, both, swap_pairs(axis, 0, nearest))  2.53 us
  transfers between devices with their start and end apart: 24, of which 11 were waited for; matrix products, arithmetic and copies ran while one was open for 1% of the time, Pallas kernels for 15%

profile of v6, /device:TPU:0, one launch (start us, length us, event | category | flops | bytes accessed | tf_op | source)
XLA Modules:
  0.0 113.2 jit_solution(9090679670022956578)
XLA Ops:
  0.0 2.0 %open.1 = (f32[224,128]{1,0:T(8,128)}, f32[224,128]{1,0:T(8,128)}, f32[8,128]{1,0:T(8,128)}, f32[3,72,128]{2,1,0:T(8,128)}) custom-call(f32[70,24,128]{2,1,0:T(8,128)} %refs_0_.1, f32[70,24,128]{2,1,0:T(8,128)} %refs_1_.1, f32[1,71]{1,0:T(1,128)} %bitcast.9, s32[1,4]{1,0:T(1,128)} %bitcast.10), custom_call_target="tpu_custom_call" | custom-call | tf_op jit(solution)/shard_map/open/pallas_call | solution.py:1174
  2.0 1.7 %collective-permute-start = (f32[224,128]{1,0:T(8,128)}, f32[224,128]{1,0:T(8,128)S(1)}, u32[]{:S(2)}, u32[]{:S(2)}) collective-permute-start(f32[224,128]{1,0:T(8,128)} %get-tuple-element.107), channel_id=1, source_target_pairs={{0,16},{1,17},{2,18},{3,19},{4,20},{5,21},{6,22},{7,23},{8,24},{9,... | collective-permute-start | bytes 344072 | tf_op jit(solution)/shard_map/ppermute | solution.py:873
  3.8 2.6 %collective-permute-start.1 = (f32[224,128]{1,0:T(8,128)}, f32[224,128]{1,0:T(8,128)S(1)}, u32[]{:S(2)}, u32[]{:S(2)}) collective-permute-start(f32[224,128]{1,0:T(8,128)} %get-tuple-element.108), channel_id=1, source_target_pairs={{0,112},{1,113},{2,114},{3,115},{4,116},{5,117},{6,118},{7,119},{8... | collective-permute-start | bytes 344072 | tf_op jit(solution)/shard_map/ppermute | solution.py:874
  8.0 2.5 %side.1 = (f32[24,72,128]{2,1,0:T(8,128)S(1)}, f32[24,72,128]{2,1,0:T(8,128)S(1)}, f32[72,216]{1,0:T(8,128)S(1)}, f32[72,216]{1,0:T(8,128)S(1)}, f32[72,216]{1,0...) custom-call(f32[1680,128]{1,0:T(8,128)S(1)} %bitcast.6, ...), custom_call_target="tpu_custom_call" | custom-call | tf_op jit(solution)/shard_map/side/pallas_call | solution.py:921
  11.1 6.5 %collective-permute-start.3 = (f32[80,128]{1,0:T(8,128)S(1)}, f32[80,128]{1,0:T(8,128)S(1)}, u32[]{:S(2)}, u32[]{:S(2)}) collective-permute-start(f32[80,128]{1,0:T(8,128)S(1)} %get-tuple-element.112), channel_id=1, source_target_pairs={{0,15},{1,2},{2,1},{3,4},{4,3},{5,6},{6,5},{7,8},{8,7},{9,10},{10,... | collective-permute-start | bytes 122888 | tf_op jit(solution)/shard_map/ppermute | solution.py:874
  17.6 1.7 %collective-permute-done.3.refs_8_ = f32[80,128]{1,0:T(8,128)S(1)} collective-permute-done((f32[80,128]{1,0:T(8,128)S(1)}, f32[80,128]{1,0:T(8,128)S(1)}, u32[]{:S(2)}, u32[]{:S(2)}) %collective-permute-start.3) | collective-permute-done | bytes 40992 | tf_op jit(solution)/shard_map/ppermute | solution.py:874
  19.3 1.7 %pre0.1 = (f32[120,128]{1,0:T(8,128)S(1)}, f32[120,128]{1,0:T(8,128)S(1)}, f32[3,72,128]{2,1,0:T(8,128)S(1)}, f32[3,72,128]{2,1,0:T(8,128)S(1)}) custom-call(f32[24,72,128]{2,1,0:T(8,128)S(1)} %get-tuple-element.104.refs_0_, f32[24,72,128]{2,1,0:T(8,128)S(1)} %get-tuple-element.105.refs_1_, f32[72,216]{1,0:T(8,128)S(1)} %get-tuple-element.106.refs_2_, ...), custom_call_target="tpu_custom_call" | custom-call | tf_op jit(solution)/shard_map/pre0/pallas_call | solution.py:921
  21.0 3.4 %collective-permute-start.5 = (f32[120,128]{1,0:T(8,128)S(1)}, f32[120,128]{1,0:T(8,128)S(1)}, u32[]{:S(2)}, u32[]{:S(2)}) collective-permute-start(f32[120,128]{1,0:T(8,128)S(1)} %get-tuple-element.122), channel_id=1, source_target_pairs={{0,112},{1,113},{2,114},{3,115},{4,116},{5,117},{6,118},{7,119},{8... | collective-permute-start | bytes 184328 | tf_op jit(solution)/shard_map/ppermute | solution.py:874
  24.4 2.1 %mid1.1 = (f32[24,72,128]{2,1,0:T(8,128)S(1)}, f32[6,72,128]{2,1,0:T(8,128)S(1)}, f32[6,72,128]{2,1,0:T(8,128)S(1)}, f32[6,72,128]{2,1,0:T(8,128)S(1)}, f32[72,1...) custom-call(f32[24,72,128]{2,1,0:T(8,128)S(1)} %get-tuple-element.104.refs_0_, ...), custom_call_target="tpu_custom_call" | custom-call | tf_op jit(solution)/shard_map/mid1/pallas_call | solution.py:921
  27.7 4.5 %collective-permute-start.7 = (f32[80,128]{1,0:T(8,128)S(1)}, f32[80,128]{1,0:T(8,128)S(1)}, u32[]{:S(2)}, u32[]{:S(2)}) collective-permute-start(f32[80,128]{1,0:T(8,128)S(1)} %get-tuple-element.126), channel_id=1, source_target_pairs={{0,15},{1,2},{2,1},{3,4},{4,3},{5,6},{6,5},{7,8},{8,7},{9,10},{10,... | collective-permute-start | bytes 122888 | tf_op jit(solution)/shard_map/ppermute | solution.py:874
  32.2 2.6 %collective-permute-done.7.refs_8_ = f32[80,128]{1,0:T(8,128)S(1)} collective-permute-done((f32[80,128]{1,0:T(8,128)S(1)}, f32[80,128]{1,0:T(8,128)S(1)}, u32[]{:S(2)}, u32[]{:S(2)}) %collective-permute-start.7) | collective-permute-done | bytes 40992 | tf_op jit(solution)/shard_map/ppermute | solution.py:874
  34.8 2.0 %pre1.1 = (f32[6,72,128]{2,1,0:T(8,128)S(1)}, f32[80,128]{1,0:T(8,128)S(1)}, f32[80,128]{1,0:T(8,128)S(1)}, f32[8,224,128]{2,1,0:T(8,128)S(1)}) custom-call(f32[6,72,128]{2,1,0:T(8,128)S(1)} %get-tuple-element.120.refs_0_, f32[6,72,128]{2,1,0:T(8,128)S(1)} %get-tuple-element.116.refs_12_.refs_7_.refs_1_, f32[72,216]{1,0:T(8,128)S(1)} %get-tuple-element.119.refs_6_.refs_2_, ...), custom_call_target="tpu_custom_call" | custom-call | tf_op jit(solution)/shard_map/pre1/pallas_call | solution.py:921
  36.9 15.4 %all_to_all.5.refs_0_ = f32[8,224,128]{2,1,0:T(8,128)S(1)} all-to-all(f32[8,224,128]{2,1,0:T(8,128)S(1)} %get-tuple-element.132), channel_id=1, replica_groups=mesh['gx'=8,'gy'=16] {'gx'}, dimensions={0} | all-to-all | bytes 1835008 | tf_op jit(solution)/shard_map/all_to_all | solution.py:1232
  53.6 4.5 %collective-permute-start.9 = (f32[80,256]{1,0:T(8,128)S(1)}, f32[80,256]{1,0:T(8,128)S(1)}, u32[]{:S(2)}, u32[]{:S(2)}) collective-permute-start(f32[80,256]{1,0:T(8,128)S(1)} %get-tuple-element.141), channel_id=1, source_target_pairs={{0,31},{1,2},{2,1},{3,4},{4,3},{5,6},{6,5},{7,24},{8,23},{9,10},{1... | collective-permute-start | bytes 245768 | tf_op jit(solution)/shard_map/ppermute | solution.py:874
  58.4 1.9 %alone2.1 = (f32[6,72,256]{2,1,0:T(8,128)S(1)}, f32[72,256]{1,0:T(8,128)S(1)}, f32[72,256]{1,0:T(8,128)S(1)}, f32[3,72,128]{2,1,0:T(8,128)S(1)}, f32[72,128]{1,0:T(8,128)S(1)}, /*index=5*/f32[72,128]{1,0:T(8,128)S(1)}) custom-call(f32[6,72,256]{2,1,0:T(8,128)S(1)} %get-tuple-element.133.refs_0_, f32[6,72,256]{2,1,0:T(8,128)S(1)} %get-tuple-element.134.refs_0_.refs_1_, ...), custom_call_target="tpu_custom_call" | custom-call | tf_op jit(solution)/shard_map/alone2/pallas_call | solution.py:921
  62.4 4.3 %collective-permute-start.11 = (f32[80,128]{1,0:T(8,128)S(1)}, f32[80,128]{1,0:T(8,128)S(1)}, u32[]{:S(2)}, u32[]{:S(2)}) collective-permute-start(f32[80,128]{1,0:T(8,128)S(1)} %get-tuple-element.153), channel_id=1, source_target_pairs={{0,31},{1,2},{2,1},{3,4},{4,3},{5,6},{6,5},{7,24},{8,23},{9,10},{1... | collective-permute-start | bytes 122888 | tf_op jit(solution)/shard_map/ppermute | solution.py:874
  66.7 2.6 %collective-permute-start.15 = (f32[80,128]{1,0:T(8,128)S(1)}, f32[80,128]{1,0:T(8,128)S(1)}, u32[]{:S(2)}, u32[]{:S(2)}) collective-permute-start(f32[80,128]{1,0:T(8,128)S(1)} %get-tuple-element.168), channel_id=1, source_target_pairs={{0,112},{1,113},{2,114},{3,115},{4,116},{5,117},{6,118},{7,119},{8... | collective-permute-start | bytes 122888 | tf_op jit(solution)/shard_map/ppermute | solution.py:874
  71.5 3.1 %collective-permute-start.13 = (f32[72,128]{1,0:T(8,128)S(1)}, f32[72,128]{1,0:T(8,128)S(1)}, u32[]{:S(2)}, u32[]{:S(2)}) collective-permute-start(f32[72,128]{1,0:T(8,128)S(1)} %get-tuple-element.162), channel_id=1, source_target_pairs={{0,31},{1,2},{2,1},{3,4},{4,3},{5,6},{6,5},{7,24},{8,23},{9,10},{1... | collective-permute-start | bytes 110600 | tf_op jit(solution)/shard_map/ppermute | solution.py:874
  76.1 2.2 %collective-permute-done.13.refs_3_ = f32[72,128]{1,0:T(8,128)S(1)} collective-permute-done((f32[72,128]{1,0:T(8,128)S(1)}, f32[72,128]{1,0:T(8,128)S(1)}, u32[]{:S(2)}, u32[]{:S(2)}) %collective-permute-start.13) | collective-permute-done | bytes 36896 | tf_op jit(solution)/shard_map/ppermute | solution.py:874
  79.2 3.1 %collective-permute-start.17 = (f32[72,256]{1,0:T(8,128)S(1)}, f32[72,256]{1,0:T(8,128)S(1)}, u32[]{:S(2)}, u32[]{:S(2)}) collective-permute-start(f32[72,256]{1,0:T(8,128)S(1)} %get-tuple-element.176), channel_id=1, source_target_pairs={{0,31},{1,2},{2,1},{3,4},{4,3},{5,6},{6,5},{7,24},{8,23},{9,10},{1... | collective-permute-start | bytes 221192 | tf_op jit(solution)/shard_map/ppermute | solution.py:874
  82.3 2.2 %again2.1 = (f32[72,256]{1,0:T(8,128)S(1)}, f32[72,256]{1,0:T(8,128)S(1)}, f32[72,256]{1,0:T(8,128)S(1)}, f32[72,256]{1,0:T(8,128)S(1)}, f32[72,128]{1,0:T(8,128...) custom-call(f32[6,72,256]{2,1,0:T(8,128)S(1)} %get-tuple-element.133.refs_0_, ...), custom_call_target="tpu_custom_call" | custom-call | tf_op jit(solution)/shard_map/again2/pallas_call | solution.py:921
  84.5 1.9 %collective-permute-done.17.refs_12_ = f32[72,256]{1,0:T(8,128)S(1)} collective-permute-done((f32[72,256]{1,0:T(8,128)S(1)}, f32[72,256]{1,0:T(8,128)S(1)}, u32[]{:S(2)}, u32[]{:S(2)}) %collective-permute-start.17) | collective-permute-done | bytes 73760 | tf_op jit(solution)/shard_map/ppermute | solution.py:874
  86.4 1.4 %post2.1 = (f32[4,72,256]{2,1,0:T(8,128)S(1)}, f32[72,128]{1,0:T(8,128)S(1)}, f32[72,128]{1,0:T(8,128)S(1)}) custom-call(f32[72,216]{1,0:T(8,128)S(1)} %get-tuple-element.135.refs_2_.refs_0_, f32[3,72,128]{2,1,0:T(8,128)S(1)} %copy-done, f32[8,256]{1,0:T(8,128)S(1)} %get-tuple-element.136.refs_1_.refs_4_.refs_2_, ...), custom_call_target="tpu_custom_call" | custom-call | tf_op jit(solution)/shard_map/post2/pallas_call | solution.py:921
  88.2 1.7 %again1.1 = (f32[6,72,128]{2,1,0:T(8,128)S(1)}, f32[6,72,128]{2,1,0:T(8,128)S(1)}, f32[72,128]{1,0:T(8,128)S(1)}, f32[72,128]{1,0:T(8,128)S(1)}, f32[72,128]{1,0:T(8,128)S(1)}) custom-call(f32[6,72,128]{2,1,0:T(8,128)S(1)} %get-tuple-element.120.refs_0_, f32[6,72,128]{2,1,0:T(8,128)S(1)} %get-tuple-element.116.refs_12_.refs_7_.refs_1_, ...), custom_call_target="tpu_custom_call" | custom-call | tf_op jit(solution)/shard_map/again1/pallas_call | solution.py:921
  89.9 5.3 %collective-permute-done.19.refs_15_ = f32[72,128]{1,0:T(8,128)S(1)} collective-permute-done((f32[72,128]{1,0:T(8,128)S(1)}, f32[72,128]{1,0:T(8,128)S(1)}, u32[]{:S(2)}, u32[]{:S(2)}) %collective-permute-start.19) | collective-permute-done | bytes 36896 | tf_op jit(solution)/shard_map/ppermute | solution.py:874
  95.2 1.7 %post1.1 = (f32[6,72,128]{2,1,0:T(8,128)S(1)}, f32[152,128]{1,0:T(8,128)S(1)}, f32[152,128]{1,0:T(8,128)S(1)}) custom-call(f32[6,72,128]{2,1,0:T(8,128)S(1)} %get-tuple-element.120.refs_0_, f32[6,72,128]{2,1,0:T(8,128)S(1)} %get-tuple-element.116.refs_12_.refs_7_.refs_1_, f32[72,216]{1,0:T(8,128)S(1)} %get-tuple-element.119.refs_6_.refs_2_, ...), custom_call_target="tpu_custom_call" | custom-call | tf_op jit(solution)/shard_map/post1/pallas_call | solution.py:921
  97.0 1.7 %collective-permute-start.21 = (f32[152,128]{1,0:T(8,128)S(1)}, f32[152,128]{1,0:T(8,128)S(1)}, u32[]{:S(2)}, u32[]{:S(2)}) collective-permute-start(f32[152,128]{1,0:T(8,128)S(1)} %get-tuple-element.194), channel_id=1, source_target_pairs={{0,112},{1,113},{2,114},{3,115},{4,116},{5,117},{6,118},{7,119},{8... | collective-permute-start | bytes 233480 | tf_op jit(solution)/shard_map/ppermute | solution.py:874
  98.6 2.2 %again0.1 = (f32[24,72,128]{2,1,0:T(8,128)S(1)}, f32[24,72,128]{2,1,0:T(8,128)S(1)}, f32[72,128]{1,0:T(8,128)S(1)}, f32[72,128]{1,0:T(8,128)S(1)}, f32[72,128]{1,0:T(8,128)S(1)}, /*index=5*/f32[72,128]{1,0:T(8,128)S(1)}) custom-call(f32[24,72,128]{2,1,0:T(8,128)S(1)} %get-tuple-element.104.refs_0_, f32[24,72,128]{2,1,0:T(8,128)S(1)} %get-tuple-element.105.refs_1_, ...), custom_call_target="tpu_custom_call" | custom-call | tf_op jit(solution)/shard_map/again0/pallas_call | solution.py:921
  101.4 2.2 %collective-permute-done.21.refs_1_.refs_14_ = f32[152,128]{1,0:T(8,128)S(1)} collective-permute-done((f32[152,128]{1,0:T(8,128)S(1)}, f32[152,128]{1,0:T(8,128)S(1)}, u32[]{:S(2)}, u32[]{:S(2)}) %collective-permute-start.21) | collective-permute-done | bytes 77856 | tf_op jit(solution)/shard_map/ppermute | solution.py:874
  103.8 3.1 %collective-permute-start.23 = (f32[72,128]{1,0:T(8,128)S(1)}, f32[72,128]{1,0:T(8,128)S(1)}, u32[]{:S(2)}, u32[]{:S(2)}) collective-permute-start(f32[72,128]{1,0:T(8,128)S(1)} %get-tuple-element.198), channel_id=1, source_target_pairs={{0,15},{1,2},{2,1},{3,4},{4,3},{5,6},{6,5},{7,8},{8,7},{9,10},{10,... | collective-permute-start | bytes 110600 | tf_op jit(solution)/shard_map/ppermute | solution.py:874
  107.9 2.9 %collective-permute-done.23.refs_16_ = f32[72,128]{1,0:T(8,128)S(1)} collective-permute-done((f32[72,128]{1,0:T(8,128)S(1)}, f32[72,128]{1,0:T(8,128)S(1)}, u32[]{:S(2)}, u32[]{:S(2)}) %collective-permute-start.23) | collective-permute-done | bytes 36896 | tf_op jit(solution)/shard_map/ppermute | solution.py:874
  110.9 2.3 %post0.1 = f32[1680,128]{1,0:T(8,128)} custom-call(f32[24,72,128]{2,1,0:T(8,128)S(1)} %get-tuple-element.104.refs_0_, f32[24,72,128]{2,1,0:T(8,128)S(1)} %get-tuple-element.105.refs_1_, f32[72,216]{1,0:T(8,128)S(1)} %get-tuple-element.106.refs_2_, f32[3,72,128]{2,1,0:T(8,128)S(1)} %copy-done, f32[8,128]{1,0:T(8,128)S(1)} %copy-done.3, ...), custom_call_target="tpu_custom_call" | custom-call | tf_op jit(solution)/shard_map/post0/pallas_call | solution.py:921
  (50 shorter events, 14.0 us)
Async XLA Ops:
  0.0 7.4 %copy-start.1 = (f32[70,24,128]{2,1,0:T(8,128)S(1)}, f32[70,24,128]{2,1,0:T(8,128)}, u32[]{:S(2)}) copy-start(f32[70,24,128]{2,1,0:T(8,128)} %refs_0_.1) | copy-start | bytes 2580484
  0.0 7.4 %copy-start.2 = (f32[70,24,128]{2,1,0:T(8,128)S(1)}, f32[70,24,128]{2,1,0:T(8,128)}, u32[]{:S(2)}) copy-start(f32[70,24,128]{2,1,0:T(8,128)} %refs_1_.1) | copy-start | bytes 2580484
  2.0 8.5 %collective-permute-start = (f32[224,128]{1,0:T(8,128)}, f32[224,128]{1,0:T(8,128)S(1)}, u32[]{:S(2)}, u32[]{:S(2)}) collective-permute-start(f32[224,128]{1,0:T(8,128)} %get-tuple-element.107), channel_id=1, source_target_pairs={{0,16},{1,17},{2,18},{3,19},{4,20},{5,21},{6,22},{7,23},{8,24},{9,... | collective-permute-start | bytes 344072 | tf_op jit(solution)/shard_map/ppermute | solution.py:873
  3.8 7.1 %collective-permute-start.1 = (f32[224,128]{1,0:T(8,128)}, f32[224,128]{1,0:T(8,128)S(1)}, u32[]{:S(2)}, u32[]{:S(2)}) collective-permute-start(f32[224,128]{1,0:T(8,128)} %get-tuple-element.108), channel_id=1, source_target_pairs={{0,112},{1,113},{2,114},{3,115},{4,116},{5,117},{6,118},{7,119},{8... | collective-permute-start | bytes 344072 | tf_op jit(solution)/shard_map/ppermute | solution.py:874
  6.4 1.0 copy-start
  7.4 0.7 copy-start.3
  11.0 6.6 %collective-permute-start.2 = (f32[80,128]{1,0:T(8,128)S(1)}, f32[80,128]{1,0:T(8,128)S(1)}, u32[]{:S(2)}, u32[]{:S(2)}) collective-permute-start(f32[80,128]{1,0:T(8,128)S(1)} %get-tuple-element.111), channel_id=1, source_target_pairs={{0,1},{1,0},{2,3},{3,2},{4,5},{5,4},{6,7},{7,6},{8,9},{9,8},{10,11... | collective-permute-start | bytes 122888 | tf_op jit(solution)/shard_map/ppermute | solution.py:873
  11.1 8.2 %collective-permute-start.3 = (f32[80,128]{1,0:T(8,128)S(1)}, f32[80,128]{1,0:T(8,128)S(1)}, u32[]{:S(2)}, u32[]{:S(2)}) collective-permute-start(f32[80,128]{1,0:T(8,128)S(1)} %get-tuple-element.112), channel_id=1, source_target_pairs={{0,15},{1,2},{2,1},{3,4},{4,3},{5,6},{6,5},{7,8},{8,7},{9,10},{10,... | collective-permute-start | bytes 122888 | tf_op jit(solution)/shard_map/ppermute | solution.py:874
  21.0 5.6 %collective-permute-start.4 = (f32[120,128]{1,0:T(8,128)S(1)}, f32[120,128]{1,0:T(8,128)S(1)}, u32[]{:S(2)}, u32[]{:S(2)}) collective-permute-start(f32[120,128]{1,0:T(8,128)S(1)} %get-tuple-element.121), channel_id=1, source_target_pairs={{0,16},{1,17},{2,18},{3,19},{4,20},{5,21},{6,22},{7,23},{8,24},{9,... | collective-permute-start | bytes 184328 | tf_op jit(solution)/shard_map/ppermute | solution.py:873
  21.0 6.4 %collective-permute-start.5 = (f32[120,128]{1,0:T(8,128)S(1)}, f32[120,128]{1,0:T(8,128)S(1)}, u32[]{:S(2)}, u32[]{:S(2)}) collective-permute-start(f32[120,128]{1,0:T(8,128)S(1)} %get-tuple-element.122), channel_id=1, source_target_pairs={{0,112},{1,113},{2,114},{3,115},{4,116},{5,117},{6,118},{7,119},{8... | collective-permute-start | bytes 184328 | tf_op jit(solution)/shard_map/ppermute | solution.py:874
  27.6 4.6 %collective-permute-start.6 = (f32[80,128]{1,0:T(8,128)S(1)}, f32[80,128]{1,0:T(8,128)S(1)}, u32[]{:S(2)}, u32[]{:S(2)}) collective-permute-start(f32[80,128]{1,0:T(8,128)S(1)} %get-tuple-element.125), channel_id=1, source_target_pairs={{0,1},{1,0},{2,3},{3,2},{4,5},{5,4},{6,7},{7,6},{8,9},{9,8},{10,11... | collective-permute-start | bytes 122888 | tf_op jit(solution)/shard_map/ppermute | solution.py:873
  27.7 7.1 %collective-permute-start.7 = (f32[80,128]{1,0:T(8,128)S(1)}, f32[80,128]{1,0:T(8,128)S(1)}, u32[]{:S(2)}, u32[]{:S(2)}) collective-permute-start(f32[80,128]{1,0:T(8,128)S(1)} %get-tuple-element.126), channel_id=1, source_target_pairs={{0,15},{1,2},{2,1},{3,4},{4,3},{5,6},{6,5},{7,8},{8,7},{9,10},{10,... | collective-permute-start | bytes 122888 | tf_op jit(solution)/shard_map/ppermute | solution.py:874
  53.5 6.8 %collective-permute-start.8 = (f32[80,256]{1,0:T(8,128)S(1)}, f32[80,256]{1,0:T(8,128)S(1)}, u32[]{:S(2)}, u32[]{:S(2)}) collective-permute-start(f32[80,256]{1,0:T(8,128)S(1)} %get-tuple-element.140), channel_id=1, source_target_pairs={{0,1},{1,0},{2,3},{3,2},{4,5},{5,4},{6,7},{7,6},{8,9},{9,8},{10,11... | collective-permute-start | bytes 245768 | tf_op jit(solution)/shard_map/ppermute | solution.py:873
  53.6 7.4 %collective-permute-start.9 = (f32[80,256]{1,0:T(8,128)S(1)}, f32[80,256]{1,0:T(8,128)S(1)}, u32[]{:S(2)}, u32[]{:S(2)}) collective-permute-start(f32[80,256]{1,0:T(8,128)S(1)} %get-tuple-element.141), channel_id=1, source_target_pairs={{0,31},{1,2},{2,1},{3,4},{4,3},{5,6},{6,5},{7,24},{8,23},{9,10},{1... | collective-permute-start | bytes 245768 | tf_op jit(solution)/shard_map/ppermute | solution.py:874
  62.4 8.1 %collective-permute-start.10 = (f32[80,128]{1,0:T(8,128)S(1)}, f32[80,128]{1,0:T(8,128)S(1)}, u32[]{:S(2)}, u32[]{:S(2)}) collective-permute-start(f32[80,128]{1,0:T(8,128)S(1)} %get-tuple-element.152), channel_id=1, source_target_pairs={{0,1},{1,0},{2,3},{3,2},{4,5},{5,4},{6,7},{7,6},{8,9},{9,8},{10,11... | collective-permute-start | bytes 122888 | tf_op jit(solution)/shard_map/ppermute | solution.py:873
  62.4 8.0 %collective-permute-start.11 = (f32[80,128]{1,0:T(8,128)S(1)}, f32[80,128]{1,0:T(8,128)S(1)}, u32[]{:S(2)}, u32[]{:S(2)}) collective-permute-start(f32[80,128]{1,0:T(8,128)S(1)} %get-tuple-element.153), channel_id=1, source_target_pairs={{0,31},{1,2},{2,1},{3,4},{4,3},{5,6},{6,5},{7,24},{8,23},{9,10},{1... | collective-permute-start | bytes 122888 | tf_op jit(solution)/shard_map/ppermute | solution.py:874
  66.7 9.4 %collective-permute-start.14 = (f32[80,128]{1,0:T(8,128)S(1)}, f32[80,128]{1,0:T(8,128)S(1)}, u32[]{:S(2)}, u32[]{:S(2)}) collective-permute-start(f32[80,128]{1,0:T(8,128)S(1)} %get-tuple-element.167), channel_id=1, source_target_pairs={{0,16},{1,17},{2,18},{3,19},{4,20},{5,21},{6,22},{7,23},{8,24},{9,... | collective-permute-start | bytes 122888 | tf_op jit(solution)/shard_map/ppermute | solution.py:873
  66.7 9.4 %collective-permute-start.15 = (f32[80,128]{1,0:T(8,128)S(1)}, f32[80,128]{1,0:T(8,128)S(1)}, u32[]{:S(2)}, u32[]{:S(2)}) collective-permute-start(f32[80,128]{1,0:T(8,128)S(1)} %get-tuple-element.168), channel_id=1, source_target_pairs={{0,112},{1,113},{2,114},{3,115},{4,116},{5,117},{6,118},{7,119},{8... | collective-permute-start | bytes 122888 | tf_op jit(solution)/shard_map/ppermute | solution.py:874
  71.4 4.7 %collective-permute-start.12 = (f32[72,128]{1,0:T(8,128)S(1)}, f32[72,128]{1,0:T(8,128)S(1)}, u32[]{:S(2)}, u32[]{:S(2)}) collective-permute-start(f32[72,128]{1,0:T(8,128)S(1)} %get-tuple-element.161), channel_id=1, source_target_pairs={{0,1},{1,0},{2,3},{3,2},{4,5},{5,4},{6,7},{7,6},{8,9},{9,8},{10,11... | collective-permute-start | bytes 110600 | tf_op jit(solution)/shard_map/ppermute | solution.py:873
  71.5 6.8 %collective-permute-start.13 = (f32[72,128]{1,0:T(8,128)S(1)}, f32[72,128]{1,0:T(8,128)S(1)}, u32[]{:S(2)}, u32[]{:S(2)}) collective-permute-start(f32[72,128]{1,0:T(8,128)S(1)} %get-tuple-element.162), channel_id=1, source_target_pairs={{0,31},{1,2},{2,1},{3,4},{4,3},{5,6},{6,5},{7,24},{8,23},{9,10},{1... | collective-permute-start | bytes 110600 | tf_op jit(solution)/shard_map/ppermute | solution.py:874
  79.1 5.4 %collective-permute-start.16 = (f32[72,256]{1,0:T(8,128)S(1)}, f32[72,256]{1,0:T(8,128)S(1)}, u32[]{:S(2)}, u32[]{:S(2)}) collective-permute-start(f32[72,256]{1,0:T(8,128)S(1)} %get-tuple-element.175), channel_id=1, source_target_pairs={{0,1},{1,0},{2,3},{3,2},{4,5},{5,4},{6,7},{7,6},{8,9},{9,8},{10,11... | collective-permute-start | bytes 221192 | tf_op jit(solution)/shard_map/ppermute | solution.py:873
  79.2 7.2 %collective-permute-start.17 = (f32[72,256]{1,0:T(8,128)S(1)}, f32[72,256]{1,0:T(8,128)S(1)}, u32[]{:S(2)}, u32[]{:S(2)}) collective-permute-start(f32[72,256]{1,0:T(8,128)S(1)} %get-tuple-element.176), channel_id=1, source_target_pairs={{0,31},{1,2},{2,1},{3,4},{4,3},{5,6},{6,5},{7,24},{8,23},{9,10},{1... | collective-permute-start | bytes 221192 | tf_op jit(solution)/shard_map/ppermute | solution.py:874
  87.8 2.1 %collective-permute-start.18 = (f32[72,128]{1,0:T(8,128)S(1)}, f32[72,128]{1,0:T(8,128)S(1)}, u32[]{:S(2)}, u32[]{:S(2)}) collective-permute-start(f32[72,128]{1,0:T(8,128)S(1)} %get-tuple-element.185), channel_id=1, source_target_pairs={{0,1},{1,0},{2,3},{3,2},{4,5},{5,4},{6,7},{7,6},{8,9},{9,8},{10,11... | collective-permute-start | bytes 110600 | tf_op jit(solution)/shard_map/ppermute | solution.py:873
  87.9 7.3 %collective-permute-start.19 = (f32[72,128]{1,0:T(8,128)S(1)}, f32[72,128]{1,0:T(8,128)S(1)}, u32[]{:S(2)}, u32[]{:S(2)}) collective-permute-start(f32[72,128]{1,0:T(8,128)S(1)} %get-tuple-element.186), channel_id=1, source_target_pairs={{0,15},{1,2},{2,1},{3,4},{4,3},{5,6},{6,5},{7,8},{8,7},{9,10},{10,... | collective-permute-start | bytes 110600 | tf_op jit(solution)/shard_map/ppermute | solution.py:874
  96.9 4.5 %collective-permute-start.20 = (f32[152,128]{1,0:T(8,128)S(1)}, f32[152,128]{1,0:T(8,128)S(1)}, u32[]{:S(2)}, u32[]{:S(2)}) collective-permute-start(f32[152,128]{1,0:T(8,128)S(1)} %get-tuple-element.193), channel_id=1, source_target_pairs={{0,16},{1,17},{2,18},{3,19},{4,20},{5,21},{6,22},{7,23},{8,24},{9,... | collective-permute-start | bytes 233480 | tf_op jit(solution)/shard_map/ppermute | solution.py:873
  97.0 6.6 %collective-permute-start.21 = (f32[152,128]{1,0:T(8,128)S(1)}, f32[152,128]{1,0:T(8,128)S(1)}, u32[]{:S(2)}, u32[]{:S(2)}) collective-permute-start(f32[152,128]{1,0:T(8,128)S(1)} %get-tuple-element.194), channel_id=1, source_target_pairs={{0,112},{1,113},{2,114},{3,115},{4,116},{5,117},{6,118},{7,119},{8... | collective-permute-start | bytes 233480 | tf_op jit(solution)/shard_map/ppermute | solution.py:874
  103.7 4.2 %collective-permute-start.22 = (f32[72,128]{1,0:T(8,128)S(1)}, f32[72,128]{1,0:T(8,128)S(1)}, u32[]{:S(2)}, u32[]{:S(2)}) collective-permute-start(f32[72,128]{1,0:T(8,128)S(1)} %get-tuple-element.197.refs_5_), channel_id=1, source_target_pairs={{0,1},{1,0},{2,3},{3,2},{4,5},{5,4},{6,7},{7,6},{8,9},{9,8},{10,11... | collective-permute-start | bytes 110600 | tf_op jit(solution)/shard_map/ppermute | solution.py:873
  103.8 7.1 %collective-permute-start.23 = (f32[72,128]{1,0:T(8,128)S(1)}, f32[72,128]{1,0:T(8,128)S(1)}, u32[]{:S(2)}, u32[]{:S(2)}) collective-permute-start(f32[72,128]{1,0:T(8,128)S(1)} %get-tuple-element.198), channel_id=1, source_target_pairs={{0,15},{1,2},{2,1},{3,4},{4,3},{5,6},{6,5},{7,8},{8,7},{9,10},{10,... | collective-permute-start | bytes 110600 | tf_op jit(solution)/shard_map/ppermute | solution.py:874

commit v7 on v6

--- a/solution.py
+++ b/solution.py
@@ -1090,15 +1090,15 @@
         chunks[t, 3 * Z : 3 * Z + 8, :] = own[...]
 
 
-def again0_kernel(f, c, w, vz, e, v, g, part, columns, c_columns, yup, ydown):
+def again0_kernel(f, c, w, vz, e, v, g, part, columns, yup, ydown):
     prolong_add(GEOM[0], GEOM[1], e, v, g)
     put_y(GEOM[0], g, None, yup, ydown)
     columns[...] = own_columns(GEOM[0], g)
+    relax_tile(GEOM[0], w[...].astype(BF16), Coef(vz), g, f, c, ALONE, Setter(part))
+
+
+def twice0_kernel(f, c, w, vz, part, _after, twice, c_columns):
     c_columns[...] = own_columns(GEOM[0], c)
-    relax_tile(GEOM[0], w[...].astype(BF16), Coef(vz), g, f, c, ALONE, Setter(part))
-
-
-def twice0_kernel(f, c, w, vz, part, _after, twice):
     relax_tile(GEOM[0], w[...].astype(BF16), Coef(vz), part, f, c, ALONE, Setter(twice))
 
 
@@ -1299,14 +1299,14 @@
         send=((1, "gx"),),
     )
     xlo, xhi = swap(up, down, "gx")
-    g0, part, columns, c_columns, yup, ydown = call(
-        again0_kernel, [t0, t0, ys, ys, ys, ys], [f, c, w[0], vz, e1, v0], name="again0"
+    g0, part, columns, yup, ydown = call(
+        again0_kernel, [t0, t0, ys, ys, ys], [f, c, w[0], vz, e1, v0], name="again0"
     )
     up, down = call(
         merge_kernel(0, 2), [ys, ys], [xlo, xhi, own, yup, ydown], name="merge0", got=((0, "gx"),), send=((0, "gy"),)
     )
     side = swap(up, down, "gy")
-    (twice,) = call(twice0_kernel, [t0], [f, c, w[0], vz, part, up], name="twice0", after=1)
+    twice, c_columns = call(twice0_kernel, [t0, ys], [f, c, w[0], vz, part, up], name="twice0", after=1)
     (out,) = call(
         post0_kernel,
         [(NZ * 24, LANES)],

time: 113 us -> 113 us (level)
  no operation moved by 1% of the time
where the time goes in v7:
time: 113 us
  starting transfers between devices  42.1 us (37%)
  Pallas kernels  32.3 us (29%)
  waiting for transfers between devices  21.4 us (19%)
  blocking collectives  15.4 us (14%)
  local copies, waits for them, and re-layouts  1.6 us (1%)
    ppermute x12, starting transfers between devices, swap(): lax.ppermute(second, both, swap_pairs(axis, 1, nearest))  39.6 us
    pallas_call x23, Pallas kernels, call(): pl.pallas_call(by_swaps(kernel, len(args), len(outs), got, send), out_sha...  30.3 us
    ppermute x12, waiting for transfers between devices, swap(): lax.ppermute(second, both, swap_pairs(axis, 1, nearest))  20.4 us
    all_to_all x1, blocking collectives, on_device(): chunks = lax.all_to_all(chunks, 'gx', 0, 0)  15.4 us
    ppermute x12, starting transfers between devices, swap(): lax.ppermute(first, both, swap_pairs(axis, 0, nearest))  2.53 us
  transfers between devices with their start and end apart: 24, of which 11 were waited for; matrix products, arithmetic and copies ran while one was open for 1% of the time, Pallas kernels for 15%

profile of v7, /device:TPU:0, one launch (start us, length us, event | category | flops | bytes accessed | tf_op | source)
XLA Modules:
  0.0 113.2 jit_solution(5361093518429018694)
XLA Ops:
  0.0 2.0 %open.1 = (f32[224,128]{1,0:T(8,128)}, f32[224,128]{1,0:T(8,128)}, f32[8,128]{1,0:T(8,128)}, f32[3,72,128]{2,1,0:T(8,128)}) custom-call(f32[70,24,128]{2,1,0:T(8,128)} %refs_0_.1, f32[70,24,128]{2,1,0:T(8,128)} %refs_1_.1, f32[1,71]{1,0:T(1,128)} %bitcast.9, s32[1,4]{1,0:T(1,128)} %bitcast.10), custom_call_target="tpu_custom_call" | custom-call | tf_op jit(solution)/shard_map/open/pallas_call | solution.py:1174
  2.0 1.7 %collective-permute-start = (f32[224,128]{1,0:T(8,128)}, f32[224,128]{1,0:T(8,128)S(1)}, u32[]{:S(2)}, u32[]{:S(2)}) collective-permute-start(f32[224,128]{1,0:T(8,128)} %get-tuple-element.108), channel_id=1, source_target_pairs={{0,16},{1,17},{2,18},{3,19},{4,20},{5,21},{6,22},{7,23},{8,24},{9,... | collective-permute-start | bytes 344072 | tf_op jit(solution)/shard_map/ppermute | solution.py:873
  3.8 2.6 %collective-permute-start.1 = (f32[224,128]{1,0:T(8,128)}, f32[224,128]{1,0:T(8,128)S(1)}, u32[]{:S(2)}, u32[]{:S(2)}) collective-permute-start(f32[224,128]{1,0:T(8,128)} %get-tuple-element.109), channel_id=1, source_target_pairs={{0,112},{1,113},{2,114},{3,115},{4,116},{5,117},{6,118},{7,119},{8... | collective-permute-start | bytes 344072 | tf_op jit(solution)/shard_map/ppermute | solution.py:874
  8.0 2.5 %side.1 = (f32[24,72,128]{2,1,0:T(8,128)S(1)}, f32[24,72,128]{2,1,0:T(8,128)S(1)}, f32[72,216]{1,0:T(8,128)S(1)}, f32[72,216]{1,0:T(8,128)S(1)}, f32[72,216]{1,0...) custom-call(f32[1680,128]{1,0:T(8,128)S(1)} %bitcast.6, ...), custom_call_target="tpu_custom_call" | custom-call | tf_op jit(solution)/shard_map/side/pallas_call | solution.py:921
  11.1 6.5 %collective-permute-start.3 = (f32[80,128]{1,0:T(8,128)S(1)}, f32[80,128]{1,0:T(8,128)S(1)}, u32[]{:S(2)}, u32[]{:S(2)}) collective-permute-start(f32[80,128]{1,0:T(8,128)S(1)} %get-tuple-element.113), channel_id=1, source_target_pairs={{0,15},{1,2},{2,1},{3,4},{4,3},{5,6},{6,5},{7,8},{8,7},{9,10},{10,... | collective-permute-start | bytes 122888 | tf_op jit(solution)/shard_map/ppermute | solution.py:874
  17.7 1.7 %collective-permute-done.3.refs_8_ = f32[80,128]{1,0:T(8,128)S(1)} collective-permute-done((f32[80,128]{1,0:T(8,128)S(1)}, f32[80,128]{1,0:T(8,128)S(1)}, u32[]{:S(2)}, u32[]{:S(2)}) %collective-permute-start.3) | collective-permute-done | bytes 40992 | tf_op jit(solution)/shard_map/ppermute | solution.py:874
  19.3 1.7 %pre0.1 = (f32[120,128]{1,0:T(8,128)S(1)}, f32[120,128]{1,0:T(8,128)S(1)}, f32[3,72,128]{2,1,0:T(8,128)S(1)}, f32[3,72,128]{2,1,0:T(8,128)S(1)}) custom-call(f32[24,72,128]{2,1,0:T(8,128)S(1)} %get-tuple-element.105.refs_0_, f32[24,72,128]{2,1,0:T(8,128)S(1)} %get-tuple-element.106.refs_1_, f32[72,216]{1,0:T(8,128)S(1)} %get-tuple-element.107.refs_2_, ...), custom_call_target="tpu_custom_call" | custom-call | tf_op jit(solution)/shard_map/pre0/pallas_call | solution.py:921
  21.1 3.3 %collective-permute-start.5 = (f32[120,128]{1,0:T(8,128)S(1)}, f32[120,128]{1,0:T(8,128)S(1)}, u32[]{:S(2)}, u32[]{:S(2)}) collective-permute-start(f32[120,128]{1,0:T(8,128)S(1)} %get-tuple-element.123), channel_id=1, source_target_pairs={{0,112},{1,113},{2,114},{3,115},{4,116},{5,117},{6,118},{7,119},{8... | collective-permute-start | bytes 184328 | tf_op jit(solution)/shard_map/ppermute | solution.py:874
  24.4 2.2 %mid1.1 = (f32[24,72,128]{2,1,0:T(8,128)S(1)}, f32[6,72,128]{2,1,0:T(8,128)S(1)}, f32[6,72,128]{2,1,0:T(8,128)S(1)}, f32[6,72,128]{2,1,0:T(8,128)S(1)}, f32[72,1...) custom-call(f32[24,72,128]{2,1,0:T(8,128)S(1)} %get-tuple-element.105.refs_0_, ...), custom_call_target="tpu_custom_call" | custom-call | tf_op jit(solution)/shard_map/mid1/pallas_call | solution.py:921
  27.8 4.5 %collective-permute-start.7 = (f32[80,128]{1,0:T(8,128)S(1)}, f32[80,128]{1,0:T(8,128)S(1)}, u32[]{:S(2)}, u32[]{:S(2)}) collective-permute-start(f32[80,128]{1,0:T(8,128)S(1)} %get-tuple-element.127), channel_id=1, source_target_pairs={{0,15},{1,2},{2,1},{3,4},{4,3},{5,6},{6,5},{7,8},{8,7},{9,10},{10,... | collective-permute-start | bytes 122888 | tf_op jit(solution)/shard_map/ppermute | solution.py:874
  32.2 2.7 %collective-permute-done.7.refs_8_ = f32[80,128]{1,0:T(8,128)S(1)} collective-permute-done((f32[80,128]{1,0:T(8,128)S(1)}, f32[80,128]{1,0:T(8,128)S(1)}, u32[]{:S(2)}, u32[]{:S(2)}) %collective-permute-start.7) | collective-permute-done | bytes 40992 | tf_op jit(solution)/shard_map/ppermute | solution.py:874
  34.9 2.0 %pre1.1 = (f32[6,72,128]{2,1,0:T(8,128)S(1)}, f32[80,128]{1,0:T(8,128)S(1)}, f32[80,128]{1,0:T(8,128)S(1)}, f32[8,224,128]{2,1,0:T(8,128)S(1)}) custom-call(f32[6,72,128]{2,1,0:T(8,128)S(1)} %get-tuple-element.121.refs_0_, f32[6,72,128]{2,1,0:T(8,128)S(1)} %get-tuple-element.117.refs_12_.refs_7_.refs_1_, f32[72,216]{1,0:T(8,128)S(1)} %get-tuple-element.120.refs_6_.refs_2_, ...), custom_call_target="tpu_custom_call" | custom-call | tf_op jit(solution)/shard_map/pre1/pallas_call | solution.py:921
  36.9 15.4 %all_to_all.5.refs_0_ = f32[8,224,128]{2,1,0:T(8,128)S(1)} all-to-all(f32[8,224,128]{2,1,0:T(8,128)S(1)} %get-tuple-element.133), channel_id=1, replica_groups=mesh['gx'=8,'gy'=16] {'gx'}, dimensions={0} | all-to-all | bytes 1835008 | tf_op jit(solution)/shard_map/all_to_all | solution.py:1232
  53.5 4.5 %collective-permute-start.9 = (f32[80,256]{1,0:T(8,128)S(1)}, f32[80,256]{1,0:T(8,128)S(1)}, u32[]{:S(2)}, u32[]{:S(2)}) collective-permute-start(f32[80,256]{1,0:T(8,128)S(1)} %get-tuple-element.142), channel_id=1, source_target_pairs={{0,31},{1,2},{2,1},{3,4},{4,3},{5,6},{6,5},{7,24},{8,23},{9,10},{1... | collective-permute-start | bytes 245768 | tf_op jit(solution)/shard_map/ppermute | solution.py:874
  58.4 1.9 %alone2.1 = (f32[6,72,256]{2,1,0:T(8,128)S(1)}, f32[72,256]{1,0:T(8,128)S(1)}, f32[72,256]{1,0:T(8,128)S(1)}, f32[3,72,128]{2,1,0:T(8,128)S(1)}, f32[72,128]{1,0:T(8,128)S(1)}, /*index=5*/f32[72,128]{1,0:T(8,128)S(1)}) custom-call(f32[6,72,256]{2,1,0:T(8,128)S(1)} %get-tuple-element.134.refs_0_, f32[6,72,256]{2,1,0:T(8,128)S(1)} %get-tuple-element.135.refs_0_.refs_1_, ...), custom_call_target="tpu_custom_call" | custom-call | tf_op jit(solution)/shard_map/alone2/pallas_call | solution.py:921
  62.4 4.3 %collective-permute-start.11 = (f32[80,128]{1,0:T(8,128)S(1)}, f32[80,128]{1,0:T(8,128)S(1)}, u32[]{:S(2)}, u32[]{:S(2)}) collective-permute-start(f32[80,128]{1,0:T(8,128)S(1)} %get-tuple-element.154), channel_id=1, source_target_pairs={{0,31},{1,2},{2,1},{3,4},{4,3},{5,6},{6,5},{7,24},{8,23},{9,10},{1... | collective-permute-start | bytes 122888 | tf_op jit(solution)/shard_map/ppermute | solution.py:874
  66.7 2.6 %collective-permute-start.15 = (f32[80,128]{1,0:T(8,128)S(1)}, f32[80,128]{1,0:T(8,128)S(1)}, u32[]{:S(2)}, u32[]{:S(2)}) collective-permute-start(f32[80,128]{1,0:T(8,128)S(1)} %get-tuple-element.169), channel_id=1, source_target_pairs={{0,112},{1,113},{2,114},{3,115},{4,116},{5,117},{6,118},{7,119},{8... | collective-permute-start | bytes 122888 | tf_op jit(solution)/shard_map/ppermute | solution.py:874
  71.5 3.1 %collective-permute-start.13 = (f32[72,128]{1,0:T(8,128)S(1)}, f32[72,128]{1,0:T(8,128)S(1)}, u32[]{:S(2)}, u32[]{:S(2)}) collective-permute-start(f32[72,128]{1,0:T(8,128)S(1)} %get-tuple-element.163), channel_id=1, source_target_pairs={{0,31},{1,2},{2,1},{3,4},{4,3},{5,6},{6,5},{7,24},{8,23},{9,10},{1... | collective-permute-start | bytes 110600 | tf_op jit(solution)/shard_map/ppermute | solution.py:874
  76.1 2.2 %collective-permute-done.13.refs_3_ = f32[72,128]{1,0:T(8,128)S(1)} collective-permute-done((f32[72,128]{1,0:T(8,128)S(1)}, f32[72,128]{1,0:T(8,128)S(1)}, u32[]{:S(2)}, u32[]{:S(2)}) %collective-permute-start.13) | collective-permute-done | bytes 36896 | tf_op jit(solution)/shard_map/ppermute | solution.py:874
  79.2 3.1 %collective-permute-start.17 = (f32[72,256]{1,0:T(8,128)S(1)}, f32[72,256]{1,0:T(8,128)S(1)}, u32[]{:S(2)}, u32[]{:S(2)}) collective-permute-start(f32[72,256]{1,0:T(8,128)S(1)} %get-tuple-element.177), channel_id=1, source_target_pairs={{0,31},{1,2},{2,1},{3,4},{4,3},{5,6},{6,5},{7,24},{8,23},{9,10},{1... | collective-permute-start | bytes 221192 | tf_op jit(solution)/shard_map/ppermute | solution.py:874
  82.3 2.2 %again2.1 = (f32[72,256]{1,0:T(8,128)S(1)}, f32[72,256]{1,0:T(8,128)S(1)}, f32[72,256]{1,0:T(8,128)S(1)}, f32[72,256]{1,0:T(8,128)S(1)}, f32[72,128]{1,0:T(8,128...) custom-call(f32[6,72,256]{2,1,0:T(8,128)S(1)} %get-tuple-element.134.refs_0_, ...), custom_call_target="tpu_custom_call" | custom-call | tf_op jit(solution)/shard_map/again2/pallas_call | solution.py:921
  84.5 1.9 %collective-permute-done.17.refs_12_ = f32[72,256]{1,0:T(8,128)S(1)} collective-permute-done((f32[72,256]{1,0:T(8,128)S(1)}, f32[72,256]{1,0:T(8,128)S(1)}, u32[]{:S(2)}, u32[]{:S(2)}) %collective-permute-start.17) | collective-permute-done | bytes 73760 | tf_op jit(solution)/shard_map/ppermute | solution.py:874
  86.4 1.4 %post2.1 = (f32[4,72,256]{2,1,0:T(8,128)S(1)}, f32[72,128]{1,0:T(8,128)S(1)}, f32[72,128]{1,0:T(8,128)S(1)}) custom-call(f32[72,216]{1,0:T(8,128)S(1)} %get-tuple-element.136.refs_2_.refs_0_, f32[3,72,128]{2,1,0:T(8,128)S(1)} %copy-done, f32[8,256]{1,0:T(8,128)S(1)} %get-tuple-element.137.refs_1_.refs_4_.refs_2_, ...), custom_call_target="tpu_custom_call" | custom-call | tf_op jit(solution)/shard_map/post2/pallas_call | solution.py:921
  88.2 1.7 %again1.1 = (f32[6,72,128]{2,1,0:T(8,128)S(1)}, f32[6,72,128]{2,1,0:T(8,128)S(1)}, f32[72,128]{1,0:T(8,128)S(1)}, f32[72,128]{1,0:T(8,128)S(1)}, f32[72,128]{1,0:T(8,128)S(1)}) custom-call(f32[6,72,128]{2,1,0:T(8,128)S(1)} %get-tuple-element.121.refs_0_, f32[6,72,128]{2,1,0:T(8,128)S(1)} %get-tuple-element.117.refs_12_.refs_7_.refs_1_, ...), custom_call_target="tpu_custom_call" | custom-call | tf_op jit(solution)/shard_map/again1/pallas_call | solution.py:921
  89.9 5.3 %collective-permute-done.19.refs_15_ = f32[72,128]{1,0:T(8,128)S(1)} collective-permute-done((f32[72,128]{1,0:T(8,128)S(1)}, f32[72,128]{1,0:T(8,128)S(1)}, u32[]{:S(2)}, u32[]{:S(2)}) %collective-permute-start.19) | collective-permute-done | bytes 36896 | tf_op jit(solution)/shard_map/ppermute | solution.py:874
  95.2 1.7 %post1.1 = (f32[6,72,128]{2,1,0:T(8,128)S(1)}, f32[152,128]{1,0:T(8,128)S(1)}, f32[152,128]{1,0:T(8,128)S(1)}) custom-call(f32[6,72,128]{2,1,0:T(8,128)S(1)} %get-tuple-element.121.refs_0_, f32[6,72,128]{2,1,0:T(8,128)S(1)} %get-tuple-element.117.refs_12_.refs_7_.refs_1_, f32[72,216]{1,0:T(8,128)S(1)} %get-tuple-element.120.refs_6_.refs_2_, ...), custom_call_target="tpu_custom_call" | custom-call | tf_op jit(solution)/shard_map/post1/pallas_call | solution.py:921
  97.0 1.7 %collective-permute-start.21 = (f32[152,128]{1,0:T(8,128)S(1)}, f32[152,128]{1,0:T(8,128)S(1)}, u32[]{:S(2)}, u32[]{:S(2)}) collective-permute-start(f32[152,128]{1,0:T(8,128)S(1)} %get-tuple-element.194), channel_id=1, source_target_pairs={{0,112},{1,113},{2,114},{3,115},{4,116},{5,117},{6,118},{7,119},{8... | collective-permute-start | bytes 233480 | tf_op jit(solution)/shard_map/ppermute | solution.py:874
  98.6 1.8 %again0.1 = (f32[24,72,128]{2,1,0:T(8,128)S(1)}, f32[24,72,128]{2,1,0:T(8,128)S(1)}, f32[72,128]{1,0:T(8,128)S(1)}, f32[72,128]{1,0:T(8,128)S(1)}, f32[72,128]{1,0:T(8,128)S(1)}) custom-call(f32[24,72,128]{2,1,0:T(8,128)S(1)} %get-tuple-element.105.refs_0_, f32[24,72,128]{2,1,0:T(8,128)S(1)} %get-tuple-element.106.refs_1_, ...), custom_call_target="tpu_custom_call" | custom-call | tf_op jit(solution)/shard_map/again0/pallas_call | solution.py:921
  101.4 2.2 %collective-permute-done.21.refs_1_.refs_14_ = f32[152,128]{1,0:T(8,128)S(1)} collective-permute-done((f32[152,128]{1,0:T(8,128)S(1)}, f32[152,128]{1,0:T(8,128)S(1)}, u32[]{:S(2)}, u32[]{:S(2)}) %collective-permute-start.21) | collective-permute-done | bytes 77856 | tf_op jit(solution)/shard_map/ppermute | solution.py:874
  103.8 3.0 %collective-permute-start.23 = (f32[72,128]{1,0:T(8,128)S(1)}, f32[72,128]{1,0:T(8,128)S(1)}, u32[]{:S(2)}, u32[]{:S(2)}) collective-permute-start(f32[72,128]{1,0:T(8,128)S(1)} %get-tuple-element.200), channel_id=1, source_target_pairs={{0,15},{1,2},{2,1},{3,4},{4,3},{5,6},{6,5},{7,8},{8,7},{9,10},{10,... | collective-permute-start | bytes 110600 | tf_op jit(solution)/shard_map/ppermute | solution.py:874
  108.2 2.7 %collective-permute-done.23.refs_16_ = f32[72,128]{1,0:T(8,128)S(1)} collective-permute-done((f32[72,128]{1,0:T(8,128)S(1)}, f32[72,128]{1,0:T(8,128)S(1)}, u32[]{:S(2)}, u32[]{:S(2)}) %collective-permute-start.23) | collective-permute-done | bytes 36896 | tf_op jit(solution)/shard_map/ppermute | solution.py:874
  110.9 2.3 %post0.1 = f32[1680,128]{1,0:T(8,128)} custom-call(f32[24,72,128]{2,1,0:T(8,128)S(1)} %get-tuple-element.105.refs_0_, f32[24,72,128]{2,1,0:T(8,128)S(1)} %get-tuple-element.106.refs_1_, f32[72,216]{1,0:T(8,128)S(1)} %get-tuple-element.107.refs_2_, f32[3,72,128]{2,1,0:T(8,128)S(1)} %copy-done, f32[8,128]{1,0:T(8,128)S(1)} %copy-done.3, ...), custom_call_target="tpu_custom_call" | custom-call | tf_op jit(solution)/shard_map/post0/pallas_call | solution.py:921
  (50 shorter events, 14.5 us)
Async XLA Ops:
  0.0 7.4 %copy-start.1 = (f32[70,24,128]{2,1,0:T(8,128)S(1)}, f32[70,24,128]{2,1,0:T(8,128)}, u32[]{:S(2)}) copy-start(f32[70,24,128]{2,1,0:T(8,128)} %refs_0_.1) | copy-start | bytes 2580484
  0.0 7.4 %copy-start.2 = (f32[70,24,128]{2,1,0:T(8,128)S(1)}, f32[70,24,128]{2,1,0:T(8,128)}, u32[]{:S(2)}) copy-start(f32[70,24,128]{2,1,0:T(8,128)} %refs_1_.1) | copy-start | bytes 2580484
  2.0 8.6 %collective-permute-start = (f32[224,128]{1,0:T(8,128)}, f32[224,128]{1,0:T(8,128)S(1)}, u32[]{:S(2)}, u32[]{:S(2)}) collective-permute-start(f32[224,128]{1,0:T(8,128)} %get-tuple-element.108), channel_id=1, source_target_pairs={{0,16},{1,17},{2,18},{3,19},{4,20},{5,21},{6,22},{7,23},{8,24},{9,... | collective-permute-start | bytes 344072 | tf_op jit(solution)/shard_map/ppermute | solution.py:873
  3.8 7.1 %collective-permute-start.1 = (f32[224,128]{1,0:T(8,128)}, f32[224,128]{1,0:T(8,128)S(1)}, u32[]{:S(2)}, u32[]{:S(2)}) collective-permute-start(f32[224,128]{1,0:T(8,128)} %get-tuple-element.109), channel_id=1, source_target_pairs={{0,112},{1,113},{2,114},{3,115},{4,116},{5,117},{6,118},{7,119},{8... | collective-permute-start | bytes 344072 | tf_op jit(solution)/shard_map/ppermute | solution.py:874
  6.4 1.0 copy-start
  7.4 0.7 copy-start.3
  11.0 6.6 %collective-permute-start.2 = (f32[80,128]{1,0:T(8,128)S(1)}, f32[80,128]{1,0:T(8,128)S(1)}, u32[]{:S(2)}, u32[]{:S(2)}) collective-permute-start(f32[80,128]{1,0:T(8,128)S(1)} %get-tuple-element.112), channel_id=1, source_target_pairs={{0,1},{1,0},{2,3},{3,2},{4,5},{5,4},{6,7},{7,6},{8,9},{9,8},{10,11... | collective-permute-start | bytes 122888 | tf_op jit(solution)/shard_map/ppermute | solution.py:873
  11.1 8.2 %collective-permute-start.3 = (f32[80,128]{1,0:T(8,128)S(1)}, f32[80,128]{1,0:T(8,128)S(1)}, u32[]{:S(2)}, u32[]{:S(2)}) collective-permute-start(f32[80,128]{1,0:T(8,128)S(1)} %get-tuple-element.113), channel_id=1, source_target_pairs={{0,15},{1,2},{2,1},{3,4},{4,3},{5,6},{6,5},{7,8},{8,7},{9,10},{10,... | collective-permute-start | bytes 122888 | tf_op jit(solution)/shard_map/ppermute | solution.py:874
  21.0 5.6 %collective-permute-start.4 = (f32[120,128]{1,0:T(8,128)S(1)}, f32[120,128]{1,0:T(8,128)S(1)}, u32[]{:S(2)}, u32[]{:S(2)}) collective-permute-start(f32[120,128]{1,0:T(8,128)S(1)} %get-tuple-element.122), channel_id=1, source_target_pairs={{0,16},{1,17},{2,18},{3,19},{4,20},{5,21},{6,22},{7,23},{8,24},{9,... | collective-permute-start | bytes 184328 | tf_op jit(solution)/shard_map/ppermute | solution.py:873
  21.1 6.4 %collective-permute-start.5 = (f32[120,128]{1,0:T(8,128)S(1)}, f32[120,128]{1,0:T(8,128)S(1)}, u32[]{:S(2)}, u32[]{:S(2)}) collective-permute-start(f32[120,128]{1,0:T(8,128)S(1)} %get-tuple-element.123), channel_id=1, source_target_pairs={{0,112},{1,113},{2,114},{3,115},{4,116},{5,117},{6,118},{7,119},{8... | collective-permute-start | bytes 184328 | tf_op jit(solution)/shard_map/ppermute | solution.py:874
  27.7 4.6 %collective-permute-start.6 = (f32[80,128]{1,0:T(8,128)S(1)}, f32[80,128]{1,0:T(8,128)S(1)}, u32[]{:S(2)}, u32[]{:S(2)}) collective-permute-start(f32[80,128]{1,0:T(8,128)S(1)} %get-tuple-element.126), channel_id=1, source_target_pairs={{0,1},{1,0},{2,3},{3,2},{4,5},{5,4},{6,7},{7,6},{8,9},{9,8},{10,11... | collective-permute-start | bytes 122888 | tf_op jit(solution)/shard_map/ppermute | solution.py:873
  27.8 7.1 %collective-permute-start.7 = (f32[80,128]{1,0:T(8,128)S(1)}, f32[80,128]{1,0:T(8,128)S(1)}, u32[]{:S(2)}, u32[]{:S(2)}) collective-permute-start(f32[80,128]{1,0:T(8,128)S(1)} %get-tuple-element.127), channel_id=1, source_target_pairs={{0,15},{1,2},{2,1},{3,4},{4,3},{5,6},{6,5},{7,8},{8,7},{9,10},{10,... | collective-permute-start | bytes 122888 | tf_op jit(solution)/shard_map/ppermute | solution.py:874
  53.4 6.8 %collective-permute-start.8 = (f32[80,256]{1,0:T(8,128)S(1)}, f32[80,256]{1,0:T(8,128)S(1)}, u32[]{:S(2)}, u32[]{:S(2)}) collective-permute-start(f32[80,256]{1,0:T(8,128)S(1)} %get-tuple-element.141), channel_id=1, source_target_pairs={{0,1},{1,0},{2,3},{3,2},{4,5},{5,4},{6,7},{7,6},{8,9},{9,8},{10,11... | collective-permute-start | bytes 245768 | tf_op jit(solution)/shard_map/ppermute | solution.py:873
  53.5 7.4 %collective-permute-start.9 = (f32[80,256]{1,0:T(8,128)S(1)}, f32[80,256]{1,0:T(8,128)S(1)}, u32[]{:S(2)}, u32[]{:S(2)}) collective-permute-start(f32[80,256]{1,0:T(8,128)S(1)} %get-tuple-element.142), channel_id=1, source_target_pairs={{0,31},{1,2},{2,1},{3,4},{4,3},{5,6},{6,5},{7,24},{8,23},{9,10},{1... | collective-permute-start | bytes 245768 | tf_op jit(solution)/shard_map/ppermute | solution.py:874
  62.3 8.1 %collective-permute-start.10 = (f32[80,128]{1,0:T(8,128)S(1)}, f32[80,128]{1,0:T(8,128)S(1)}, u32[]{:S(2)}, u32[]{:S(2)}) collective-permute-start(f32[80,128]{1,0:T(8,128)S(1)} %get-tuple-element.153), channel_id=1, source_target_pairs={{0,1},{1,0},{2,3},{3,2},{4,5},{5,4},{6,7},{7,6},{8,9},{9,8},{10,11... | collective-permute-start | bytes 122888 | tf_op jit(solution)/shard_map/ppermute | solution.py:873
  62.4 8.0 %collective-permute-start.11 = (f32[80,128]{1,0:T(8,128)S(1)}, f32[80,128]{1,0:T(8,128)S(1)}, u32[]{:S(2)}, u32[]{:S(2)}) collective-permute-start(f32[80,128]{1,0:T(8,128)S(1)} %get-tuple-element.154), channel_id=1, source_target_pairs={{0,31},{1,2},{2,1},{3,4},{4,3},{5,6},{6,5},{7,24},{8,23},{9,10},{1... | collective-permute-start | bytes 122888 | tf_op jit(solution)/shard_map/ppermute | solution.py:874
  66.7 9.4 %collective-permute-start.14 = (f32[80,128]{1,0:T(8,128)S(1)}, f32[80,128]{1,0:T(8,128)S(1)}, u32[]{:S(2)}, u32[]{:S(2)}) collective-permute-start(f32[80,128]{1,0:T(8,128)S(1)} %get-tuple-element.168), channel_id=1, source_target_pairs={{0,16},{1,17},{2,18},{3,19},{4,20},{5,21},{6,22},{7,23},{8,24},{9,... | collective-permute-start | bytes 122888 | tf_op jit(solution)/shard_map/ppermute | solution.py:873
  66.7 9.4 %collective-permute-start.15 = (f32[80,128]{1,0:T(8,128)S(1)}, f32[80,128]{1,0:T(8,128)S(1)}, u32[]{:S(2)}, u32[]{:S(2)}) collective-permute-start(f32[80,128]{1,0:T(8,128)S(1)} %get-tuple-element.169), channel_id=1, source_target_pairs={{0,112},{1,113},{2,114},{3,115},{4,116},{5,117},{6,118},{7,119},{8... | collective-permute-start | bytes 122888 | tf_op jit(solution)/shard_map/ppermute | solution.py:874
  71.4 4.7 %collective-permute-start.12 = (f32[72,128]{1,0:T(8,128)S(1)}, f32[72,128]{1,0:T(8,128)S(1)}, u32[]{:S(2)}, u32[]{:S(2)}) collective-permute-start(f32[72,128]{1,0:T(8,128)S(1)} %get-tuple-element.162), channel_id=1, source_target_pairs={{0,1},{1,0},{2,3},{3,2},{4,5},{5,4},{6,7},{7,6},{8,9},{9,8},{10,11... | collective-permute-start | bytes 110600 | tf_op jit(solution)/shard_map/ppermute | solution.py:873
  71.5 6.8 %collective-permute-start.13 = (f32[72,128]{1,0:T(8,128)S(1)}, f32[72,128]{1,0:T(8,128)S(1)}, u32[]{:S(2)}, u32[]{:S(2)}) collective-permute-start(f32[72,128]{1,0:T(8,128)S(1)} %get-tuple-element.163), channel_id=1, source_target_pairs={{0,31},{1,2},{2,1},{3,4},{4,3},{5,6},{6,5},{7,24},{8,23},{9,10},{1... | collective-permute-start | bytes 110600 | tf_op jit(solution)/shard_map/ppermute | solution.py:874
  79.1 5.4 %collective-permute-start.16 = (f32[72,256]{1,0:T(8,128)S(1)}, f32[72,256]{1,0:T(8,128)S(1)}, u32[]{:S(2)}, u32[]{:S(2)}) collective-permute-start(f32[72,256]{1,0:T(8,128)S(1)} %get-tuple-element.176), channel_id=1, source_target_pairs={{0,1},{1,0},{2,3},{3,2},{4,5},{5,4},{6,7},{7,6},{8,9},{9,8},{10,11... | collective-permute-start | bytes 221192 | tf_op jit(solution)/shard_map/ppermute | solution.py:873
  79.2 7.2 %collective-permute-start.17 = (f32[72,256]{1,0:T(8,128)S(1)}, f32[72,256]{1,0:T(8,128)S(1)}, u32[]{:S(2)}, u32[]{:S(2)}) collective-permute-start(f32[72,256]{1,0:T(8,128)S(1)} %get-tuple-element.177), channel_id=1, source_target_pairs={{0,31},{1,2},{2,1},{3,4},{4,3},{5,6},{6,5},{7,24},{8,23},{9,10},{1... | collective-permute-start | bytes 221192 | tf_op jit(solution)/shard_map/ppermute | solution.py:874
  87.8 2.1 %collective-permute-start.18 = (f32[72,128]{1,0:T(8,128)S(1)}, f32[72,128]{1,0:T(8,128)S(1)}, u32[]{:S(2)}, u32[]{:S(2)}) collective-permute-start(f32[72,128]{1,0:T(8,128)S(1)} %get-tuple-element.186), channel_id=1, source_target_pairs={{0,1},{1,0},{2,3},{3,2},{4,5},{5,4},{6,7},{7,6},{8,9},{9,8},{10,11... | collective-permute-start | bytes 110600 | tf_op jit(solution)/shard_map/ppermute | solution.py:873
  87.9 7.3 %collective-permute-start.19 = (f32[72,128]{1,0:T(8,128)S(1)}, f32[72,128]{1,0:T(8,128)S(1)}, u32[]{:S(2)}, u32[]{:S(2)}) collective-permute-start(f32[72,128]{1,0:T(8,128)S(1)} %get-tuple-element.187), channel_id=1, source_target_pairs={{0,15},{1,2},{2,1},{3,4},{4,3},{5,6},{6,5},{7,8},{8,7},{9,10},{10,... | collective-permute-start | bytes 110600 | tf_op jit(solution)/shard_map/ppermute | solution.py:874
  96.9 4.5 %collective-permute-start.20 = (f32[152,128]{1,0:T(8,128)S(1)}, f32[152,128]{1,0:T(8,128)S(1)}, u32[]{:S(2)}, u32[]{:S(2)}) collective-permute-start(f32[152,128]{1,0:T(8,128)S(1)} %get-tuple-element.193), channel_id=1, source_target_pairs={{0,16},{1,17},{2,18},{3,19},{4,20},{5,21},{6,22},{7,23},{8,24},{9,... | collective-permute-start | bytes 233480 | tf_op jit(solution)/shard_map/ppermute | solution.py:873
  97.0 6.6 %collective-permute-start.21 = (f32[152,128]{1,0:T(8,128)S(1)}, f32[152,128]{1,0:T(8,128)S(1)}, u32[]{:S(2)}, u32[]{:S(2)}) collective-permute-start(f32[152,128]{1,0:T(8,128)S(1)} %get-tuple-element.194), channel_id=1, source_target_pairs={{0,112},{1,113},{2,114},{3,115},{4,116},{5,117},{6,118},{7,119},{8... | collective-permute-start | bytes 233480 | tf_op jit(solution)/shard_map/ppermute | solution.py:874
  103.7 4.5 %collective-permute-start.22 = (f32[72,128]{1,0:T(8,128)S(1)}, f32[72,128]{1,0:T(8,128)S(1)}, u32[]{:S(2)}, u32[]{:S(2)}) collective-permute-start(f32[72,128]{1,0:T(8,128)S(1)} %get-tuple-element.197.refs_5_), channel_id=1, source_target_pairs={{0,1},{1,0},{2,3},{3,2},{4,5},{5,4},{6,7},{7,6},{8,9},{9,8},{10,11... | collective-permute-start | bytes 110600 | tf_op jit(solution)/shard_map/ppermute | solution.py:873
  103.8 7.1 %collective-permute-start.23 = (f32[72,128]{1,0:T(8,128)S(1)}, f32[72,128]{1,0:T(8,128)S(1)}, u32[]{:S(2)}, u32[]{:S(2)}) collective-permute-start(f32[72,128]{1,0:T(8,128)S(1)} %get-tuple-element.200), channel_id=1, source_target_pairs={{0,15},{1,2},{2,1},{3,4},{4,3},{5,6},{6,5},{7,8},{8,7},{9,10},{10,... | collective-permute-start | bytes 110600 | tf_op jit(solution)/shard_map/ppermute | solution.py:874

commit v8 on v7

--- a/solution.py
+++ b/solution.py
@@ -739,16 +739,20 @@
         down[:, half] = base_down[:, half] + lane_dot(small_down[...], spread)
 
 
-def base_message_kernel(part, flags, terms, v, up, down):
+def base_message_kernel(part, flags, terms, tile_v, xlo, xhi, own, v, up, down, yup, ydown):
     strip = STRIPS[2]
     lt = in_tile(strip)
     for m in range(6):
         x = jnp.where(lt == 0, roll(terms[0], -m), 0.0)
         v[m] = part[m] + jnp.where(lt == strip[1] - 1, roll(terms[1], strip[1] - 1 - m), x)
     strip_message(strip, v, None, strip_ends(strip, v, flags), up, down)
-
-
-def again2_kernel(f, c, w, vz, flags, v, e, tile_v, xlo, xhi, own, low, high, part_low, part_high, yup, ydown, twice, g, part):
+    put_y(GEOM[1], tile_v, None, yup, ydown)
+    add_up, add_down = relayed(tail_of(GEOM[1], xlo, 2), tail_of(GEOM[1], xhi, 2), own)
+    yup[...] = yup[...] + add_up
+    ydown[...] = ydown[...] + add_down
+
+
+def again2_kernel(f, c, w, vz, flags, v, e, low, high, part_low, part_high, twice, g, part):
     strip = STRIPS[2]
     a, b = iota2(LANES, LANES)
     for m in range(3):
@@ -764,10 +768,6 @@
     strip_relax(strip, winv, co, part, f, c, flags, None, Setter(twice))
     part_low[...] = strip_column(strip, twice, 0, 0, zero)
     part_high[...] = strip_column(strip, twice, strip[1] - 1, 0, zero)
-    put_y(GEOM[1], tile_v, None, yup, ydown)
-    add_up, add_down = relayed(tail_of(GEOM[1], xlo, 2), tail_of(GEOM[1], xhi, 2), own)
-    yup[...] = yup[...] + add_up
-    ydown[...] = ydown[...] + add_down
 
 
 def alone3_kernel(f, c, w, vz, flags, low, high, part_low, part_high, twice, v, part):
@@ -1261,7 +1261,13 @@
     )
     side = swap(up, down, "gy", True)
     (part,) = call(again3_kernel, [s3], [f3, c3, w[3], vz, fl3, twice, terms], [s3], name="again3")
-    v2, base_up, base_down = call(base_message_kernel, [s2, m2, m2], [part2, fl2, terms2], name="base2")
+    v2, base_up, base_down, yup, ydown = call(
+        base_message_kernel,
+        [s2, m2, m2, ys, ys],
+        [part2, fl2, terms2, v1, v1_lo, v1_hi, own],
+        name="base2",
+        got=((4, "gx"),),
+    )
     e3, up, down = call(
         last_strip_kernel,
         [s3, m2, m2],
@@ -1273,8 +1279,8 @@
         send=((1, "gy"),),
     )
     side = swap(up, down, "gy", True)
-    first, last, part_low, part_high, yup, ydown, twice = call(
-        again2_kernel, [m2] * 4 + [ys, ys, s2], [f2, c2, w[2], vz, fl2, v2, e3, v1, v1_lo, v1_hi, own], [s2, s2], name="again2", got=((8, "gx"),)
+    first, last, part_low, part_high, twice = call(
+        again2_kernel, [m2] * 4 + [s2], [f2, c2, w[2], vz, fl2, v2, e3], [s2, s2], name="again2"
     )
     terms, up, down = call(
         post_strip_kernel,

time: 113 us -> 113 us (level)
  no operation moved by 1% of the time
where the time goes in v8:
time: 113 us
  starting transfers between devices  42.1 us (37%)
  Pallas kernels  32.3 us (29%)
  waiting for transfers between devices  21.5 us (19%)
  blocking collectives  15.4 us (14%)
  local copies, waits for them, and re-layouts  1.6 us (1%)
    ppermute x12, starting transfers between devices, swap(): lax.ppermute(second, both, swap_pairs(axis, 1, nearest))  39.5 us
    pallas_call x23, Pallas kernels, call(): pl.pallas_call(by_swaps(kernel, len(args), len(outs), got, send), out_sha...  30.2 us
    ppermute x12, waiting for transfers between devices, swap(): lax.ppermute(second, both, swap_pairs(axis, 1, nearest))  20.5 us
    all_to_all x1, blocking collectives, on_device(): chunks = lax.all_to_all(chunks, 'gx', 0, 0)  15.4 us
    ppermute x12, starting transfers between devices, swap(): lax.ppermute(first, both, swap_pairs(axis, 0, nearest))  2.53 us
  transfers between devices with their start and end apart: 24, of which 11 were waited for; matrix products, arithmetic and copies ran while one was open for 1% of the time, Pallas kernels for 15%

profile of v8, /device:TPU:0, one launch (start us, length us, event | category | flops | bytes accessed | tf_op | source)
XLA Modules:
  0.0 113.2 jit_solution(15444019815628432307)
XLA Ops:
  0.0 2.0 %open.1 = (f32[224,128]{1,0:T(8,128)}, f32[224,128]{1,0:T(8,128)}, f32[8,128]{1,0:T(8,128)}, f32[3,72,128]{2,1,0:T(8,128)}) custom-call(f32[70,24,128]{2,1,0:T(8,128)} %refs_0_.1, f32[70,24,128]{2,1,0:T(8,128)} %refs_1_.1, f32[1,71]{1,0:T(1,128)} %bitcast.9, s32[1,4]{1,0:T(1,128)} %bitcast.10), custom_call_target="tpu_custom_call" | custom-call | tf_op jit(solution)/shard_map/open/pallas_call | solution.py:1174
  2.0 1.7 %collective-permute-start = (f32[224,128]{1,0:T(8,128)}, f32[224,128]{1,0:T(8,128)S(1)}, u32[]{:S(2)}, u32[]{:S(2)}) collective-permute-start(f32[224,128]{1,0:T(8,128)} %get-tuple-element.108), channel_id=1, source_target_pairs={{0,16},{1,17},{2,18},{3,19},{4,20},{5,21},{6,22},{7,23},{8,24},{9,... | collective-permute-start | bytes 344072 | tf_op jit(solution)/shard_map/ppermute | solution.py:873
  3.8 2.6 %collective-permute-start.1 = (f32[224,128]{1,0:T(8,128)}, f32[224,128]{1,0:T(8,128)S(1)}, u32[]{:S(2)}, u32[]{:S(2)}) collective-permute-start(f32[224,128]{1,0:T(8,128)} %get-tuple-element.109), channel_id=1, source_target_pairs={{0,112},{1,113},{2,114},{3,115},{4,116},{5,117},{6,118},{7,119},{8... | collective-permute-start | bytes 344072 | tf_op jit(solution)/shard_map/ppermute | solution.py:874
  8.0 2.5 %side.1 = (f32[24,72,128]{2,1,0:T(8,128)S(1)}, f32[24,72,128]{2,1,0:T(8,128)S(1)}, f32[72,216]{1,0:T(8,128)S(1)}, f32[72,216]{1,0:T(8,128)S(1)}, f32[72,216]{1,0...) custom-call(f32[1680,128]{1,0:T(8,128)S(1)} %bitcast.6, ...), custom_call_target="tpu_custom_call" | custom-call | tf_op jit(solution)/shard_map/side/pallas_call | solution.py:921
  11.1 6.5 %collective-permute-start.3 = (f32[80,128]{1,0:T(8,128)S(1)}, f32[80,128]{1,0:T(8,128)S(1)}, u32[]{:S(2)}, u32[]{:S(2)}) collective-permute-start(f32[80,128]{1,0:T(8,128)S(1)} %get-tuple-element.113), channel_id=1, source_target_pairs={{0,15},{1,2},{2,1},{3,4},{4,3},{5,6},{6,5},{7,8},{8,7},{9,10},{10,... | collective-permute-start | bytes 122888 | tf_op jit(solution)/shard_map/ppermute | solution.py:874
  17.7 1.7 %collective-permute-done.3.refs_8_ = f32[80,128]{1,0:T(8,128)S(1)} collective-permute-done((f32[80,128]{1,0:T(8,128)S(1)}, f32[80,128]{1,0:T(8,128)S(1)}, u32[]{:S(2)}, u32[]{:S(2)}) %collective-permute-start.3) | collective-permute-done | bytes 40992 | tf_op jit(solution)/shard_map/ppermute | solution.py:874
  19.3 1.7 %pre0.1 = (f32[120,128]{1,0:T(8,128)S(1)}, f32[120,128]{1,0:T(8,128)S(1)}, f32[3,72,128]{2,1,0:T(8,128)S(1)}, f32[3,72,128]{2,1,0:T(8,128)S(1)}) custom-call(f32[24,72,128]{2,1,0:T(8,128)S(1)} %get-tuple-element.105.refs_0_, f32[24,72,128]{2,1,0:T(8,128)S(1)} %get-tuple-element.106.refs_1_, f32[72,216]{1,0:T(8,128)S(1)} %get-tuple-element.107.refs_2_, ...), custom_call_target="tpu_custom_call" | custom-call | tf_op jit(solution)/shard_map/pre0/pallas_call | solution.py:921
  21.1 3.3 %collective-permute-start.5 = (f32[120,128]{1,0:T(8,128)S(1)}, f32[120,128]{1,0:T(8,128)S(1)}, u32[]{:S(2)}, u32[]{:S(2)}) collective-permute-start(f32[120,128]{1,0:T(8,128)S(1)} %get-tuple-element.123), channel_id=1, source_target_pairs={{0,112},{1,113},{2,114},{3,115},{4,116},{5,117},{6,118},{7,119},{8... | collective-permute-start | bytes 184328 | tf_op jit(solution)/shard_map/ppermute | solution.py:874
  24.4 2.2 %mid1.1 = (f32[24,72,128]{2,1,0:T(8,128)S(1)}, f32[6,72,128]{2,1,0:T(8,128)S(1)}, f32[6,72,128]{2,1,0:T(8,128)S(1)}, f32[6,72,128]{2,1,0:T(8,128)S(1)}, f32[72,1...) custom-call(f32[24,72,128]{2,1,0:T(8,128)S(1)} %get-tuple-element.105.refs_0_, ...), custom_call_target="tpu_custom_call" | custom-call | tf_op jit(solution)/shard_map/mid1/pallas_call | solution.py:921
  27.7 4.5 %collective-permute-start.7 = (f32[80,128]{1,0:T(8,128)S(1)}, f32[80,128]{1,0:T(8,128)S(1)}, u32[]{:S(2)}, u32[]{:S(2)}) collective-permute-start(f32[80,128]{1,0:T(8,128)S(1)} %get-tuple-element.127), channel_id=1, source_target_pairs={{0,15},{1,2},{2,1},{3,4},{4,3},{5,6},{6,5},{7,8},{8,7},{9,10},{10,... | collective-permute-start | bytes 122888 | tf_op jit(solution)/shard_map/ppermute | solution.py:874
  32.2 2.7 %collective-permute-done.7.refs_8_ = f32[80,128]{1,0:T(8,128)S(1)} collective-permute-done((f32[80,128]{1,0:T(8,128)S(1)}, f32[80,128]{1,0:T(8,128)S(1)}, u32[]{:S(2)}, u32[]{:S(2)}) %collective-permute-start.7) | collective-permute-done | bytes 40992 | tf_op jit(solution)/shard_map/ppermute | solution.py:874
  34.9 2.0 %pre1.1 = (f32[6,72,128]{2,1,0:T(8,128)S(1)}, f32[80,128]{1,0:T(8,128)S(1)}, f32[80,128]{1,0:T(8,128)S(1)}, f32[8,224,128]{2,1,0:T(8,128)S(1)}) custom-call(f32[6,72,128]{2,1,0:T(8,128)S(1)} %get-tuple-element.121.refs_0_, f32[6,72,128]{2,1,0:T(8,128)S(1)} %get-tuple-element.117.refs_12_.refs_7_.refs_1_, f32[72,216]{1,0:T(8,128)S(1)} %get-tuple-element.120.refs_6_.refs_2_, ...), custom_call_target="tpu_custom_call" | custom-call | tf_op jit(solution)/shard_map/pre1/pallas_call | solution.py:921
  36.9 15.4 %all_to_all.5.refs_0_ = f32[8,224,128]{2,1,0:T(8,128)S(1)} all-to-all(f32[8,224,128]{2,1,0:T(8,128)S(1)} %get-tuple-element.133), channel_id=1, replica_groups=mesh['gx'=8,'gy'=16] {'gx'}, dimensions={0} | all-to-all | bytes 1835008 | tf_op jit(solution)/shard_map/all_to_all | solution.py:1232
  53.5 4.5 %collective-permute-start.9 = (f32[80,256]{1,0:T(8,128)S(1)}, f32[80,256]{1,0:T(8,128)S(1)}, u32[]{:S(2)}, u32[]{:S(2)}) collective-permute-start(f32[80,256]{1,0:T(8,128)S(1)} %get-tuple-element.142), channel_id=1, source_target_pairs={{0,31},{1,2},{2,1},{3,4},{4,3},{5,6},{6,5},{7,24},{8,23},{9,10},{1... | collective-permute-start | bytes 245768 | tf_op jit(solution)/shard_map/ppermute | solution.py:874
  58.4 1.9 %alone2.1 = (f32[6,72,256]{2,1,0:T(8,128)S(1)}, f32[72,256]{1,0:T(8,128)S(1)}, f32[72,256]{1,0:T(8,128)S(1)}, f32[3,72,128]{2,1,0:T(8,128)S(1)}, f32[72,128]{1,0:T(8,128)S(1)}, /*index=5*/f32[72,128]{1,0:T(8,128)S(1)}) custom-call(f32[6,72,256]{2,1,0:T(8,128)S(1)} %get-tuple-element.134.refs_0_, f32[6,72,256]{2,1,0:T(8,128)S(1)} %get-tuple-element.135.refs_0_.refs_1_, ...), custom_call_target="tpu_custom_call" | custom-call | tf_op jit(solution)/shard_map/alone2/pallas_call | solution.py:921
  62.4 4.3 %collective-permute-start.13 = (f32[80,128]{1,0:T(8,128)S(1)}, f32[80,128]{1,0:T(8,128)S(1)}, u32[]{:S(2)}, u32[]{:S(2)}) collective-permute-start(f32[80,128]{1,0:T(8,128)S(1)} %get-tuple-element.156), channel_id=1, source_target_pairs={{0,31},{1,2},{2,1},{3,4},{4,3},{5,6},{6,5},{7,24},{8,23},{9,10},{1... | collective-permute-start | bytes 122888 | tf_op jit(solution)/shard_map/ppermute | solution.py:874
  66.7 2.6 %collective-permute-start.11 = (f32[80,128]{1,0:T(8,128)S(1)}, f32[80,128]{1,0:T(8,128)S(1)}, u32[]{:S(2)}, u32[]{:S(2)}) collective-permute-start(f32[80,128]{1,0:T(8,128)S(1)} %get-tuple-element.152), channel_id=1, source_target_pairs={{0,112},{1,113},{2,114},{3,115},{4,116},{5,117},{6,118},{7,119},{8... | collective-permute-start | bytes 122888 | tf_op jit(solution)/shard_map/ppermute | solution.py:874
  71.5 3.1 %collective-permute-start.15 = (f32[72,128]{1,0:T(8,128)S(1)}, f32[72,128]{1,0:T(8,128)S(1)}, u32[]{:S(2)}, u32[]{:S(2)}) collective-permute-start(f32[72,128]{1,0:T(8,128)S(1)} %get-tuple-element.165), channel_id=1, source_target_pairs={{0,31},{1,2},{2,1},{3,4},{4,3},{5,6},{6,5},{7,24},{8,23},{9,10},{1... | collective-permute-start | bytes 110600 | tf_op jit(solution)/shard_map/ppermute | solution.py:874
  76.4 1.9 %collective-permute-done.15.refs_3_ = f32[72,128]{1,0:T(8,128)S(1)} collective-permute-done((f32[72,128]{1,0:T(8,128)S(1)}, f32[72,128]{1,0:T(8,128)S(1)}, u32[]{:S(2)}, u32[]{:S(2)}) %collective-permute-start.15) | collective-permute-done | bytes 36896 | tf_op jit(solution)/shard_map/ppermute | solution.py:874
  79.2 3.1 %collective-permute-start.17 = (f32[72,256]{1,0:T(8,128)S(1)}, f32[72,256]{1,0:T(8,128)S(1)}, u32[]{:S(2)}, u32[]{:S(2)}) collective-permute-start(f32[72,256]{1,0:T(8,128)S(1)} %get-tuple-element.177), channel_id=1, source_target_pairs={{0,31},{1,2},{2,1},{3,4},{4,3},{5,6},{6,5},{7,24},{8,23},{9,10},{1... | collective-permute-start | bytes 221192 | tf_op jit(solution)/shard_map/ppermute | solution.py:874
  82.3 1.8 %again2.1 = (f32[72,256]{1,0:T(8,128)S(1)}, f32[72,256]{1,0:T(8,128)S(1)}, f32[72,256]{1,0:T(8,128)S(1)}, f32[72,256]{1,0:T(8,128)S(1)}, f32[6,72,256]{2,1,0:T(8,128)S(1)}) custom-call(f32[6,72,256]{2,1,0:T(8,128)S(1)} %get-tuple-element.134.refs_0_, f32[6,72,256]{2,1,0:T(8,128)S(1)} %get-tuple-element.135.refs_0_.refs_1_, ...), custom_call_target="tpu_custom_call" | custom-call | tf_op jit(solution)/shard_map/again2/pallas_call | solution.py:921
  84.2 2.2 %collective-permute-done.17.refs_12_ = f32[72,256]{1,0:T(8,128)S(1)} collective-permute-done((f32[72,256]{1,0:T(8,128)S(1)}, f32[72,256]{1,0:T(8,128)S(1)}, u32[]{:S(2)}, u32[]{:S(2)}) %collective-permute-start.17) | collective-permute-done | bytes 73760 | tf_op jit(solution)/shard_map/ppermute | solution.py:874
  86.4 1.4 %post2.1 = (f32[4,72,256]{2,1,0:T(8,128)S(1)}, f32[72,128]{1,0:T(8,128)S(1)}, f32[72,128]{1,0:T(8,128)S(1)}) custom-call(f32[72,216]{1,0:T(8,128)S(1)} %get-tuple-element.136.refs_2_.refs_0_, f32[3,72,128]{2,1,0:T(8,128)S(1)} %copy-done, f32[8,256]{1,0:T(8,128)S(1)} %get-tuple-element.137.refs_1_.refs_4_.refs_2_, ...), custom_call_target="tpu_custom_call" | custom-call | tf_op jit(solution)/shard_map/post2/pallas_call | solution.py:921
  88.2 1.7 %again1.1 = (f32[6,72,128]{2,1,0:T(8,128)S(1)}, f32[6,72,128]{2,1,0:T(8,128)S(1)}, f32[72,128]{1,0:T(8,128)S(1)}, f32[72,128]{1,0:T(8,128)S(1)}, f32[72,128]{1,0:T(8,128)S(1)}) custom-call(f32[6,72,128]{2,1,0:T(8,128)S(1)} %get-tuple-element.121.refs_0_, f32[6,72,128]{2,1,0:T(8,128)S(1)} %get-tuple-element.117.refs_12_.refs_7_.refs_1_, ...), custom_call_target="tpu_custom_call" | custom-call | tf_op jit(solution)/shard_map/again1/pallas_call | solution.py:921
  89.9 5.3 %collective-permute-done.19.refs_15_ = f32[72,128]{1,0:T(8,128)S(1)} collective-permute-done((f32[72,128]{1,0:T(8,128)S(1)}, f32[72,128]{1,0:T(8,128)S(1)}, u32[]{:S(2)}, u32[]{:S(2)}) %collective-permute-start.19) | collective-permute-done | bytes 36896 | tf_op jit(solution)/shard_map/ppermute | solution.py:874
  95.2 1.7 %post1.1 = (f32[6,72,128]{2,1,0:T(8,128)S(1)}, f32[152,128]{1,0:T(8,128)S(1)}, f32[152,128]{1,0:T(8,128)S(1)}) custom-call(f32[6,72,128]{2,1,0:T(8,128)S(1)} %get-tuple-element.121.refs_0_, f32[6,72,128]{2,1,0:T(8,128)S(1)} %get-tuple-element.117.refs_12_.refs_7_.refs_1_, f32[72,216]{1,0:T(8,128)S(1)} %get-tuple-element.120.refs_6_.refs_2_, ...), custom_call_target="tpu_custom_call" | custom-call | tf_op jit(solution)/shard_map/post1/pallas_call | solution.py:921
  97.0 1.7 %collective-permute-start.21 = (f32[152,128]{1,0:T(8,128)S(1)}, f32[152,128]{1,0:T(8,128)S(1)}, u32[]{:S(2)}, u32[]{:S(2)}) collective-permute-start(f32[152,128]{1,0:T(8,128)S(1)} %get-tuple-element.194), channel_id=1, source_target_pairs={{0,112},{1,113},{2,114},{3,115},{4,116},{5,117},{6,118},{7,119},{8... | collective-permute-start | bytes 233480 | tf_op jit(solution)/shard_map/ppermute | solution.py:874
  98.6 1.8 %again0.1 = (f32[24,72,128]{2,1,0:T(8,128)S(1)}, f32[24,72,128]{2,1,0:T(8,128)S(1)}, f32[72,128]{1,0:T(8,128)S(1)}, f32[72,128]{1,0:T(8,128)S(1)}, f32[72,128]{1,0:T(8,128)S(1)}) custom-call(f32[24,72,128]{2,1,0:T(8,128)S(1)} %get-tuple-element.105.refs_0_, f32[24,72,128]{2,1,0:T(8,128)S(1)} %get-tuple-element.106.refs_1_, ...), custom_call_target="tpu_custom_call" | custom-call | tf_op jit(solution)/shard_map/again0/pallas_call | solution.py:921
  101.4 2.2 %collective-permute-done.21.refs_1_.refs_14_ = f32[152,128]{1,0:T(8,128)S(1)} collective-permute-done((f32[152,128]{1,0:T(8,128)S(1)}, f32[152,128]{1,0:T(8,128)S(1)}, u32[]{:S(2)}, u32[]{:S(2)}) %collective-permute-start.21) | collective-permute-done | bytes 77856 | tf_op jit(solution)/shard_map/ppermute | solution.py:874
  103.8 3.0 %collective-permute-start.23 = (f32[72,128]{1,0:T(8,128)S(1)}, f32[72,128]{1,0:T(8,128)S(1)}, u32[]{:S(2)}, u32[]{:S(2)}) collective-permute-start(f32[72,128]{1,0:T(8,128)S(1)} %get-tuple-element.200), channel_id=1, source_target_pairs={{0,15},{1,2},{2,1},{3,4},{4,3},{5,6},{6,5},{7,8},{8,7},{9,10},{10,... | collective-permute-start | bytes 110600 | tf_op jit(solution)/shard_map/ppermute | solution.py:874
  108.2 2.7 %collective-permute-done.23.refs_16_ = f32[72,128]{1,0:T(8,128)S(1)} collective-permute-done((f32[72,128]{1,0:T(8,128)S(1)}, f32[72,128]{1,0:T(8,128)S(1)}, u32[]{:S(2)}, u32[]{:S(2)}) %collective-permute-start.23) | collective-permute-done | bytes 36896 | tf_op jit(solution)/shard_map/ppermute | solution.py:874
  110.9 2.3 %post0.1 = f32[1680,128]{1,0:T(8,128)} custom-call(f32[24,72,128]{2,1,0:T(8,128)S(1)} %get-tuple-element.105.refs_0_, f32[24,72,128]{2,1,0:T(8,128)S(1)} %get-tuple-element.106.refs_1_, f32[72,216]{1,0:T(8,128)S(1)} %get-tuple-element.107.refs_2_, f32[3,72,128]{2,1,0:T(8,128)S(1)} %copy-done, f32[8,128]{1,0:T(8,128)S(1)} %copy-done.3, ...), custom_call_target="tpu_custom_call" | custom-call | tf_op jit(solution)/shard_map/post0/pallas_call | solution.py:921
  (50 shorter events, 14.8 us)
Async XLA Ops:
  0.0 7.4 %copy-start.1 = (f32[70,24,128]{2,1,0:T(8,128)S(1)}, f32[70,24,128]{2,1,0:T(8,128)}, u32[]{:S(2)}) copy-start(f32[70,24,128]{2,1,0:T(8,128)} %refs_0_.1) | copy-start | bytes 2580484
  0.0 7.4 %copy-start.2 = (f32[70,24,128]{2,1,0:T(8,128)S(1)}, f32[70,24,128]{2,1,0:T(8,128)}, u32[]{:S(2)}) copy-start(f32[70,24,128]{2,1,0:T(8,128)} %refs_1_.1) | copy-start | bytes 2580484
  2.0 8.6 %collective-permute-start = (f32[224,128]{1,0:T(8,128)}, f32[224,128]{1,0:T(8,128)S(1)}, u32[]{:S(2)}, u32[]{:S(2)}) collective-permute-start(f32[224,128]{1,0:T(8,128)} %get-tuple-element.108), channel_id=1, source_target_pairs={{0,16},{1,17},{2,18},{3,19},{4,20},{5,21},{6,22},{7,23},{8,24},{9,... | collective-permute-start | bytes 344072 | tf_op jit(solution)/shard_map/ppermute | solution.py:873
  3.8 7.1 %collective-permute-start.1 = (f32[224,128]{1,0:T(8,128)}, f32[224,128]{1,0:T(8,128)S(1)}, u32[]{:S(2)}, u32[]{:S(2)}) collective-permute-start(f32[224,128]{1,0:T(8,128)} %get-tuple-element.109), channel_id=1, source_target_pairs={{0,112},{1,113},{2,114},{3,115},{4,116},{5,117},{6,118},{7,119},{8... | collective-permute-start | bytes 344072 | tf_op jit(solution)/shard_map/ppermute | solution.py:874
  6.4 1.0 copy-start
  7.4 0.7 copy-start.3
  11.0 6.6 %collective-permute-start.2 = (f32[80,128]{1,0:T(8,128)S(1)}, f32[80,128]{1,0:T(8,128)S(1)}, u32[]{:S(2)}, u32[]{:S(2)}) collective-permute-start(f32[80,128]{1,0:T(8,128)S(1)} %get-tuple-element.112), channel_id=1, source_target_pairs={{0,1},{1,0},{2,3},{3,2},{4,5},{5,4},{6,7},{7,6},{8,9},{9,8},{10,11... | collective-permute-start | bytes 122888 | tf_op jit(solution)/shard_map/ppermute | solution.py:873
  11.1 8.2 %collective-permute-start.3 = (f32[80,128]{1,0:T(8,128)S(1)}, f32[80,128]{1,0:T(8,128)S(1)}, u32[]{:S(2)}, u32[]{:S(2)}) collective-permute-start(f32[80,128]{1,0:T(8,128)S(1)} %get-tuple-element.113), channel_id=1, source_target_pairs={{0,15},{1,2},{2,1},{3,4},{4,3},{5,6},{6,5},{7,8},{8,7},{9,10},{10,... | collective-permute-start | bytes 122888 | tf_op jit(solution)/shard_map/ppermute | solution.py:874
  21.0 5.6 %collective-permute-start.4 = (f32[120,128]{1,0:T(8,128)S(1)}, f32[120,128]{1,0:T(8,128)S(1)}, u32[]{:S(2)}, u32[]{:S(2)}) collective-permute-start(f32[120,128]{1,0:T(8,128)S(1)} %get-tuple-element.122), channel_id=1, source_target_pairs={{0,16},{1,17},{2,18},{3,19},{4,20},{5,21},{6,22},{7,23},{8,24},{9,... | collective-permute-start | bytes 184328 | tf_op jit(solution)/shard_map/ppermute | solution.py:873
  21.1 6.4 %collective-permute-start.5 = (f32[120,128]{1,0:T(8,128)S(1)}, f32[120,128]{1,0:T(8,128)S(1)}, u32[]{:S(2)}, u32[]{:S(2)}) collective-permute-start(f32[120,128]{1,0:T(8,128)S(1)} %get-tuple-element.123), channel_id=1, source_target_pairs={{0,112},{1,113},{2,114},{3,115},{4,116},{5,117},{6,118},{7,119},{8... | collective-permute-start | bytes 184328 | tf_op jit(solution)/shard_map/ppermute | solution.py:874
  27.7 4.6 %collective-permute-start.6 = (f32[80,128]{1,0:T(8,128)S(1)}, f32[80,128]{1,0:T(8,128)S(1)}, u32[]{:S(2)}, u32[]{:S(2)}) collective-permute-start(f32[80,128]{1,0:T(8,128)S(1)} %get-tuple-element.126), channel_id=1, source_target_pairs={{0,1},{1,0},{2,3},{3,2},{4,5},{5,4},{6,7},{7,6},{8,9},{9,8},{10,11... | collective-permute-start | bytes 122888 | tf_op jit(solution)/shard_map/ppermute | solution.py:873
  27.7 7.1 %collective-permute-start.7 = (f32[80,128]{1,0:T(8,128)S(1)}, f32[80,128]{1,0:T(8,128)S(1)}, u32[]{:S(2)}, u32[]{:S(2)}) collective-permute-start(f32[80,128]{1,0:T(8,128)S(1)} %get-tuple-element.127), channel_id=1, source_target_pairs={{0,15},{1,2},{2,1},{3,4},{4,3},{5,6},{6,5},{7,8},{8,7},{9,10},{10,... | collective-permute-start | bytes 122888 | tf_op jit(solution)/shard_map/ppermute | solution.py:874
  53.5 6.8 %collective-permute-start.8 = (f32[80,256]{1,0:T(8,128)S(1)}, f32[80,256]{1,0:T(8,128)S(1)}, u32[]{:S(2)}, u32[]{:S(2)}) collective-permute-start(f32[80,256]{1,0:T(8,128)S(1)} %get-tuple-element.141), channel_id=1, source_target_pairs={{0,1},{1,0},{2,3},{3,2},{4,5},{5,4},{6,7},{7,6},{8,9},{9,8},{10,11... | collective-permute-start | bytes 245768 | tf_op jit(solution)/shard_map/ppermute | solution.py:873
  53.5 7.4 %collective-permute-start.9 = (f32[80,256]{1,0:T(8,128)S(1)}, f32[80,256]{1,0:T(8,128)S(1)}, u32[]{:S(2)}, u32[]{:S(2)}) collective-permute-start(f32[80,256]{1,0:T(8,128)S(1)} %get-tuple-element.142), channel_id=1, source_target_pairs={{0,31},{1,2},{2,1},{3,4},{4,3},{5,6},{6,5},{7,24},{8,23},{9,10},{1... | collective-permute-start | bytes 245768 | tf_op jit(solution)/shard_map/ppermute | solution.py:874
  62.3 8.1 %collective-permute-start.12 = (f32[80,128]{1,0:T(8,128)S(1)}, f32[80,128]{1,0:T(8,128)S(1)}, u32[]{:S(2)}, u32[]{:S(2)}) collective-permute-start(f32[80,128]{1,0:T(8,128)S(1)} %get-tuple-element.155), channel_id=1, source_target_pairs={{0,1},{1,0},{2,3},{3,2},{4,5},{5,4},{6,7},{7,6},{8,9},{9,8},{10,11... | collective-permute-start | bytes 122888 | tf_op jit(solution)/shard_map/ppermute | solution.py:873
  62.4 8.0 %collective-permute-start.13 = (f32[80,128]{1,0:T(8,128)S(1)}, f32[80,128]{1,0:T(8,128)S(1)}, u32[]{:S(2)}, u32[]{:S(2)}) collective-permute-start(f32[80,128]{1,0:T(8,128)S(1)} %get-tuple-element.156), channel_id=1, source_target_pairs={{0,31},{1,2},{2,1},{3,4},{4,3},{5,6},{6,5},{7,24},{8,23},{9,10},{1... | collective-permute-start | bytes 122888 | tf_op jit(solution)/shard_map/ppermute | solution.py:874
  66.7 7.9 %collective-permute-start.10 = (f32[80,128]{1,0:T(8,128)S(1)}, f32[80,128]{1,0:T(8,128)S(1)}, u32[]{:S(2)}, u32[]{:S(2)}) collective-permute-start(f32[80,128]{1,0:T(8,128)S(1)} %get-tuple-element.151), channel_id=1, source_target_pairs={{0,16},{1,17},{2,18},{3,19},{4,20},{5,21},{6,22},{7,23},{8,24},{9,... | collective-permute-start | bytes 122888 | tf_op jit(solution)/shard_map/ppermute | solution.py:873
  66.7 7.9 %collective-permute-start.11 = (f32[80,128]{1,0:T(8,128)S(1)}, f32[80,128]{1,0:T(8,128)S(1)}, u32[]{:S(2)}, u32[]{:S(2)}) collective-permute-start(f32[80,128]{1,0:T(8,128)S(1)} %get-tuple-element.152), channel_id=1, source_target_pairs={{0,112},{1,113},{2,114},{3,115},{4,116},{5,117},{6,118},{7,119},{8... | collective-permute-start | bytes 122888 | tf_op jit(solution)/shard_map/ppermute | solution.py:874
  71.4 5.0 %collective-permute-start.14 = (f32[72,128]{1,0:T(8,128)S(1)}, f32[72,128]{1,0:T(8,128)S(1)}, u32[]{:S(2)}, u32[]{:S(2)}) collective-permute-start(f32[72,128]{1,0:T(8,128)S(1)} %get-tuple-element.164), channel_id=1, source_target_pairs={{0,1},{1,0},{2,3},{3,2},{4,5},{5,4},{6,7},{7,6},{8,9},{9,8},{10,11... | collective-permute-start | bytes 110600 | tf_op jit(solution)/shard_map/ppermute | solution.py:873
  71.5 6.8 %collective-permute-start.15 = (f32[72,128]{1,0:T(8,128)S(1)}, f32[72,128]{1,0:T(8,128)S(1)}, u32[]{:S(2)}, u32[]{:S(2)}) collective-permute-start(f32[72,128]{1,0:T(8,128)S(1)} %get-tuple-element.165), channel_id=1, source_target_pairs={{0,31},{1,2},{2,1},{3,4},{4,3},{5,6},{6,5},{7,24},{8,23},{9,10},{1... | collective-permute-start | bytes 110600 | tf_op jit(solution)/shard_map/ppermute | solution.py:874
  79.1 5.1 %collective-permute-start.16 = (f32[72,256]{1,0:T(8,128)S(1)}, f32[72,256]{1,0:T(8,128)S(1)}, u32[]{:S(2)}, u32[]{:S(2)}) collective-permute-start(f32[72,256]{1,0:T(8,128)S(1)} %get-tuple-element.176), channel_id=1, source_target_pairs={{0,1},{1,0},{2,3},{3,2},{4,5},{5,4},{6,7},{7,6},{8,9},{9,8},{10,11... | collective-permute-start | bytes 221192 | tf_op jit(solution)/shard_map/ppermute | solution.py:873
  79.2 7.2 %collective-permute-start.17 = (f32[72,256]{1,0:T(8,128)S(1)}, f32[72,256]{1,0:T(8,128)S(1)}, u32[]{:S(2)}, u32[]{:S(2)}) collective-permute-start(f32[72,256]{1,0:T(8,128)S(1)} %get-tuple-element.177), channel_id=1, source_target_pairs={{0,31},{1,2},{2,1},{3,4},{4,3},{5,6},{6,5},{7,24},{8,23},{9,10},{1... | collective-permute-start | bytes 221192 | tf_op jit(solution)/shard_map/ppermute | solution.py:874
  87.8 2.1 %collective-permute-start.18 = (f32[72,128]{1,0:T(8,128)S(1)}, f32[72,128]{1,0:T(8,128)S(1)}, u32[]{:S(2)}, u32[]{:S(2)}) collective-permute-start(f32[72,128]{1,0:T(8,128)S(1)} %get-tuple-element.186), channel_id=1, source_target_pairs={{0,1},{1,0},{2,3},{3,2},{4,5},{5,4},{6,7},{7,6},{8,9},{9,8},{10,11... | collective-permute-start | bytes 110600 | tf_op jit(solution)/shard_map/ppermute | solution.py:873
  87.9 7.3 %collective-permute-start.19 = (f32[72,128]{1,0:T(8,128)S(1)}, f32[72,128]{1,0:T(8,128)S(1)}, u32[]{:S(2)}, u32[]{:S(2)}) collective-permute-start(f32[72,128]{1,0:T(8,128)S(1)} %get-tuple-element.187), channel_id=1, source_target_pairs={{0,15},{1,2},{2,1},{3,4},{4,3},{5,6},{6,5},{7,8},{8,7},{9,10},{10,... | collective-permute-start | bytes 110600 | tf_op jit(solution)/shard_map/ppermute | solution.py:874
  96.9 4.5 %collective-permute-start.20 = (f32[152,128]{1,0:T(8,128)S(1)}, f32[152,128]{1,0:T(8,128)S(1)}, u32[]{:S(2)}, u32[]{:S(2)}) collective-permute-start(f32[152,128]{1,0:T(8,128)S(1)} %get-tuple-element.193), channel_id=1, source_target_pairs={{0,16},{1,17},{2,18},{3,19},{4,20},{5,21},{6,22},{7,23},{8,24},{9,... | collective-permute-start | bytes 233480 | tf_op jit(solution)/shard_map/ppermute | solution.py:873
  97.0 6.6 %collective-permute-start.21 = (f32[152,128]{1,0:T(8,128)S(1)}, f32[152,128]{1,0:T(8,128)S(1)}, u32[]{:S(2)}, u32[]{:S(2)}) collective-permute-start(f32[152,128]{1,0:T(8,128)S(1)} %get-tuple-element.194), channel_id=1, source_target_pairs={{0,112},{1,113},{2,114},{3,115},{4,116},{5,117},{6,118},{7,119},{8... | collective-permute-start | bytes 233480 | tf_op jit(solution)/shard_map/ppermute | solution.py:874
  103.7 4.5 %collective-permute-start.22 = (f32[72,128]{1,0:T(8,128)S(1)}, f32[72,128]{1,0:T(8,128)S(1)}, u32[]{:S(2)}, u32[]{:S(2)}) collective-permute-start(f32[72,128]{1,0:T(8,128)S(1)} %get-tuple-element.197.refs_5_), channel_id=1, source_target_pairs={{0,1},{1,0},{2,3},{3,2},{4,5},{5,4},{6,7},{7,6},{8,9},{9,8},{10,11... | collective-permute-start | bytes 110600 | tf_op jit(solution)/shard_map/ppermute | solution.py:873
  103.8 7.1 %collective-permute-start.23 = (f32[72,128]{1,0:T(8,128)S(1)}, f32[72,128]{1,0:T(8,128)S(1)}, u32[]{:S(2)}, u32[]{:S(2)}) collective-permute-start(f32[72,128]{1,0:T(8,128)S(1)} %get-tuple-element.200), channel_id=1, source_target_pairs={{0,15},{1,2},{2,1},{3,4},{4,3},{5,6},{6,5},{7,8},{8,7},{9,10},{10,... | collective-permute-start | bytes 110600 | tf_op jit(solution)/shard_map/ppermute | solution.py:874
